TPU v7x, 32 devices: a whole 2x2x4 slice. The times are simulated.
32 devices in a mesh: dp: 4 (over z), mp: 8 (over y, x, core).
Axes of the slice: x: 2, y: 2, z: 4, core: 2. Of those that a mesh axis runs over, the one named last changes fastest.
Arguments:
- inputs: bfloat16 [8, 1536, 2048], P('dp', 'mp'), may hold values from -6 to 6
- cotangent: bfloat16 [8, 1536, 2048], P('dp', 'mp'), may hold values from -12 to 12
- lengths: int32 [8, 8], P('dp'), may hold values from 1 to 1024, 1536 in all within a row
- w_query: float32 [2048, 2048], P('dp', 'mp'), may hold values from -0.125 to 0.125
- w_keyval: float32 [2048, 256], P('dp'), may hold values from -0.125 to 0.125
- w_out: float32 [2048, 2048], P('dp', 'mp'), may hold values from -0.5 to 0.5
- w_gate_up: float32 [2048, 2, 5632], P('dp', None, 'mp'), may hold values from -0.125 to 0.125
- w_down: float32 [2048, 5632], P('dp', 'mp'), may hold values from -0.078125 to 0.078125
- gains: float32 [2, 2048], replicated, may hold values from 0.35 to 3.3
- m_query: float32 [2048, 2048], P('dp', 'mp'), may hold values from -1330.215 to 1330.215
- m_keyval: float32 [2048, 256], P('dp'), may hold values from -5320.86 to 5320.86
- m_out: float32 [2048, 2048], P('dp', 'mp'), may hold values from -199.53226 to 199.53226
- m_gate_up: float32 [2048, 2, 5632], P('dp', None, 'mp'), may hold values from -199.53226 to 199.53226
- m_down: float32 [2048, 5632], P('dp', 'mp'), may hold values from -332.55374 to 332.55374
- m_gains: float32 [2, 2048], replicated, may hold values from -665.1075 to 665.1075
Outputs:
- output: bfloat16 [8, 1536, 2048], P('dp', 'mp')
- input_grad: bfloat16 [8, 1536, 2048], P('dp', 'mp')
- grad_query: float32 [2048, 2048], P('dp', 'mp')
- grad_keyval: float32 [2048, 256], P('dp')
- grad_out: float32 [2048, 2048], P('dp', 'mp')
- grad_gate_up: float32 [2048, 2, 5632], P('dp', None, 'mp')
- grad_down: float32 [2048, 5632], P('dp', 'mp')
- grad_gains: float32 [2, 2048], replicated
- moment_query: float32 [2048, 2048], P('dp', 'mp')
- moment_keyval: float32 [2048, 256], P('dp')
- moment_out: float32 [2048, 2048], P('dp', 'mp')
- moment_gate_up: float32 [2048, 2, 5632], P('dp', None, 'mp')
- moment_down: float32 [2048, 5632], P('dp', 'mp')
- moment_gains: float32 [2, 2048], replicated
- new_query: float32 [2048, 2048], P('dp', 'mp')
- new_keyval: float32 [2048, 256], P('dp')
- new_out: float32 [2048, 2048], P('dp', 'mp')
- new_gate_up: float32 [2048, 2, 5632], P('dp', None, 'mp')
- new_down: float32 [2048, 5632], P('dp', 'mp')
- new_gains: float32 [2, 2048], replicated
Inputs may be any that keep to these rules, and one draw needn't show every extreme that they name: Each row holds 8 lengths that add up to 1536, the largest exactly 1024.
All inputs are finite; a program needn't handle non-finite values.
Results may differ from a plain program's by a relative error of at most 0.025.
Values may be sent and summed in bfloat16 or wider, within the bound.
No kernel may reach another device: no remote copies, remote signals or barrier semaphores. Data moves between devices by JAX's collectives and lax.ppermute only.
A program may use at most 384 MiB of HBM per device.

v0:
```python
import jax
import jax.numpy as jnp
from jax import lax
from jax.sharding import PartitionSpec as P

FF_BLOCK = 352
QBLOCK = 512
NS_ITERS = 5


EPS = 1e-05
THETA = 10000.0
NS_A = 3.4445
NS_B = -4.775
NS_C = 2.0315
MUON_RATE = 0.8
GAIN_RATE = 0.002
DECAY = 0.5
HIGH = lax.Precision.HIGHEST
MASKED = -1e30


def doc_layout(doc_lengths, seq_len):
    ends = jnp.cumsum(doc_lengths)
    starts = ends - doc_lengths
    positions = jnp.arange(seq_len, dtype=jnp.int32)
    segment = jnp.sum((positions[:, None] >= ends[None, :]).astype(jnp.int32), axis=1)
    member = (
        segment[:, None] == jnp.arange(doc_lengths.shape[0], dtype=jnp.int32)[None, :]
    ).astype(jnp.int32)
    offset = positions - jnp.sum(member * starts[None, :], axis=1)
    return (segment, offset)


def rotary_tables(offset, half_dim):
    freqs = jnp.power(THETA, -jnp.arange(half_dim, dtype=jnp.float32) / half_dim)
    angle = offset.astype(jnp.float32)[:, None] * freqs[None, :]
    return (jnp.cos(angle), jnp.sin(angle))


def rotate(vector, cosine, sine):
    half_dim = vector.shape[-1] // 2
    first_half = vector[..., :half_dim]
    second_half = vector[..., half_dim:]
    return jnp.concatenate(
        [first_half * cosine - second_half * sine, second_half * cosine + first_half * sine],
        axis=-1,
    )


def inverse_scale(vector):
    return lax.rsqrt(jnp.mean(vector * vector, axis=-1, keepdims=True) + EPS)


def norm_back(grad_rows, value_rows, scale_rows, gain_row):
    weighted = grad_rows * gain_row
    cubed = scale_rows * scale_rows * scale_rows
    return scale_rows * weighted - value_rows * cubed * jnp.mean(
        weighted * value_rows, axis=-1, keepdims=True
    )


def plain_dot(left, right):
    return jnp.dot(left, right, preferred_element_type=jnp.float32)


def rows_dot(left, right):
    return lax.dot_general(
        left, right, (((1,), (1,)), ((), ())), preferred_element_type=jnp.float32
    )


def outer_sum(left, right):
    return lax.dot_general(
        left, right, (((0,), (0,)), ((), ())), preferred_element_type=jnp.float32
    )


def block_scores(query_block, key_rows, allowed, score_scale):
    scores = (
        jnp.einsum("qhd,kd->hqk", query_block, key_rows, preferred_element_type=jnp.float32)
        * score_scale
    )
    return jnp.where(allowed[None], scores, MASKED)


def block_gram(matrix):
    return jnp.einsum("rnb,rnc->nbc", matrix, matrix, precision=HIGH)


def gram_sum(matrices):
    return (
        lax.psum(block_gram(matrices[0]).astype(jnp.bfloat16), "dp").astype(jnp.float32),
        lax.psum(block_gram(matrices[1]).astype(jnp.bfloat16), "dp").astype(jnp.float32),
        lax.psum(block_gram(matrices[2]).astype(jnp.bfloat16), "dp").astype(jnp.float32),
        lax.psum(block_gram(matrices[3]).astype(jnp.bfloat16), "dp").astype(jnp.float32),
        lax.psum(block_gram(matrices[4]).astype(jnp.bfloat16), "dp").astype(jnp.float32),
    )


def newton_step(current_block, gram_block):
    poly = NS_B * gram_block + NS_C * jnp.einsum(
        "nab,nbc->nac", gram_block, gram_block, precision=HIGH
    )
    return NS_A * current_block + jnp.einsum("rnb,nbc->rnc", current_block, poly, precision=HIGH)


def orthogonalize(matrices):
    first_grams = gram_sum(matrices)
    norms = [
        jnp.sqrt(jnp.sum(jnp.diagonal(gram_block, axis1=1, axis2=2), axis=1)) + 1e-07
        for gram_block in first_grams
    ]
    current = [matrix / norm_item[None, :, None] for matrix, norm_item in zip(matrices, norms)]
    grams = [
        gram_block / (norm_item * norm_item)[:, None, None]
        for gram_block, norm_item in zip(first_grams, norms)
    ]
    for iteration in range(NS_ITERS):
        if iteration > 0:
            grams = gram_sum(current)
        current = [
            newton_step(current_block, gram_block)
            for current_block, gram_block in zip(current, grams)
        ]
    return current


def shards(
    inputs,
    cotangent,
    lengths,
    w_query,
    w_keyval,
    w_out,
    w_gate_up,
    w_down,
    gains,
    m_query,
    m_keyval,
    m_out,
    m_gate_up,
    m_down,
    m_gains,
):
    batches, own_rows, model_width = inputs.shape
    head_dim = w_keyval.shape[1] // 2
    half_dim = head_dim // 2
    heads_here = w_query.shape[1] // head_dim
    units_here = w_down.shape[1]
    score_scale = head_dim ** (-0.5)
    row_start = lax.axis_index("mp") * own_rows
    full_inputs, full_cot = (
        lax.all_gather(inputs, "mp", axis=1, tiled=True),
        lax.all_gather(cotangent, "mp", axis=1, tiled=True),
    )
    seq_len = full_inputs.shape[1]
    full_query, full_keyval, full_out, full_gate_up, full_down = (
        lax.all_gather(w_query.astype(jnp.bfloat16), "dp", axis=0, tiled=True),
        lax.all_gather(w_keyval.astype(jnp.bfloat16), "dp", axis=0, tiled=True),
        lax.all_gather(w_out.astype(jnp.bfloat16), "dp", axis=0, tiled=True),
        lax.all_gather(w_gate_up.astype(jnp.bfloat16), "dp", axis=0, tiled=True),
        lax.all_gather(w_down.astype(jnp.bfloat16), "dp", axis=0, tiled=True),
    )
    gate_up_flat = full_gate_up.reshape(model_width, 2 * units_here)
    positions = jnp.arange(seq_len, dtype=jnp.int32)
    row_block = min(QBLOCK, seq_len)
    acc_query = jnp.zeros(full_query.shape, jnp.float32)
    acc_keyval = jnp.zeros(full_keyval.shape, jnp.float32)
    acc_out = jnp.zeros(full_out.shape, jnp.float32)
    acc_gate_up = jnp.zeros(gate_up_flat.shape, jnp.float32)
    acc_down = jnp.zeros(full_down.shape, jnp.float32)
    gain_part = jnp.zeros((2, model_width), jnp.float32)
    output_rows = []
    input_rows = []
    for batch_index in range(batches):
        x_full = full_inputs[batch_index].astype(jnp.float32)
        x_rows = inputs[batch_index].astype(jnp.float32)
        cot_full = full_cot[batch_index]
        segment, offset = doc_layout(lengths[batch_index], seq_len)
        cosine, sine = rotary_tables(offset, half_dim)
        normed = (x_full * inverse_scale(x_full) * gains[0]).astype(jnp.bfloat16)
        keyval = plain_dot(normed, full_keyval)
        key_rows = rotate(keyval[:, :head_dim], cosine, sine).astype(jnp.bfloat16)
        value_rows = keyval[:, head_dim:].astype(jnp.bfloat16)
        queries = plain_dot(normed, full_query).reshape(seq_len, heads_here, head_dim)
        queries = rotate(queries, cosine[:, None, :], sine[:, None, :]).astype(jnp.bfloat16)
        context_parts = []
        log_totals = []
        for first_row in range(0, seq_len, row_block):
            query_rows = slice(first_row, first_row + row_block)
            allowed = (segment[query_rows, None] == segment[None, :]) & (
                positions[query_rows, None] >= positions[None, :]
            )
            scores = block_scores(queries[query_rows], key_rows, allowed, score_scale)
            top_score = jnp.max(scores, axis=-1, keepdims=True)
            powers = jnp.exp(scores - top_score)
            row_total = jnp.sum(powers, axis=-1, keepdims=True)
            attn_probs = (powers / row_total).astype(jnp.bfloat16)
            log_totals.append(top_score + jnp.log(row_total))
            context_parts.append(
                jnp.einsum(
                    "hqk,kd->qhd", attn_probs, value_rows, preferred_element_type=jnp.float32
                ).astype(jnp.bfloat16)
            )
        context = jnp.concatenate(context_parts, axis=0).reshape(seq_len, heads_here * head_dim)
        attn_part = rows_dot(context, full_out)
        attn_full = lax.psum(attn_part.astype(jnp.bfloat16), "mp").astype(jnp.float32)
        mid_full = x_full + attn_full
        mid_scale = inverse_scale(mid_full)
        normed_mid = (mid_full * mid_scale * gains[1]).astype(jnp.bfloat16)
        mid_rows = lax.dynamic_slice_in_dim(mid_full, row_start, own_rows, 0)
        mid_rows_scale = lax.dynamic_slice_in_dim(mid_scale, row_start, own_rows, 0)
        gate_up = plain_dot(normed_mid, gate_up_flat)
        gate = gate_up[:, :units_here]
        upward = gate_up[:, units_here:]
        sigma = jax.nn.sigmoid(gate)
        swish = gate * sigma
        hidden = (swish * upward).astype(jnp.bfloat16)
        mlp_rows = lax.psum_scatter(
            rows_dot(hidden, full_down).astype(jnp.bfloat16), "mp", scatter_dimension=0, tiled=True
        ).astype(jnp.float32)
        output_rows.append((mid_rows + mlp_rows).astype(jnp.bfloat16))
        d_hidden = plain_dot(cot_full, full_down)
        d_gate = d_hidden * upward * sigma * (1.0 + gate * (1.0 - sigma))
        d_up = d_hidden * swish
        d_gate_up = jnp.concatenate([d_gate, d_up], axis=1).astype(jnp.bfloat16)
        acc_down = acc_down + outer_sum(cot_full, hidden)
        acc_gate_up = acc_gate_up + outer_sum(normed_mid, d_gate_up)
        d_mid_part = rows_dot(d_gate_up, gate_up_flat)
        d_mid_full = lax.psum(d_mid_part.astype(jnp.bfloat16), "mp").astype(jnp.float32)
        resid_full = cot_full.astype(jnp.float32) + norm_back(
            d_mid_full, mid_full, mid_scale, gains[1]
        )
        d_res_rows = lax.dynamic_slice_in_dim(resid_full, row_start, own_rows, 0)
        d_mid_rows = lax.dynamic_slice_in_dim(d_mid_full, row_start, own_rows, 0)
        resid_low = resid_full.astype(jnp.bfloat16)
        gain_mid = jnp.sum(d_mid_rows * mid_rows * mid_rows_scale, axis=0)
        acc_out = acc_out + outer_sum(resid_low, context)
        d_context = (
            plain_dot(resid_low, full_out)
            .astype(jnp.bfloat16)
            .reshape(seq_len, heads_here, head_dim)
        )
        d_keys = jnp.zeros((seq_len, head_dim), jnp.float32)
        d_values = jnp.zeros((seq_len, head_dim), jnp.float32)
        d_query_parts = []
        for block_number, first_row in enumerate(range(0, seq_len, row_block)):
            query_rows = slice(first_row, first_row + row_block)
            allowed = (segment[query_rows, None] == segment[None, :]) & (
                positions[query_rows, None] >= positions[None, :]
            )
            scores = block_scores(queries[query_rows], key_rows, allowed, score_scale)
            probs_full = jnp.exp(scores - log_totals[block_number])
            probs_low = probs_full.astype(jnp.bfloat16)
            d_block = d_context[query_rows]
            d_probs = jnp.einsum(
                "qhd,kd->hqk", d_block, value_rows, preferred_element_type=jnp.float32
            )
            centre = jnp.sum(d_probs * probs_full, axis=-1, keepdims=True)
            d_scores = (probs_full * (d_probs - centre)).astype(jnp.bfloat16)
            d_values = d_values + jnp.einsum(
                "hqk,qhd->kd", probs_low, d_block, preferred_element_type=jnp.float32
            )
            d_keys = (
                d_keys
                + jnp.einsum(
                    "hqk,qhd->kd", d_scores, queries[query_rows], preferred_element_type=jnp.float32
                )
                * score_scale
            )
            d_query_parts.append(
                jnp.einsum("hqk,kd->qhd", d_scores, key_rows, preferred_element_type=jnp.float32)
                * score_scale
            )
        d_queries = jnp.concatenate(d_query_parts, axis=0)
        d_queries = (
            rotate(d_queries, cosine[:, None, :], -sine[:, None, :])
            .reshape(seq_len, heads_here * head_dim)
            .astype(jnp.bfloat16)
        )
        acc_query = acc_query + outer_sum(normed, d_queries)
        d_keyval = lax.psum(
            jnp.concatenate([d_keys, d_values], axis=1).astype(jnp.bfloat16), "mp"
        ).astype(jnp.float32)
        d_keyval = jnp.concatenate(
            [rotate(d_keyval[:, :head_dim], cosine, -sine), d_keyval[:, head_dim:]], axis=1
        ).astype(jnp.bfloat16)
        acc_keyval = acc_keyval + outer_sum(normed, d_keyval)
        d_keyval_rows = lax.dynamic_slice_in_dim(d_keyval, row_start, own_rows, 0)
        d_norm_rows = lax.psum_scatter(
            rows_dot(d_queries, full_query).astype(jnp.bfloat16),
            "mp",
            scatter_dimension=0,
            tiled=True,
        ).astype(jnp.float32) + rows_dot(d_keyval_rows, full_keyval)
        x_scale = inverse_scale(x_rows)
        input_rows.append(
            (d_res_rows + norm_back(d_norm_rows, x_rows, x_scale, gains[0])).astype(jnp.bfloat16)
        )
        gain_input = jnp.sum(d_norm_rows * x_rows * x_scale, axis=0)
        gain_part = gain_part + jnp.stack([gain_input, gain_mid], axis=0)
    grad_query, grad_keyval, grad_out, grad_gate_up, grad_down = (
        lax.psum_scatter(
            acc_query.astype(jnp.bfloat16), "dp", scatter_dimension=0, tiled=True
        ).astype(jnp.float32),
        lax.psum_scatter(
            acc_keyval.astype(jnp.bfloat16), "dp", scatter_dimension=0, tiled=True
        ).astype(jnp.float32),
        lax.psum_scatter(
            acc_out.astype(jnp.bfloat16), "dp", scatter_dimension=0, tiled=True
        ).astype(jnp.float32),
        lax.psum_scatter(
            acc_gate_up.reshape(full_gate_up.shape).astype(jnp.bfloat16),
            "dp",
            scatter_dimension=0,
            tiled=True,
        ).astype(jnp.float32),
        lax.psum_scatter(
            acc_down.astype(jnp.bfloat16), "dp", scatter_dimension=0, tiled=True
        ).astype(jnp.float32),
    )
    grad_gains = lax.psum(gain_part, ("dp", "mp"))
    grad_list = (grad_query, grad_keyval, grad_out, grad_gate_up, grad_down)
    weight_list = (w_query, w_keyval, w_out, w_gate_up, w_down)
    old_list = (m_query, m_keyval, m_out, m_gate_up, m_down)
    width_list = (head_dim, 2 * head_dim, head_dim, FF_BLOCK, FF_BLOCK)
    moments = [DECAY * old_item + grad_item for old_item, grad_item in zip(old_list, grad_list)]
    matrices = [
        moment.reshape(moment.shape[0], -1, block_width)
        for moment, block_width in zip(moments, width_list)
    ]
    ortho = orthogonalize(matrices)
    news = [
        weight - MUON_RATE * ortho_item.reshape(weight.shape)
        for weight, ortho_item in zip(weight_list, ortho)
    ]
    moment_gains = DECAY * m_gains + grad_gains
    new_gains = gains - GAIN_RATE * moment_gains
    return (
        jnp.stack(output_rows, axis=0),
        jnp.stack(input_rows, axis=0),
        grad_query,
        grad_keyval,
        grad_out,
        grad_gate_up,
        grad_down,
        grad_gains,
        moments[0],
        moments[1],
        moments[2],
        moments[3],
        moments[4],
        moment_gains,
        news[0],
        news[1],
        news[2],
        news[3],
        news[4],
        new_gains,
    )


def solution(mesh):
    placed = (
        P("dp", "mp", None),
        P("dp", "mp", None),
        P("dp", None),
        P("dp", "mp"),
        P("dp", None),
        P("dp", "mp"),
        P("dp", None, "mp"),
        P("dp", "mp"),
        P(),
        P("dp", "mp"),
        P("dp", None),
        P("dp", "mp"),
        P("dp", None, "mp"),
        P("dp", "mp"),
        P(),
    )
    return jax.shard_map(
        shards,
        mesh=mesh,
        in_specs=placed,
        out_specs=(
            P("dp", "mp", None),
            P("dp", "mp", None),
            P("dp", "mp"),
            P("dp", None),
            P("dp", "mp"),
            P("dp", None, "mp"),
            P("dp", "mp"),
            P(),
            P("dp", "mp"),
            P("dp", None),
            P("dp", "mp"),
            P("dp", None, "mp"),
            P("dp", "mp"),
            P(),
            P("dp", "mp"),
            P("dp", None),
            P("dp", "mp"),
            P("dp", None, "mp"),
            P("dp", "mp"),
            P(),
        ),
        check_vma=False,
    )
```

profile of v0, /device:TPU:0, one launch (start us, length us, event | category | flops | bytes accessed | tf_op | source)
XLA Modules:
  0.0 2203.6 jit_solution(10827743098894339034)
XLA Ops:
  18.4 22.4 %all-gather.12.cloned.1.call-done = bf16[2048,256]{1,0:T(8,128)(2,1)} async-done(((bf16[512,256]{1,0:T(8,128)(2,1)}), bf16[2048,256]{1,0:T(8,128)(2,1)}) %all-gather.12.cloned.1.call-update) | async-done | bytes 1048592 | tf_op jit(solution)/shard_map/all_gather | solution.py:159
  42.3 72.1 %all-gather.8.cloned.1.call-done = bf16[2,1536,2048]{2,1,0:T(8,128)(2,1)} async-done(((bf16[2,192,2048]{2,1,0:T(8,128)(2,1)}), bf16[2,1536,2048]{2,1,0:T(8,128)(2,1)}) %all-gather.8.cloned.1.call-update) | async-done | bytes 12582928 | tf_op jit(solution)/shard_map/all_gather | solution.py:154
  120.8 23.8 %all-gather.10.cloned.1.call-done = bf16[2048,256]{1,0:T(8,128)(2,1)} async-done(((bf16[512,256]{1,0:T(8,128)(2,1)}), bf16[2048,256]{1,0:T(8,128)(2,1)}) %all-gather.10.cloned.1.call-update) | async-done | bytes 1048592 | tf_op jit(solution)/shard_map/all_gather | solution.py:160
  212.7 166.0 %all-reduce.21.cloned.1.call-done = (bf16[1536,2048]{1,0:T(8,128)(2,1)}, bf16[1536,2048]{1,0:T(8,128)(2,1)}) async-done(((bf16[1536,2048]{1,0:T(8,128)(2,1)}, bf16[1536,2048]{1,0:T(8,128)(2,1)}), (bf16[1536,2048]{1,0:T(8,128)(2,1)}, bf16[1536,2048]{1,0:T(8,128)(2,1)})) %all-reduce.21.cloned.1.call-update) | async-done | bytes 12582928 | tf_op jit(solution)/shard_map/psum | solution.py:208
  378.7 9.9 multiply_reduce_fusion.3
  388.7 98.9 %all-gather.16.cloned.1.call-done = bf16[2048,2,704]{0,2,1:T(8,128)(2,1)} async-done(((bf16[512,2,704]{0,2,1:T(8,128)(2,1)}), bf16[2048,2,704]{0,2,1:T(8,128)(2,1)}) %all-gather.16.cloned.1.call-update) | async-done | bytes 5767184 | tf_op jit(solution)/shard_map/all_gather | solution.py:162
  487.6 16.5 fusion.421
  504.1 43.1 %all-gather.18.cloned.1.call-done = bf16[2048,704]{0,1:T(8,128)(2,1)} async-done(((bf16[512,704]{0,1:T(8,128)(2,1)}), bf16[2048,704]{0,1:T(8,128)(2,1)}) %all-gather.18.cloned.1.call-update) | async-done | bytes 2883600 | tf_op jit(solution)/shard_map/all_gather | solution.py:163
  547.3 72.9 %all-gather.20.cloned.1.call-done = bf16[2,1536,2048]{2,1,0:T(8,128)(2,1)} async-done(((bf16[2,192,2048]{2,1,0:T(8,128)(2,1)}), bf16[2,1536,2048]{2,1,0:T(8,128)(2,1)}) %all-gather.20.cloned.1.call-update) | async-done | bytes 12582928 | tf_op jit(solution)/shard_map/all_gather | solution.py:155
  620.2 12.0 multiply_convert_fusion.3
  632.2 12.3 convolution_convert_fusion.4
  644.6 14.8 fusion.420
  659.4 11.5 multiply_convert_fusion.5
  672.9 12.1 convolution_convert_fusion.5
  686.7 9.3 fusion.54
  696.0 161.9 %all-reduce.19.cloned.1.call-done = (bf16[1536,2048]{1,0:T(8,128)(2,1)}, bf16[1536,2048]{1,0:T(8,128)(2,1)}) async-done(((bf16[1536,2048]{1,0:T(8,128)(2,1)}, bf16[1536,2048]{1,0:T(8,128)(2,1)}), (bf16[1536,2048]{1,0:T(8,128)(2,1)}, bf16[1536,2048]{1,0:T(8,128)(2,1)})) %all-reduce.19.cloned.1.call-update) | async-done | bytes 12582928 | tf_op jit(solution)/shard_map/psum | solution.py:231
  857.9 14.0 multiply_reduce_fusion.1
  872.0 31.5 %subtract_add_fusion.1 = (f32[1536,2048]{1,0:T(8,128)}, f32[1536,2048]{1,0:T(8,128)}, f32[1536,2048]{1,0:T(8,128)}, f32[1536,2048]{1,0:T(8,128)}) fusion(f32[1536]{0:T(1024)S(1)} %broadcast_multiply_fusion.1, f32[1536]{0:T(1024)S(1)} %get-tuple-element.123, bf16[1536,2048]{1,0:T(8,128)(2,1)} %get-tuple-element.36, f32[2048]{0:T(1024)S(1)} %bitcast.800, ...), kind=kLoop, calls=%fused_computation.27 | loop fusion | flops 69206016 | bytes 100708352 | tf_op jit(solution)/shard_map/add | solution.py:232
  903.6 6.6 fusion.114
  995.6 6.5 fusion.33
  1010.9 11.3 fusion.98
  1030.9 6.8 fusion.74
  1043.1 27.0 %all-reduce.17.cloned.1.call-done = (bf16[1536,256]{0,1:T(8,128)(2,1)}, bf16[1536,256]{0,1:T(8,128)(2,1)}) async-done(((bf16[1536,256]{0,1:T(8,128)(2,1)}, bf16[1536,256]{0,1:T(8,128)(2,1)}), (bf16[1536,256]{0,1:T(8,128)(2,1)}, bf16[1536,256]{0,1:T(8,128)(2,1)})) %all-reduce.17.cloned.1.call-update) | async-done | bytes 1572880 | tf_op jit(solution)/shard_map/psum | solution.py:283
  1077.9 6.4 fusion.36
  1088.9 16.3 fusion.100
  1110.9 6.4 fusion.110
  1117.4 17.2 add_convert_fusion
  1141.7 16.8 reduce-scatter.22.cloned.1.call-done
  1161.9 25.4 %reduce-scatter.18.cloned.1.call-done = bf16[512,256]{1,0:T(8,128)(2,1)} async-done(((bf16[2048,256]{1,0:T(8,128)(2,1)}), bf16[512,256]{1,0:T(8,128)(2,1)}) %reduce-scatter.18.cloned.1.call-update) | async-done | bytes 262160 | tf_op jit(solution)/shard_map/reduce_scatter | solution.py:304
  1189.5 26.5 %reduce-scatter.20.cloned.1.call-done = bf16[512,256]{1,0:T(8,128)(2,1)} async-done(((bf16[2048,256]{1,0:T(8,128)(2,1)}), bf16[512,256]{1,0:T(8,128)(2,1)}) %reduce-scatter.20.cloned.1.call-update) | async-done | bytes 262160 | tf_op jit(solution)/shard_map/reduce_scatter | solution.py:307
  1221.6 97.4 %reduce-scatter.24.cloned.1.call-done = bf16[512,2,704]{0,2,1:T(8,128)(2,1)} async-done(((bf16[2048,2,704]{0,2,1:T(8,128)(2,1)}), bf16[512,2,704]{0,2,1:T(8,128)(2,1)}) %reduce-scatter.24.cloned.1.call-update) | async-done | bytes 1441808 | tf_op jit(solution)/shard_map/reduce_scatter | solution.py:313
  1331.2 81.4 %all-reduce.31.cloned.1.call-done = (bf16[2,128,128]{2,1,0:T(8,128)(2,1)}, bf16[1,256,256]{2,1,0:T(8,128)(2,1)}, bf16[2,128,128]{2,1,0:T(8,128)(2,1)}, bf16[4,352,352]{2,1,0:T(8,128)(2,1)}, bf16[2,352,352]{2,1,0:T(8,128)(2,1)}) async-done(((bf16[2,128,128]{2,1,0:T(8,128)(2,1)}, bf16[1,256,256]{2,1,0:T(8,128)(2,1)}, bf16[2,128,128]{2,1,0:T(8,128)(2,1)}, bf16[4,352,352]{2,1,0:T(8,128)(2,1)}, ...) | async-done | bytes 1749008 | tf_op jit(solution)/shard_map/psum | solution.py:93
  1412.7 25.2 %copy.341 = f32[2,352,352]{0,2,1:T(8,128)} copy(bf16[2,352,352]{2,1,0:T(8,128)(2,1)} %get-tuple-element.64) | data formatting | bytes 1486848 | tf_op jit(solution)/shard_map/convert_element_type | solution.py:97
  1437.9 9.9 gather_fusion.4
  1456.3 24.5 %copy.335 = f32[4,352,352]{0,2,1:T(8,128)} copy(bf16[4,352,352]{2,1,0:T(8,128)(2,1)S(1)} %copy-done.121) | data formatting | bytes 2973696 | tf_op jit(solution)/shard_map/convert_element_type | solution.py:96
  1480.8 10.3 gather_fusion.3
  1536.1 79.7 %all-reduce.29.cloned.1.call-done = (bf16[2,128,128]{2,1,0:T(8,128)(2,1)}, bf16[1,256,256]{2,1,0:T(8,128)(2,1)}, bf16[2,128,128]{2,1,0:T(8,128)(2,1)}, bf16[4,352,352]{2,1,0:T(8,128)(2,1)}, bf16[2,352,352]{2,1,0:T(8,128)(2,1)}) async-done(((bf16[2,128,128]{2,1,0:T(8,128)(2,1)}, bf16[1,256,256]{2,1,0:T(8,128)(2,1)}, bf16[2,128,128]{2,1,0:T(8,128)(2,1)}, bf16[4,352,352]{2,1,0:T(8,128)(2,1)}, ...) | async-done | bytes 1749008 | tf_op jit(solution)/shard_map/psum | solution.py:93
  1642.6 9.1 convolution_convert_fusion.7
  1651.8 9.1 convolution_convert_fusion.6
  1676.5 9.0 convert_element_type.567
  1692.4 30.2 %all-reduce.27.cloned.1.call-done = (bf16[2,128,128]{2,1,0:T(8,128)(2,1)}, bf16[1,256,256]{2,1,0:T(8,128)(2,1)}, bf16[2,128,128]{2,1,0:T(8,128)(2,1)}, bf16[4,352,352]{2,1,0:T(8,128)(2,1)}, bf16[2,352,352]{2,1,0:T(8,128)(2,1)}) async-done(((bf16[2,128,128]{2,1,0:T(8,128)(2,1)}, bf16[1,256,256]{2,1,0:T(8,128)(2,1)}, bf16[2,128,128]{2,1,0:T(8,128)(2,1)}, bf16[4,352,352]{2,1,0:T(8,128)(2,1)}, ...) | async-done | bytes 1749008 | tf_op jit(solution)/shard_map/psum | solution.py:93
  1755.6 31.5 %reduce-scatter.10.cloned.1.call-done = bf16[192,2048]{1,0:T(8,128)(2,1)} async-done(((bf16[1536,2048]{1,0:T(8,128)(2,1)}), bf16[192,2048]{1,0:T(8,128)(2,1)}) %reduce-scatter.10.cloned.1.call-update) | async-done | bytes 786448 | tf_op jit(solution)/shard_map/reduce_scatter | solution.py:220
  1790.5 61.6 %reduce-scatter.12.cloned.1.call-done = bf16[192,2048]{1,0:T(8,128)(2,1)} async-done(((bf16[1536,2048]{1,0:T(8,128)(2,1)}), bf16[192,2048]{1,0:T(8,128)(2,1)}) %reduce-scatter.12.cloned.1.call-update) | async-done | bytes 786448 | tf_op jit(solution)/shard_map/reduce_scatter | solution.py:220
  1856.0 61.7 %reduce-scatter.16.cloned.1.call-done = bf16[192,2048]{1,0:T(8,128)(2,1)} async-done(((bf16[1536,2048]{1,0:T(8,128)(2,1)}), bf16[192,2048]{1,0:T(8,128)(2,1)}) %reduce-scatter.16.cloned.1.call-update) | async-done | bytes 786448 | tf_op jit(solution)/shard_map/reduce_scatter | solution.py:291
  1920.9 61.9 %reduce-scatter.14.cloned.1.call-done = bf16[192,2048]{1,0:T(8,128)(2,1)} async-done(((bf16[1536,2048]{1,0:T(8,128)(2,1)}), bf16[192,2048]{1,0:T(8,128)(2,1)}) %reduce-scatter.14.cloned.1.call-update) | async-done | bytes 786448 | tf_op jit(solution)/shard_map/reduce_scatter | solution.py:291
  1987.6 43.0 %psum.230 = f32[2,2048]{1,0:T(2,128)S(1)} all-reduce(f32[2,2048]{1,0:T(2,128)S(1)} %maximum_add_fusion), channel_id=1, replica_groups=mesh['dp'=4,'mp'=8] {'dp','mp'}, use_global_device_ids=true, to_apply=%region_53.54 | all-reduce | flops 4096 | bytes 32768 | tf_op jit(solution)/shard_map/psum | solution.py:323
  2030.6 37.9 %all-reduce.25.cloned.1.call-done = (bf16[2,128,128]{2,1,0:T(8,128)(2,1)}, bf16[1,256,256]{2,1,0:T(8,128)(2,1)}, bf16[2,128,128]{2,1,0:T(8,128)(2,1)}, bf16[4,352,352]{2,1,0:T(8,128)(2,1)}, bf16[2,352,352]{2,1,0:T(8,128)(2,1)}) async-done(((bf16[2,128,128]{2,1,0:T(8,128)(2,1)}, bf16[1,256,256]{2,1,0:T(8,128)(2,1)}, bf16[2,128,128]{2,1,0:T(8,128)(2,1)}, bf16[4,352,352]{2,1,0:T(8,128)(2,1)}, ...) | async-done | bytes 1749008 | tf_op jit(solution)/shard_map/psum | solution.py:93
  2100.9 74.4 %all-reduce.23.cloned.1.call-done = (bf16[2,128,128]{2,1,0:T(8,128)(2,1)}, bf16[1,256,256]{2,1,0:T(8,128)(2,1)}, bf16[2,128,128]{2,1,0:T(8,128)(2,1)}, bf16[4,352,352]{2,1,0:T(8,128)(2,1)}, bf16[2,352,352]{2,1,0:T(8,128)(2,1)}) async-done(((bf16[2,128,128]{2,1,0:T(8,128)(2,1)}, bf16[1,256,256]{2,1,0:T(8,128)(2,1)}, bf16[2,128,128]{2,1,0:T(8,128)(2,1)}, bf16[4,352,352]{2,1,0:T(8,128)(2,1)}, ...) | async-done | bytes 1749008 | tf_op jit(solution)/shard_map/psum | solution.py:93
  (740 shorter events, 448.8 us)
Async XLA Ops:
  7.2 33.6 %all-gather.12.cloned.1.call-start = ((), (), s32[]{:S(2)}) async-start(), calls=%async_computation.11 | async-start | bytes 1310720 | tf_op jit(solution)/shard_map/all_gather | solution.py:159
  9.1 105.3 %all-gather.8.cloned.1.call-start = ((), (), s32[]{:S(2)}) async-start(), calls=%async_computation.9 | async-start | bytes 14155776 | tf_op jit(solution)/shard_map/all_gather | solution.py:154
  9.9 134.7 %all-gather.10.cloned.1.call-start = ((), (), s32[]{:S(2)}) async-start(), calls=%async_computation.10 | async-start | bytes 1310720 | tf_op jit(solution)/shard_map/all_gather | solution.py:160
  11.7 184.1 %all-gather.14.cloned.1.call-start = ((), (), s32[]{:S(2)}) async-start(), calls=%async_computation.12 | async-start | bytes 1310720 | tf_op jit(solution)/shard_map/all_gather | solution.py:161
  12.5 366.2 %all-reduce.21.cloned.1.call-start = ((), (), s32[]{:S(2)}) async-start(), calls=%async_computation.27 | async-start | bytes 25165824 | tf_op jit(solution)/shard_map/psum | solution.py:208
  12.6 141.9 %copy-start.184 = (f32[64]{0:T(128)}, f32[64]{0:T(128)S(1)}, u32[]{:S(2)}) copy-start(f32[64]{0:T(128)S(1)} %multiply_power_fusion) | copy-start | bytes 772
  12.6 164.8 %copy-start.161 = (f32[1,2048]{1,0:T(1,128)}, f32[1,2048]{1,0:T(1,128)S(1)}, u32[]{:S(2)}) copy-start(f32[1,2048]{1,0:T(1,128)S(1)} %get-tuple-element.116) | copy-start | bytes 24580
  12.7 859.3 %copy-start.150 = (f32[1,2048]{1,0:T(1,128)}, f32[1,2048]{1,0:T(1,128)S(1)}, u32[]{:S(2)}) copy-start(f32[1,2048]{1,0:T(1,128)S(1)} %get-tuple-element.115) | copy-start | bytes 24580
  13.4 141.1 %copy-start.146 = (f32[1536]{0:T(1024)}, f32[1536]{0:T(1024)S(1)}, u32[]{:S(2)}) copy-start(f32[1536]{0:T(1024)S(1)} %subtract_convert_fusion.2) | copy-start | bytes 18436
  13.4 141.1 %copy-start.148 = (f32[1536]{0:T(1024)}, f32[1536]{0:T(1024)S(1)}, u32[]{:S(2)}) copy-start(f32[1536]{0:T(1024)S(1)} %subtract_convert_fusion.3) | copy-start | bytes 18436
  120.7 37.1 %copy-start.179 = (f32[1536]{0:T(1024)}, f32[1536]{0:T(1024)S(1)}, u32[]{:S(2)}) copy-start(f32[1536]{0:T(1024)S(1)} %get-tuple-element.190) | copy-start | bytes 18436
  120.8 56.7 %copy-start.181 = (f32[1536]{0:T(1024)}, f32[1536]{0:T(1024)S(1)}, u32[]{:S(2)}) copy-start(f32[1536]{0:T(1024)S(1)} %get-tuple-element.191) | copy-start | bytes 18436
  154.5 38.1 %copy-start.58 = (f32[1536,256]{0,1:T(8,128)}, f32[1536,256]{0,1:T(8,128)S(1)}, u32[]{:S(2)}) copy-start(f32[1536,256]{0,1:T(8,128)S(1)} %fusion.316) | copy-start | bytes 4718596
  157.8 32.4 %copy-start.87 = (bf16[1536,64]{0,1:T(8,128)(2,1)}, bf16[1536,64]{0,1:T(8,128)(2,1)S(1)}, u32[]{:S(2)}) copy-start(bf16[1536,64]{0,1:T(8,128)(2,1)S(1)} %get-tuple-element.163) | copy-start | bytes 589828
  157.9 32.4 %copy-start.89 = (bf16[1536,64]{0,1:T(8,128)(2,1)}, bf16[1536,64]{0,1:T(8,128)(2,1)S(1)}, u32[]{:S(2)}) copy-start(bf16[1536,64]{0,1:T(8,128)(2,1)S(1)} %get-tuple-element.164) | copy-start | bytes 589828
  206.4 281.2 %all-gather.16.cloned.1.call-start = ((), (), s32[]{:S(2)}) async-start(), calls=%async_computation.13 | async-start | bytes 7208960 | tf_op jit(solution)/shard_map/all_gather | solution.py:162
  209.5 337.8 %all-gather.18.cloned.1.call-start = ((), (), s32[]{:S(2)}) async-start(), calls=%async_computation.14 | async-start | bytes 3604480 | tf_op jit(solution)/shard_map/all_gather | solution.py:163
  211.9 408.3 %all-gather.20.cloned.1.call-start = ((), (), s32[]{:S(2)}) async-start(), calls=%async_computation.17 | async-start | bytes 14155776 | tf_op jit(solution)/shard_map/all_gather | solution.py:155
  212.6 645.3 %all-reduce.19.cloned.1.call-start = ((), (), s32[]{:S(2)}) async-start(), calls=%async_computation.26 | async-start | bytes 25165824 | tf_op jit(solution)/shard_map/psum | solution.py:231
  388.6 483.3 %copy-start.157 = (f32[1536]{0:T(1024)}, f32[1536]{0:T(1024)S(1)}, u32[]{:S(2)}) copy-start(f32[1536]{0:T(1024)S(1)} %get-tuple-element.124) | copy-start | bytes 18436
  388.7 483.3 %copy-start.159 = (f32[1536]{0:T(1024)}, f32[1536]{0:T(1024)S(1)}, u32[]{:S(2)}) copy-start(f32[1536]{0:T(1024)S(1)} %get-tuple-element.126) | copy-start | bytes 18436
  685.1 385.1 %all-reduce.17.cloned.1.call-start = ((), (), s32[]{:S(2)}) async-start(), calls=%async_computation.25 | async-start | bytes 3145728 | tf_op jit(solution)/shard_map/psum | solution.py:283
  872.0 31.5 %copy-start.26 = (bf16[2048,256]{1,0:T(8,128)(2,1)S(1)}, bf16[2048,256]{1,0:T(8,128)(2,1)}, u32[]{:S(2)}) copy-start(bf16[2048,256]{1,0:T(8,128)(2,1)} %all-gather.14.cloned.1.call-done) | copy-start | bytes 3145732
  1010.8 124.1 %reduce-scatter.26.cloned.1.call-start = ((), (), s32[]{:S(2)}) async-start(), calls=%async_computation.24 | async-start | bytes 3604480 | tf_op jit(solution)/shard_map/reduce_scatter | solution.py:319
  1022.3 136.3 %reduce-scatter.22.cloned.1.call-start = ((), (), s32[]{:S(2)}) async-start(), calls=%async_computation.22 | async-start | bytes 1310720 | tf_op jit(solution)/shard_map/reduce_scatter | solution.py:310
  1041.3 146.0 %reduce-scatter.18.cloned.1.call-start = ((), (), s32[]{:S(2)}) async-start(), calls=%async_computation.20 | async-start | bytes 1310720 | tf_op jit(solution)/shard_map/reduce_scatter | solution.py:304
  1043.1 29.8 %copy-start.147 = (f32[1536]{0:T(1024)S(1)}, f32[1536]{0:T(1024)}, u32[]{:S(2)}) copy-start(f32[1536]{0:T(1024)} %copy-done.146) | copy-start | bytes 18436
  1043.1 29.8 %copy-start.149 = (f32[1536]{0:T(1024)S(1)}, f32[1536]{0:T(1024)}, u32[]{:S(2)}) copy-start(f32[1536]{0:T(1024)} %copy-done.148) | copy-start | bytes 18436
  1076.9 34.0 %copy-start.127 = (bf16[1536,64]{0,1:T(8,128)(2,1)}, bf16[1536,64]{0,1:T(8,128)(2,1)S(1)}, u32[]{:S(2)}) copy-start(bf16[1536,64]{0,1:T(8,128)(2,1)S(1)} %get-tuple-element.159) | copy-start | bytes 589828
  1076.9 34.0 %copy-start.129 = (bf16[1536,64]{0,1:T(8,128)(2,1)}, bf16[1536,64]{0,1:T(8,128)(2,1)S(1)}, u32[]{:S(2)}) copy-start(bf16[1536,64]{0,1:T(8,128)(2,1)S(1)} %get-tuple-element.160) | copy-start | bytes 589828
  1088.4 127.5 %reduce-scatter.20.cloned.1.call-start = ((), (), s32[]{:S(2)}) async-start(), calls=%async_computation.21 | async-start | bytes 1310720 | tf_op jit(solution)/shard_map/reduce_scatter | solution.py:307
  1117.3 201.7 %reduce-scatter.24.cloned.1.call-start = ((), (), s32[]{:S(2)}) async-start(), calls=%async_computation.23 | async-start | bytes 7208960 | tf_op jit(solution)/shard_map/reduce_scatter | solution.py:313
  1134.7 278.0 %all-reduce.31.cloned.1.call-start = ((), (), s32[]{:S(2)}) async-start(), calls=%async_computation.32 | async-start | bytes 3768320 | tf_op jit(solution)/shard_map/psum | solution.py:93
  1138.4 311.8 %copy-start.28 = (f32[512,704]{0,1:T(8,128)}, f32[512,704]{0,1:T(8,128)S(1)}, u32[]{:S(2)}) copy-start(f32[512,704]{0,1:T(8,128)S(1)} %get-tuple-element.67) | copy-start | bytes 4325380
  1189.2 134.1 %copy-start.108 = (f32[512,256]{1,0:T(8,128)}, f32[512,256]{1,0:T(8,128)S(1)}, u32[]{:S(2)}) copy-start(f32[512,256]{1,0:T(8,128)S(1)} %get-tuple-element.75) | copy-start | bytes 1572868
  1189.5 133.9 %copy-start.73 = (f32[512,256]{0,1:T(8,128)}, f32[512,256]{0,1:T(8,128)S(1)}, u32[]{:S(2)}) copy-start(f32[512,256]{0,1:T(8,128)S(1)} %copy.450) | copy-start | bytes 1572868
  1330.9 284.8 %all-reduce.29.cloned.1.call-start = ((), (), s32[]{:S(2)}) async-start(), calls=%async_computation.31 | async-start | bytes 3768320 | tf_op jit(solution)/shard_map/psum | solution.py:93
  1412.7 35.2 %copy-start.134 = (bf16[2,352,352]{2,1,0:T(8,128)(2,1)S(1)}, bf16[2,352,352]{2,1,0:T(8,128)(2,1)}, u32[]{:S(2)}) copy-start(bf16[2,352,352]{2,1,0:T(8,128)(2,1)} %get-tuple-element.64) | copy-start | bytes 1486852
  1535.6 187.0 %all-reduce.27.cloned.1.call-start = ((), (), s32[]{:S(2)}) async-start(), calls=%async_computation.30 | async-start | bytes 3768320 | tf_op jit(solution)/shard_map/psum | solution.py:93
  1642.5 144.6 %reduce-scatter.10.cloned.1.call-start = ((), (), s32[]{:S(2)}) async-start(), calls=%async_computation.15 | async-start | bytes 7077888 | tf_op jit(solution)/shard_map/reduce_scatter | solution.py:220
  1651.7 200.4 %reduce-scatter.12.cloned.1.call-start = ((), (), s32[]{:S(2)}) async-start(), calls=%async_computation.16 | async-start | bytes 7077888 | tf_op jit(solution)/shard_map/reduce_scatter | solution.py:220
  1660.9 256.7 %reduce-scatter.16.cloned.1.call-start = ((), (), s32[]{:S(2)}) async-start(), calls=%async_computation.19 | async-start | bytes 7077888 | tf_op jit(solution)/shard_map/reduce_scatter | solution.py:291
  1666.9 315.9 %reduce-scatter.14.cloned.1.call-start = ((), (), s32[]{:S(2)}) async-start(), calls=%async_computation.18 | async-start | bytes 7077888 | tf_op jit(solution)/shard_map/reduce_scatter | solution.py:291
  1672.5 396.0 %all-reduce.25.cloned.1.call-start = ((), (), s32[]{:S(2)}) async-start(), calls=%async_computation.29 | async-start | bytes 3768320 | tf_op jit(solution)/shard_map/psum | solution.py:93
  1753.6 421.8 %all-reduce.23.cloned.1.call-start = ((), (), s32[]{:S(2)}) async-start(), calls=%async_computation.28 | async-start | bytes 3768320 | tf_op jit(solution)/shard_map/psum | solution.py:93
  1854.7 128.1 %copy-start.163 = (f32[1,2048]{1,0:T(1,128)S(1)}, f32[1,2048]{1,0:T(1,128)}, u32[]{:S(2)}) copy-start(f32[1,2048]{1,0:T(1,128)} %copy-done.161) | copy-start | bytes 24580
  2030.6 69.7 %copy-start.156 = (f32[2,2048]{1,0:T(2,128)}, f32[2,2048]{1,0:T(2,128)S(1)}, u32[]{:S(2)}) copy-start(f32[2,2048]{1,0:T(2,128)S(1)} %psum.230) | copy-start | bytes 49156
  2099.0 78.4 %copy-start.24 = (f32[512,2,352]{0,2,1:T(8,128)S(1)}, f32[512,2,352]{0,2,1:T(8,128)}, u32[]{:S(2)}) copy-start(f32[512,2,352]{0,2,1:T(8,128)} %copy-done.23) | copy-start | bytes 4325380
  (197 other events, 1177.9 us)
Sparse Core Ops, SparseCore 0:
  10.2 30.6 all-gather.11
  42.8 71.6 all-gather.7
  116.6 27.9 all-gather.9
  146.5 27.4 all-gather.13
  206.5 172.1 all-reduce.20
  380.8 106.7 all-gather.15
  489.8 57.3 all-gather.17
  549.3 70.8 all-gather.19
  685.2 172.6 all-reduce.18
  1011.0 59.1 all-reduce.16
  1073.2 55.5 reduce-scatter.25
  1131.6 26.9 reduce-scatter.21
  1161.4 25.7 reduce-scatter.17
  1190.1 25.7 reduce-scatter.19
  1218.1 100.9 reduce-scatter.23
  1331.0 81.5 all-reduce.30
  1535.7 79.9 all-reduce.28
  1642.6 79.9 all-reduce.26
  1726.4 60.6 reduce-scatter.9
  1790.3 61.7 reduce-scatter.11
  1855.9 61.7 reduce-scatter.15
  1921.0 61.6 reduce-scatter.13
  1986.3 82.1 all-reduce.24
  2095.4 79.9 all-reduce.22
where the time goes:
time: 2210 us; the launch traced here: 2200 us
  waiting for transfers between devices  1380 us (62%)
  matrix products  460 us (21%)
  other arithmetic  181 us (8%)
  local copies, waits for them, and re-layouts  122 us (6%)
  blocking collectives  43 us (2%)
    psum x5, waiting for transfers between devices, gram_sum(): lax.psum(block_gram(matrices[0]).astype(jnp.bfloat16), 'dp')  304 us
    psum x1, waiting for transfers between devices, shards(): lax.psum(attn_part.astype(jnp.bfloat16), 'mp').astype(jnp.float32)  166 us
    psum x1, waiting for transfers between devices, shards(): lax.psum(d_mid_part.astype(jnp.bfloat16), 'mp').astype(jnp.float32)  162 us
    reduce_scatter x2, waiting for transfers between devices, shards(): lax.psum_scatter(rows_dot(d_queries, full_query).astype(jnp.bfloat16), 'm...  124 us
    all_gather x1, waiting for transfers between devices, shards(): lax.all_gather(w_gate_up.astype(jnp.bfloat16), 'dp', axis=0, tiled=True)  98.9 us
    reduce_scatter x1, waiting for transfers between devices, shards(): lax.psum_scatter(acc_gate_up.reshape(full_gate_up.shape).astype(jnp.bfloa...  97.4 us
    reduce_scatter x2, waiting for transfers between devices, shards(): lax.psum_scatter(rows_dot(hidden, full_down).astype(jnp.bfloat16), 'mp',...  93.1 us
    dot_general x10, matrix products, outer_sum(): lax.dot_general(left, right, (((0,), (0,)), ((), ())), preferred_element_...  86.3 us
  transfers between devices with their start and end apart: 24, of which 22 were waited for; matrix products, arithmetic and copies ran while one was open for 14% of the time, Pallas kernels for 0%

commit v1 on v0

v1 whole, which is shorter than its diff:
```python
import functools

import jax
import jax.numpy as jnp
from jax import lax
from jax.experimental import pallas as pl
from jax.experimental.pallas import tpu as pltpu
from jax.sharding import PartitionSpec as P

FF_BLOCK = 352
NS_ITERS = 5
HEADS_PER_STEP = 4

EPS = 1e-05
THETA = 10000.0
NS_A = 3.4445
NS_B = -4.775
NS_C = 2.0315
MUON_RATE = 0.8
GAIN_RATE = 0.002
DECAY = 0.5
HIGH = lax.Precision.HIGHEST
MASKED = -1e30
VMEM_LIMIT = 40 * 1024 * 1024
LOW = jnp.bfloat16


def doc_layout(doc_lengths, positions):
    ends = jnp.cumsum(doc_lengths)
    starts = ends - doc_lengths
    segment = jnp.sum((positions[:, None] >= ends[None, :]).astype(jnp.int32), axis=1)
    member = (
        segment[:, None] == jnp.arange(doc_lengths.shape[0], dtype=jnp.int32)[None, :]
    ).astype(jnp.int32)
    offset = positions - jnp.sum(member * starts[None, :], axis=1)
    return (segment, offset)


def rotary_tables(offset, half_dim):
    freqs = jnp.power(THETA, -jnp.arange(half_dim, dtype=jnp.float32) / half_dim)
    angle = offset.astype(jnp.float32)[..., None] * freqs
    return (jnp.cos(angle), jnp.sin(angle))


def rotate(vector, cosine, sine):
    half_dim = vector.shape[-1] // 2
    first_half = vector[..., :half_dim]
    second_half = vector[..., half_dim:]
    return jnp.concatenate(
        [first_half * cosine - second_half * sine, second_half * cosine + first_half * sine],
        axis=-1,
    )


def inverse_scale(vector):
    return lax.rsqrt(jnp.mean(vector * vector, axis=-1, keepdims=True) + EPS)


def norm_back(grad_rows, value_rows, scale_rows, gain_row):
    weighted = grad_rows * gain_row
    cubed = scale_rows * scale_rows * scale_rows
    return scale_rows * weighted - value_rows * cubed * jnp.mean(
        weighted * value_rows, axis=-1, keepdims=True
    )


def contract(left, right, left_dim, right_dim):
    return lax.dot_general(
        left,
        right,
        (((left_dim,), (right_dim,)), ((), ())),
        preferred_element_type=jnp.float32,
    )


def plain_dot(left, right):
    return contract(left, right, 1, 0)


def rows_dot(left, right):
    return contract(left, right, 1, 1)


def outer_sum(left, right):
    return contract(left, right, 0, 0)


def swap(value, flip, size):
    return lax.ppermute(value, "mp", [(i, i ^ flip) for i in range(size)])


def tie(*values):
    return lax.optimization_barrier(values)


class Gather:
    def __init__(self, value, size):
        self.size = size
        self.half = value.shape[0] // 2
        self.parts = {"own": value}

    def swap(self, name, flip):
        return swap(self.parts[name], flip, self.size)

    def first(self):
        parts = self.parts
        if self.size != 8:
            for s in range(1, self.size):
                parts[str(s)] = self.swap("own", s)
            return
        parts["one"] = self.swap("own", 1)
        parts["two"] = self.swap("own", 2)
        parts["four"] = self.swap("own", 4)

    def second(self):
        parts = self.parts
        if self.size != 8:
            return
        parts["six_top"] = swap(parts["two"][: self.half], 4, self.size)
        parts["six_low"] = swap(parts["four"][self.half :], 2, self.size)
        parts["three"] = self.swap("two", 1)
        parts["five"] = self.swap("four", 1)

    def third(self):
        parts = self.parts
        if self.size != 8:
            return
        parts["seven_top"] = self.swap("six_top", 1)
        parts["seven_low"] = self.swap("six_low", 1)

    def pieces(self):
        parts = self.parts
        if self.size != 8:
            return [[(0, parts["own"])]] + [[(0, parts[str(s)])] for s in range(1, self.size)]
        names = ("own", "one", "two", "three", "four", "five", "six", "seven")
        return [
            [(0, parts[name])]
            if name in parts
            else [(0, parts[name + "_top"]), (self.half, parts[name + "_low"])]
            for name in names
        ]


def flips_of(size):
    flips = [1 << bit for bit in range(size.bit_length() - 1)]
    return flips[1:] + flips[:1]


def gather_order(size):
    order = [0]
    for flip in flips_of(size):
        order = order + [s ^ flip for s in order]
    return order


def gather_small(value, size):
    value = value[None]
    for flip in flips_of(size):
        value = jnp.concatenate([value, swap(value, flip, size)], axis=0)
    return value


def scatter_small(parts, size):
    for flip in flips_of(size)[::-1]:
        half = parts.shape[0] // 2
        parts = wide(parts[:half]) + wide(swap(parts[half:].astype(LOW), flip, size))
    return parts[0]


def wide(value):
    return value.astype(jnp.float32)


def step_order(size):
    if size == 8:
        return [(3, 0), (1, 0), (3, 1), (2, 1)], [(1, 1), (2, 0), (0, 0), (0, 1)]
    steps = [(pair, half) for pair in range(size // 2) for half in range(2)]
    return steps[: len(steps) // 2], steps[len(steps) // 2 :]


class Scatter:
    def __init__(self, size):
        self.size = size
        self.runs = []
        self.parts = {}

    def first(self, evens, odds):
        self.runs.append((evens, odds))
        if self.size == 8:
            self.parts["core" + str(len(self.runs))] = swap(odds, 1, self.size)

    def second(self):
        if self.size != 8:
            steps = step_order(self.size)
            place = {step: (run, n) for run in (0, 1) for n, step in enumerate(steps[run])}
            total = 0.0
            for s in range(self.size):
                halves = []
                for half in (0, 1):
                    run, n = place[(s // 2, half)]
                    halves.append(self.runs[run][s % 2][n])
                part = jnp.concatenate(halves, axis=0)
                total = total + wide(swap(part, s, self.size) if s else part)
            self.parts["total"] = total
            return
        pair = wide(self.runs[0][0]) + wide(self.parts.pop("core1"))
        self.parts["two"] = swap(pair[:2].astype(LOW), 2, self.size)
        self.parts["four"] = swap(pair[2:].astype(LOW), 4, self.size)

    def third(self):
        if self.size != 8:
            return
        evens, core = self.runs[1][0], self.parts["core2"]
        low = wide(evens[0]) + wide(core[0]) + wide(self.parts["four"][0])
        top = wide(evens[1]) + wide(core[1]) + wide(self.parts["two"][0])
        self.parts["low"] = swap(low.astype(LOW), 2, self.size)
        self.parts["top"] = swap(top.astype(LOW), 4, self.size)

    def total(self):
        parts = self.parts
        if self.size != 8:
            return parts["total"]
        evens, core = self.runs[1][0], parts["core2"]
        top = wide(evens[2]) + wide(core[2]) + wide(parts["two"][1]) + wide(parts["top"])
        low = wide(evens[3]) + wide(core[3]) + wide(parts["four"][1]) + wide(parts["low"])
        return jnp.concatenate([top, low], axis=0)


def add_all(value, axis):
    size = lax.axis_size(axis)
    if size & (size - 1):
        return lax.psum(value, axis)
    flip = 1
    while flip < size:
        value = value + lax.ppermute(value, axis, [(i, i ^ flip) for i in range(size)])
        flip = 2 * flip
    return value


def masked_bias(qid_ref, kid_ref):
    rows = qid_ref[0]
    keys = kid_ref[0]
    allowed = (rows[:, 0:1] == keys[0:1, :]) & (rows[:, 1:2] >= keys[1:2, :])
    return jnp.where(allowed, 0.0, MASKED)


def forward_kernel(heads, head_dim, q_ref, kv_ref, qid_ref, kid_ref, ctx_ref, log_ref, bias_ref):
    @pl.when(pl.program_id(1) == 0)
    def _():
        bias_ref[...] = masked_bias(qid_ref, kid_ref)

    keys = kv_ref[0, :, :head_dim]
    values = kv_ref[0, :, head_dim:]
    for head in range(heads):
        cols = slice(head * head_dim, (head + 1) * head_dim)
        scores = contract(q_ref[0, :, cols], keys, 1, 1) * head_dim ** (-0.5) + bias_ref[...]
        top = jnp.max(scores, axis=-1, keepdims=True)
        powers = jnp.exp(scores - top)
        total = jnp.sum(powers, axis=-1, keepdims=True)
        log_ref[0, :, cols] = jnp.broadcast_to(top + jnp.log(total), (scores.shape[0], head_dim))
        probs = (powers * (1.0 / total)).astype(LOW)
        ctx_ref[0, :, cols] = contract(probs, values, 1, 0).astype(LOW)


def attention_forward(batch, queries, keyval, qid, kid, head_dim):
    unused, rows, width = queries.shape
    batches = 1
    seq_len = keyval.shape[1]
    heads = min(HEADS_PER_STEP, width // head_dim)
    block = pl.BlockSpec((1, rows, heads * head_dim), lambda b, h: (batch, 0, h))
    own = pl.BlockSpec((1, rows, heads * head_dim), lambda b, h: (0, 0, h))
    work = batches * rows * width * seq_len
    return pl.pallas_call(
        functools.partial(forward_kernel, heads, head_dim),
        grid=(batches, width // (heads * head_dim)),
        in_specs=[
            block,
            pl.BlockSpec((1, seq_len, 2 * head_dim), lambda b, h: (batch, 0, 0)),
            pl.BlockSpec((1, rows, 2), lambda b, h: (batch, 0, 0)),
            pl.BlockSpec((1, 2, seq_len), lambda b, h: (batch, 0, 0)),
        ],
        out_specs=[own, own],
        out_shape=[
            jax.ShapeDtypeStruct((batches, rows, width), LOW),
            jax.ShapeDtypeStruct((batches, rows, width), jnp.float32),
        ],
        scratch_shapes=[pltpu.VMEM((rows, seq_len), jnp.float32)],
        compiler_params=pltpu.CompilerParams(vmem_limit_bytes=VMEM_LIMIT),
        cost_estimate=pl.CostEstimate(
            flops=8 * work, bytes_accessed=8 * batches * rows * width, transcendentals=work // head_dim
        ),
        name="attention_forward",
    )(queries, keyval, qid, kid)


def backward_kernel(
    heads,
    head_dim,
    q_ref,
    dctx_ref,
    log_ref,
    kv_ref,
    qid_ref,
    kid_ref,
    cos_ref,
    sin_ref,
    dq_ref,
    dkv_ref,
    bias_ref,
):
    @pl.when(pl.program_id(1) == 0)
    def _():
        bias_ref[...] = masked_bias(qid_ref, kid_ref)
        dkv_ref[...] = jnp.zeros_like(dkv_ref)

    scale = head_dim ** (-0.5)
    half = head_dim // 2
    keys = kv_ref[0, :, :head_dim]
    values = kv_ref[0, :, head_dim:]
    cosine = cos_ref[0]
    sine = sin_ref[0]
    d_keys = 0.0
    d_values = 0.0
    for head in range(heads):
        cols = slice(head * head_dim, (head + 1) * head_dim)
        queries = q_ref[0, :, cols]
        d_context = dctx_ref[0, :, cols]
        scores = contract(queries, keys, 1, 1) * scale + bias_ref[...]
        probs = jnp.exp(scores - log_ref[0, :, head * head_dim : head * head_dim + 1])
        d_probs = contract(d_context, values, 1, 1)
        centre = jnp.sum(d_probs * probs, axis=-1, keepdims=True)
        d_scores = (probs * (d_probs - centre)).astype(LOW)
        d_keys = d_keys + contract(d_scores, queries, 0, 0)
        d_values = d_values + contract(probs.astype(LOW), d_context, 0, 0)
        d_query = contract(d_scores, keys, 1, 0) * scale
        first = d_query[:, :half]
        second = d_query[:, half:]
        dq_ref[0, :, cols] = jnp.concatenate(
            [first * cosine + second * sine, second * cosine - first * sine], axis=1
        ).astype(LOW)
    dkv_ref[0, :, :head_dim] += d_keys * scale
    dkv_ref[0, :, head_dim:] += d_values


def attention_backward(batch, queries, d_context, logs, keyval, qid, kid, cosine, sine, head_dim):
    unused, rows, width = queries.shape
    batches = 1
    seq_len = keyval.shape[1]
    heads = min(HEADS_PER_STEP, width // head_dim)
    block = pl.BlockSpec((1, rows, heads * head_dim), lambda b, h: (batch, 0, h))
    own = pl.BlockSpec((1, rows, heads * head_dim), lambda b, h: (0, 0, h))
    work = batches * rows * width * seq_len

    def whole(*shape):
        return pl.BlockSpec((1,) + shape, lambda b, h: (batch, 0, 0))

    return pl.pallas_call(
        functools.partial(backward_kernel, heads, head_dim),
        grid=(batches, width // (heads * head_dim)),
        in_specs=[
            block,
            block,
            own,
            whole(seq_len, 2 * head_dim),
            whole(rows, 2),
            whole(2, seq_len),
            whole(rows, head_dim // 2),
            whole(rows, head_dim // 2),
        ],
        out_specs=[own, pl.BlockSpec((1, seq_len, 2 * head_dim), lambda b, h: (0, 0, 0))],
        out_shape=[
            jax.ShapeDtypeStruct((batches, rows, width), LOW),
            jax.ShapeDtypeStruct((batches, seq_len, 2 * head_dim), jnp.float32),
        ],
        scratch_shapes=[pltpu.VMEM((rows, seq_len), jnp.float32)],
        compiler_params=pltpu.CompilerParams(vmem_limit_bytes=VMEM_LIMIT),
        cost_estimate=pl.CostEstimate(
            flops=20 * work,
            bytes_accessed=12 * batches * rows * width,
            transcendentals=work // head_dim,
        ),
        name="attention_backward",
    )(queries, d_context, logs, keyval, qid, kid, cosine, sine)


def flat_pieces(blocks):
    places = []
    arrays = []
    for number, pieces in enumerate(blocks):
        for first, rows in pieces:
            places.append((number, first, rows.shape[0]))
            arrays.append(rows)
    return places, arrays


def fetch_all(places, piece_refs, weight_ref, sem_ref):
    copies = []
    for number, (block, first, rows) in enumerate(places):
        copies.append(
            pltpu.make_async_copy(
                piece_refs[number],
                weight_ref.at[block, pl.ds(first, rows)],
                sem_ref.at[number],
            )
        )
    for copy in copies:
        copy.start()
    return copies


def project_kernel(places, head_dim, turned, *refs):
    count = len(places)
    piece_refs, refs = refs[:count], refs[count:]
    if turned:
        rows_ref, cos_ref, sin_ref, out_ref, weight_ref, sem_ref = refs
    else:
        rows_ref, out_ref, weight_ref, sem_ref = refs
    copies = fetch_all(places, piece_refs, weight_ref, sem_ref)
    depth = rows_ref.shape[1]
    width = weight_ref.shape[2]
    half = head_dim // 2
    for block in range(weight_ref.shape[0]):
        for number, place in enumerate(places):
            if place[0] == block:
                copies[number].wait()
        product = contract(rows_ref[...], weight_ref[block, :depth], 1, 0)
        if turned:
            for head in range(width // head_dim):
                first = product[:, head * head_dim : head * head_dim + half]
                second = product[:, head * head_dim + half : (head + 1) * head_dim]
                cosine = cos_ref[...]
                sine = sin_ref[...]
                place = block * width + head * head_dim
                out_ref[:, place : place + head_dim] = jnp.concatenate(
                    [first * cosine - second * sine, second * cosine + first * sine], axis=1
                ).astype(LOW)
        else:
            out_ref[:, block * width : (block + 1) * width] = product.astype(LOW)


def project(rows, blocks, head_dim, tables=None):
    places, arrays = flat_pieces(blocks)
    size = len(blocks)
    depth = max(first + count for _, first, count in places)
    width = arrays[0].shape[1]
    vmem = pl.BlockSpec(memory_space=pltpu.VMEM)
    turned = tables is not None
    return pl.pallas_call(
        functools.partial(project_kernel, places, head_dim, turned),
        in_specs=[pl.BlockSpec(memory_space=pl.ANY)] * len(arrays) + [vmem] * (3 if turned else 1),
        out_specs=vmem,
        out_shape=jax.ShapeDtypeStruct((rows.shape[0], size * width), LOW),
        scratch_shapes=[
            pltpu.VMEM((size, depth, width), LOW),
            pltpu.SemaphoreType.DMA((len(arrays),)),
        ],
        compiler_params=pltpu.CompilerParams(vmem_limit_bytes=VMEM_LIMIT),
        cost_estimate=pl.CostEstimate(
            flops=2 * rows.size * size * width,
            bytes_accessed=2 * (size * depth * width + 2 * rows.size),
            transcendentals=0,
        ),
        name="project",
    )(*arrays, rows, *(tables if turned else ()))


def project_back_kernel(places, *refs):
    count = len(places)
    piece_refs, (rows_ref, out_ref, weight_ref, sem_ref) = refs[:count], refs[count:]
    copies = fetch_all(places, piece_refs, weight_ref, sem_ref)
    depth = out_ref.shape[1]
    width = weight_ref.shape[2]
    for block in range(weight_ref.shape[0]):
        for number, place in enumerate(places):
            if place[0] == block:
                copies[number].wait()
        product = contract(
            rows_ref[:, block * width : (block + 1) * width], weight_ref[block, :depth], 1, 1
        )
        if block == 0:
            out_ref[...] = product
        else:
            out_ref[...] += product


def project_back(rows, blocks, depth):
    places, arrays = flat_pieces(blocks)
    size = len(blocks)
    height = max(first + count for _, first, count in places)
    width = arrays[0].shape[1]
    vmem = pl.BlockSpec(memory_space=pltpu.VMEM)
    return pl.pallas_call(
        functools.partial(project_back_kernel, places),
        in_specs=[pl.BlockSpec(memory_space=pl.ANY)] * len(arrays) + [vmem],
        out_specs=vmem,
        out_shape=jax.ShapeDtypeStruct((rows.shape[0], depth), jnp.float32),
        scratch_shapes=[
            pltpu.VMEM((size, height, width), LOW),
            pltpu.SemaphoreType.DMA((len(arrays),)),
        ],
        compiler_params=pltpu.CompilerParams(vmem_limit_bytes=VMEM_LIMIT),
        cost_estimate=pl.CostEstimate(
            flops=2 * rows.size * depth,
            bytes_accessed=2 * (size * height * width + 3 * rows.size),
            transcendentals=0,
        ),
        name="project_back",
    )(*arrays, rows)


def hidden_kernel(places, steps_order, turn, *refs):
    count = len(places)
    piece_refs = refs[:count]
    weight_ref, all_ref, gate_ref, up_ref, hidden_ref, turned_ref, slot_ref, sem_ref = refs[count:]
    step = pl.program_id(0)
    steps = pl.num_programs(0)
    half = slot_ref.shape[1] // 2

    def each(number, act):
        slot = lax.rem(number, 2)
        for static, (pair, side) in enumerate(steps_order):

            @pl.when(number == static)
            def _(pair=pair, side=side):
                for parity in range(2):
                    block, start = 2 * pair + parity, side * half
                    for index, (owner, first, rows) in enumerate(places):
                        if owner == block and first <= start < first + rows:
                            act(
                                pltpu.make_async_copy(
                                    piece_refs[index].at[pl.ds(start - first, half)],
                                    slot_ref.at[slot, pl.ds(parity * half, half)],
                                    sem_ref.at[slot, parity],
                                )
                            )

    @pl.when(step == 0)
    def _():
        each(step, lambda copy: copy.start())

    @pl.when(step + 1 < steps)
    def _():
        each(step + 1, lambda copy: copy.start())

    each(step, lambda copy: copy.wait())
    rows = slot_ref[lax.rem(step, 2)]
    all_ref[...] = rows
    groups, _, _, chunk = weight_ref.shape
    gate = 0.0
    upward = 0.0
    for group in range(groups):
        part = rows[:, group * chunk : (group + 1) * chunk]
        gate = gate + contract(part, weight_ref[group, 0], 1, 1)
        upward = upward + contract(part, weight_ref[group, 1], 1, 1)
    gate_ref[...] = gate
    up_ref[...] = upward
    hidden = gate * jax.nn.sigmoid(gate) * upward
    hidden_ref[...] = hidden.astype(LOW)
    turned_ref[...] = (hidden.T if turn else hidden).astype(LOW)


def in_steps(blocks):
    half = sum(piece.shape[0] for _, piece in blocks[0]) // 2
    rows = []
    for pair, side in sum(step_order(len(blocks)), []):
        start = side * half
        for pieces in blocks[2 * pair : 2 * pair + 2]:
            for first, piece in pieces:
                if first <= start < first + piece.shape[0]:
                    rows.append(piece[start - first : start - first + half])
    return jnp.concatenate(rows, axis=0)


def hidden_units(blocks, gate_up):
    places, arrays = flat_pieces(blocks)
    size = len(blocks)
    rows = max(first + count for _, first, count in places)
    depth = arrays[0].shape[1]
    units = gate_up.shape[2]
    turn = rows % 128 == 0

    def block(width):
        return pl.BlockSpec((rows, width), lambda s: (s, 0))

    turned = pl.BlockSpec((units, rows), lambda s: (0, s)) if turn else block(units)
    turned_shape = (units, size * rows) if turn else (size * rows, units)
    return pl.pallas_call(
        functools.partial(hidden_kernel, places, sum(step_order(size), []), turn),
        grid=(size,),
        in_specs=[pl.BlockSpec(memory_space=pl.ANY)] * len(arrays)
        + [pl.BlockSpec(gate_up.shape, lambda s: (0, 0, 0, 0), pipeline_mode=pl.Buffered(1))],
        out_specs=[block(depth), block(units), block(units), block(units), turned],
        out_shape=[
            jax.ShapeDtypeStruct((size * rows, depth), LOW),
            jax.ShapeDtypeStruct((size * rows, units), jnp.float32),
            jax.ShapeDtypeStruct((size * rows, units), jnp.float32),
            jax.ShapeDtypeStruct((size * rows, units), LOW),
            jax.ShapeDtypeStruct(turned_shape, LOW),
        ],
        scratch_shapes=[pltpu.VMEM((2, rows, depth), LOW), pltpu.SemaphoreType.DMA((2, 2))],
        compiler_params=pltpu.CompilerParams(vmem_limit_bytes=VMEM_LIMIT),
        cost_estimate=pl.CostEstimate(
            flops=4 * size * rows * depth * units,
            bytes_accessed=4 * size * rows * depth,
            transcendentals=size * rows * units,
        ),
        name="hidden_units",
    )(*arrays, gate_up)


def hidden_back_kernel(
    turn, cot_ref, gate_ref, up_ref, gate_up_ref, down_ref, dg_ref, du_ref, even_ref, odd_ref
):
    groups, _, chunk = down_ref.shape
    gate = gate_ref[...]
    upward = up_ref[...]
    sigma = jax.nn.sigmoid(gate)
    d_hidden = 0.0
    for group in range(groups):
        cols = slice(group * chunk, (group + 1) * chunk)
        d_hidden = d_hidden + contract(cot_ref[:, cols], down_ref[group], 1, 1)
    d_gate = d_hidden * upward * sigma * (1.0 + gate * (1.0 - sigma))
    d_up = d_hidden * gate * sigma
    dg_ref[...] = (d_gate.T if turn else d_gate).astype(LOW)
    du_ref[...] = (d_up.T if turn else d_up).astype(LOW)
    d_gate = d_gate.astype(LOW)
    d_up = d_up.astype(LOW)
    for group in range(groups):
        part = contract(d_gate, gate_up_ref[group, 0], 1, 0)
        part = (part + contract(d_up, gate_up_ref[group, 1], 1, 0)).astype(LOW)
        cols = slice(group * chunk, (group + 1) * chunk)
        even_ref[0, :, cols] = part[: part.shape[0] // 2]
        odd_ref[0, :, cols] = part[part.shape[0] // 2 :]


def hidden_back(run, cotangent, gate, upward, gate_up, down, size):
    tokens, depth = cotangent.shape
    rows = tokens // size
    units = gate.shape[1]
    steps = len(step_order(size)[run])
    first = run * steps
    turn = rows % 128 == 0

    def block(width):
        return pl.BlockSpec((rows, width), lambda s: (first + s, 0))

    if turn:
        turned = pl.BlockSpec((units, rows), lambda s: (0, s))
        turned_shape = (units, steps * rows)
    else:
        turned = pl.BlockSpec((rows, units), lambda s: (s, 0))
        turned_shape = (steps * rows, units)
    half = pl.BlockSpec((1, rows // 2, depth), lambda s: (s, 0, 0))
    return pl.pallas_call(
        functools.partial(hidden_back_kernel, turn),
        grid=(steps,),
        in_specs=[
            block(depth),
            block(units),
            block(units),
            pl.BlockSpec(gate_up.shape, lambda s: (0, 0, 0, 0), pipeline_mode=pl.Buffered(1)),
            pl.BlockSpec(down.shape, lambda s: (0, 0, 0), pipeline_mode=pl.Buffered(1)),
        ],
        out_specs=[turned, turned, half, half],
        out_shape=[
            jax.ShapeDtypeStruct(turned_shape, LOW),
            jax.ShapeDtypeStruct(turned_shape, LOW),
            jax.ShapeDtypeStruct((steps, rows // 2, depth), LOW),
            jax.ShapeDtypeStruct((steps, rows // 2, depth), LOW),
        ],
        compiler_params=pltpu.CompilerParams(vmem_limit_bytes=VMEM_LIMIT),
        cost_estimate=pl.CostEstimate(
            flops=6 * steps * rows * depth * units,
            bytes_accessed=4 * steps * rows * depth,
            transcendentals=steps * rows * units,
        ),
        name="hidden_back",
    )(cotangent, gate, upward, gate_up, down)


def hidden_out_kernel(hidden_ref, down_ref, even_ref, odd_ref):
    groups, _, chunk = down_ref.shape
    for group in range(groups):
        part = contract(hidden_ref[...], down_ref[group], 1, 0).astype(LOW)
        cols = slice(group * chunk, (group + 1) * chunk)
        even_ref[0, :, cols] = part[: part.shape[0] // 2]
        odd_ref[0, :, cols] = part[part.shape[0] // 2 :]


def hidden_out(run, hidden, down, size):
    tokens, units = hidden.shape
    rows = tokens // size
    steps = len(step_order(size)[run])
    depth = down.shape[0] * down.shape[2]
    return pl.pallas_call(
        hidden_out_kernel,
        grid=(steps,),
        in_specs=[
            pl.BlockSpec((rows, units), lambda s: (run * steps + s, 0)),
            pl.BlockSpec(down.shape, lambda s: (0, 0, 0), pipeline_mode=pl.Buffered(1)),
        ],
        out_specs=[pl.BlockSpec((1, rows // 2, depth), lambda s: (s, 0, 0))] * 2,
        out_shape=[jax.ShapeDtypeStruct((steps, rows // 2, depth), LOW)] * 2,
        compiler_params=pltpu.CompilerParams(vmem_limit_bytes=VMEM_LIMIT),
        cost_estimate=pl.CostEstimate(
            flops=2 * steps * rows * depth * units,
            bytes_accessed=2 * steps * rows * depth,
            transcendentals=0,
        ),
        name="hidden_out",
    )(hidden, down)


def units_sum_kernel(count, turn, *refs):
    unit_refs, row_ref, out_ref = refs[:count], refs[count], refs[count + 1]
    first = 0
    total = 0.0
    for unit_ref in unit_refs:
        tokens = unit_ref.shape[1 if turn else 0]
        rows = row_ref[first : first + tokens, :]
        total = total + contract(unit_ref[...], rows, 1 if turn else 0, 0)
        first = first + tokens
    out_ref[0] = total.astype(LOW)


def units_sum(units, rows, groups):
    tokens, depth = rows.shape
    turn = sum(part.shape[1] for part in units) == tokens
    width = units[0].shape[0 if turn else 1]
    chunk = depth // groups
    cut = 2
    return pl.pallas_call(
        functools.partial(units_sum_kernel, len(units), turn),
        grid=(groups * cut,),
        in_specs=[
            pl.BlockSpec(part.shape, lambda s: (0, 0), pipeline_mode=pl.Buffered(1))
            for part in units
        ]
        + [pl.BlockSpec((tokens, chunk // cut), lambda s: (0, s))],
        out_specs=pl.BlockSpec((1, width, chunk // cut), lambda s: (s // cut, 0, lax.rem(s, cut))),
        out_shape=jax.ShapeDtypeStruct((groups, width, chunk), LOW),
        compiler_params=pltpu.CompilerParams(vmem_limit_bytes=VMEM_LIMIT),
        cost_estimate=pl.CostEstimate(
            flops=2 * tokens * depth * width,
            bytes_accessed=2 * tokens * (depth + width),
            transcendentals=0,
        ),
        name="units_sum",
    )(*units, rows)


def pick(values, index):
    value = values[0]
    for number in range(1, len(values)):
        value = jnp.where(index == number, values[number], value)
    return value


def blocks_sum_kernel(row_ref, col_ref, even_ref, odd_ref):
    part = contract(row_ref[...], col_ref[...], 0, 0).astype(LOW)
    even_ref[0] = part[:, : part.shape[1] // 2]
    odd_ref[0] = part[:, part.shape[1] // 2 :]


def blocks_sum(run, rows, cols, size):
    tokens, depth = rows.shape
    width = cols.shape[1] // size
    order = step_order(size)[run]
    pairs = [pair for pair, _ in order]
    sides = [side for _, side in order]
    return pl.pallas_call(
        blocks_sum_kernel,
        grid=(len(order),),
        in_specs=[
            pl.BlockSpec((tokens, depth // 2), lambda s: (0, pick(sides, s))),
            pl.BlockSpec((tokens, 2 * width), lambda s: (0, pick(pairs, s))),
        ],
        out_specs=[pl.BlockSpec((1, depth // 2, width), lambda s: (s, 0, 0))] * 2,
        out_shape=[jax.ShapeDtypeStruct((len(order), depth // 2, width), LOW)] * 2,
        compiler_params=pltpu.CompilerParams(vmem_limit_bytes=VMEM_LIMIT),
        cost_estimate=pl.CostEstimate(
            flops=tokens * depth * len(order) * 2 * width,
            bytes_accessed=2 * depth * len(order) * width,
            transcendentals=0,
        ),
        name="blocks_sum",
    )(rows, cols)


def fine_dot(left, right, left_dim=1, right_dim=0):
    return lax.dot_general(
        left,
        right,
        (((left_dim,), (right_dim,)), ((), ())),
        precision=HIGH,
        preferred_element_type=jnp.float32,
    )


def gram_kernel(width, by_rows, matrix_ref, *gram_refs):
    for block, gram_ref in enumerate(gram_refs):
        place = slice(block * width, (block + 1) * width)
        if by_rows:
            gram_ref[...] = fine_dot(matrix_ref[place, :], matrix_ref[place, :], 1, 1)
        else:
            gram_ref[...] = fine_dot(matrix_ref[:, place], matrix_ref[:, place], 0, 0)


def block_grams(matrix, width, by_rows):
    count = matrix.shape[0 if by_rows else 1] // width
    return pl.pallas_call(
        functools.partial(gram_kernel, width, by_rows),
        out_shape=[jax.ShapeDtypeStruct((width, width), jnp.float32)] * count,
        compiler_params=pltpu.CompilerParams(vmem_limit_bytes=VMEM_LIMIT),
        cost_estimate=pl.CostEstimate(
            flops=12 * matrix.size * width, bytes_accessed=4 * matrix.size, transcendentals=0
        ),
        name="block_grams",
    )(matrix)


def newton_factor(gram):
    width = gram.shape[0]
    row = lax.broadcasted_iota(jnp.int32, (width, width), 0)
    col = lax.broadcasted_iota(jnp.int32, (width, width), 1)
    eye = jnp.where(row == col, 1.0, 0.0)
    trace = jnp.sum(jnp.sum(gram * eye, axis=1, keepdims=True), axis=0, keepdims=True)
    inverse = 1.0 / (jnp.sqrt(trace) + 1e-07)
    gram = gram * inverse * inverse
    total = None
    for iteration in range(NS_ITERS):
        poly = NS_A * eye + NS_B * gram + NS_C * fine_dot(gram, gram)
        total = poly if total is None else fine_dot(total, poly)
        if iteration < NS_ITERS - 1:
            gram = fine_dot(fine_dot(poly, gram), poly)
    return total * inverse


def factor_kernel(own_ref, *refs):
    part_refs, factor_ref = refs[:-1], refs[-1]

    @pl.when(own_ref[0] != 0)
    def _():
        gram = part_refs[0][...]
        for part_ref in part_refs[1:]:
            gram = gram + part_ref[...]
        factor_ref[...] = newton_factor(gram)

    @pl.when(own_ref[0] == 0)
    def _():
        factor_ref[...] = jnp.zeros_like(factor_ref)


def block_factor(own, parts):
    width = parts[0].shape[0]
    vmem = pl.BlockSpec(memory_space=pltpu.VMEM)
    return pl.pallas_call(
        factor_kernel,
        in_specs=[pl.BlockSpec(memory_space=pltpu.SMEM)] + [vmem] * len(parts),
        out_specs=vmem,
        out_shape=jax.ShapeDtypeStruct((width, width), jnp.float32),
        compiler_params=pltpu.CompilerParams(vmem_limit_bytes=VMEM_LIMIT),
        cost_estimate=pl.CostEstimate(
            flops=200 * width**3, bytes_accessed=20 * width * width, transcendentals=0
        ),
        name="block_factor",
    )(own, *parts)


def apply_kernel(width, count, place_ref, matrix_ref, weight_ref, *refs):
    choice_refs, new_ref, factor_ref = refs[:-2], refs[-2], refs[-1]
    for block in range(count):
        for number, choice_ref in enumerate(choice_refs):

            @pl.when(place_ref[block] == number)
            def _(choice_ref=choice_ref):
                factor_ref[...] = choice_ref[...].astype(jnp.float32)

        rows = slice(block * width, (block + 1) * width)
        new_ref[rows, :] = weight_ref[rows, :] - MUON_RATE * fine_dot(
            factor_ref[...], matrix_ref[rows, :]
        )


def apply_factors(matrix, weight, places, choices):
    width = choices[0].shape[0]
    count = matrix.shape[0] // width
    vmem = pl.BlockSpec(memory_space=pltpu.VMEM)
    return pl.pallas_call(
        functools.partial(apply_kernel, width, count),
        in_specs=[pl.BlockSpec(memory_space=pltpu.SMEM)] + [vmem] * (2 + len(choices)),
        out_specs=vmem,
        out_shape=jax.ShapeDtypeStruct(matrix.shape, jnp.float32),
        scratch_shapes=[pltpu.VMEM((width, width), jnp.float32)],
        compiler_params=pltpu.CompilerParams(vmem_limit_bytes=VMEM_LIMIT),
        cost_estimate=pl.CostEstimate(
            flops=12 * matrix.size * width, bytes_accessed=12 * matrix.size, transcendentals=0
        ),
        name="apply_factors",
    )(places, matrix, weight, *choices)


def update_kernel(width, count, by_rows, matrix_ref, weight_ref, *refs):
    part_refs, new_ref = refs[:-1], refs[-1]
    for block in range(count):
        gram = part_refs[0][block]
        for part_ref in part_refs[1:]:
            gram = gram + part_ref[block]
        factor = newton_factor(gram)
        place = slice(block * width, (block + 1) * width)
        if by_rows:
            new_ref[place, :] = weight_ref[place, :] - MUON_RATE * fine_dot(
                factor, matrix_ref[place, :]
            )
        else:
            new_ref[:, place] = weight_ref[:, place] - MUON_RATE * fine_dot(
                matrix_ref[:, place], factor
            )


def gather_grams(moment, width, by_rows):
    grams = jnp.stack(block_grams(moment, width, by_rows))
    size = lax.axis_size("dp")
    return [grams] + [
        lax.ppermute(grams, "dp", [(i, (i + shift) % size) for i in range(size)])
        for shift in range(1, size)
    ]


def small_update(moment, weight, width, by_rows, parts=None):
    if parts is None:
        parts = gather_grams(moment, width, by_rows)
    size = len(parts)
    grams = parts[0]
    vmem = pl.BlockSpec(memory_space=pltpu.VMEM)
    count = grams.shape[0]
    return pl.pallas_call(
        functools.partial(update_kernel, width, count, by_rows),
        in_specs=[vmem] * (2 + size),
        out_specs=vmem,
        out_shape=jax.ShapeDtypeStruct(moment.shape, jnp.float32),
        compiler_params=pltpu.CompilerParams(vmem_limit_bytes=VMEM_LIMIT),
        cost_estimate=pl.CostEstimate(
            flops=200 * count * width**3, bytes_accessed=12 * moment.size, transcendentals=0
        ),
        name="small_update",
    )(moment, weight, *parts)


def exchange(values, owners):
    size = lax.axis_size("dp")
    me = lax.axis_index("dp")
    parts = []
    for shift in range(size):
        target = (me + shift) % size
        part = values[0]
        for value, owner in zip(values[1:], owners[1:]):
            part = jnp.where(target == owner, value, part)
        if shift:
            pairs = [((o - shift) % size, o) for o in owners]
            part = lax.ppermute(part, "dp", pairs)
        parts.append(part)
    return parts


def share_out(factor, owners):
    size = lax.axis_size("dp")
    return [factor] + [
        lax.ppermute(factor, "dp", [(o, (o + shift) % size) for o in owners])
        for shift in range(1, size)
    ]


def owned_factor(parts, owners):
    me = lax.axis_index("dp")
    own = jnp.zeros((1,), jnp.int32)
    for o in owners:
        own = own + (me == o).astype(jnp.int32)
    return block_factor(own, parts).astype(LOW)


def owned_update(moment, weight, choices, owners):
    size = lax.axis_size("dp")
    me = lax.axis_index("dp")
    places = jnp.stack([(me - o) % size for o in owners]).astype(jnp.int32)
    return apply_factors(moment, weight, places, choices)


def shards(
    inputs,
    cotangent,
    lengths,
    w_query,
    w_keyval,
    w_out,
    w_gate_up,
    w_down,
    gains,
    m_query,
    m_keyval,
    m_out,
    m_gate_up,
    m_down,
    m_gains,
):
    batches, own_rows, model_width = inputs.shape
    head_dim = w_keyval.shape[1] // 2
    half_dim = head_dim // 2
    units_here = w_down.shape[1]
    query_cols = w_query.shape[1]
    size = lax.axis_size("mp")
    me = lax.axis_index("mp")
    tokens = batches * own_rows
    seq_len = size * own_rows

    groups = lax.axis_size("dp")
    share = w_keyval.shape[0] // size

    def rows_of(value):
        return lax.all_gather(value, "dp", axis=0, tiled=False)

    gate_up_t = jnp.transpose(w_gate_up, (1, 2, 0))
    down_t = jnp.transpose(w_down)
    low_keyval = w_keyval.astype(LOW).reshape(-1, query_cols)
    query_block = rows_of(jnp.concatenate([w_query.astype(LOW), low_keyval], axis=0))
    out_block = rows_of(w_out.astype(LOW))
    full_gate_up = rows_of(gate_up_t.astype(LOW))
    out_block, low_down = tie(out_block, down_t.astype(LOW))
    full_down = rows_of(low_down)

    cot_rows = cotangent.reshape(tokens, model_width)
    cot = Gather(cot_rows, size)
    cot.first()
    cot.second()
    full_keyval = query_block[:, w_query.shape[0] :].reshape(model_width, 2 * head_dim)
    query_block = query_block[:, : w_query.shape[0]].reshape(model_width, query_cols)
    cot.parts, query_block = tie(cot.parts, query_block)
    query_gather = Gather(query_block, size)
    query_gather.first()
    cot.third()

    own_positions = me * own_rows + jnp.arange(own_rows, dtype=jnp.int32)
    key_positions = jnp.concatenate(
        [(me ^ s) * own_rows + jnp.arange(own_rows, dtype=jnp.int32) for s in gather_order(size)]
    )
    qid = []
    kid = []
    offsets = []
    for batch_index in range(batches):
        own_segment, own_offset = doc_layout(lengths[batch_index], own_positions)
        key_segment, unused = doc_layout(lengths[batch_index], key_positions)
        qid.append(jnp.stack([own_segment, own_positions], axis=1))
        kid.append(jnp.stack([key_segment, key_positions], axis=0))
        offsets.append(own_offset)
    qid = jnp.stack(qid)
    kid = jnp.stack(kid)
    cosine, sine = rotary_tables(jnp.stack(offsets), half_dim)
    flat_cos = cosine.reshape(tokens, half_dim)
    flat_sin = sine.reshape(tokens, half_dim)

    x_rows = wide(inputs).reshape(tokens, model_width)
    x_scale = inverse_scale(x_rows)
    normed = (x_rows * x_scale * gains[0]).astype(LOW)
    own_keyval = plain_dot(normed, full_keyval)
    own_keyval = jnp.concatenate(
        [rotate(own_keyval[:, :head_dim], flat_cos, flat_sin), own_keyval[:, head_dim:]], axis=1
    ).astype(LOW)
    keyval = gather_small(own_keyval.reshape(batches, own_rows, 2 * head_dim), size)
    keyval = jnp.swapaxes(keyval, 0, 1).reshape(batches, seq_len, 2 * head_dim)
    query_gather.second()
    query_gather.parts, out_block = tie(query_gather.parts, out_block)
    out_gather = Gather(out_block.reshape(model_width, query_cols), size)
    out_gather.first()
    query_gather.third()
    query_pieces = query_gather.pieces()
    queries = project(normed, query_pieces, head_dim, (flat_cos, flat_sin))
    queries = queries.reshape(batches, own_rows, -1)
    contexts = []
    logs = []
    for batch in range(batches):
        context, log_sums = attention_forward(batch, queries, keyval, qid, kid, head_dim)
        contexts.append(context)
        logs.append(log_sums)
        if batch == 0:
            out_gather.parts, queries, contexts = tie(out_gather.parts, queries, contexts)
            out_gather.second()
    out_gather.parts, contexts = tie(out_gather.parts, contexts)
    out_gather.third()
    context = jnp.concatenate(contexts, axis=0).reshape(tokens, -1)
    full_cot = in_steps(cot.pieces())
    out_pieces = out_gather.pieces()
    mid = x_rows + project_back(context, out_pieces, model_width)
    mid_scale = inverse_scale(mid)
    normed_mid_rows = (mid * mid_scale * gains[1]).astype(LOW)
    mid_gather = Gather(normed_mid_rows, size)
    mid_gather.first()
    mid_gather.parts, full_cot = tie(mid_gather.parts, full_cot)
    mid_gather.second()
    mid_gather.third()

    normed_mid, gate, upward, hidden, hidden_t = hidden_units(mid_gather.pieces(), full_gate_up)
    sum_down = units_sum([hidden_t], full_cot, groups)
    sum_down, gate = tie(sum_down, gate)
    d_mid_sum = Scatter(size)
    backs = []
    for run in range(2):
        *turned, evens, odds = hidden_back(
            run, full_cot, gate, upward, full_gate_up, full_down, size
        )
        backs.append(turned)
        if run == 0:
            odds, gate = tie(odds, gate)
        else:
            d_mid_sum.parts, odds = tie(d_mid_sum.parts, odds)
        d_mid_sum.first(evens, odds)
    d_mid_sum.second()
    sum_gate = units_sum([back[0] for back in backs], normed_mid, groups)

    def scatter_rows(value):
        return lax.psum_scatter(value, "dp", scatter_dimension=0, tiled=False)

    old_gate_up = jnp.transpose(m_gate_up, (1, 2, 0))
    old_down = jnp.transpose(m_down)
    grad_down = scatter_rows(sum_down)
    sum_gate, backs = tie(sum_gate, backs)
    grad_gate = scatter_rows(sum_gate)
    sum_up = units_sum([back[1] for back in backs], normed_mid, groups)
    d_mid_sum.parts, sum_up, hidden, grad_down = tie(d_mid_sum.parts, sum_up, hidden, grad_down)
    grad_up = scatter_rows(sum_up)
    d_mid_sum.third()
    mlp_sum = Scatter(size)
    mlp_parts = [hidden_out(run, hidden, full_down, size) for run in range(2)]
    d_mid_sum.parts, mlp_parts = tie(d_mid_sum.parts, mlp_parts)
    for evens, odds in mlp_parts:
        mlp_sum.first(evens, odds)
    d_mid_norm = d_mid_sum.total()
    d_mid = wide(cot_rows) + norm_back(d_mid_norm, mid, mid_scale, gains[1])
    gain_mid = jnp.sum(d_mid_norm * mid * mid_scale, axis=0)

    d_mid_low = d_mid.astype(LOW)
    out_sum = Scatter(size)
    out_parts = [blocks_sum(run, d_mid_low, context, size) for run in range(2)]
    mlp_sum.parts, out_parts, d_mid_low = tie(mlp_sum.parts, out_parts, d_mid_low)
    for evens, odds in out_parts:
        out_sum.first(evens, odds)
    mlp_sum.second()
    d_context = project(d_mid_low, out_pieces, head_dim).reshape(batches, own_rows, -1)
    out_sum.parts, d_context = tie(out_sum.parts, d_context)
    out_sum.second()
    fast = groups == 4 and units_here == 2 * FF_BLOCK
    grad_down = wide(grad_down)
    moment_down = DECAY * old_down + grad_down
    moment_gate = DECAY * old_gate_up[0] + wide(grad_gate)
    first_owners = (0, 1, 2, 3)
    last_owners = (1, 2)
    backs = []
    for batch in range(batches):
        backs.append(
            attention_backward(
                batch, queries, d_context, logs[batch], keyval, qid, kid, cosine, sine, head_dim
            )
        )
        if batch == 0:
            backs, mlp_sum.parts, d_context, moment_down, moment_gate = tie(
                backs, mlp_sum.parts, d_context, moment_down, moment_gate
            )
            mlp_sum.third()
            if fast:
                down_grams = block_grams(moment_down, FF_BLOCK, True)
                gate_grams = block_grams(moment_gate, FF_BLOCK, True)
                first_parts = exchange(
                    (gate_grams[0], down_grams[0], down_grams[1], gate_grams[1]), first_owners
                )
    backs, out_sum.parts, grad_up = tie(backs, out_sum.parts, grad_up)
    out_sum.third()
    d_queries = jnp.concatenate([back[0] for back in backs], axis=0).reshape(tokens, -1)
    d_keyval = jnp.concatenate([back[1] for back in backs], axis=0).astype(LOW)

    def own_rows_of(total, width):
        return scatter_rows(total.astype(LOW).reshape(groups, -1, width))

    query_sum = Scatter(size)
    for run in range(2):
        evens, odds = blocks_sum(run, normed, d_queries, size)
        query_sum.first(evens, odds)
    query_sum.parts, out_sum.parts, d_queries = tie(query_sum.parts, out_sum.parts, d_queries)
    query_sum.second()
    grad_out = own_rows_of(out_sum.total(), query_cols)
    d_keyval = d_keyval.reshape(batches, size, own_rows, 2 * head_dim)
    d_keyval = scatter_small(jnp.swapaxes(d_keyval, 0, 1), size).reshape(tokens, 2 * head_dim)
    output = (mid + mlp_sum.total()).astype(LOW).reshape(inputs.shape)
    d_normed = project_back(d_queries, query_pieces, model_width)
    d_keyval, d_normed = tie(d_keyval, d_normed)
    d_keyval = jnp.concatenate(
        [rotate(d_keyval[:, :head_dim], flat_cos, -flat_sin), d_keyval[:, head_dim:]], axis=1
    ).astype(LOW)
    sum_keyval = outer_sum(normed, d_keyval).astype(LOW)
    sum_keyval = jnp.swapaxes(sum_keyval.reshape(groups, size, share, 2 * head_dim), 0, 1)
    order = jnp.array(gather_order(size), jnp.int32)
    sum_keyval = sum_keyval[me ^ order]
    moment_up = DECAY * old_gate_up[1] + wide(grad_up)
    if fast:
        up_grams = block_grams(moment_up, FF_BLOCK, True)
        up_grams, sum_keyval = tie(up_grams, sum_keyval)
        last_parts = exchange(up_grams, last_owners)
    share_sums = scatter_small(sum_keyval, size).astype(LOW)
    d_normed = d_normed + rows_dot(d_keyval, full_keyval)
    input_grad = (d_mid + norm_back(d_normed, x_rows, x_scale, gains[0])).astype(LOW)
    input_grad = input_grad.reshape(inputs.shape)
    gain_input = jnp.sum(d_normed * x_rows * x_scale, axis=0)
    if fast:
        share_sums, first_parts, input_grad = tie(share_sums, first_parts, input_grad)
        first_factor = owned_factor(first_parts, first_owners)
        query_sum.parts, first_factor = tie(query_sum.parts, first_factor)
    query_sum.third()
    my_group = lax.axis_index("dp")
    share_parts = [share_sums[my_group]]
    for shift in range(1, groups):
        part = share_sums[(my_group + shift) % groups]
        pairs = [(i, (i + shift) % groups) for i in range(groups)]
        share_parts.append(lax.ppermute(part, "dp", pairs))
    if fast:
        first_factor, share_parts = tie(first_factor, share_parts)
        first_choices = share_out(first_factor, first_owners)
    grad_keyval = wide(share_parts[0])
    for part in share_parts[1:]:
        grad_keyval = grad_keyval + wide(part)
    grad_keyval = gather_small(grad_keyval.astype(LOW), size)
    if fast:
        last_factor = owned_factor(last_parts, last_owners)
        query_sum.parts, grad_keyval, last_factor = tie(
            query_sum.parts, grad_keyval, last_factor
        )
        last_choices = share_out(last_factor, last_owners)
    grad_query = own_rows_of(query_sum.total(), query_cols)
    place = jnp.zeros((size,), jnp.int32).at[order].set(jnp.arange(size, dtype=jnp.int32))
    grad_keyval = grad_keyval[place[me ^ jnp.arange(size)]]
    grad_keyval = wide(grad_keyval).reshape(w_keyval.shape)
    moment_keyval = DECAY * m_keyval + grad_keyval
    keyval_grams = gather_grams(moment_keyval, 2 * head_dim, False)
    grad_out = wide(grad_out)
    moment_out = DECAY * m_out + grad_out
    out_grams = gather_grams(moment_out, head_dim, False)
    if fast:
        new_down = owned_update(moment_down, down_t, first_choices, (1, 2))
        new_gate = owned_update(moment_gate, gate_up_t[0], first_choices, (0, 3))
        new_down, new_gate, grad_query = tie(new_down, new_gate, grad_query)
    else:
        new_down = small_update(moment_down, down_t, FF_BLOCK, True)
        new_gate = small_update(moment_gate, gate_up_t[0], FF_BLOCK, True)
    grad_query = wide(grad_query)
    moment_query = DECAY * m_query + grad_query
    query_grams = gather_grams(moment_query, head_dim, False)
    if fast:
        new_up = owned_update(moment_up, gate_up_t[1], last_choices, last_owners)
    else:
        new_up = small_update(moment_up, gate_up_t[1], FF_BLOCK, True)
    new_out = small_update(moment_out, w_out, head_dim, False, out_grams)
    new_keyval = small_update(moment_keyval, w_keyval, 2 * head_dim, False, keyval_grams)
    new_query = small_update(moment_query, w_query, head_dim, False, query_grams)
    grad_gains = add_all(add_all(jnp.stack([gain_input, gain_mid], axis=0), "mp"), "dp")
    grad_gate_up = wide(jnp.stack([grad_gate, grad_up]))
    moment_gate_up = DECAY * old_gate_up + grad_gate_up
    new_gate_up = jnp.stack([new_gate, new_up])

    def back(value):
        return jnp.transpose(value, (2, 0, 1))

    moment_gains = DECAY * m_gains + grad_gains
    new_gains = gains - GAIN_RATE * moment_gains
    return (
        output,
        input_grad,
        grad_query,
        grad_keyval,
        grad_out,
        back(grad_gate_up),
        jnp.transpose(grad_down),
        grad_gains,
        moment_query,
        moment_keyval,
        moment_out,
        back(moment_gate_up),
        jnp.transpose(moment_down),
        moment_gains,
        new_query,
        new_keyval,
        new_out,
        back(new_gate_up),
        jnp.transpose(new_down),
        new_gains,
    )


def solution(mesh):
    rows = P("dp", None)
    both = P("dp", "mp")
    tokens = P("dp", "mp", None)
    gate_up = P("dp", None, "mp")
    weights = (both, rows, both, gate_up, both, P())
    return jax.shard_map(
        shards,
        mesh=mesh,
        in_specs=(tokens, tokens, rows) + weights + weights,
        out_specs=(tokens, tokens) + weights + weights + weights,
        check_vma=False,
    )
```

time: 2210 us -> 898 us (0.41)
  waiting for transfers between devices: 1380 us -> 209 us
  matrix products: 460 us -> 7.28 us
  Pallas kernels: 0 us -> 315 us
  starting transfers between devices: 2.98 us -> 144 us
  other arithmetic: 181 us -> 95.2 us
  blocking collectives: 43 us -> 0 us
    psum x8 -> x0, waiting for transfers between devices: 659 us -> none  [the longest x5 304 us: gram_sum(): lax.psum(block_gram(matrices[0]).astype(jnp.bfloat16), 'dp')]
    dot_general x141 -> x3, matrix products: 460 us -> 7.28 us  [contract(): lax.dot_general(left, right, (((left_dim,), (right_dim,)), ((), ())), pre...]
    reduce_scatter x9 -> x5, waiting for transfers between devices: 383 us -> 0.01 us  [scatter_rows(): return lax.psum_scatter(value, 'dp', scatter_dimension=0, tiled=False)]
    all_gather x7 -> x4, waiting for transfers between devices: 333 us -> 2.99 us  [rows_of(): return lax.all_gather(value, 'dp', axis=0, tiled=False)]
    pallas_call x0 -> x34, Pallas kernels: none -> 315 us  [the longest x2 44.1 us: attention_backward(): pl.pallas_call(functools.partial(backward_kernel, heads, head_dim), grid=...]
    ppermute x0 -> x101, waiting for transfers between devices: none -> 206 us  [the longest x72 157 us: swap(): return lax.ppermute(value, 'mp', [(i, i ^ flip) for i in range(size)])]
    ppermute x0 -> x101, starting transfers between devices: none -> 143 us  [the longest x72 47.6 us: swap(): return lax.ppermute(value, 'mp', [(i, i ^ flip) for i in range(size)])]
    convert_element_type x4 -> x1, local copies, waits for them, and re-layouts: 58.3 us -> 0.09 us  [rotary_tables(): angle = offset.astype(jnp.float32)[..., None] * freqs]
  transfers between devices with their start and end apart: 24 -> 110, of which waited for: 22 -> 31; matrix products, arithmetic and copies ran while one was open for 14% -> 18% of each run, Pallas kernels for 0% -> 35%
where the time goes in v1:
time: 898 us; the launch traced here: 890 us
  Pallas kernels  315 us (35%)
  waiting for transfers between devices  209 us (23%)
  starting transfers between devices  144 us (16%)
  local copies, waits for them, and re-layouts  102 us (11%)
  other arithmetic  95.2 us (11%)
  between operations  17 us (2%)
    ppermute x72, waiting for transfers between devices, swap(): return lax.ppermute(value, 'mp', [(i, i ^ flip) for i in range(size)])  157 us
    unnamed x357, local copies, waits for them, and re-layouts  74.2 us
    ppermute x72, starting transfers between devices, swap(): return lax.ppermute(value, 'mp', [(i, i ^ flip) for i in range(size)])  47.6 us
    pallas_call x2, Pallas kernels, attention_backward(): pl.pallas_call(functools.partial(backward_kernel, heads, head_dim), grid=...  44.1 us
    pallas_call x2, Pallas kernels, hidden_back(): pl.pallas_call(functools.partial(hidden_back_kernel, turn), grid=(steps,)...  43.8 us
    pallas_call x3, Pallas kernels, units_sum(): pl.pallas_call(functools.partial(units_sum_kernel, len(units), turn), gri...  37.4 us
    ppermute x6, waiting for transfers between devices, share_out(): lax.ppermute(factor, 'dp', [(o, (o + shift) % size) for o in owners])  37.2 us
    ppermute x9, starting transfers between devices, gather_grams(): lax.ppermute(grams, 'dp', [(i, (i + shift) % size) for i in range(size)])  34.2 us
  transfers between devices with their start and end apart: 110, of which 31 were waited for; matrix products, arithmetic and copies ran while one was open for 18% of the time, Pallas kernels for 35%

profile of v1, /device:TPU:0, one launch (start us, length us, event | category | flops | bytes accessed | tf_op | source)
XLA Modules:
  0.0 889.7 jit_solution(17428167353272444563)
XLA Ops:
  24.1 28.2 %collective-permute-done = bf16[384,2048]{1,0:T(8,128)(2,1)} collective-permute-done((bf16[384,2048]{1,0:T(8,128)(2,1)}, bf16[384,2048]{1,0:T(8,128)(2,1)}, u32[]{:S(2)}, u32[]{:S(2)}) %collective-permute-start) | collective-permute-done | bytes 1572896 | tf_op jit(solution)/shard_map/ppermute | solution.py:89
  69.3 9.0 %collective-permute-done.3 = bf16[192,2048]{1,0:T(8,128)(2,1)} collective-permute-done((bf16[192,2048]{1,0:T(8,128)(2,1)}, bf16[192,2048]{1,0:T(8,128)(2,1)}, u32[]{:S(2)}, u32[]{:S(2)}) %collective-permute-start.3) | collective-permute-done | bytes 786464 | tf_op jit(solution)/shard_map/ppermute | solution.py:89
  106.6 10.8 %collective-permute-done.7.refs_4_ = bf16[2048,256]{1,0:T(8,128)(2,1)S(1)} collective-permute-done((bf16[2048,256]{1,0:T(8,128)(2,1)S(1)}, bf16[2048,256]{1,0:T(8,128)(2,1)S(1)}, u32[]{:S(2)}, u32[]{:S(2)}) %collective-permute-start.7) | collective-permute-done | bytes 1048608 | tf_op jit(solution)/shard_map/ppermute | solution.py:89
  125.5 7.6 collective-permute-done.10.refs_7_
  139.8 9.9 %project.2 = bf16[384,2048]{1,0:T(8,128)(2,1)S(1)} custom-call(bf16[2048,256]{1,0:T(8,128)(2,1)S(1)} %bitcast.214, bf16[2048,256]{1,0:T(8,128)(2,1)S(1)} %collective-permute-done.9.refs_1_, bf16[2048,256]{1,0:T(8,128)(2,1)S(1)} %collective-permute-done.11.refs_2_, bf16[2048,256]{1,0:T(8,128)(2,1)S(1)} %collective-permute-done.13.refs_3_, ...), custom_call_target="tpu_custom_call" | custom-call | flops 3221225472 | bytes 11534336 | tf_op jit(solution)/shard_map/project/pallas_call | solution.py:448
  149.8 12.6 %attention_forward.2 = (bf16[1,192,2048]{2,1,0:T(8,128)(2,1)S(1)}, f32[1,192,2048]{2,1,0:T(8,128)S(1)}) custom-call(bf16[2,192,2048]{2,1,0:T(8,128)(2,1)S(1)} %bitcast.226, bf16[2,1536,256]{2,1,0:T(8,128)(2,1)S(1)} %bitcast.222, s32[2,192,2]{2,1,0:T(8,128)S(1)} %copy.59.qid_ref, s32[2,2,1536]{2,1,0:T(2,128)S(1)} %pad_add_fusion.kid_ref), custom_call_target="tpu_custom_call" | custom-call | flops 4831838208 | bytes 3145728 | tf_op jit(solution)/shard_map/attention_forward/pallas_call | solution.py:273
  172.1 13.0 %attention_forward.3 = (bf16[1,192,2048]{2,1,0:T(8,128)(2,1)S(1)}, f32[1,192,2048]{2,1,0:T(8,128)S(1)}) custom-call(bf16[2,192,2048]{2,1,0:T(8,128)(2,1)S(1)} %bitcast.227, bf16[2,1536,256]{2,1,0:T(8,128)(2,1)S(1)} %bitcast.223, s32[2,192,2]{2,1,0:T(8,128)S(1)} %copy.59.qid_ref, s32[2,2,1536]{2,1,0:T(2,128)S(1)} %pad_add_fusion.kid_ref), custom_call_target="tpu_custom_call" | custom-call | flops 4831838208 | bytes 3145728 | tf_op jit(solution)/shard_map/attention_forward/pallas_call | solution.py:273
  188.7 5.2 project_back.2
  205.7 26.8 %collective-permute-done.28.refs_4_ = bf16[384,2048]{1,0:T(8,128)(2,1)} collective-permute-done((bf16[384,2048]{1,0:T(8,128)(2,1)S(1)}, bf16[384,2048]{1,0:T(8,128)(2,1)}, u32[]{:S(2)}, u32[]{:S(2)}) %collective-permute-start.28) | collective-permute-done | bytes 1572896 | tf_op jit(solution)/shard_map/ppermute | solution.py:89
  238.7 16.4 %collective-permute-done.35.refs_6_ = bf16[192,2048]{1,0:T(8,128)(2,1)} collective-permute-done((bf16[192,2048]{1,0:T(8,128)(2,1)S(1)}, bf16[192,2048]{1,0:T(8,128)(2,1)}, u32[]{:S(2)}, u32[]{:S(2)}) %collective-permute-start.35) | collective-permute-done | bytes 786464 | tf_op jit(solution)/shard_map/ppermute | solution.py:89
  261.5 29.0 %hidden_units.1 = (bf16[3072,2048]{1,0:T(8,128)(2,1)}, f32[3072,704]{1,0:T(8,128)}, f32[3072,704]{1,0:T(8,128)}, bf16[3072,704]{1,0:T(8,128)(2,1)}, bf16[704,3072]{1,0:T(8,128)(2,1)}) custom-call(bf16[384,2048]{1,0:T(8,128)(2,1)S(1)} %multiply_convert_fusion.refs_0_, bf16[384,2048]{1,0:T(8,128)(2,1)S(1)} %copy-done.100, ...), custom_call_target="tpu_custom_call" | custom-call | flops 17716740096 | bytes 25165824 | tf_op jit(solution)/shard_map/hidden_units/pallas_call | solution.py:587
  292.7 12.5 %units_sum.3 = bf16[4,704,512]{2,1,0:T(8,128)(2,1)S(1)} custom-call(bf16[704,3072]{1,0:T(8,128)(2,1)S(1)} %copy-done.109, bf16[3072,2048]{1,0:T(8,128)(2,1)} %slice_dynamic-update-slice_fusion.refs_1_.cot_ref), custom_call_target="tpu_custom_call" | custom-call | flops 8858370048 | bytes 16908288 | tf_op jit(solution)/shard_map/units_sum/pallas_call | solution.py:732
  308.8 22.5 %hidden_back.2 = (bf16[704,1536]{1,0:T(8,128)(2,1)S(1)}, bf16[704,1536]{1,0:T(8,128)(2,1)S(1)}, bf16[4,192,2048]{2,1,0:T(8,128)(2,1)S(1)}, bf16[4,192,2048]{2,1,0:T(8,128)(2,1)}) custom-call(bf16[3072,2048]{1,0:T(8,128)(2,1)} %slice_dynamic-update-slice_fusion.refs_1_.cot_ref, f32[3072,704]{1,0:T(8,128)} %get-tuple-element.241.gate_ref, ...), custom_call_target="tpu_custom_call" | custom-call | flops 13287555072 | bytes 12582912 | tf_op jit(solution)/shard_map/hidden_back/pallas_call | solution.py:654
  334.4 21.3 %hidden_back.3 = (bf16[704,1536]{1,0:T(8,128)(2,1)S(1)}, bf16[704,1536]{1,0:T(8,128)(2,1)S(1)}, bf16[4,192,2048]{2,1,0:T(8,128)(2,1)S(1)}, bf16[4,192,2048]{2,1,0:T(8,128)(2,1)S(1)}) custom-call(bf16[3072,2048]{1,0:T(8,128)(2,1)} %slice_dynamic-update-slice_fusion.refs_1_.cot_ref, f32[3072,704]{1,0:T(8,128)} %get-tuple-element.241.gate_ref, ...), custom_call_target="tpu_custom_call" | custom-call | flops 13287555072 | bytes 12582912 | tf_op jit(solution)/shard_map/hidden_back/pallas_call | solution.py:654
  360.4 12.3 %units_sum.4 = bf16[4,704,512]{2,1,0:T(8,128)(2,1)S(1)} custom-call(bf16[704,1536]{1,0:T(8,128)(2,1)S(1)} %get-tuple-element.246.refs_0_, bf16[704,1536]{1,0:T(8,128)(2,1)S(1)} %get-tuple-element.247.refs_1_, bf16[3072,2048]{1,0:T(8,128)(2,1)} %get-tuple-element.248.refs_2_), custom_call_target="tpu_custom_call" | custom-call | flops 8858370048 | bytes 16908288 | tf_op jit(solution)/shard_map/units_sum/pallas_call | solution.py:732
  376.4 4.2 add_convert_fusion.1
  384.5 12.6 %units_sum.5 = bf16[4,704,512]{2,1,0:T(8,128)(2,1)S(1)} custom-call(bf16[704,1536]{1,0:T(8,128)(2,1)S(1)} %copy-done.106, bf16[704,1536]{1,0:T(8,128)(2,1)S(1)} %copy-done.108, bf16[3072,2048]{1,0:T(8,128)(2,1)} %get-tuple-element.248.refs_2_), custom_call_target="tpu_custom_call" | custom-call | flops 8858370048 | bytes 16908288 | tf_op jit(solution)/shard_map/units_sum/pallas_call | solution.py:732
  398.7 20.4 %collective-permute-done.41 = bf16[2,192,2048]{2,1,0:T(8,128)(2,1)S(1)} collective-permute-done((bf16[2,192,2048]{2,1,0:T(8,128)(2,1)}, bf16[2,192,2048]{2,1,0:T(8,128)(2,1)S(1)}, u32[]{:S(2)}, u32[]{:S(2)}) %collective-permute-start.41) | collective-permute-done | bytes 1572896 | tf_op jit(solution)/shard_map/ppermute | solution.py:89
  426.8 6.4 hidden_out.2
  434.8 6.5 hidden_out.3
  456.2 4.1 fusion.67
  460.3 4.3 blocks_sum.4
  464.6 4.1 blocks_sum.5
  480.9 8.4 project.3
  493.3 22.1 %attention_backward.2 = (bf16[1,192,2048]{2,1,0:T(8,128)(2,1)S(1)}, f32[1,1536,256]{2,1,0:T(8,128)S(1)}) custom-call(bf16[2,192,2048]{2,1,0:T(8,128)(2,1)S(1)} %bitcast.228, bf16[2,192,2048]{2,1,0:T(8,128)(2,1)S(1)} %bitcast.242, f32[1,192,2048]{2,1,0:T(8,128)S(1)} %copy-done.113, bf16[2,1536,256]{2,1,0:T(8,128)(2,1)S(1)} %bitcast.224, ...), custom_call_target="tpu_custom_call" | custom-call | flops 12079595520 | bytes 4718592 | tf_op jit(solution)/shard_map/attention_backward/pallas_call | solution.py:357
  526.4 21.9 %attention_backward.3 = (bf16[1,192,2048]{2,1,0:T(8,128)(2,1)S(1)}, f32[1,1536,256]{2,1,0:T(8,128)S(1)}) custom-call(bf16[2,192,2048]{2,1,0:T(8,128)(2,1)S(1)} %bitcast.229, bf16[2,192,2048]{2,1,0:T(8,128)(2,1)S(1)} %bitcast.243, f32[1,192,2048]{2,1,0:T(8,128)S(1)} %copy-done.111, bf16[2,1536,256]{2,1,0:T(8,128)(2,1)S(1)} %bitcast.225, ...), custom_call_target="tpu_custom_call" | custom-call | flops 12079595520 | bytes 4718592 | tf_op jit(solution)/shard_map/attention_backward/pallas_call | solution.py:357
  554.8 4.6 bitcast_add_fusion.2
  589.7 6.0 collective-permute-done.57
  601.3 5.6 project_back.3
  614.7 4.7 fusion.12
  623.2 5.6 fusion.9
  635.6 5.8 collective-permute-done.63
  647.9 15.8 %collective-permute-start.70 = (bf16[64,256]{1,0:T(8,128)(2,1)S(1)}, bf16[64,256]{1,0:T(8,128)(2,1)S(1)}, u32[]{:S(2)}, u32[]{:S(2)}) collective-permute-start(bf16[64,256]{1,0:T(8,128)(2,1)S(1)} %get-tuple-element.429), channel_id=1, source_target_pairs={{0,8},{8,16},{16,24},{24,0},{1,9},{9,17},{17,25},{25,1},{2,10},{10... | collective-permute-start | bytes 98312 | tf_op jit(solution)/shard_map/ppermute | solution.py:1221
  666.1 24.4 %block_factor.2 = f32[352,352]{1,0:T(8,128)S(1)} custom-call(s32[1]{0:T(128)S(6)} %add.613.own_ref, f32[352,352]{1,0:T(8,128)S(1)} %copy-done.72, f32[352,352]{1,0:T(8,128)} %collective-permute-done.65.refs_1_, f32[352,352]{1,0:T(8,128)} %collective-permute-done.66.refs_2_, f32[352,352]{1,0:T(8,128)} %collective-permute-done.67.refs_3_), custom_call_target="tpu_custom_call" | custom-call | flops 8722841600 | bytes 2478080 | tf_op jit(solution)/shard_map/block_factor/pallas_call | solution.py:857
  710.0 8.3 collective-permute-done.82.refs_2_
  718.3 7.8 block_factor.3
  732.2 19.0 %collective-permute-start.73 = (bf16[352,352]{1,0:T(8,128)(2,1)S(1)}, bf16[352,352]{1,0:T(8,128)(2,1)S(1)}, u32[]{:S(2)}, u32[]{:S(2)}) collective-permute-start(bf16[352,352]{1,0:T(8,128)(2,1)S(1)} %convert_element_type.566.refs_0_), channel_id=1, source_target_pairs={{0,8},{8,16},{16,24},{24,0},{1,9},{9,17},{17,25},{25,1},{2,10},{10... | collective-permute-start | bytes 743432 | tf_op jit(solution)/shard_map/ppermute | solution.py:969
  754.7 8.7 collective-permute-done.73.refs_1_
  763.4 14.3 %collective-permute-done.74.refs_2_ = bf16[352,352]{1,0:T(8,128)(2,1)S(1)} collective-permute-done((bf16[352,352]{1,0:T(8,128)(2,1)S(1)}, bf16[352,352]{1,0:T(8,128)(2,1)S(1)}, u32[]{:S(2)}, u32[]{:S(2)}) %collective-permute-start.74) | collective-permute-done | bytes 247840 | tf_op jit(solution)/shard_map/ppermute | solution.py:969
  777.7 7.8 collective-permute-done.75.refs_3_
  785.5 4.4 apply_factors.3
  803.2 11.4 %collective-permute-start.92 = (f32[1,256,256]{2,1,0:T(8,128)}, f32[1,256,256]{2,1,0:T(8,128)}, u32[]{:S(2)}, u32[]{:S(2)}) collective-permute-start(f32[1,256,256]{2,1,0:T(8,128)} %bitcast.105.refs_0_), channel_id=1, source_target_pairs={{0,8},{8,16},{16,24},{24,0},{1,9},{9,17},{17,25},{25,1},{2,10},{10... | collective-permute-start | bytes 786440 | tf_op jit(solution)/shard_map/ppermute | solution.py:925
  819.7 6.4 collective-permute-done.99.refs_2_
  834.0 7.7 collective-permute-start.95
  844.4 9.9 %small_update.4 = f32[512,256]{1,0:T(8,128)} custom-call(f32[512,256]{1,0:T(8,128)S(1)} %get-tuple-element.377.matrix_ref, f32[512,256]{1,0:T(8,128)S(1)} %copy-done.88, f32[1,256,256]{2,1,0:T(8,128)} %bitcast.105.refs_0_, f32[1,256,256]{2,1,0:T(8,128)} %collective-permute-done.92.refs_1_, f32[1,256,256]{2,1,0:T(8,128)} %collective-permute-done.93.refs_2_, ...), custom_call_target="tpu_custom_call" | custom-call | flops 3355443200 | bytes 1572864 | tf_op jit(solution)/shard_map/small_update/pallas_call | solution.py:937
  854.3 7.2 small_update.5
  864.1 4.6 collective-permute-start.89
  875.5 7.2 small_update.3
  (722 shorter events, 323.2 us)
Async XLA Ops:
  7.2 54.5 %all-gather.9.cloned.1.call-start = ((), (), s32[]{:S(2)}) async-start(), calls=%async_computation.10 | async-start | bytes 2621440 | tf_op jit(solution)/shard_map/all_gather | solution.py:1020
  10.3 77.6 %all-gather.11.cloned.1.call-start = ((), (), s32[]{:S(2)}) async-start(), calls=%async_computation.11 | async-start | bytes 1310720 | tf_op jit(solution)/shard_map/all_gather | solution.py:1020
  11.1 246.4 %all-gather.13.cloned.1.call-start = ((), (), s32[]{:S(2)}) async-start(), calls=%async_computation.12 | async-start | bytes 7208960 | tf_op jit(solution)/shard_map/all_gather | solution.py:1020
  14.4 292.5 %all-gather.15.cloned.1.call-start = ((), (), s32[]{:S(2)}) async-start(), calls=%async_computation.13 | async-start | bytes 3604480 | tf_op jit(solution)/shard_map/all_gather | solution.py:1020
  14.5 37.7 %collective-permute-start = (bf16[384,2048]{1,0:T(8,128)(2,1)}, bf16[384,2048]{1,0:T(8,128)(2,1)}, u32[]{:S(2)}, u32[]{:S(2)}) collective-permute-start(bf16[384,2048]{1,0:T(8,128)(2,1)} %bitcast.1), channel_id=1, source_target_pairs={{0,4},{1,5},{2,6},{3,7},{4,0},{5,1},{6,2},{7,3},{8,12},{9,13},{10,... | collective-permute-start | bytes 4718600 | tf_op jit(solution)/shard_map/ppermute | solution.py:89
  17.5 51.5 %collective-permute-start.2 = (bf16[384,2048]{1,0:T(8,128)(2,1)}, bf16[384,2048]{1,0:T(8,128)(2,1)}, u32[]{:S(2)}, u32[]{:S(2)}) collective-permute-start(bf16[384,2048]{1,0:T(8,128)(2,1)} %bitcast.1), channel_id=1, source_target_pairs={{0,1},{1,0},{2,3},{3,2},{4,5},{5,4},{6,7},{7,6},{8,9},{9,8},{10,11... | collective-permute-start | bytes 4718600 | tf_op jit(solution)/shard_map/ppermute | solution.py:89
  17.5 37.1 %collective-permute-start.4 = (bf16[384,2048]{1,0:T(8,128)(2,1)}, bf16[384,2048]{1,0:T(8,128)(2,1)}, u32[]{:S(2)}, u32[]{:S(2)}) collective-permute-start(bf16[384,2048]{1,0:T(8,128)(2,1)} %bitcast.1), channel_id=1, source_target_pairs={{0,2},{1,3},{2,0},{3,1},{4,6},{5,7},{6,4},{7,5},{8,10},{9,11},{10,... | collective-permute-start | bytes 4718600 | tf_op jit(solution)/shard_map/ppermute | solution.py:89
  52.2 29.0 %collective-permute-start.1 = (bf16[384,2048]{1,0:T(8,128)(2,1)}, bf16[384,2048]{1,0:T(8,128)(2,1)}, u32[]{:S(2)}, u32[]{:S(2)}) collective-permute-start(bf16[384,2048]{1,0:T(8,128)(2,1)} %collective-permute-done), channel_id=1, source_target_pairs={{0,1},{1,0},{2,3},{3,2},{4,5},{5,4},{6,7},{7,6},{8,9},{9,8},{10,11... | collective-permute-start | bytes 4718600 | tf_op jit(solution)/shard_map/ppermute | solution.py:89
  87.9 331.3 %reduce-scatter.6.cloned.1.call-start = ((), (), s32[]{:S(2)}) async-start(), calls=%async_computation.5 | async-start | bytes 3604480 | tf_op jit(solution)/shard_map/reduce_scatter | solution.py:1120
  88.0 29.4 %collective-permute-start.7 = (bf16[2048,256]{1,0:T(8,128)(2,1)S(1)}, bf16[2048,256]{1,0:T(8,128)(2,1)S(1)}, u32[]{:S(2)}, u32[]{:S(2)}) collective-permute-start(bf16[2048,256]{1,0:T(8,128)(2,1)S(1)} %bitcast.211), channel_id=1, source_target_pairs={{0,4},{1,5},{2,6},{3,7},{4,0},{5,1},{6,2},{7,3},{8,12},{9,13},{10,... | collective-permute-start | bytes 3145736 | tf_op jit(solution)/shard_map/ppermute | solution.py:89
  89.5 31.1 %collective-permute-start.9 = (bf16[2048,256]{1,0:T(8,128)(2,1)S(1)}, bf16[2048,256]{1,0:T(8,128)(2,1)S(1)}, u32[]{:S(2)}, u32[]{:S(2)}) collective-permute-start(bf16[2048,256]{1,0:T(8,128)(2,1)S(1)} %bitcast.212), channel_id=1, source_target_pairs={{0,1},{1,0},{2,3},{3,2},{4,5},{5,4},{6,7},{7,6},{8,9},{9,8},{10,11... | collective-permute-start | bytes 3145736 | tf_op jit(solution)/shard_map/ppermute | solution.py:89
  97.6 38.3 %collective-permute-start.21 = (bf16[4,2,192,256]{3,2,1,0:T(8,128)(2,1)S(1)}, bf16[4,2,192,256]{3,2,1,0:T(8,128)(2,1)S(1)}, u32[]{:S(2)}, u32[]{:S(2)}) collective-permute-start(bf16[4,2,192,256]{3,2,1,0:T(8,128)(2,1)S(1)} %pad_maximum_fusion.6), channel_id=1, source_target_pairs={{0,1},{1,0},{2,3},{3,2},{4,5},{5,4},{6,7},{7,6},{8,9},{9,8},{10,11... | collective-permute-start | bytes 2359304 | tf_op jit(solution)/shard_map/ppermute | solution.py:89
  134.4 29.1 %collective-permute-start.14 = (bf16[2048,256]{1,0:T(8,128)(2,1)S(1)}, bf16[2048,256]{1,0:T(8,128)(2,1)S(1)}, u32[]{:S(2)}, u32[]{:S(2)}) collective-permute-start(bf16[2048,256]{1,0:T(8,128)(2,1)S(1)} %copy-done.60), channel_id=1, source_target_pairs={{0,4},{1,5},{2,6},{3,7},{4,0},{5,1},{6,2},{7,3},{8,12},{9,13},{10,... | collective-permute-start | bytes 3145736 | tf_op jit(solution)/shard_map/ppermute | solution.py:89
  135.0 28.5 %collective-permute-start.15 = (bf16[2048,256]{1,0:T(8,128)(2,1)S(1)}, bf16[2048,256]{1,0:T(8,128)(2,1)S(1)}, u32[]{:S(2)}, u32[]{:S(2)}) collective-permute-start(bf16[2048,256]{1,0:T(8,128)(2,1)S(1)} %copy-done.60), channel_id=1, source_target_pairs={{0,1},{1,0},{2,3},{3,2},{4,5},{5,4},{6,7},{7,6},{8,9},{9,8},{10,11... | collective-permute-start | bytes 3145736 | tf_op jit(solution)/shard_map/ppermute | solution.py:89
  135.0 28.5 %collective-permute-start.16 = (bf16[2048,256]{1,0:T(8,128)(2,1)S(1)}, bf16[2048,256]{1,0:T(8,128)(2,1)S(1)}, u32[]{:S(2)}, u32[]{:S(2)}) collective-permute-start(bf16[2048,256]{1,0:T(8,128)(2,1)S(1)} %copy-done.60), channel_id=1, source_target_pairs={{0,2},{1,3},{2,0},{3,1},{4,6},{5,7},{6,4},{7,5},{8,10},{9,11},{10,... | collective-permute-start | bytes 3145736 | tf_op jit(solution)/shard_map/ppermute | solution.py:89
  196.1 36.4 %collective-permute-start.28 = (bf16[384,2048]{1,0:T(8,128)(2,1)S(1)}, bf16[384,2048]{1,0:T(8,128)(2,1)}, u32[]{:S(2)}, u32[]{:S(2)}) collective-permute-start(bf16[384,2048]{1,0:T(8,128)(2,1)S(1)} %multiply_convert_fusion.refs_0_), channel_id=1, source_target_pairs={{0,4},{1,5},{2,6},{3,7},{4,0},{5,1},{6,2},{7,3},{8,12},{9,13},{10,... | collective-permute-start | bytes 4718600 | tf_op jit(solution)/shard_map/ppermute | solution.py:89
  196.7 35.9 %collective-permute-start.29 = (bf16[384,2048]{1,0:T(8,128)(2,1)S(1)}, bf16[384,2048]{1,0:T(8,128)(2,1)S(1)}, u32[]{:S(2)}, u32[]{:S(2)}) collective-permute-start(bf16[384,2048]{1,0:T(8,128)(2,1)S(1)} %multiply_convert_fusion.refs_0_), channel_id=1, source_target_pairs={{0,1},{1,0},{2,3},{3,2},{4,5},{5,4},{6,7},{7,6},{8,9},{9,8},{10,11... | collective-permute-start | bytes 4718600 | tf_op jit(solution)/shard_map/ppermute | solution.py:89
  196.7 37.1 %collective-permute-start.30 = (bf16[384,2048]{1,0:T(8,128)(2,1)S(1)}, bf16[384,2048]{1,0:T(8,128)(2,1)}, u32[]{:S(2)}, u32[]{:S(2)}) collective-permute-start(bf16[384,2048]{1,0:T(8,128)(2,1)S(1)} %multiply_convert_fusion.refs_0_), channel_id=1, source_target_pairs={{0,2},{1,3},{2,0},{3,1},{4,6},{5,7},{6,4},{7,5},{8,10},{9,11},{10,... | collective-permute-start | bytes 4718600 | tf_op jit(solution)/shard_map/ppermute | solution.py:89
  306.9 141.7 %reduce-scatter.8.cloned.1.call-start = ((), (), s32[]{:S(2)}) async-start(), calls=%async_computation.6 | async-start | bytes 3604480 | tf_op jit(solution)/shard_map/reduce_scatter | solution.py:1120
  334.4 40.6 %collective-permute-start.39 = (bf16[4,192,2048]{2,1,0:T(8,128)(2,1)}, bf16[4,192,2048]{2,1,0:T(8,128)(2,1)}, u32[]{:S(2)}, u32[]{:S(2)}) collective-permute-start(bf16[4,192,2048]{2,1,0:T(8,128)(2,1)} %get-tuple-element.240), channel_id=1, source_target_pairs={{0,1},{1,0},{2,3},{3,2},{4,5},{5,4},{6,7},{7,6},{8,9},{9,8},{10,11... | collective-permute-start | bytes 9437192 | tf_op jit(solution)/shard_map/ppermute | solution.py:89
  374.3 185.1 %reduce-scatter.10.cloned.1.call-start = ((), (), s32[]{:S(2)}) async-start(), calls=%async_computation.7 | async-start | bytes 3604480 | tf_op jit(solution)/shard_map/reduce_scatter | solution.py:1120
  375.0 44.2 %collective-permute-start.40 = (bf16[4,192,2048]{2,1,0:T(8,128)(2,1)}, bf16[4,192,2048]{2,1,0:T(8,128)(2,1)}, u32[]{:S(2)}, u32[]{:S(2)}) collective-permute-start(bf16[4,192,2048]{2,1,0:T(8,128)(2,1)} %copy-done.96), channel_id=1, source_target_pairs={{0,1},{1,0},{2,3},{3,2},{4,5},{5,4},{6,7},{7,6},{8,9},{9,8},{10,11... | collective-permute-start | bytes 9437192 | tf_op jit(solution)/shard_map/ppermute | solution.py:89
  382.5 36.6 %collective-permute-start.41 = (bf16[2,192,2048]{2,1,0:T(8,128)(2,1)}, bf16[2,192,2048]{2,1,0:T(8,128)(2,1)S(1)}, u32[]{:S(2)}, u32[]{:S(2)}) collective-permute-start(bf16[2,192,2048]{2,1,0:T(8,128)(2,1)} %get-tuple-element.404), channel_id=1, source_target_pairs={{0,4},{1,5},{2,6},{3,7},{4,0},{5,1},{6,2},{7,3},{8,12},{9,13},{10,... | collective-permute-start | bytes 4718600 | tf_op jit(solution)/shard_map/ppermute | solution.py:89
  382.8 36.5 %collective-permute-start.42 = (bf16[2,192,2048]{2,1,0:T(8,128)(2,1)}, bf16[2,192,2048]{2,1,0:T(8,128)(2,1)}, u32[]{:S(2)}, u32[]{:S(2)}) collective-permute-start(bf16[2,192,2048]{2,1,0:T(8,128)(2,1)} %get-tuple-element.403), channel_id=1, source_target_pairs={{0,2},{1,3},{2,0},{3,1},{4,6},{5,7},{6,4},{7,5},{8,10},{9,11},{10,... | collective-permute-start | bytes 4718600 | tf_op jit(solution)/shard_map/ppermute | solution.py:89
  451.5 379.8 %reduce-scatter.14.cloned.1.call-start = ((), (), s32[]{:S(2)}) async-start(), calls=%async_computation.9 | async-start | bytes 1310720 | tf_op jit(solution)/shard_map/reduce_scatter | solution.py:1120
  477.2 38.3 %collective-permute-start.49 = (bf16[2,192,2048]{2,1,0:T(8,128)(2,1)}, bf16[2,192,2048]{2,1,0:T(8,128)(2,1)}, u32[]{:S(2)}, u32[]{:S(2)}) collective-permute-start(bf16[2,192,2048]{2,1,0:T(8,128)(2,1)} %get-tuple-element.402), channel_id=1, source_target_pairs={{0,4},{1,5},{2,6},{3,7},{4,0},{5,1},{6,2},{7,3},{8,12},{9,13},{10,... | collective-permute-start | bytes 4718600 | tf_op jit(solution)/shard_map/ppermute | solution.py:89
  477.8 37.7 %collective-permute-start.50 = (bf16[2,192,2048]{2,1,0:T(8,128)(2,1)}, bf16[2,192,2048]{2,1,0:T(8,128)(2,1)}, u32[]{:S(2)}, u32[]{:S(2)}) collective-permute-start(bf16[2,192,2048]{2,1,0:T(8,128)(2,1)} %get-tuple-element.401), channel_id=1, source_target_pairs={{0,2},{1,3},{2,0},{3,1},{4,6},{5,7},{6,4},{7,5},{8,10},{9,11},{10,... | collective-permute-start | bytes 4718600 | tf_op jit(solution)/shard_map/ppermute | solution.py:89
  518.6 36.2 %collective-permute-start.51 = (bf16[192,2048]{1,0:T(8,128)(2,1)S(1)}, bf16[192,2048]{1,0:T(8,128)(2,1)S(1)}, u32[]{:S(2)}, u32[]{:S(2)}) collective-permute-start(bf16[192,2048]{1,0:T(8,128)(2,1)S(1)} %get-tuple-element.387), channel_id=1, source_target_pairs={{0,4},{1,5},{2,6},{3,7},{4,0},{5,1},{6,2},{7,3},{8,12},{9,13},{10,... | collective-permute-start | bytes 2359304 | tf_op jit(solution)/shard_map/ppermute | solution.py:89
  520.1 34.6 %collective-permute-start.52 = (bf16[192,2048]{1,0:T(8,128)(2,1)S(1)}, bf16[192,2048]{1,0:T(8,128)(2,1)S(1)}, u32[]{:S(2)}, u32[]{:S(2)}) collective-permute-start(bf16[192,2048]{1,0:T(8,128)(2,1)S(1)} %get-tuple-element.388), channel_id=1, source_target_pairs={{0,2},{1,3},{2,0},{3,1},{4,6},{5,7},{6,4},{7,5},{8,10},{9,11},{10,... | collective-permute-start | bytes 2359304 | tf_op jit(solution)/shard_map/ppermute | solution.py:89
  524.0 35.9 %collective-permute-start.53 = (bf16[2,1024,256]{2,1,0:T(8,128)(2,1)}, bf16[2,1024,256]{2,1,0:T(8,128)(2,1)}, u32[]{:S(2)}, u32[]{:S(2)}) collective-permute-start(bf16[2,1024,256]{2,1,0:T(8,128)(2,1)} %get-tuple-element.414), channel_id=1, source_target_pairs={{0,4},{1,5},{2,6},{3,7},{4,0},{5,1},{6,2},{7,3},{8,12},{9,13},{10,... | collective-permute-start | bytes 3145736 | tf_op jit(solution)/shard_map/ppermute | solution.py:89
  525.7 35.5 %collective-permute-start.54 = (bf16[2,1024,256]{2,1,0:T(8,128)(2,1)}, bf16[2,1024,256]{2,1,0:T(8,128)(2,1)}, u32[]{:S(2)}, u32[]{:S(2)}) collective-permute-start(bf16[2,1024,256]{2,1,0:T(8,128)(2,1)} %get-tuple-element.413), channel_id=1, source_target_pairs={{0,2},{1,3},{2,0},{3,1},{4,6},{5,7},{6,4},{7,5},{8,10},{9,11},{10,... | collective-permute-start | bytes 3145736 | tf_op jit(solution)/shard_map/ppermute | solution.py:89
  568.1 33.1 %collective-permute-start.58 = (bf16[4,1024,256]{2,1,0:T(8,128)(2,1)S(1)}, bf16[4,1024,256]{2,1,0:T(8,128)(2,1)}, u32[]{:S(2)}, u32[]{:S(2)}) collective-permute-start(bf16[4,1024,256]{2,1,0:T(8,128)(2,1)S(1)} %get-tuple-element.308), channel_id=1, source_target_pairs={{0,1},{1,0},{2,3},{3,2},{4,5},{5,4},{6,7},{7,6},{8,9},{9,8},{10,11... | collective-permute-start | bytes 6291464 | tf_op jit(solution)/shard_map/ppermute | solution.py:89
  571.5 29.8 %collective-permute-start.59 = (bf16[4,1024,256]{2,1,0:T(8,128)(2,1)S(1)}, bf16[4,1024,256]{2,1,0:T(8,128)(2,1)}, u32[]{:S(2)}, u32[]{:S(2)}) collective-permute-start(bf16[4,1024,256]{2,1,0:T(8,128)(2,1)S(1)} %get-tuple-element.309), channel_id=1, source_target_pairs={{0,1},{1,0},{2,3},{3,2},{4,5},{5,4},{6,7},{7,6},{8,9},{9,8},{10,11... | collective-permute-start | bytes 6291464 | tf_op jit(solution)/shard_map/ppermute | solution.py:89
  595.7 52.1 %collective-permute-start.65 = (f32[352,352]{1,0:T(8,128)}, f32[352,352]{1,0:T(8,128)}, u32[]{:S(2)}, u32[]{:S(2)}) collective-permute-start(f32[352,352]{1,0:T(8,128)} %get-tuple-element.409), channel_id=1, source_target_pairs={{24,0},{0,8},{8,16},{16,24},{25,1},{1,9},{9,17},{17,25},{26,2},{2,... | collective-permute-start | bytes 1486856 | tf_op jit(solution)/shard_map/ppermute | solution.py:961
  597.1 50.7 %collective-permute-start.66 = (f32[352,352]{1,0:T(8,128)}, f32[352,352]{1,0:T(8,128)}, u32[]{:S(2)}, u32[]{:S(2)}) collective-permute-start(f32[352,352]{1,0:T(8,128)} %get-tuple-element.408), channel_id=1, source_target_pairs={{16,0},{24,8},{0,16},{8,24},{17,1},{25,9},{1,17},{9,25},{18,2},{26... | collective-permute-start | bytes 1486856 | tf_op jit(solution)/shard_map/ppermute | solution.py:961
  599.9 47.9 %collective-permute-start.67 = (f32[352,352]{1,0:T(8,128)}, f32[352,352]{1,0:T(8,128)}, u32[]{:S(2)}, u32[]{:S(2)}) collective-permute-start(f32[352,352]{1,0:T(8,128)} %get-tuple-element.407), channel_id=1, source_target_pairs={{8,0},{16,8},{24,16},{0,24},{9,1},{17,9},{25,17},{1,25},{10,2},{18... | collective-permute-start | bytes 1486856 | tf_op jit(solution)/shard_map/ppermute | solution.py:961
  622.7 238.8 %reduce-scatter.12.cloned.1.call-start = ((), (), s32[]{:S(2)}) async-start(), calls=%async_computation.8 | async-start | bytes 1310720 | tf_op jit(solution)/shard_map/reduce_scatter | solution.py:1120
  643.0 47.6 %collective-permute-start.68 = (bf16[2,1024,256]{2,1,0:T(8,128)(2,1)S(1)}, bf16[2,1024,256]{2,1,0:T(8,128)(2,1)S(1)}, u32[]{:S(2)}, u32[]{:S(2)}) collective-permute-start(bf16[2,1024,256]{2,1,0:T(8,128)(2,1)S(1)} %get-tuple-element.412), channel_id=1, source_target_pairs={{0,4},{1,5},{2,6},{3,7},{4,0},{5,1},{6,2},{7,3},{8,12},{9,13},{10,... | collective-permute-start | bytes 3145736 | tf_op jit(solution)/shard_map/ppermute | solution.py:89
  646.5 45.2 %collective-permute-start.69 = (bf16[2,1024,256]{2,1,0:T(8,128)(2,1)S(1)}, bf16[2,1024,256]{2,1,0:T(8,128)(2,1)S(1)}, u32[]{:S(2)}, u32[]{:S(2)}) collective-permute-start(bf16[2,1024,256]{2,1,0:T(8,128)(2,1)S(1)} %get-tuple-element.411), channel_id=1, source_target_pairs={{0,2},{1,3},{2,0},{3,1},{4,6},{5,7},{6,4},{7,5},{8,10},{9,11},{10,... | collective-permute-start | bytes 3145736 | tf_op jit(solution)/shard_map/ppermute | solution.py:89
  647.9 43.8 %collective-permute-start.70 = (bf16[64,256]{1,0:T(8,128)(2,1)S(1)}, bf16[64,256]{1,0:T(8,128)(2,1)S(1)}, u32[]{:S(2)}, u32[]{:S(2)}) collective-permute-start(bf16[64,256]{1,0:T(8,128)(2,1)S(1)} %get-tuple-element.429), channel_id=1, source_target_pairs={{0,8},{8,16},{16,24},{24,0},{1,9},{9,17},{17,25},{25,1},{2,10},{10... | collective-permute-start | bytes 98312 | tf_op jit(solution)/shard_map/ppermute | solution.py:1221
  663.7 28.1 %collective-permute-start.71 = (bf16[64,256]{1,0:T(8,128)(2,1)S(1)}, bf16[64,256]{1,0:T(8,128)(2,1)S(1)}, u32[]{:S(2)}, u32[]{:S(2)}) collective-permute-start(bf16[64,256]{1,0:T(8,128)(2,1)S(1)} %get-tuple-element.428), channel_id=1, source_target_pairs={{0,16},{8,24},{16,0},{24,8},{1,17},{9,25},{17,1},{25,9},{2,18},{10... | collective-permute-start | bytes 98312 | tf_op jit(solution)/shard_map/ppermute | solution.py:1221
  698.5 55.5 %collective-permute-start.88 = (f32[2,2048]{1,0:T(2,128)S(1)}, f32[2,2048]{1,0:T(2,128)S(1)}, u32[]{:S(2)}, u32[]{:S(2)}) collective-permute-start(f32[2,2048]{1,0:T(2,128)S(1)} %add.649), channel_id=1, source_target_pairs={{0,16},{8,24},{16,0},{24,8},{1,17},{9,25},{17,1},{25,9},{2,18},{10... | collective-permute-start | bytes 49160 | tf_op jit(solution)/shard_map/ppermute | solution.py:235
  732.2 31.2 %collective-permute-start.73 = (bf16[352,352]{1,0:T(8,128)(2,1)S(1)}, bf16[352,352]{1,0:T(8,128)(2,1)S(1)}, u32[]{:S(2)}, u32[]{:S(2)}) collective-permute-start(bf16[352,352]{1,0:T(8,128)(2,1)S(1)} %convert_element_type.566.refs_0_), channel_id=1, source_target_pairs={{0,8},{8,16},{16,24},{24,0},{1,9},{9,17},{17,25},{25,1},{2,10},{10... | collective-permute-start | bytes 743432 | tf_op jit(solution)/shard_map/ppermute | solution.py:969
  751.2 34.3 %collective-permute-start.75 = (bf16[352,352]{1,0:T(8,128)(2,1)S(1)}, bf16[352,352]{1,0:T(8,128)(2,1)S(1)}, u32[]{:S(2)}, u32[]{:S(2)}) collective-permute-start(bf16[352,352]{1,0:T(8,128)(2,1)S(1)} %convert_element_type.566.refs_0_), channel_id=1, source_target_pairs={{0,24},{8,0},{16,8},{24,16},{1,25},{9,1},{17,9},{25,17},{2,26},{10... | collective-permute-start | bytes 743432 | tf_op jit(solution)/shard_map/ppermute | solution.py:969
  795.8 30.4 %collective-permute-start.99 = (bf16[352,352]{1,0:T(8,128)(2,1)}, bf16[352,352]{1,0:T(8,128)(2,1)}, u32[]{:S(2)}, u32[]{:S(2)}) collective-permute-start(bf16[352,352]{1,0:T(8,128)(2,1)} %convert_element_type.583.refs_0_), channel_id=1, source_target_pairs={{8,24},{16,0},{9,25},{17,1},{10,26},{18,2},{11,27},{19,3},{12,28},... | collective-permute-start | bytes 743432 | tf_op jit(solution)/shard_map/ppermute | solution.py:969
  797.1 29.1 %collective-permute-start.100 = (bf16[352,352]{1,0:T(8,128)(2,1)}, bf16[352,352]{1,0:T(8,128)(2,1)}, u32[]{:S(2)}, u32[]{:S(2)}) collective-permute-start(bf16[352,352]{1,0:T(8,128)(2,1)} %convert_element_type.583.refs_0_), channel_id=1, source_target_pairs={{8,0},{16,8},{9,1},{17,9},{10,2},{18,10},{11,3},{19,11},{12,4},{20... | collective-permute-start | bytes 743432 | tf_op jit(solution)/shard_map/ppermute | solution.py:969
  803.2 38.5 %collective-permute-start.92 = (f32[1,256,256]{2,1,0:T(8,128)}, f32[1,256,256]{2,1,0:T(8,128)}, u32[]{:S(2)}, u32[]{:S(2)}) collective-permute-start(f32[1,256,256]{2,1,0:T(8,128)} %bitcast.105.refs_0_), channel_id=1, source_target_pairs={{0,8},{8,16},{16,24},{24,0},{1,9},{9,17},{17,25},{25,1},{2,10},{10... | collective-permute-start | bytes 786440 | tf_op jit(solution)/shard_map/ppermute | solution.py:925
  814.7 29.7 %collective-permute-start.93 = (f32[1,256,256]{2,1,0:T(8,128)}, f32[1,256,256]{2,1,0:T(8,128)}, u32[]{:S(2)}, u32[]{:S(2)}) collective-permute-start(f32[1,256,256]{2,1,0:T(8,128)} %bitcast.105.refs_0_), channel_id=1, source_target_pairs={{0,16},{8,24},{16,0},{24,8},{1,17},{9,25},{17,1},{25,9},{2,18},{10... | collective-permute-start | bytes 786440 | tf_op jit(solution)/shard_map/ppermute | solution.py:925
  (232 other events, 3376.1 us)
Sparse Core Ops, SparseCore 0:
  10.4 48.6 all-gather.8
  61.2 26.6 all-gather.10
  90.1 106.1 all-gather.12
  198.3 57.4 all-gather.14
  307.0 55.6 reduce-scatter.5
  374.5 55.6 reduce-scatter.7
  451.6 56.8 reduce-scatter.9
  622.9 34.1 reduce-scatter.13
  729.9 55.7 reduce-scatter.11

commit v2 on v1

--- a/solution.py
+++ b/solution.py
@@ -19,7 +19,6 @@
 MUON_RATE = 0.8
 GAIN_RATE = 0.002
 DECAY = 0.5
-HIGH = lax.Precision.HIGHEST
 MASKED = -1e30
 VMEM_LIMIT = 40 * 1024 * 1024
 LOW = jnp.bfloat16
@@ -118,6 +117,11 @@
             return
         parts["six_top"] = swap(parts["two"][: self.half], 4, self.size)
         parts["six_low"] = swap(parts["four"][self.half :], 2, self.size)
+
+    def relay(self):
+        parts = self.parts
+        if self.size != 8:
+            return
         parts["three"] = self.swap("two", 1)
         parts["five"] = self.swap("four", 1)
 
@@ -132,13 +136,15 @@
         parts = self.parts
         if self.size != 8:
             return [[(0, parts["own"])]] + [[(0, parts[str(s)])] for s in range(1, self.size)]
-        names = ("own", "one", "two", "three", "four", "five", "six", "seven")
-        return [
-            [(0, parts[name])]
-            if name in parts
-            else [(0, parts[name + "_top"]), (self.half, parts[name + "_low"])]
-            for name in names
-        ]
+        blocks = []
+        for name in ("own", "one", "two", "three", "four", "five", "six", "seven"):
+            if name in parts:
+                blocks.append([(0, parts[name])])
+            elif name + "_top" in parts:
+                blocks.append([(0, parts[name + "_top"]), (self.half, parts[name + "_low"])])
+            else:
+                blocks.append([])
+        return blocks
 
 
 def flips_of(size):
@@ -189,7 +195,7 @@
         if self.size == 8:
             self.parts["core" + str(len(self.runs))] = swap(odds, 1, self.size)
 
-    def second(self):
+    def second(self, later=None):
         if self.size != 8:
             steps = step_order(self.size)
             place = {step: (run, n) for run in (0, 1) for n, step in enumerate(steps[run])}
@@ -202,19 +208,25 @@
                 part = jnp.concatenate(halves, axis=0)
                 total = total + wide(swap(part, s, self.size) if s else part)
             self.parts["total"] = total
-            return
-        pair = wide(self.runs[0][0]) + wide(self.parts.pop("core1"))
-        self.parts["two"] = swap(pair[:2].astype(LOW), 2, self.size)
-        self.parts["four"] = swap(pair[2:].astype(LOW), 4, self.size)
-
-    def third(self):
+            return later
+        evens, core = self.runs[0][0], self.parts.pop("core1")
+        two = (wide(evens[:2]) + wide(core[:2])).astype(LOW)
+        four = (wide(evens[2:]) + wide(core[2:])).astype(LOW)
+        two, four, later = tie(two, four, later)
+        self.parts["two"] = swap(two, 2, self.size)
+        self.parts["four"] = swap(four, 4, self.size)
+        return later
+
+    def third(self, later=None):
         if self.size != 8:
-            return
+            return later
         evens, core = self.runs[1][0], self.parts["core2"]
         low = wide(evens[0]) + wide(core[0]) + wide(self.parts["four"][0])
         top = wide(evens[1]) + wide(core[1]) + wide(self.parts["two"][0])
-        self.parts["low"] = swap(low.astype(LOW), 2, self.size)
-        self.parts["top"] = swap(top.astype(LOW), 4, self.size)
+        low, top, later = tie(low.astype(LOW), top.astype(LOW), later)
+        self.parts["low"] = swap(low, 2, self.size)
+        self.parts["top"] = swap(top, 4, self.size)
+        return later
 
     def total(self):
         parts = self.parts
@@ -468,6 +480,10 @@
     count = len(places)
     piece_refs, (rows_ref, out_ref, weight_ref, sem_ref) = refs[:count], refs[count:]
     copies = fetch_all(places, piece_refs, weight_ref, sem_ref)
+    project_back_blocks(places, copies, rows_ref, out_ref, weight_ref)
+
+
+def project_back_blocks(places, copies, rows_ref, out_ref, weight_ref):
     depth = out_ref.shape[1]
     width = weight_ref.shape[2]
     for block in range(weight_ref.shape[0]):
@@ -559,10 +575,10 @@
     turned_ref[...] = (hidden.T if turn else hidden).astype(LOW)
 
 
-def in_steps(blocks):
+def in_steps(run, blocks):
     half = sum(piece.shape[0] for _, piece in blocks[0]) // 2
     rows = []
-    for pair, side in sum(step_order(len(blocks)), []):
+    for pair, side in step_order(len(blocks))[run]:
         start = side * half
         for pieces in blocks[2 * pair : 2 * pair + 2]:
             for first, piece in pieces:
@@ -571,9 +587,11 @@
     return jnp.concatenate(rows, axis=0)
 
 
-def hidden_units(blocks, gate_up):
-    places, arrays = flat_pieces(blocks)
+def hidden_units(run, blocks, gate_up):
     size = len(blocks)
+    steps = step_order(size)[run]
+    used = {2 * pair + parity for pair, _ in steps for parity in (0, 1)}
+    places, arrays = flat_pieces([part if s in used else [] for s, part in enumerate(blocks)])
     rows = max(first + count for _, first, count in places)
     depth = arrays[0].shape[1]
     units = gate_up.shape[2]
@@ -583,26 +601,26 @@
         return pl.BlockSpec((rows, width), lambda s: (s, 0))
 
     turned = pl.BlockSpec((units, rows), lambda s: (0, s)) if turn else block(units)
-    turned_shape = (units, size * rows) if turn else (size * rows, units)
+    turned_shape = (units, len(steps) * rows) if turn else (len(steps) * rows, units)
     return pl.pallas_call(
-        functools.partial(hidden_kernel, places, sum(step_order(size), []), turn),
-        grid=(size,),
+        functools.partial(hidden_kernel, places, steps, turn),
+        grid=(len(steps),),
         in_specs=[pl.BlockSpec(memory_space=pl.ANY)] * len(arrays)
         + [pl.BlockSpec(gate_up.shape, lambda s: (0, 0, 0, 0), pipeline_mode=pl.Buffered(1))],
         out_specs=[block(depth), block(units), block(units), block(units), turned],
         out_shape=[
-            jax.ShapeDtypeStruct((size * rows, depth), LOW),
-            jax.ShapeDtypeStruct((size * rows, units), jnp.float32),
-            jax.ShapeDtypeStruct((size * rows, units), jnp.float32),
-            jax.ShapeDtypeStruct((size * rows, units), LOW),
+            jax.ShapeDtypeStruct((len(steps) * rows, depth), LOW),
+            jax.ShapeDtypeStruct((len(steps) * rows, units), jnp.float32),
+            jax.ShapeDtypeStruct((len(steps) * rows, units), jnp.float32),
+            jax.ShapeDtypeStruct((len(steps) * rows, units), LOW),
             jax.ShapeDtypeStruct(turned_shape, LOW),
         ],
         scratch_shapes=[pltpu.VMEM((2, rows, depth), LOW), pltpu.SemaphoreType.DMA((2, 2))],
         compiler_params=pltpu.CompilerParams(vmem_limit_bytes=VMEM_LIMIT),
         cost_estimate=pl.CostEstimate(
-            flops=4 * size * rows * depth * units,
-            bytes_accessed=4 * size * rows * depth,
-            transcendentals=size * rows * units,
+            flops=4 * len(steps) * rows * depth * units,
+            bytes_accessed=4 * len(steps) * rows * depth,
+            transcendentals=len(steps) * rows * units,
         ),
         name="hidden_units",
     )(*arrays, gate_up)
@@ -633,16 +651,14 @@
         odd_ref[0, :, cols] = part[part.shape[0] // 2 :]
 
 
-def hidden_back(run, cotangent, gate, upward, gate_up, down, size):
+def hidden_back(cotangent, gate, upward, gate_up, down, steps):
     tokens, depth = cotangent.shape
-    rows = tokens // size
+    rows = tokens // steps
     units = gate.shape[1]
-    steps = len(step_order(size)[run])
-    first = run * steps
     turn = rows % 128 == 0
 
     def block(width):
-        return pl.BlockSpec((rows, width), lambda s: (first + s, 0))
+        return pl.BlockSpec((rows, width), lambda s: (s, 0))
 
     if turn:
         turned = pl.BlockSpec((units, rows), lambda s: (0, s))
@@ -687,16 +703,15 @@
         odd_ref[0, :, cols] = part[part.shape[0] // 2 :]
 
 
-def hidden_out(run, hidden, down, size):
+def hidden_out(hidden, down, steps):
     tokens, units = hidden.shape
-    rows = tokens // size
-    steps = len(step_order(size)[run])
+    rows = tokens // steps
     depth = down.shape[0] * down.shape[2]
     return pl.pallas_call(
         hidden_out_kernel,
         grid=(steps,),
         in_specs=[
-            pl.BlockSpec((rows, units), lambda s: (run * steps + s, 0)),
+            pl.BlockSpec((rows, units), lambda s: (s, 0)),
             pl.BlockSpec(down.shape, lambda s: (0, 0, 0), pipeline_mode=pl.Buffered(1)),
         ],
         out_specs=[pl.BlockSpec((1, rows // 2, depth), lambda s: (s, 0, 0))] * 2,
@@ -711,42 +726,44 @@
     )(hidden, down)
 
 
-def units_sum_kernel(count, turn, *refs):
-    unit_refs, row_ref, out_ref = refs[:count], refs[count], refs[count + 1]
-    first = 0
-    total = 0.0
-    for unit_ref in unit_refs:
-        tokens = unit_ref.shape[1 if turn else 0]
-        rows = row_ref[first : first + tokens, :]
-        total = total + contract(unit_ref[...], rows, 1 if turn else 0, 0)
-        first = first + tokens
-    out_ref[0] = total.astype(LOW)
+def units_sum_kernel(runs, turn, *refs):
+    row_refs, refs = refs[:runs], refs[runs:]
+    sums = len(refs) // (runs + 1)
+    unit_refs, out_refs = refs[: runs * sums], refs[runs * sums :]
+    for number, out_ref in enumerate(out_refs):
+        total = 0.0
+        for run, row_ref in enumerate(row_refs):
+            unit_ref = unit_refs[number * runs + run]
+            total = total + contract(unit_ref[...], row_ref[...], 1 if turn else 0, 0)
+        out_ref[0] = total.astype(LOW)
 
 
 def units_sum(units, rows, groups):
-    tokens, depth = rows.shape
-    turn = sum(part.shape[1] for part in units) == tokens
-    width = units[0].shape[0 if turn else 1]
+    tokens, depth = rows[0].shape
+    turn = units[0][0].shape[1] == tokens
+    width = units[0][0].shape[0 if turn else 1]
     chunk = depth // groups
     cut = 2
+    flat = [part for parts in units for part in parts]
+    out = pl.BlockSpec((1, width, chunk // cut), lambda s: (s // cut, 0, lax.rem(s, cut)))
     return pl.pallas_call(
-        functools.partial(units_sum_kernel, len(units), turn),
+        functools.partial(units_sum_kernel, len(rows), turn),
         grid=(groups * cut,),
-        in_specs=[
+        in_specs=[pl.BlockSpec((tokens, chunk // cut), lambda s: (0, s))] * len(rows)
+        + [
             pl.BlockSpec(part.shape, lambda s: (0, 0), pipeline_mode=pl.Buffered(1))
-            for part in units
-        ]
-        + [pl.BlockSpec((tokens, chunk // cut), lambda s: (0, s))],
-        out_specs=pl.BlockSpec((1, width, chunk // cut), lambda s: (s // cut, 0, lax.rem(s, cut))),
-        out_shape=jax.ShapeDtypeStruct((groups, width, chunk), LOW),
+            for part in flat
+        ],
+        out_specs=[out] * len(units),
+        out_shape=[jax.ShapeDtypeStruct((groups, width, chunk), LOW)] * len(units),
         compiler_params=pltpu.CompilerParams(vmem_limit_bytes=VMEM_LIMIT),
         cost_estimate=pl.CostEstimate(
-            flops=2 * tokens * depth * width,
-            bytes_accessed=2 * tokens * (depth + width),
+            flops=2 * len(flat) * tokens * depth * width,
+            bytes_accessed=2 * len(flat) * tokens * (depth + width),
             transcendentals=0,
         ),
         name="units_sum",
-    )(*units, rows)
+    )(*rows, *flat)
 
 
 def pick(values, index):
@@ -787,14 +804,50 @@
     )(rows, cols)
 
 
+def split(value):
+    high = value.astype(LOW)
+    return high, (value - wide(high)).astype(LOW)
+
+
 def fine_dot(left, right, left_dim=1, right_dim=0):
-    return lax.dot_general(
-        left,
-        right,
-        (((left_dim,), (right_dim,)), ((), ())),
-        precision=HIGH,
-        preferred_element_type=jnp.float32,
-    )
+    left_high, left_low = split(left)
+    right_high, right_low = split(right)
+    small = contract(left_high, right_low, left_dim, right_dim)
+    small = small + contract(left_low, right_high, left_dim, right_dim)
+    return contract(left_high, right_high, left_dim, right_dim) + small
+
+
+def eye_of(width):
+    row = lax.broadcasted_iota(jnp.int32, (width, width), 0)
+    col = lax.broadcasted_iota(jnp.int32, (width, width), 1)
+    return row, col, jnp.where(row == col, 1.0, 0.0)
+
+
+def packed_kernel(width, matrix_ref, *gram_refs):
+    row, col, eye = eye_of(width)
+    for block, gram_ref in enumerate(gram_refs):
+        part = matrix_ref[block * width : (block + 1) * width, :]
+        gram = fine_dot(part, part, 1, 1)
+        high = wide(gram.astype(LOW))
+        low = gram - high
+        gram_ref[:width, :] = jnp.where(col >= row, high, low).astype(LOW)
+        last = jnp.sum(low * eye, axis=0, keepdims=True)
+        gram_ref[width:, :] = jnp.broadcast_to(
+            last, (gram_ref.shape[0] - width, width)
+        ).astype(LOW)
+
+
+def packed_grams(matrix, width):
+    count = matrix.shape[0] // width
+    return pl.pallas_call(
+        functools.partial(packed_kernel, width),
+        out_shape=[jax.ShapeDtypeStruct((width + 16, width), LOW)] * count,
+        compiler_params=pltpu.CompilerParams(vmem_limit_bytes=VMEM_LIMIT),
+        cost_estimate=pl.CostEstimate(
+            flops=6 * matrix.size * width, bytes_accessed=4 * matrix.size, transcendentals=0
+        ),
+        name="packed_grams",
+    )(matrix)
 
 
 def gram_kernel(width, by_rows, matrix_ref, *gram_refs):
@@ -820,10 +873,7 @@
 
 
 def newton_factor(gram):
-    width = gram.shape[0]
-    row = lax.broadcasted_iota(jnp.int32, (width, width), 0)
-    col = lax.broadcasted_iota(jnp.int32, (width, width), 1)
-    eye = jnp.where(row == col, 1.0, 0.0)
+    _, _, eye = eye_of(gram.shape[0])
     trace = jnp.sum(jnp.sum(gram * eye, axis=1, keepdims=True), axis=0, keepdims=True)
     inverse = 1.0 / (jnp.sqrt(trace) + 1e-07)
     gram = gram * inverse * inverse
@@ -838,13 +888,17 @@
 
 def factor_kernel(own_ref, *refs):
     part_refs, factor_ref = refs[:-1], refs[-1]
+    width = factor_ref.shape[0]
 
     @pl.when(own_ref[0] != 0)
     def _():
-        gram = part_refs[0][...]
+        total = wide(part_refs[0][...])
         for part_ref in part_refs[1:]:
-            gram = gram + part_ref[...]
-        factor_ref[...] = newton_factor(gram)
+            total = total + wide(part_ref[...])
+        _, _, eye = eye_of(width)
+        packed = total[:width]
+        gram = packed + packed.T + eye * (total[width : width + 1] - packed)
+        factor_ref[...] = newton_factor(gram).astype(LOW)
 
     @pl.when(own_ref[0] == 0)
     def _():
@@ -852,16 +906,16 @@
 
 
 def block_factor(own, parts):
-    width = parts[0].shape[0]
+    width = parts[0].shape[1]
     vmem = pl.BlockSpec(memory_space=pltpu.VMEM)
     return pl.pallas_call(
         factor_kernel,
         in_specs=[pl.BlockSpec(memory_space=pltpu.SMEM)] + [vmem] * len(parts),
         out_specs=vmem,
-        out_shape=jax.ShapeDtypeStruct((width, width), jnp.float32),
+        out_shape=jax.ShapeDtypeStruct((width, width), LOW),
         compiler_params=pltpu.CompilerParams(vmem_limit_bytes=VMEM_LIMIT),
         cost_estimate=pl.CostEstimate(
-            flops=200 * width**3, bytes_accessed=20 * width * width, transcendentals=0
+            flops=100 * width**3, bytes_accessed=20 * width * width, transcendentals=0
         ),
         name="block_factor",
     )(own, *parts)
@@ -874,12 +928,12 @@
 
             @pl.when(place_ref[block] == number)
             def _(choice_ref=choice_ref):
-                factor_ref[...] = choice_ref[...].astype(jnp.float32)
+                factor_ref[...] = choice_ref[...]
 
         rows = slice(block * width, (block + 1) * width)
-        new_ref[rows, :] = weight_ref[rows, :] - MUON_RATE * fine_dot(
-            factor_ref[...], matrix_ref[rows, :]
-        )
+        high, low = split(matrix_ref[rows, :])
+        product = contract(factor_ref[...], high, 1, 0) + contract(factor_ref[...], low, 1, 0)
+        new_ref[rows, :] = weight_ref[rows, :] - MUON_RATE * product
 
 
 def apply_factors(matrix, weight, places, choices):
@@ -891,10 +945,10 @@
         in_specs=[pl.BlockSpec(memory_space=pltpu.SMEM)] + [vmem] * (2 + len(choices)),
         out_specs=vmem,
         out_shape=jax.ShapeDtypeStruct(matrix.shape, jnp.float32),
-        scratch_shapes=[pltpu.VMEM((width, width), jnp.float32)],
+        scratch_shapes=[pltpu.VMEM((width, width), LOW)],
         compiler_params=pltpu.CompilerParams(vmem_limit_bytes=VMEM_LIMIT),
         cost_estimate=pl.CostEstimate(
-            flops=12 * matrix.size * width, bytes_accessed=12 * matrix.size, transcendentals=0
+            flops=4 * matrix.size * width, bytes_accessed=12 * matrix.size, transcendentals=0
         ),
         name="apply_factors",
     )(places, matrix, weight, *choices)
@@ -950,6 +1004,9 @@
 def exchange(values, owners):
     size = lax.axis_size("dp")
     me = lax.axis_index("dp")
+    if owners == tuple(range(size)):
+        parts = lax.all_to_all(jnp.stack(values), "dp", 0, 0, tiled=True)
+        return [parts[number] for number in range(size)]
     parts = []
     for shift in range(size):
         target = (me + shift) % size
@@ -971,12 +1028,58 @@
     ]
 
 
-def owned_factor(parts, owners):
+def back_factor_kernel(places, parts, *refs):
+    own_ref, refs = refs[0], refs[1:]
+    count = len(places)
+    piece_refs, refs = refs[:count], refs[count:]
+    rows_ref, part_refs = refs[0], refs[1 : 1 + parts]
+    out_ref, factor_ref, weight_ref, sem_ref = refs[1 + parts :]
+    copies = fetch_all(places, piece_refs, weight_ref, sem_ref)
+    factor_kernel(own_ref, *part_refs, factor_ref)
+    project_back_blocks(places, copies, rows_ref, out_ref, weight_ref)
+
+
+def back_and_factor(rows, blocks, depth, own, parts):
+    places, arrays = flat_pieces(blocks)
+    size = len(blocks)
+    height = max(first + count for _, first, count in places)
+    width = arrays[0].shape[1]
+    gram_width = parts[0].shape[1]
+    vmem = pl.BlockSpec(memory_space=pltpu.VMEM)
+    return pl.pallas_call(
+        functools.partial(back_factor_kernel, places, len(parts)),
+        in_specs=[pl.BlockSpec(memory_space=pltpu.SMEM)]
+        + [pl.BlockSpec(memory_space=pl.ANY)] * len(arrays)
+        + [vmem] * (1 + len(parts)),
+        out_specs=[vmem, vmem],
+        out_shape=[
+            jax.ShapeDtypeStruct((rows.shape[0], depth), jnp.float32),
+            jax.ShapeDtypeStruct((gram_width, gram_width), LOW),
+        ],
+        scratch_shapes=[
+            pltpu.VMEM((size, height, width), LOW),
+            pltpu.SemaphoreType.DMA((len(arrays),)),
+        ],
+        compiler_params=pltpu.CompilerParams(vmem_limit_bytes=VMEM_LIMIT),
+        cost_estimate=pl.CostEstimate(
+            flops=2 * rows.size * depth + 100 * gram_width**3,
+            bytes_accessed=2 * (size * height * width + 3 * rows.size),
+            transcendentals=0,
+        ),
+        name="back_and_factor",
+    )(own, *arrays, rows, *parts)
+
+
+def is_owner(owners):
     me = lax.axis_index("dp")
     own = jnp.zeros((1,), jnp.int32)
     for o in owners:
         own = own + (me == o).astype(jnp.int32)
-    return block_factor(own, parts).astype(LOW)
+    return own
+
+
+def owned_factor(parts, owners):
+    return block_factor(is_owner(owners), parts)
 
 
 def owned_update(moment, weight, choices, owners):
@@ -1027,17 +1130,19 @@
     full_gate_up = rows_of(gate_up_t.astype(LOW))
     out_block, low_down = tie(out_block, down_t.astype(LOW))
     full_down = rows_of(low_down)
+    order = jnp.array(gather_order(size), jnp.int32)
+    place = jnp.zeros((size,), jnp.int32).at[order].set(jnp.arange(size, dtype=jnp.int32))
+    place = place[me ^ jnp.arange(size)]
 
     cot_rows = cotangent.reshape(tokens, model_width)
     cot = Gather(cot_rows, size)
     cot.first()
-    cot.second()
     full_keyval = query_block[:, w_query.shape[0] :].reshape(model_width, 2 * head_dim)
     query_block = query_block[:, : w_query.shape[0]].reshape(model_width, query_cols)
     cot.parts, query_block = tie(cot.parts, query_block)
     query_gather = Gather(query_block, size)
     query_gather.first()
-    cot.third()
+    cot.relay()
 
     own_positions = me * own_rows + jnp.arange(own_rows, dtype=jnp.int32)
     key_positions = jnp.concatenate(
@@ -1067,7 +1172,9 @@
     ).astype(LOW)
     keyval = gather_small(own_keyval.reshape(batches, own_rows, 2 * head_dim), size)
     keyval = jnp.swapaxes(keyval, 0, 1).reshape(batches, seq_len, 2 * head_dim)
+    query_gather.parts, cot.parts, keyval = tie(query_gather.parts, cot.parts, keyval)
     query_gather.second()
+    query_gather.relay()
     query_gather.parts, out_block = tie(query_gather.parts, out_block)
     out_gather = Gather(out_block.reshape(model_width, query_cols), size)
     out_gather.first()
@@ -1084,37 +1191,45 @@
         if batch == 0:
             out_gather.parts, queries, contexts = tie(out_gather.parts, queries, contexts)
             out_gather.second()
-    out_gather.parts, contexts = tie(out_gather.parts, contexts)
+            out_gather.relay()
+    out_gather.parts, contexts, cot.parts = tie(out_gather.parts, contexts, cot.parts)
     out_gather.third()
+    cot.second()
     context = jnp.concatenate(contexts, axis=0).reshape(tokens, -1)
-    full_cot = in_steps(cot.pieces())
     out_pieces = out_gather.pieces()
     mid = x_rows + project_back(context, out_pieces, model_width)
     mid_scale = inverse_scale(mid)
     normed_mid_rows = (mid * mid_scale * gains[1]).astype(LOW)
     mid_gather = Gather(normed_mid_rows, size)
     mid_gather.first()
+    cot.third()
+    full_cot = [in_steps(run, cot.pieces()) for run in range(2)]
     mid_gather.parts, full_cot = tie(mid_gather.parts, full_cot)
     mid_gather.second()
+    mid_gather.relay()
+    units = [None, None]
+    units[1] = hidden_units(1, mid_gather.pieces(), full_gate_up)
+    mid_gather.parts, units[1] = tie(mid_gather.parts, units[1])
     mid_gather.third()
-
-    normed_mid, gate, upward, hidden, hidden_t = hidden_units(mid_gather.pieces(), full_gate_up)
-    sum_down = units_sum([hidden_t], full_cot, groups)
-    sum_down, gate = tie(sum_down, gate)
+    units[0] = hidden_units(0, mid_gather.pieces(), full_gate_up)
+    normed_mid = [unit[0] for unit in units]
+    (sum_down,) = units_sum([[unit[4] for unit in units]], full_cot, groups)
+    sum_down, units = tie(sum_down, units)
     d_mid_sum = Scatter(size)
-    backs = []
+    steps = size // 2
+    turned = []
     for run in range(2):
-        *turned, evens, odds = hidden_back(
-            run, full_cot, gate, upward, full_gate_up, full_down, size
+        _, gate, upward, _, _ = units[run]
+        *grads, evens, odds = hidden_back(
+            full_cot[run], gate, upward, full_gate_up, full_down, steps
         )
-        backs.append(turned)
+        turned.append(grads)
         if run == 0:
-            odds, gate = tie(odds, gate)
+            odds, units = tie(odds, units)
         else:
             d_mid_sum.parts, odds = tie(d_mid_sum.parts, odds)
         d_mid_sum.first(evens, odds)
-    d_mid_sum.second()
-    sum_gate = units_sum([back[0] for back in backs], normed_mid, groups)
+    turned = d_mid_sum.second(turned)
 
     def scatter_rows(value):
         return lax.psum_scatter(value, "dp", scatter_dimension=0, tiled=False)
@@ -1122,14 +1237,17 @@
     old_gate_up = jnp.transpose(m_gate_up, (1, 2, 0))
     old_down = jnp.transpose(m_down)
     grad_down = scatter_rows(sum_down)
-    sum_gate, backs = tie(sum_gate, backs)
+    sum_gate, sum_up = units_sum(
+        [[grads[0] for grads in turned], [grads[1] for grads in turned]], normed_mid, groups
+    )
+    d_mid_sum.parts, sum_gate, sum_up, grad_down = tie(
+        d_mid_sum.parts, sum_gate, sum_up, grad_down
+    )
     grad_gate = scatter_rows(sum_gate)
-    sum_up = units_sum([back[1] for back in backs], normed_mid, groups)
-    d_mid_sum.parts, sum_up, hidden, grad_down = tie(d_mid_sum.parts, sum_up, hidden, grad_down)
     grad_up = scatter_rows(sum_up)
-    d_mid_sum.third()
+    hidden = d_mid_sum.third([unit[3] for unit in units])
     mlp_sum = Scatter(size)
-    mlp_parts = [hidden_out(run, hidden, full_down, size) for run in range(2)]
+    mlp_parts = [hidden_out(part, full_down, steps) for part in hidden]
     d_mid_sum.parts, mlp_parts = tie(d_mid_sum.parts, mlp_parts)
     for evens, odds in mlp_parts:
         mlp_sum.first(evens, odds)
@@ -1143,16 +1261,24 @@
     mlp_sum.parts, out_parts, d_mid_low = tie(mlp_sum.parts, out_parts, d_mid_low)
     for evens, odds in out_parts:
         out_sum.first(evens, odds)
-    mlp_sum.second()
+    d_mid_low = mlp_sum.second(d_mid_low)
     d_context = project(d_mid_low, out_pieces, head_dim).reshape(batches, own_rows, -1)
-    out_sum.parts, d_context = tie(out_sum.parts, d_context)
-    out_sum.second()
+    out_sum.parts, d_context, grad_gate = tie(out_sum.parts, d_context, grad_gate)
+    d_context = out_sum.second(d_context)
     fast = groups == 4 and units_here == 2 * FF_BLOCK
     grad_down = wide(grad_down)
     moment_down = DECAY * old_down + grad_down
     moment_gate = DECAY * old_gate_up[0] + wide(grad_gate)
     first_owners = (0, 1, 2, 3)
     last_owners = (1, 2)
+    if fast:
+        moment_down, moment_gate, d_context = tie(moment_down, moment_gate, d_context)
+        down_grams = packed_grams(moment_down, FF_BLOCK)
+        gate_grams = packed_grams(moment_gate, FF_BLOCK)
+        down_grams, gate_grams, d_context = tie(down_grams, gate_grams, d_context)
+        first_parts = exchange(
+            (gate_grams[0], down_grams[0], down_grams[1], gate_grams[1]), first_owners
+        )
     backs = []
     for batch in range(batches):
         backs.append(
@@ -1161,18 +1287,12 @@
             )
         )
         if batch == 0:
-            backs, mlp_sum.parts, d_context, moment_down, moment_gate = tie(
-                backs, mlp_sum.parts, d_context, moment_down, moment_gate
-            )
-            mlp_sum.third()
-            if fast:
-                down_grams = block_grams(moment_down, FF_BLOCK, True)
-                gate_grams = block_grams(moment_gate, FF_BLOCK, True)
-                first_parts = exchange(
-                    (gate_grams[0], down_grams[0], down_grams[1], gate_grams[1]), first_owners
-                )
+            backs, mlp_sum.parts, d_context = tie(backs, mlp_sum.parts, d_context)
+            d_context = mlp_sum.third(d_context)
+    if fast:
+        backs, first_parts = tie(backs, first_parts)
     backs, out_sum.parts, grad_up = tie(backs, out_sum.parts, grad_up)
-    out_sum.third()
+    backs = out_sum.third(backs)
     d_queries = jnp.concatenate([back[0] for back in backs], axis=0).reshape(tokens, -1)
     d_keyval = jnp.concatenate([back[1] for back in backs], axis=0).astype(LOW)
 
@@ -1180,82 +1300,75 @@
         return scatter_rows(total.astype(LOW).reshape(groups, -1, width))
 
     query_sum = Scatter(size)
-    for run in range(2):
-        evens, odds = blocks_sum(run, normed, d_queries, size)
+    query_parts = [blocks_sum(run, normed, d_queries, size) for run in range(2)]
+    for evens, odds in query_parts:
         query_sum.first(evens, odds)
-    query_sum.parts, out_sum.parts, d_queries = tie(query_sum.parts, out_sum.parts, d_queries)
-    query_sum.second()
+    d_keyval = d_keyval.reshape(batches, size, own_rows, 2 * head_dim)
+    d_keyval = jnp.swapaxes(d_keyval, 0, 1)[place]
+    d_keyval = lax.all_to_all(d_keyval, "mp", 0, 0, tiled=True)
+    output = (mid + mlp_sum.total()).astype(LOW).reshape(inputs.shape)
+    moment_up = DECAY * old_gate_up[1] + wide(grad_up)
+    query_parts, d_queries, moment_up = tie(query_parts, d_queries, moment_up)
+    if fast:
+        up_grams = packed_grams(moment_up, FF_BLOCK)
+        query_sum.parts, up_grams, d_queries = tie(query_sum.parts, up_grams, d_queries)
+        last_parts = exchange(up_grams, last_owners)
+    out_sum.parts, d_queries = tie(out_sum.parts, d_queries)
     grad_out = own_rows_of(out_sum.total(), query_cols)
-    d_keyval = d_keyval.reshape(batches, size, own_rows, 2 * head_dim)
-    d_keyval = scatter_small(jnp.swapaxes(d_keyval, 0, 1), size).reshape(tokens, 2 * head_dim)
-    output = (mid + mlp_sum.total()).astype(LOW).reshape(inputs.shape)
-    d_normed = project_back(d_queries, query_pieces, model_width)
-    d_keyval, d_normed = tie(d_keyval, d_normed)
+    d_queries = query_sum.second(d_queries)
+    if fast:
+        d_normed, first_factor = back_and_factor(
+            d_queries, query_pieces, model_width, is_owner(first_owners), first_parts
+        )
+    else:
+        d_normed = project_back(d_queries, query_pieces, model_width)
+    d_keyval, d_normed, query_sum.parts = tie(d_keyval, d_normed, query_sum.parts)
+    d_normed = query_sum.third(d_normed)
+    d_keyval = jnp.sum(wide(d_keyval), axis=0).reshape(tokens, 2 * head_dim)
     d_keyval = jnp.concatenate(
         [rotate(d_keyval[:, :head_dim], flat_cos, -flat_sin), d_keyval[:, head_dim:]], axis=1
     ).astype(LOW)
     sum_keyval = outer_sum(normed, d_keyval).astype(LOW)
     sum_keyval = jnp.swapaxes(sum_keyval.reshape(groups, size, share, 2 * head_dim), 0, 1)
-    order = jnp.array(gather_order(size), jnp.int32)
-    sum_keyval = sum_keyval[me ^ order]
-    moment_up = DECAY * old_gate_up[1] + wide(grad_up)
+    sum_keyval = lax.all_to_all(sum_keyval, "mp", 0, 0, tiled=True)
     if fast:
-        up_grams = block_grams(moment_up, FF_BLOCK, True)
-        up_grams, sum_keyval = tie(up_grams, sum_keyval)
-        last_parts = exchange(up_grams, last_owners)
-    share_sums = scatter_small(sum_keyval, size).astype(LOW)
+        last_parts, d_keyval = tie(last_parts, d_keyval)
+        last_factor = owned_factor(last_parts, last_owners)
+        query_sum.parts, last_factor, d_normed = tie(query_sum.parts, last_factor, d_normed)
+        first_choices = share_out(first_factor, first_owners)
+        last_choices = share_out(last_factor, last_owners)
+    grad_query = own_rows_of(query_sum.total(), query_cols)
     d_normed = d_normed + rows_dot(d_keyval, full_keyval)
     input_grad = (d_mid + norm_back(d_normed, x_rows, x_scale, gains[0])).astype(LOW)
     input_grad = input_grad.reshape(inputs.shape)
     gain_input = jnp.sum(d_normed * x_rows * x_scale, axis=0)
-    if fast:
-        share_sums, first_parts, input_grad = tie(share_sums, first_parts, input_grad)
-        first_factor = owned_factor(first_parts, first_owners)
-        query_sum.parts, first_factor = tie(query_sum.parts, first_factor)
-    query_sum.third()
-    my_group = lax.axis_index("dp")
-    share_parts = [share_sums[my_group]]
-    for shift in range(1, groups):
-        part = share_sums[(my_group + shift) % groups]
-        pairs = [(i, (i + shift) % groups) for i in range(groups)]
-        share_parts.append(lax.ppermute(part, "dp", pairs))
-    if fast:
-        first_factor, share_parts = tie(first_factor, share_parts)
-        first_choices = share_out(first_factor, first_owners)
-    grad_keyval = wide(share_parts[0])
-    for part in share_parts[1:]:
-        grad_keyval = grad_keyval + wide(part)
-    grad_keyval = gather_small(grad_keyval.astype(LOW), size)
-    if fast:
-        last_factor = owned_factor(last_parts, last_owners)
-        query_sum.parts, grad_keyval, last_factor = tie(
-            query_sum.parts, grad_keyval, last_factor
-        )
-        last_choices = share_out(last_factor, last_owners)
-    grad_query = own_rows_of(query_sum.total(), query_cols)
-    place = jnp.zeros((size,), jnp.int32).at[order].set(jnp.arange(size, dtype=jnp.int32))
-    grad_keyval = grad_keyval[place[me ^ jnp.arange(size)]]
-    grad_keyval = wide(grad_keyval).reshape(w_keyval.shape)
-    moment_keyval = DECAY * m_keyval + grad_keyval
-    keyval_grams = gather_grams(moment_keyval, 2 * head_dim, False)
+    share_sums = jnp.sum(wide(sum_keyval), axis=0).astype(LOW)
+    share_sums, input_grad = tie(share_sums, input_grad)
+    share_parts = lax.all_to_all(share_sums, "dp", 0, 0, tiled=True)
     grad_out = wide(grad_out)
     moment_out = DECAY * m_out + grad_out
     out_grams = gather_grams(moment_out, head_dim, False)
     if fast:
         new_down = owned_update(moment_down, down_t, first_choices, (1, 2))
         new_gate = owned_update(moment_gate, gate_up_t[0], first_choices, (0, 3))
-        new_down, new_gate, grad_query = tie(new_down, new_gate, grad_query)
     else:
         new_down = small_update(moment_down, down_t, FF_BLOCK, True)
         new_gate = small_update(moment_gate, gate_up_t[0], FF_BLOCK, True)
-    grad_query = wide(grad_query)
-    moment_query = DECAY * m_query + grad_query
-    query_grams = gather_grams(moment_query, head_dim, False)
+    share_parts, new_gate = tie(share_parts, new_gate)
+    grad_keyval = jnp.sum(wide(share_parts), axis=0)
+    grad_keyval = gather_small(grad_keyval.astype(LOW), size)
     if fast:
         new_up = owned_update(moment_up, gate_up_t[1], last_choices, last_owners)
     else:
         new_up = small_update(moment_up, gate_up_t[1], FF_BLOCK, True)
     new_out = small_update(moment_out, w_out, head_dim, False, out_grams)
+    grad_keyval, new_out, new_up = tie(grad_keyval, new_out, new_up)
+    grad_keyval = wide(grad_keyval[place]).reshape(w_keyval.shape)
+    moment_keyval = DECAY * m_keyval + grad_keyval
+    keyval_grams = gather_grams(moment_keyval, 2 * head_dim, False)
+    grad_query = wide(grad_query)
+    moment_query = DECAY * m_query + grad_query
+    query_grams = gather_grams(moment_query, head_dim, False)
     new_keyval = small_update(moment_keyval, w_keyval, 2 * head_dim, False, keyval_grams)
     new_query = small_update(moment_query, w_query, head_dim, False, query_grams)
     grad_gains = add_all(add_all(jnp.stack([gain_input, gain_mid], axis=0), "mp"), "dp")

time: 898 us -> 810 us (0.902)
  waiting for transfers between devices: 209 us -> 154 us
  starting transfers between devices: 144 us -> 111 us
  Pallas kernels: 315 us -> 293 us
  local copies, waits for them, and re-layouts: 102 us -> 118 us
  other arithmetic: 95.2 us -> 105 us
    ppermute x72 -> x66, waiting for transfers between devices: 157 us -> 95.9 us  [swap(): return lax.ppermute(value, 'mp', [(i, i ^ flip) for i in range(size)])]
    all_gather x4, waiting for transfers between devices: 2.99 us -> 41.6 us  [rows_of(): return lax.all_gather(value, 'dp', axis=0, tiled=False)]
    ppermute x6, waiting for transfers between devices: 37.2 us -> 0.02 us  [share_out(): lax.ppermute(factor, 'dp', [(o, (o + shift) % size) for o in owners])]
    pallas_call x4 -> x8, Pallas kernels: 66.4 us -> 89 us  [the longest x2 35 us: hidden_units(): pl.pallas_call(functools.partial(hidden_kernel, places, steps, turn), gri...]
    pallas_call x2 -> x1, Pallas kernels: 32.3 us -> 10.5 us  [block_factor(): pl.pallas_call(factor_kernel, in_specs=[pl.BlockSpec(memory_space=pltpu.S...]
    ppermute x9, starting transfers between devices: 34.2 us -> 12.9 us  [gather_grams(): lax.ppermute(grams, 'dp', [(i, (i + shift) % size) for i in range(size)])]
    convert_element_type x7 -> x8, other arithmetic: 11.1 us -> 32 us  [the longest x4 16.8 us: second(): four = (wide(evens[2:]) + wide(core[2:])).astype(LOW)]
    all_to_all x0 -> x4, starting transfers between devices: none -> 19.2 us  [the longest x1 6.19 us: shards(): share_parts = lax.all_to_all(share_sums, 'dp', 0, 0, tiled=True)]
  transfers between devices with their start and end apart: 110 -> 102, of which waited for: 31 -> 24; matrix products, arithmetic and copies ran while one was open for 18% -> 20% of each run, Pallas kernels for 35% -> 33%
where the time goes in v2:
time: 810 us; the launch traced here: 802 us
  Pallas kernels  293 us (36%)
  waiting for transfers between devices  154 us (19%)
  local copies, waits for them, and re-layouts  118 us (15%)
  starting transfers between devices  111 us (14%)
  other arithmetic  105 us (13%)
  between operations  16.7 us (2%)
    ppermute x66, waiting for transfers between devices, swap(): return lax.ppermute(value, 'mp', [(i, i ^ flip) for i in range(size)])  95.9 us
    unnamed x363, local copies, waits for them, and re-layouts  82.7 us
    ppermute x66, starting transfers between devices, swap(): return lax.ppermute(value, 'mp', [(i, i ^ flip) for i in range(size)])  47.8 us
    pallas_call x2, Pallas kernels, hidden_back(): pl.pallas_call(functools.partial(hidden_back_kernel, turn), grid=(steps,)...  45.2 us
    pallas_call x2, Pallas kernels, attention_backward(): pl.pallas_call(functools.partial(backward_kernel, heads, head_dim), grid=...  42.8 us
    all_gather x4, waiting for transfers between devices, rows_of(): return lax.all_gather(value, 'dp', axis=0, tiled=False)  41.6 us
    pallas_call x2, Pallas kernels, hidden_units(): pl.pallas_call(functools.partial(hidden_kernel, places, steps, turn), gri...  35 us
    pallas_call x2, Pallas kernels, units_sum(): pl.pallas_call(functools.partial(units_sum_kernel, len(rows), turn), grid...  33.8 us
  transfers between devices with their start and end apart: 102, of which 24 were waited for; matrix products, arithmetic and copies ran while one was open for 20% of the time, Pallas kernels for 33%

profile of v2, /device:TPU:0, one launch (start us, length us, event | category | flops | bytes accessed | tf_op | source)
XLA Modules:
  0.0 801.6 jit_solution(8467513452806546710)
XLA Ops:
  17.6 41.6 %all-gather.9.cloned.1.call-done = bf16[4096,256]{1,0:T(8,128)(2,1)} async-done(((bf16[1024,256]{1,0:T(8,128)(2,1)}), bf16[4096,256]{1,0:T(8,128)(2,1)}) %all-gather.9.cloned.1.call-update) | async-done | bytes 2097168 | tf_op jit(solution)/shard_map/all_gather | solution.py:1123
  66.3 5.2 collective-permute-done.8
  74.0 7.7 collective-permute-done.9
  93.4 14.8 %collective-permute-done.3.refs_4_.refs_5_ = bf16[2048,256]{1,0:T(8,128)(2,1)} collective-permute-done((bf16[2048,256]{1,0:T(8,128)(2,1)S(1)}, bf16[2048,256]{1,0:T(8,128)(2,1)}, u32[]{:S(2)}, u32[]{:S(2)}) %collective-permute-start.3) | collective-permute-done | bytes 1048608 | tf_op jit(solution)/shard_map/ppermute | solution.py:88
  127.0 10.4 %collective-permute-done.12.refs_7_.refs_8_ = bf16[1024,256]{1,0:T(8,128)(2,1)} collective-permute-done((bf16[1024,256]{1,0:T(8,128)(2,1)}, bf16[1024,256]{1,0:T(8,128)(2,1)}, u32[]{:S(2)}, u32[]{:S(2)}) %collective-permute-start.12) | collective-permute-done | bytes 524320 | tf_op jit(solution)/shard_map/ppermute | solution.py:88
  145.7 9.3 %project.2 = bf16[384,2048]{1,0:T(8,128)(2,1)S(1)} custom-call(bf16[2048,256]{1,0:T(8,128)(2,1)S(1)} %bitcast.228, bf16[2048,256]{1,0:T(8,128)(2,1)S(1)} %copy-done.52, bf16[2048,256]{1,0:T(8,128)(2,1)} %collective-permute-done.5.refs_2_.refs_3_, bf16[2048,256]{1,0:T(8,128)(2,1)} %collective-permute-done.14.refs_3_.refs_4_, ...), custom_call_target="tpu_custom_call" | custom-call | flops 3221225472 | bytes 11534336 | tf_op jit(solution)/shard_map/project/pallas_call | solution.py:460
  155.1 12.6 %attention_forward.2 = (bf16[1,192,2048]{2,1,0:T(8,128)(2,1)S(1)}, f32[1,192,2048]{2,1,0:T(8,128)S(1)}) custom-call(bf16[2,192,2048]{2,1,0:T(8,128)(2,1)S(1)} %bitcast.237, bf16[2,1536,256]{2,1,0:T(8,128)(2,1)S(1)} %bitcast.230, s32[2,192,2]{2,1,0:T(8,128)S(1)} %copy.65.qid_ref, s32[2,2,1536]{2,1,0:T(2,128)S(1)} %pad_add_fusion.kid_ref), custom_call_target="tpu_custom_call" | custom-call | flops 4831838208 | bytes 3145728 | tf_op jit(solution)/shard_map/attention_forward/pallas_call | solution.py:285
  173.9 12.8 %attention_forward.3 = (bf16[1,192,2048]{2,1,0:T(8,128)(2,1)S(1)}, f32[1,192,2048]{2,1,0:T(8,128)S(1)}) custom-call(bf16[2,192,2048]{2,1,0:T(8,128)(2,1)S(1)} %bitcast.238, bf16[2,1536,256]{2,1,0:T(8,128)(2,1)S(1)} %bitcast.231, s32[2,192,2]{2,1,0:T(8,128)S(1)} %copy.65.qid_ref, s32[2,2,1536]{2,1,0:T(2,128)S(1)} %pad_add_fusion.kid_ref), custom_call_target="tpu_custom_call" | custom-call | flops 4831838208 | bytes 3145728 | tf_op jit(solution)/shard_map/attention_forward/pallas_call | solution.py:285
  192.7 5.8 project_back.1
  199.0 9.8 %collective-permute-done.29 = bf16[192,2048]{1,0:T(8,128)(2,1)S(1)} collective-permute-done((bf16[192,2048]{1,0:T(8,128)(2,1)S(1)}, bf16[192,2048]{1,0:T(8,128)(2,1)S(1)}, u32[]{:S(2)}, u32[]{:S(2)}) %collective-permute-start.29) | collective-permute-done | bytes 786464 | tf_op jit(solution)/shard_map/ppermute | solution.py:88
  225.6 20.5 %collective-permute-done.26.refs_4_.refs_2_ = bf16[384,2048]{1,0:T(8,128)(2,1)} collective-permute-done((bf16[384,2048]{1,0:T(8,128)(2,1)S(1)}, bf16[384,2048]{1,0:T(8,128)(2,1)}, u32[]{:S(2)}, u32[]{:S(2)}) %collective-permute-start.26) | collective-permute-done | bytes 1572896 | tf_op jit(solution)/shard_map/ppermute | solution.py:88
  255.3 17.9 %hidden_units.2 = (bf16[1536,2048]{1,0:T(8,128)(2,1)}, f32[1536,704]{1,0:T(8,128)}, f32[1536,704]{1,0:T(8,128)}, bf16[1536,704]{1,0:T(8,128)(2,1)S(1)}, bf16[704,1536]{1,0:T(8,128)(2,1)S(1)}) custom-call(bf16[384,2048]{1,0:T(8,128)(2,1)S(1)} %multiply_convert_fusion.refs_0_, bf16[384,2048]{1,0:T(8,128)(2,1)S(1)} %copy-done.99, ...), custom_call_target="tpu_custom_call" | custom-call | flops 8858370048 | bytes 12582912 | tf_op jit(solution)/shard_map/hidden_units/pallas_call | solution.py:605
  279.7 17.1 %hidden_units.3 = (bf16[1536,2048]{1,0:T(8,128)(2,1)}, f32[1536,704]{1,0:T(8,128)}, f32[1536,704]{1,0:T(8,128)}, bf16[1536,704]{1,0:T(8,128)(2,1)S(1)}, bf16[704,1536]{1,0:T(8,128)(2,1)S(1)}) custom-call(bf16[384,2048]{1,0:T(8,128)(2,1)} %collective-permute-done.28.refs_2_.refs_0_, bf16[384,2048]{1,0:T(8,128)(2,1)} %collective-permute-done.36.refs_3_.refs_1_, ...), custom_call_target="tpu_custom_call" | custom-call | flops 8858370048 | bytes 12582912 | tf_op jit(solution)/shard_map/hidden_units/pallas_call | solution.py:605
  299.8 12.6 %units_sum.2 = bf16[4,704,512]{2,1,0:T(8,128)(2,1)S(1)} custom-call(bf16[1536,2048]{1,0:T(8,128)(2,1)S(1)} %bitcast.250, bf16[1536,2048]{1,0:T(8,128)(2,1)} %copy-done.146, bf16[704,1536]{1,0:T(8,128)(2,1)S(1)} %get-tuple-element.343.refs_2_, bf16[704,1536]{1,0:T(8,128)(2,1)S(1)} %copy-done.107), custom_call_target="tpu_custom_call" | custom-call | flops 8858370048 | bytes 16908288 | tf_op jit(solution)/shard_map/units_sum/pallas_call | solution.py:749
  315.8 22.2 %hidden_back.2 = (bf16[704,1536]{1,0:T(8,128)(2,1)S(1)}, bf16[704,1536]{1,0:T(8,128)(2,1)S(1)}, bf16[4,192,2048]{2,1,0:T(8,128)(2,1)S(1)}, bf16[4,192,2048]{2,1,0:T(8,128)(2,1)}) custom-call(bf16[1536,2048]{1,0:T(8,128)(2,1)} %copy-done.92, f32[1536,704]{1,0:T(8,128)} %get-tuple-element.353.gate_ref, f32[1536,704]{1,0:T(8,128)} %get-tuple-element.354.up_ref, ...), custom_call_target="tpu_custom_call" | custom-call | flops 13287555072 | bytes 12582912 | tf_op jit(solution)/shard_map/hidden_back/pallas_call | solution.py:670
  344.3 23.0 %hidden_back.3 = (bf16[704,1536]{1,0:T(8,128)(2,1)S(1)}, bf16[704,1536]{1,0:T(8,128)(2,1)S(1)}, bf16[4,192,2048]{2,1,0:T(8,128)(2,1)S(1)}, bf16[4,192,2048]{2,1,0:T(8,128)(2,1)}) custom-call(bf16[1536,2048]{1,0:T(8,128)(2,1)} %copy-done.146, f32[1536,704]{1,0:T(8,128)} %get-tuple-element.362.gate_ref, f32[1536,704]{1,0:T(8,128)} %get-tuple-element.363.up_ref, ...), custom_call_target="tpu_custom_call" | custom-call | flops 13287555072 | bytes 12582912 | tf_op jit(solution)/shard_map/hidden_back/pallas_call | solution.py:670
  367.8 4.2 add_convert_fusion.2
  374.2 21.3 %units_sum.3 = (bf16[4,704,512]{2,1,0:T(8,128)(2,1)S(1)}, bf16[4,704,512]{2,1,0:T(8,128)(2,1)S(1)}) custom-call(bf16[1536,2048]{1,0:T(8,128)(2,1)} %get-tuple-element.345.refs_0_, bf16[1536,2048]{1,0:T(8,128)(2,1)} %get-tuple-element.349.refs_1_, bf16[704,1536]{1,0:T(8,128)(2,1)S(1)} %copy-done.113, bf16[704,1536]{1,0:T(8,128)(2,1)S(1)} %get-tuple-element.375.refs_3_, ...), custom_call_target="tpu_custom_call" | custom-call | flops 17716740096 | bytes 33816576 | tf_op jit(solution)/shard_map/units_sum/pallas_call | solution.py:749
  398.7 10.0 %collective-permute-done.41 = bf16[2,192,2048]{2,1,0:T(8,128)(2,1)S(1)} collective-permute-done((bf16[2,192,2048]{2,1,0:T(8,128)(2,1)S(1)}, bf16[2,192,2048]{2,1,0:T(8,128)(2,1)S(1)}, u32[]{:S(2)}, u32[]{:S(2)}) %collective-permute-start.41) | collective-permute-done | bytes 1572896 | tf_op jit(solution)/shard_map/ppermute | solution.py:88
  410.3 4.2 fusion.23
  417.1 5.8 hidden_out.2
  424.5 5.6 hidden_out.3
  443.3 4.0 fusion.61
  447.3 4.2 blocks_sum.5
  452.8 4.1 blocks_sum.4
  464.7 5.4 add_convert_fusion
  471.8 8.5 %project.3 = bf16[384,2048]{1,0:T(8,128)(2,1)S(1)} custom-call(bf16[2048,256]{1,0:T(8,128)(2,1)S(1)} %copy-done.55, bf16[2048,256]{1,0:T(8,128)(2,1)} %collective-permute-done.16.refs_1_, bf16[2048,256]{1,0:T(8,128)(2,1)} %collective-permute-done.17.refs_2_, bf16[2048,256]{1,0:T(8,128)(2,1)S(1)} %copy-done.59, ...), custom_call_target="tpu_custom_call" | custom-call | flops 3221225472 | bytes 11534336 | tf_op jit(solution)/shard_map/project/pallas_call | solution.py:460
  489.8 4.4 all-to-all-start
  501.6 21.2 %attention_backward.2 = (bf16[1,192,2048]{2,1,0:T(8,128)(2,1)S(1)}, f32[1,1536,256]{2,1,0:T(8,128)S(1)}) custom-call(bf16[2,192,2048]{2,1,0:T(8,128)(2,1)S(1)} %bitcast.239, bf16[2,192,2048]{2,1,0:T(8,128)(2,1)S(1)} %bitcast.259, f32[1,192,2048]{2,1,0:T(8,128)S(1)} %copy-done.111, bf16[2,1536,256]{2,1,0:T(8,128)(2,1)S(1)} %bitcast.232, ...), custom_call_target="tpu_custom_call" | custom-call | flops 12079595520 | bytes 4718592 | tf_op jit(solution)/shard_map/attention_backward/pallas_call | solution.py:369
  522.8 4.7 fusion.25
  531.5 21.6 %attention_backward.3 = (bf16[1,192,2048]{2,1,0:T(8,128)(2,1)S(1)}, f32[1,1536,256]{2,1,0:T(8,128)S(1)}) custom-call(bf16[2,192,2048]{2,1,0:T(8,128)(2,1)S(1)} %bitcast.240, bf16[2,192,2048]{2,1,0:T(8,128)(2,1)S(1)} %bitcast.260, f32[1,192,2048]{2,1,0:T(8,128)S(1)} %copy-done.109, bf16[2,1536,256]{2,1,0:T(8,128)(2,1)S(1)} %bitcast.233, ...), custom_call_target="tpu_custom_call" | custom-call | flops 12079595520 | bytes 4718592 | tf_op jit(solution)/shard_map/attention_backward/pallas_call | solution.py:369
  569.0 4.1 blocks_sum.7
  574.4 4.1 blocks_sum.6
  579.0 3.7 bitcast_add_fusion.2
  592.9 4.3 all-to-all-start.1
  608.3 4.6 collective-permute-start.63
  631.8 16.1 %back_and_factor.1 = (f32[384,2048]{1,0:T(8,128)S(1)}, bf16[352,352]{1,0:T(8,128)(2,1)S(1)}) custom-call(s32[1]{0:T(128)S(6)} %add.552.refs_0_, bf16[2048,256]{1,0:T(8,128)(2,1)S(1)} %bitcast.229, bf16[2048,256]{1,0:T(8,128)(2,1)S(1)} %copy-done.53, bf16[2048,256]{1,0:T(8,128)(2,1)} %collective-permute-done.5.refs_2_.refs_3_, ...), custom_call_target="tpu_custom_call" | custom-call | flops 7582646272 | bytes 13107200 | tf_op jit(solution)/shard_map/back_and_factor/pallas_call | solution.py:1049
  655.4 4.7 collective-permute-start.67
  661.3 4.2 all-to-all-start.2
  666.6 10.5 %block_factor.1.refs_0_ = bf16[352,352]{1,0:T(8,128)(2,1)} custom-call(s32[1]{0:T(128)S(6)} %add.561.own_ref, bf16[368,352]{1,0:T(8,128)(2,1)S(1)} %copy-done.83, bf16[368,352]{1,0:T(8,128)(2,1)} %collective-permute-done.63.refs_1_, bf16[368,352]{1,0:T(8,128)(2,1)} %collective-permute-done.64.refs_2_, bf16[368,352]{1,0:T(8,128)(2,1)} %collective-permute-done.65.refs_3_), custom_call_target="tpu_custom_call" | custom-call | flops 4361420800 | bytes 2478080 | tf_op jit(solution)/shard_map/block_factor/pallas_call | solution.py:911
  685.7 5.5 fusion.9
  693.3 6.2 all-to-all-start.3
  716.4 7.7 collective-permute-start.82
  728.8 3.7 collective-permute-done.70
  743.3 5.7 small_update.3
  767.1 12.1 %collective-permute-done.87.refs_2_ = f32[1,256,256]{2,1,0:T(8,128)} collective-permute-done((f32[1,256,256]{2,1,0:T(8,128)}, f32[1,256,256]{2,1,0:T(8,128)}, u32[]{:S(2)}, u32[]{:S(2)}) %collective-permute-start.87) | collective-permute-done | bytes 262176 | tf_op jit(solution)/shard_map/ppermute | solution.py:979
  779.2 6.6 small_update.5
  788.9 5.7 small_update.4
  (698 shorter events, 303.1 us)
Async XLA Ops:
  7.2 52.0 %all-gather.9.cloned.1.call-start = ((), (), s32[]{:S(2)}) async-start(), calls=%async_computation.14 | async-start | bytes 2621440 | tf_op jit(solution)/shard_map/all_gather | solution.py:1123
  10.4 116.6 %all-gather.11.cloned.1.call-start = ((), (), s32[]{:S(2)}) async-start(), calls=%async_computation.15 | async-start | bytes 1310720 | tf_op jit(solution)/shard_map/all_gather | solution.py:1123
  10.4 71.5 %collective-permute-start = (bf16[384,2048]{1,0:T(8,128)(2,1)}, bf16[384,2048]{1,0:T(8,128)(2,1)}, u32[]{:S(2)}, u32[]{:S(2)}) collective-permute-start(bf16[384,2048]{1,0:T(8,128)(2,1)} %bitcast.1), channel_id=1, source_target_pairs={{0,4},{1,5},{2,6},{3,7},{4,0},{5,1},{6,2},{7,3},{8,12},{9,13},{10,... | collective-permute-start | bytes 4718600 | tf_op jit(solution)/shard_map/ppermute | solution.py:88
  13.5 68.5 %collective-permute-start.1 = (bf16[384,2048]{1,0:T(8,128)(2,1)}, bf16[384,2048]{1,0:T(8,128)(2,1)}, u32[]{:S(2)}, u32[]{:S(2)}) collective-permute-start(bf16[384,2048]{1,0:T(8,128)(2,1)} %bitcast.1), channel_id=1, source_target_pairs={{0,1},{1,0},{2,3},{3,2},{4,5},{5,4},{6,7},{7,6},{8,9},{9,8},{10,11... | collective-permute-start | bytes 4718600 | tf_op jit(solution)/shard_map/ppermute | solution.py:88
  13.5 68.5 %collective-permute-start.2 = (bf16[384,2048]{1,0:T(8,128)(2,1)}, bf16[384,2048]{1,0:T(8,128)(2,1)}, u32[]{:S(2)}, u32[]{:S(2)}) collective-permute-start(bf16[384,2048]{1,0:T(8,128)(2,1)} %bitcast.1), channel_id=1, source_target_pairs={{0,2},{1,3},{2,0},{3,1},{4,6},{5,7},{6,4},{7,5},{8,10},{9,11},{10,... | collective-permute-start | bytes 4718600 | tf_op jit(solution)/shard_map/ppermute | solution.py:88
  73.9 179.9 %all-gather.13.cloned.1.call-start = ((), (), s32[]{:S(2)}) async-start(), calls=%async_computation.16 | async-start | bytes 7208960 | tf_op jit(solution)/shard_map/all_gather | solution.py:1123
  82.0 28.7 %collective-permute-start.6 = (bf16[384,2048]{1,0:T(8,128)(2,1)}, bf16[384,2048]{1,0:T(8,128)(2,1)}, u32[]{:S(2)}, u32[]{:S(2)}) collective-permute-start(bf16[384,2048]{1,0:T(8,128)(2,1)} %collective-permute-done), channel_id=1, source_target_pairs={{0,1},{1,0},{2,3},{3,2},{4,5},{5,4},{6,7},{7,6},{8,9},{9,8},{10,11... | collective-permute-start | bytes 4718600 | tf_op jit(solution)/shard_map/ppermute | solution.py:88
  82.5 28.1 %collective-permute-start.7 = (bf16[384,2048]{1,0:T(8,128)(2,1)}, bf16[384,2048]{1,0:T(8,128)(2,1)}, u32[]{:S(2)}, u32[]{:S(2)}) collective-permute-start(bf16[384,2048]{1,0:T(8,128)(2,1)} %collective-permute-done.2), channel_id=1, source_target_pairs={{0,1},{1,0},{2,3},{3,2},{4,5},{5,4},{6,7},{7,6},{8,9},{9,8},{10,11... | collective-permute-start | bytes 4718600 | tf_op jit(solution)/shard_map/ppermute | solution.py:88
  82.6 25.6 %collective-permute-start.3 = (bf16[2048,256]{1,0:T(8,128)(2,1)S(1)}, bf16[2048,256]{1,0:T(8,128)(2,1)}, u32[]{:S(2)}, u32[]{:S(2)}) collective-permute-start(bf16[2048,256]{1,0:T(8,128)(2,1)S(1)} %bitcast.225), channel_id=1, source_target_pairs={{0,4},{1,5},{2,6},{3,7},{4,0},{5,1},{6,2},{7,3},{8,12},{9,13},{10,... | collective-permute-start | bytes 3145736 | tf_op jit(solution)/shard_map/ppermute | solution.py:88
  85.1 25.5 %collective-permute-start.5 = (bf16[2048,256]{1,0:T(8,128)(2,1)S(1)}, bf16[2048,256]{1,0:T(8,128)(2,1)}, u32[]{:S(2)}, u32[]{:S(2)}) collective-permute-start(bf16[2048,256]{1,0:T(8,128)(2,1)S(1)} %bitcast.227), channel_id=1, source_target_pairs={{0,2},{1,3},{2,0},{3,1},{4,6},{5,7},{6,4},{7,5},{8,10},{9,11},{10,... | collective-permute-start | bytes 3145736 | tf_op jit(solution)/shard_map/ppermute | solution.py:88
  89.7 224.3 %all-gather.15.cloned.1.call-start = ((), (), s32[]{:S(2)}) async-start(), calls=%async_computation.17 | async-start | bytes 3604480 | tf_op jit(solution)/shard_map/all_gather | solution.py:1123
  110.6 27.9 %collective-permute-start.11 = (bf16[2048,256]{1,0:T(8,128)(2,1)}, bf16[2048,256]{1,0:T(8,128)(2,1)}, u32[]{:S(2)}, u32[]{:S(2)}) collective-permute-start(bf16[2048,256]{1,0:T(8,128)(2,1)} %collective-permute-done.3.refs_4_.refs_5_), channel_id=1, source_target_pairs={{0,1},{1,0},{2,3},{3,2},{4,5},{5,4},{6,7},{7,6},{8,9},{9,8},{10,11... | collective-permute-start | bytes 3145736 | tf_op jit(solution)/shard_map/ppermute | solution.py:88
  110.6 27.8 %collective-permute-start.14 = (bf16[2048,256]{1,0:T(8,128)(2,1)}, bf16[2048,256]{1,0:T(8,128)(2,1)}, u32[]{:S(2)}, u32[]{:S(2)}) collective-permute-start(bf16[2048,256]{1,0:T(8,128)(2,1)} %collective-permute-done.5.refs_2_.refs_3_), channel_id=1, source_target_pairs={{0,1},{1,0},{2,3},{3,2},{4,5},{5,4},{6,7},{7,6},{8,9},{9,8},{10,11... | collective-permute-start | bytes 3145736 | tf_op jit(solution)/shard_map/ppermute | solution.py:88
  139.8 29.1 %collective-permute-start.15 = (bf16[2048,256]{1,0:T(8,128)(2,1)}, bf16[2048,256]{1,0:T(8,128)(2,1)}, u32[]{:S(2)}, u32[]{:S(2)}) collective-permute-start(bf16[2048,256]{1,0:T(8,128)(2,1)} %all-gather.11.cloned.1.call-done), channel_id=1, source_target_pairs={{0,4},{1,5},{2,6},{3,7},{4,0},{5,1},{6,2},{7,3},{8,12},{9,13},{10,... | collective-permute-start | bytes 3145736 | tf_op jit(solution)/shard_map/ppermute | solution.py:88
  141.1 27.8 %collective-permute-start.16 = (bf16[2048,256]{1,0:T(8,128)(2,1)}, bf16[2048,256]{1,0:T(8,128)(2,1)}, u32[]{:S(2)}, u32[]{:S(2)}) collective-permute-start(bf16[2048,256]{1,0:T(8,128)(2,1)} %all-gather.11.cloned.1.call-done), channel_id=1, source_target_pairs={{0,1},{1,0},{2,3},{3,2},{4,5},{5,4},{6,7},{7,6},{8,9},{9,8},{10,11... | collective-permute-start | bytes 3145736 | tf_op jit(solution)/shard_map/ppermute | solution.py:88
  141.1 27.8 %collective-permute-start.17 = (bf16[2048,256]{1,0:T(8,128)(2,1)}, bf16[2048,256]{1,0:T(8,128)(2,1)}, u32[]{:S(2)}, u32[]{:S(2)}) collective-permute-start(bf16[2048,256]{1,0:T(8,128)(2,1)} %all-gather.11.cloned.1.call-done), channel_id=1, source_target_pairs={{0,2},{1,3},{2,0},{3,1},{4,6},{5,7},{6,4},{7,5},{8,10},{9,11},{10,... | collective-permute-start | bytes 3145736 | tf_op jit(solution)/shard_map/ppermute | solution.py:88
  209.2 37.0 %collective-permute-start.26 = (bf16[384,2048]{1,0:T(8,128)(2,1)S(1)}, bf16[384,2048]{1,0:T(8,128)(2,1)}, u32[]{:S(2)}, u32[]{:S(2)}) collective-permute-start(bf16[384,2048]{1,0:T(8,128)(2,1)S(1)} %multiply_convert_fusion.refs_0_), channel_id=1, source_target_pairs={{0,4},{1,5},{2,6},{3,7},{4,0},{5,1},{6,2},{7,3},{8,12},{9,13},{10,... | collective-permute-start | bytes 4718600 | tf_op jit(solution)/shard_map/ppermute | solution.py:88
  210.4 35.7 %collective-permute-start.27 = (bf16[384,2048]{1,0:T(8,128)(2,1)S(1)}, bf16[384,2048]{1,0:T(8,128)(2,1)S(1)}, u32[]{:S(2)}, u32[]{:S(2)}) collective-permute-start(bf16[384,2048]{1,0:T(8,128)(2,1)S(1)} %multiply_convert_fusion.refs_0_), channel_id=1, source_target_pairs={{0,1},{1,0},{2,3},{3,2},{4,5},{5,4},{6,7},{7,6},{8,9},{9,8},{10,11... | collective-permute-start | bytes 4718600 | tf_op jit(solution)/shard_map/ppermute | solution.py:88
  210.7 36.7 %collective-permute-start.28 = (bf16[384,2048]{1,0:T(8,128)(2,1)S(1)}, bf16[384,2048]{1,0:T(8,128)(2,1)}, u32[]{:S(2)}, u32[]{:S(2)}) collective-permute-start(bf16[384,2048]{1,0:T(8,128)(2,1)S(1)} %multiply_convert_fusion.refs_0_), channel_id=1, source_target_pairs={{0,2},{1,3},{2,0},{3,1},{4,6},{5,7},{6,4},{7,5},{8,10},{9,11},{10,... | collective-permute-start | bytes 4718600 | tf_op jit(solution)/shard_map/ppermute | solution.py:88
  247.9 161.6 %reduce-scatter.6.cloned.1.call-start = ((), (), s32[]{:S(2)}) async-start(), calls=%async_computation.9 | async-start | bytes 3604480 | tf_op jit(solution)/shard_map/reduce_scatter | solution.py:1235
  342.5 139.1 %reduce-scatter.8.cloned.1.call-start = ((), (), s32[]{:S(2)}) async-start(), calls=%async_computation.10 | async-start | bytes 3604480 | tf_op jit(solution)/shard_map/reduce_scatter | solution.py:1235
  367.3 42.2 %collective-permute-start.40 = (bf16[4,192,2048]{2,1,0:T(8,128)(2,1)}, bf16[4,192,2048]{2,1,0:T(8,128)(2,1)}, u32[]{:S(2)}, u32[]{:S(2)}) collective-permute-start(bf16[4,192,2048]{2,1,0:T(8,128)(2,1)} %get-tuple-element.365), channel_id=1, source_target_pairs={{0,1},{1,0},{2,3},{3,2},{4,5},{5,4},{6,7},{7,6},{8,9},{9,8},{10,11... | collective-permute-start | bytes 9437192 | tf_op jit(solution)/shard_map/ppermute | solution.py:88
  372.0 36.8 %collective-permute-start.41 = (bf16[2,192,2048]{2,1,0:T(8,128)(2,1)S(1)}, bf16[2,192,2048]{2,1,0:T(8,128)(2,1)S(1)}, u32[]{:S(2)}, u32[]{:S(2)}) collective-permute-start(bf16[2,192,2048]{2,1,0:T(8,128)(2,1)S(1)} %get-tuple-element.372), channel_id=1, source_target_pairs={{0,4},{1,5},{2,6},{3,7},{4,0},{5,1},{6,2},{7,3},{8,12},{9,13},{10,... | collective-permute-start | bytes 4718600 | tf_op jit(solution)/shard_map/ppermute | solution.py:88
  372.8 36.7 %collective-permute-start.42 = (bf16[2,192,2048]{2,1,0:T(8,128)(2,1)S(1)}, bf16[2,192,2048]{2,1,0:T(8,128)(2,1)}, u32[]{:S(2)}, u32[]{:S(2)}) collective-permute-start(bf16[2,192,2048]{2,1,0:T(8,128)(2,1)S(1)} %get-tuple-element.373), channel_id=1, source_target_pairs={{0,2},{1,3},{2,0},{3,1},{4,6},{5,7},{6,4},{7,5},{8,10},{9,11},{10,... | collective-permute-start | bytes 4718600 | tf_op jit(solution)/shard_map/ppermute | solution.py:88
  409.5 154.1 %reduce-scatter.10.cloned.1.call-start = ((), (), s32[]{:S(2)}) async-start(), calls=%async_computation.11 | async-start | bytes 3604480 | tf_op jit(solution)/shard_map/reduce_scatter | solution.py:1235
  470.2 52.6 %collective-permute-start.49 = (bf16[2,192,2048]{2,1,0:T(8,128)(2,1)}, bf16[2,192,2048]{2,1,0:T(8,128)(2,1)}, u32[]{:S(2)}, u32[]{:S(2)}) collective-permute-start(bf16[2,192,2048]{2,1,0:T(8,128)(2,1)} %get-tuple-element.432), channel_id=1, source_target_pairs={{0,4},{1,5},{2,6},{3,7},{4,0},{5,1},{6,2},{7,3},{8,12},{9,13},{10,... | collective-permute-start | bytes 4718600 | tf_op jit(solution)/shard_map/ppermute | solution.py:88
  471.1 51.7 %collective-permute-start.50 = (bf16[2,192,2048]{2,1,0:T(8,128)(2,1)}, bf16[2,192,2048]{2,1,0:T(8,128)(2,1)}, u32[]{:S(2)}, u32[]{:S(2)}) collective-permute-start(bf16[2,192,2048]{2,1,0:T(8,128)(2,1)} %get-tuple-element.433), channel_id=1, source_target_pairs={{0,2},{1,3},{2,0},{3,1},{4,6},{5,7},{6,4},{7,5},{8,10},{9,11},{10,... | collective-permute-start | bytes 4718600 | tf_op jit(solution)/shard_map/ppermute | solution.py:88
  489.8 65.4 %all-to-all-start = ((bf16[4,368,352]{1,2,0:T(8,128)(2,1)}), bf16[4,368,352]{1,2,0:T(8,128)(2,1)}, u32[]{:S(2)}, u32[]{:S(2)}) async-start(bf16[4,368,352]{1,2,0:T(8,128)(2,1)} %copy.69), calls=%async_computation.2 | async-start | bytes 2162688 | tf_op jit(solution)/shard_map/all_to_all | solution.py:1008
  527.5 36.2 %collective-permute-start.53 = (bf16[2,1024,256]{2,1,0:T(8,128)(2,1)}, bf16[2,1024,256]{2,1,0:T(8,128)(2,1)}, u32[]{:S(2)}, u32[]{:S(2)}) collective-permute-start(bf16[2,1024,256]{2,1,0:T(8,128)(2,1)} %get-tuple-element.456), channel_id=1, source_target_pairs={{0,4},{1,5},{2,6},{3,7},{4,0},{5,1},{6,2},{7,3},{8,12},{9,13},{10,... | collective-permute-start | bytes 3145736 | tf_op jit(solution)/shard_map/ppermute | solution.py:88
  528.6 35.0 %collective-permute-start.54 = (bf16[2,1024,256]{2,1,0:T(8,128)(2,1)}, bf16[2,1024,256]{2,1,0:T(8,128)(2,1)}, u32[]{:S(2)}, u32[]{:S(2)}) collective-permute-start(bf16[2,1024,256]{2,1,0:T(8,128)(2,1)} %get-tuple-element.457), channel_id=1, source_target_pairs={{0,2},{1,3},{2,0},{3,1},{4,6},{5,7},{6,4},{7,5},{8,10},{9,11},{10,... | collective-permute-start | bytes 3145736 | tf_op jit(solution)/shard_map/ppermute | solution.py:88
  530.0 49.0 %collective-permute-start.51 = (bf16[192,2048]{1,0:T(8,128)(2,1)}, bf16[192,2048]{1,0:T(8,128)(2,1)}, u32[]{:S(2)}, u32[]{:S(2)}) collective-permute-start(bf16[192,2048]{1,0:T(8,128)(2,1)} %get-tuple-element.438), channel_id=1, source_target_pairs={{0,4},{1,5},{2,6},{3,7},{4,0},{5,1},{6,2},{7,3},{8,12},{9,13},{10,... | collective-permute-start | bytes 2359304 | tf_op jit(solution)/shard_map/ppermute | solution.py:88
  530.9 48.1 %collective-permute-start.52 = (bf16[192,2048]{1,0:T(8,128)(2,1)}, bf16[192,2048]{1,0:T(8,128)(2,1)}, u32[]{:S(2)}, u32[]{:S(2)}) collective-permute-start(bf16[192,2048]{1,0:T(8,128)(2,1)} %get-tuple-element.439), channel_id=1, source_target_pairs={{0,2},{1,3},{2,0},{3,1},{4,6},{5,7},{6,4},{7,5},{8,10},{9,11},{10,... | collective-permute-start | bytes 2359304 | tf_op jit(solution)/shard_map/ppermute | solution.py:88
  574.4 29.3 %collective-permute-start.56 = (bf16[4,1024,256]{2,1,0:T(8,128)(2,1)}, bf16[4,1024,256]{2,1,0:T(8,128)(2,1)}, u32[]{:S(2)}, u32[]{:S(2)}) collective-permute-start(bf16[4,1024,256]{2,1,0:T(8,128)(2,1)} %get-tuple-element.472), channel_id=1, source_target_pairs={{0,1},{1,0},{2,3},{3,2},{4,5},{5,4},{6,7},{7,6},{8,9},{9,8},{10,11... | collective-permute-start | bytes 6291464 | tf_op jit(solution)/shard_map/ppermute | solution.py:88
  578.5 25.2 %collective-permute-start.55 = (bf16[4,1024,256]{2,1,0:T(8,128)(2,1)}, bf16[4,1024,256]{2,1,0:T(8,128)(2,1)}, u32[]{:S(2)}, u32[]{:S(2)}) collective-permute-start(bf16[4,1024,256]{2,1,0:T(8,128)(2,1)} %get-tuple-element.471), channel_id=1, source_target_pairs={{0,1},{1,0},{2,3},{3,2},{4,5},{5,4},{6,7},{7,6},{8,9},{9,8},{10,11... | collective-permute-start | bytes 6291464 | tf_op jit(solution)/shard_map/ppermute | solution.py:88
  592.9 55.0 %all-to-all-start.1 = ((bf16[8,2,192,256]{3,2,1,0:T(8,128)(2,1)}), bf16[8,2,192,256]{3,2,1,0:T(8,128)(2,1)}, u32[]{:S(2)}, u32[]{:S(2)}) async-start(bf16[8,2,192,256]{3,2,1,0:T(8,128)(2,1)} %gather_fusion.1), calls=%async_computation.4 | async-start | bytes 3145728 | tf_op jit(solution)/shard_map/all_to_all | solution.py:1308
  597.3 127.5 %reduce-scatter.14.cloned.1.call-start = ((), (), s32[]{:S(2)}) async-start(), calls=%async_computation.13 | async-start | bytes 1310720 | tf_op jit(solution)/shard_map/reduce_scatter | solution.py:1235
  608.3 47.0 %collective-permute-start.63 = (bf16[368,352]{1,0:T(8,128)(2,1)}, bf16[368,352]{1,0:T(8,128)(2,1)}, u32[]{:S(2)}, u32[]{:S(2)}) collective-permute-start(bf16[368,352]{1,0:T(8,128)(2,1)} %get-tuple-element.595), channel_id=1, source_target_pairs={{0,8},{8,16},{1,9},{9,17},{2,10},{10,18},{3,11},{11,19},{4,12},{12... | collective-permute-start | bytes 777224 | tf_op jit(solution)/shard_map/ppermute | solution.py:1018
  612.9 42.5 %collective-permute-start.64 = (bf16[368,352]{1,0:T(8,128)(2,1)}, bf16[368,352]{1,0:T(8,128)(2,1)}, u32[]{:S(2)}, u32[]{:S(2)}) collective-permute-start(bf16[368,352]{1,0:T(8,128)(2,1)} %get-tuple-element.594), channel_id=1, source_target_pairs={{24,8},{0,16},{25,9},{1,17},{26,10},{2,18},{27,11},{3,19},{28,12},... | collective-permute-start | bytes 777224 | tf_op jit(solution)/shard_map/ppermute | solution.py:1018
  615.1 45.1 %collective-permute-start.65 = (bf16[368,352]{1,0:T(8,128)(2,1)}, bf16[368,352]{1,0:T(8,128)(2,1)}, u32[]{:S(2)}, u32[]{:S(2)}) collective-permute-start(bf16[368,352]{1,0:T(8,128)(2,1)} %get-tuple-element.593), channel_id=1, source_target_pairs={{16,8},{24,16},{17,9},{25,17},{18,10},{26,18},{19,11},{27,19},{20,... | collective-permute-start | bytes 777224 | tf_op jit(solution)/shard_map/ppermute | solution.py:1018
  616.5 31.5 %collective-permute-start.59 = (bf16[2,1024,256]{2,1,0:T(8,128)(2,1)}, bf16[2,1024,256]{2,1,0:T(8,128)(2,1)}, u32[]{:S(2)}, u32[]{:S(2)}) collective-permute-start(bf16[2,1024,256]{2,1,0:T(8,128)(2,1)} %get-tuple-element.491), channel_id=1, source_target_pairs={{0,4},{1,5},{2,6},{3,7},{4,0},{5,1},{6,2},{7,3},{8,12},{9,13},{10,... | collective-permute-start | bytes 3145736 | tf_op jit(solution)/shard_map/ppermute | solution.py:88
  618.3 29.6 %collective-permute-start.60 = (bf16[2,1024,256]{2,1,0:T(8,128)(2,1)}, bf16[2,1024,256]{2,1,0:T(8,128)(2,1)}, u32[]{:S(2)}, u32[]{:S(2)}) collective-permute-start(bf16[2,1024,256]{2,1,0:T(8,128)(2,1)} %get-tuple-element.492), channel_id=1, source_target_pairs={{0,2},{1,3},{2,0},{3,1},{4,6},{5,7},{6,4},{7,5},{8,10},{9,11},{10,... | collective-permute-start | bytes 3145736 | tf_op jit(solution)/shard_map/ppermute | solution.py:88
  655.4 45.7 %collective-permute-start.66 = (bf16[352,352]{1,0:T(8,128)(2,1)S(1)}, bf16[352,352]{1,0:T(8,128)(2,1)}, u32[]{:S(2)}, u32[]{:S(2)}) collective-permute-start(bf16[352,352]{1,0:T(8,128)(2,1)S(1)} %get-tuple-element.516.refs_0_), channel_id=1, source_target_pairs={{0,8},{8,16},{16,24},{24,0},{1,9},{9,17},{17,25},{25,1},{2,10},{10... | collective-permute-start | bytes 743432 | tf_op jit(solution)/shard_map/ppermute | solution.py:1026
  655.4 45.7 %collective-permute-start.67 = (bf16[352,352]{1,0:T(8,128)(2,1)S(1)}, bf16[352,352]{1,0:T(8,128)(2,1)}, u32[]{:S(2)}, u32[]{:S(2)}) collective-permute-start(bf16[352,352]{1,0:T(8,128)(2,1)S(1)} %get-tuple-element.516.refs_0_), channel_id=1, source_target_pairs={{0,16},{8,24},{16,0},{24,8},{1,17},{9,25},{17,1},{25,9},{2,18},{10... | collective-permute-start | bytes 743432 | tf_op jit(solution)/shard_map/ppermute | solution.py:1026
  660.1 41.0 %collective-permute-start.68 = (bf16[352,352]{1,0:T(8,128)(2,1)S(1)}, bf16[352,352]{1,0:T(8,128)(2,1)}, u32[]{:S(2)}, u32[]{:S(2)}) collective-permute-start(bf16[352,352]{1,0:T(8,128)(2,1)S(1)} %get-tuple-element.516.refs_0_), channel_id=1, source_target_pairs={{0,24},{8,0},{16,8},{24,16},{1,25},{9,1},{17,9},{25,17},{2,26},{10... | collective-permute-start | bytes 743432 | tf_op jit(solution)/shard_map/ppermute | solution.py:1026
  661.3 29.9 %all-to-all-start.2 = ((bf16[8,4,64,256]{3,2,1,0:T(8,128)(2,1)}), bf16[8,4,64,256]{3,2,1,0:T(8,128)(2,1)}, u32[]{:S(2)}, u32[]{:S(2)}) async-start(bf16[8,4,64,256]{3,2,1,0:T(8,128)(2,1)} %bitcast.271), calls=%async_computation.5 | async-start | bytes 2097152 | tf_op jit(solution)/shard_map/all_to_all | solution.py:1333
  665.6 94.3 %reduce-scatter.12.cloned.1.call-start = ((), (), s32[]{:S(2)}) async-start(), calls=%async_computation.12 | async-start | bytes 1310720 | tf_op jit(solution)/shard_map/reduce_scatter | solution.py:1235
  693.3 30.8 %all-to-all-start.3 = ((bf16[4,64,256]{2,1,0:T(8,128)(2,1)}), bf16[4,64,256]{2,1,0:T(8,128)(2,1)S(1)}, u32[]{:S(2)}, u32[]{:S(2)}) async-start(bf16[4,64,256]{2,1,0:T(8,128)(2,1)} %reduce_sum.163), calls=%async_computation.7 | async-start | bytes 262144 | tf_op jit(solution)/shard_map/all_to_all | solution.py:1347
  762.7 26.2 %collective-permute-start.84 = (f32[2,128,128]{2,1,0:T(8,128)S(1)}, f32[2,128,128]{2,1,0:T(8,128)S(1)}, u32[]{:S(2)}, u32[]{:S(2)}) collective-permute-start(f32[2,128,128]{2,1,0:T(8,128)S(1)} %pad_maximum_fusion.15.refs_0_), channel_id=1, source_target_pairs={{0,16},{8,24},{16,0},{24,8},{1,17},{9,25},{17,1},{25,9},{2,18},{10... | collective-permute-start | bytes 393224 | tf_op jit(solution)/shard_map/ppermute | solution.py:979
  (227 other events, 2491.9 us)
Sparse Core Ops, SparseCore 0:
  10.5 48.6 all-gather.8
  74.1 25.9 all-gather.10
  102.2 106.1 all-gather.12
  248.0 57.1 all-gather.14
  342.6 55.2 reduce-scatter.5
  409.7 54.7 reduce-scatter.7
  467.4 73.1 reduce-scatter.9
  623.2 27.0 reduce-scatter.13
  684.0 32.3 reduce-scatter.11

commit v3 on v2

--- a/solution.py
+++ b/solution.py
@@ -9,7 +9,8 @@
 
 FF_BLOCK = 352
 NS_ITERS = 5
-HEADS_PER_STEP = 4
+FORWARD_HEADS = 8
+BACKWARD_HEADS = 4
 
 EPS = 1e-05
 THETA = 10000.0
@@ -21,6 +22,7 @@
 DECAY = 0.5
 MASKED = -1e30
 VMEM_LIMIT = 40 * 1024 * 1024
+VMEM_MOST = 58 * 1024 * 1024
 LOW = jnp.bfloat16
 
 
@@ -97,6 +99,7 @@
         self.size = size
         self.half = value.shape[0] // 2
         self.parts = {"own": value}
+        self.cuts = []
 
     def swap(self, name, flip):
         return swap(self.parts[name], flip, self.size)
@@ -111,12 +114,22 @@
         parts["two"] = self.swap("own", 2)
         parts["four"] = self.swap("own", 4)
 
+    def cut(self, value):
+        parts = self.parts
+        if self.size != 8:
+            return value
+        top, low = parts["two"][: self.half], parts["four"][self.half :]
+        self.cuts = list(tie(top, low, value))
+        return self.cuts.pop()
+
     def second(self):
         parts = self.parts
         if self.size != 8:
             return
-        parts["six_top"] = swap(parts["two"][: self.half], 4, self.size)
-        parts["six_low"] = swap(parts["four"][self.half :], 2, self.size)
+        if not self.cuts:
+            self.cut(jnp.zeros((), jnp.float32))
+        parts["six_top"] = swap(self.cuts[0], 4, self.size)
+        parts["six_low"] = swap(self.cuts[1], 2, self.size)
 
     def relay(self):
         parts = self.parts
@@ -256,31 +269,36 @@
     return jnp.where(allowed, 0.0, MASKED)
 
 
-def forward_kernel(heads, head_dim, q_ref, kv_ref, qid_ref, kid_ref, ctx_ref, log_ref, bias_ref):
+def forward_kernel(heads, head_dim, q_ref, kv_ref, qid_ref, kid_ref, *refs):
+    ctx_ref, log_ref, bias_ref, probs_ref = refs[-4:]
+
     @pl.when(pl.program_id(1) == 0)
     def _():
         bias_ref[...] = masked_bias(qid_ref, kid_ref)
 
     keys = kv_ref[0, :, :head_dim]
     values = kv_ref[0, :, head_dim:]
+    rows = q_ref.shape[1]
     for head in range(heads):
         cols = slice(head * head_dim, (head + 1) * head_dim)
         scores = contract(q_ref[0, :, cols], keys, 1, 1) * head_dim ** (-0.5) + bias_ref[...]
         top = jnp.max(scores, axis=-1, keepdims=True)
         powers = jnp.exp(scores - top)
         total = jnp.sum(powers, axis=-1, keepdims=True)
-        log_ref[0, :, cols] = jnp.broadcast_to(top + jnp.log(total), (scores.shape[0], head_dim))
-        probs = (powers * (1.0 / total)).astype(LOW)
-        ctx_ref[0, :, cols] = contract(probs, values, 1, 0).astype(LOW)
-
-
-def attention_forward(batch, queries, keyval, qid, kid, head_dim):
-    unused, rows, width = queries.shape
+        log_ref[0, :, cols] = jnp.broadcast_to(top + jnp.log(total), (rows, head_dim))
+        probs_ref[head * rows : (head + 1) * rows] = (powers * (1.0 / total)).astype(LOW)
+    context = contract(probs_ref[...], values, 1, 0).astype(LOW)
+    for head in range(heads):
+        cols = slice(head * head_dim, (head + 1) * head_dim)
+        ctx_ref[0, :, cols] = context[head * rows : (head + 1) * rows]
+
+
+def attention_forward(batch, queries, keyval, qid, kid, head_dim, earlier=()):
+    all_batches, rows, width = queries.shape
     batches = 1
     seq_len = keyval.shape[1]
-    heads = min(HEADS_PER_STEP, width // head_dim)
+    heads = min(FORWARD_HEADS, width // head_dim)
     block = pl.BlockSpec((1, rows, heads * head_dim), lambda b, h: (batch, 0, h))
-    own = pl.BlockSpec((1, rows, heads * head_dim), lambda b, h: (0, 0, h))
     work = batches * rows * width * seq_len
     return pl.pallas_call(
         functools.partial(forward_kernel, heads, head_dim),
@@ -290,19 +308,24 @@
             pl.BlockSpec((1, seq_len, 2 * head_dim), lambda b, h: (batch, 0, 0)),
             pl.BlockSpec((1, rows, 2), lambda b, h: (batch, 0, 0)),
             pl.BlockSpec((1, 2, seq_len), lambda b, h: (batch, 0, 0)),
+        ]
+        + [pl.BlockSpec(memory_space=pltpu.HBM)] * len(earlier),
+        out_specs=[block, block],
+        out_shape=[
+            jax.ShapeDtypeStruct((all_batches, rows, width), LOW),
+            jax.ShapeDtypeStruct((all_batches, rows, width), jnp.float32),
         ],
-        out_specs=[own, own],
-        out_shape=[
-            jax.ShapeDtypeStruct((batches, rows, width), LOW),
-            jax.ShapeDtypeStruct((batches, rows, width), jnp.float32),
+        input_output_aliases={4 + n: n for n in range(len(earlier))},
+        scratch_shapes=[
+            pltpu.VMEM((rows, seq_len), jnp.float32),
+            pltpu.VMEM((heads * rows, seq_len), LOW),
         ],
-        scratch_shapes=[pltpu.VMEM((rows, seq_len), jnp.float32)],
         compiler_params=pltpu.CompilerParams(vmem_limit_bytes=VMEM_LIMIT),
         cost_estimate=pl.CostEstimate(
             flops=8 * work, bytes_accessed=8 * batches * rows * width, transcendentals=work // head_dim
         ),
         name="attention_forward",
-    )(queries, keyval, qid, kid)
+    )(queries, keyval, qid, kid, *earlier)
 
 
 def backward_kernel(
@@ -316,10 +339,10 @@
     kid_ref,
     cos_ref,
     sin_ref,
-    dq_ref,
-    dkv_ref,
-    bias_ref,
+    *refs,
 ):
+    dq_ref, out_ref, dkv_ref, bias_ref, probs_ref, ds_ref = refs[-6:]
+
     @pl.when(pl.program_id(1) == 0)
     def _():
         bias_ref[...] = masked_bias(qid_ref, kid_ref)
@@ -331,36 +354,45 @@
     values = kv_ref[0, :, head_dim:]
     cosine = cos_ref[0]
     sine = sin_ref[0]
-    d_keys = 0.0
-    d_values = 0.0
+    rows = q_ref.shape[1]
     for head in range(heads):
         cols = slice(head * head_dim, (head + 1) * head_dim)
-        queries = q_ref[0, :, cols]
-        d_context = dctx_ref[0, :, cols]
-        scores = contract(queries, keys, 1, 1) * scale + bias_ref[...]
+        place = slice(head * rows, (head + 1) * rows)
+        scores = contract(q_ref[0, :, cols], keys, 1, 1) * scale + bias_ref[...]
         probs = jnp.exp(scores - log_ref[0, :, head * head_dim : head * head_dim + 1])
-        d_probs = contract(d_context, values, 1, 1)
+        d_probs = contract(dctx_ref[0, :, cols], values, 1, 1)
         centre = jnp.sum(d_probs * probs, axis=-1, keepdims=True)
-        d_scores = (probs * (d_probs - centre)).astype(LOW)
-        d_keys = d_keys + contract(d_scores, queries, 0, 0)
-        d_values = d_values + contract(probs.astype(LOW), d_context, 0, 0)
-        d_query = contract(d_scores, keys, 1, 0) * scale
-        first = d_query[:, :half]
-        second = d_query[:, half:]
-        dq_ref[0, :, cols] = jnp.concatenate(
+        ds_ref[place] = (probs * (d_probs - centre)).astype(LOW)
+        probs_ref[place] = probs.astype(LOW)
+    queries = jnp.concatenate(
+        [q_ref[0, :, head * head_dim : (head + 1) * head_dim] for head in range(heads)], axis=0
+    )
+    d_context = jnp.concatenate(
+        [dctx_ref[0, :, head * head_dim : (head + 1) * head_dim] for head in range(heads)], axis=0
+    )
+    dkv_ref[:, :head_dim] += contract(queries, ds_ref[...], 0, 0).T * scale
+    dkv_ref[:, head_dim:] += contract(d_context, probs_ref[...], 0, 0).T
+    d_query = contract(ds_ref[...], keys, 1, 0) * scale
+    for head in range(heads):
+        first = d_query[head * rows : (head + 1) * rows, :half]
+        second = d_query[head * rows : (head + 1) * rows, half:]
+        dq_ref[0, :, head * head_dim : (head + 1) * head_dim] = jnp.concatenate(
             [first * cosine + second * sine, second * cosine - first * sine], axis=1
         ).astype(LOW)
-    dkv_ref[0, :, :head_dim] += d_keys * scale
-    dkv_ref[0, :, head_dim:] += d_values
-
-
-def attention_backward(batch, queries, d_context, logs, keyval, qid, kid, cosine, sine, head_dim):
-    unused, rows, width = queries.shape
+
+    @pl.when(pl.program_id(1) == pl.num_programs(1) - 1)
+    def _():
+        out_ref[0] = dkv_ref[...].astype(LOW)
+
+
+def attention_backward(
+    batch, queries, d_context, logs, keyval, qid, kid, cosine, sine, head_dim, earlier=()
+):
+    all_batches, rows, width = queries.shape
     batches = 1
     seq_len = keyval.shape[1]
-    heads = min(HEADS_PER_STEP, width // head_dim)
+    heads = min(BACKWARD_HEADS, width // head_dim)
     block = pl.BlockSpec((1, rows, heads * head_dim), lambda b, h: (batch, 0, h))
-    own = pl.BlockSpec((1, rows, heads * head_dim), lambda b, h: (0, 0, h))
     work = batches * rows * width * seq_len
 
     def whole(*shape):
@@ -372,19 +404,26 @@
         in_specs=[
             block,
             block,
-            own,
+            block,
             whole(seq_len, 2 * head_dim),
             whole(rows, 2),
             whole(2, seq_len),
             whole(rows, head_dim // 2),
             whole(rows, head_dim // 2),
+        ]
+        + [pl.BlockSpec(memory_space=pltpu.HBM)] * len(earlier),
+        out_specs=[block, whole(seq_len, 2 * head_dim)],
+        out_shape=[
+            jax.ShapeDtypeStruct((all_batches, rows, width), LOW),
+            jax.ShapeDtypeStruct((all_batches, seq_len, 2 * head_dim), LOW),
         ],
-        out_specs=[own, pl.BlockSpec((1, seq_len, 2 * head_dim), lambda b, h: (0, 0, 0))],
-        out_shape=[
-            jax.ShapeDtypeStruct((batches, rows, width), LOW),
-            jax.ShapeDtypeStruct((batches, seq_len, 2 * head_dim), jnp.float32),
+        input_output_aliases={8 + n: n for n in range(len(earlier))},
+        scratch_shapes=[
+            pltpu.VMEM((seq_len, 2 * head_dim), jnp.float32),
+            pltpu.VMEM((rows, seq_len), jnp.float32),
+            pltpu.VMEM((heads * rows, seq_len), LOW),
+            pltpu.VMEM((heads * rows, seq_len), LOW),
         ],
-        scratch_shapes=[pltpu.VMEM((rows, seq_len), jnp.float32)],
         compiler_params=pltpu.CompilerParams(vmem_limit_bytes=VMEM_LIMIT),
         cost_estimate=pl.CostEstimate(
             flops=20 * work,
@@ -392,7 +431,7 @@
             transcendentals=work // head_dim,
         ),
         name="attention_backward",
-    )(queries, d_context, logs, keyval, qid, kid, cosine, sine)
+    )(queries, d_context, logs, keyval, qid, kid, cosine, sine, *earlier)
 
 
 def flat_pieces(blocks):
@@ -459,7 +498,7 @@
     turned = tables is not None
     return pl.pallas_call(
         functools.partial(project_kernel, places, head_dim, turned),
-        in_specs=[pl.BlockSpec(memory_space=pl.ANY)] * len(arrays) + [vmem] * (3 if turned else 1),
+        in_specs=[pl.BlockSpec(memory_space=pltpu.HBM)] * len(arrays) + [vmem] * (3 if turned else 1),
         out_specs=vmem,
         out_shape=jax.ShapeDtypeStruct((rows.shape[0], size * width), LOW),
         scratch_shapes=[
@@ -507,7 +546,7 @@
     vmem = pl.BlockSpec(memory_space=pltpu.VMEM)
     return pl.pallas_call(
         functools.partial(project_back_kernel, places),
-        in_specs=[pl.BlockSpec(memory_space=pl.ANY)] * len(arrays) + [vmem],
+        in_specs=[pl.BlockSpec(memory_space=pltpu.HBM)] * len(arrays) + [vmem],
         out_specs=vmem,
         out_shape=jax.ShapeDtypeStruct((rows.shape[0], depth), jnp.float32),
         scratch_shapes=[
@@ -524,10 +563,39 @@
     )(*arrays, rows)
 
 
+def beside(source_refs, weight_ref, sem_ref, whole=(), whole_ref=None):
+    @pl.when(pl.program_id(0) == 0)
+    def _():
+        copies = []
+        for number, source_ref in enumerate(source_refs):
+            groups, _, chunk = source_ref.shape
+            for group in range(groups):
+                cols = pl.ds(group * chunk, chunk)
+                copies.append(
+                    pltpu.make_async_copy(
+                        source_ref.at[group],
+                        weight_ref.at[number, :, cols],
+                        sem_ref.at[number, group],
+                    )
+                )
+        for ref, number in whole:
+            copies.append(
+                pltpu.make_async_copy(
+                    ref, whole_ref.at[number], sem_ref.at[len(source_refs) + number, 0]
+                )
+            )
+        for copy in copies:
+            copy.start()
+        for copy in copies:
+            copy.wait()
+
+
 def hidden_kernel(places, steps_order, turn, *refs):
     count = len(places)
     piece_refs = refs[:count]
-    weight_ref, all_ref, gate_ref, up_ref, hidden_ref, turned_ref, slot_ref, sem_ref = refs[count:]
+    source_refs = refs[count : count + 2]
+    all_ref, gate_ref, up_ref, hidden_ref, turned_ref = refs[count + 2 : count + 7]
+    slot_ref, weight_ref, sem_ref, weight_sem_ref = refs[count + 7 :]
     step = pl.program_id(0)
     steps = pl.num_programs(0)
     half = slot_ref.shape[1] // 2
@@ -558,16 +626,12 @@
     def _():
         each(step + 1, lambda copy: copy.start())
 
+    beside(source_refs, weight_ref, weight_sem_ref)
     each(step, lambda copy: copy.wait())
     rows = slot_ref[lax.rem(step, 2)]
     all_ref[...] = rows
-    groups, _, _, chunk = weight_ref.shape
-    gate = 0.0
-    upward = 0.0
-    for group in range(groups):
-        part = rows[:, group * chunk : (group + 1) * chunk]
-        gate = gate + contract(part, weight_ref[group, 0], 1, 1)
-        upward = upward + contract(part, weight_ref[group, 1], 1, 1)
+    gate = contract(rows, weight_ref[0], 1, 1)
+    upward = contract(rows, weight_ref[1], 1, 1)
     gate_ref[...] = gate
     up_ref[...] = upward
     hidden = gate * jax.nn.sigmoid(gate) * upward
@@ -587,14 +651,14 @@
     return jnp.concatenate(rows, axis=0)
 
 
-def hidden_units(run, blocks, gate_up):
+def hidden_units(run, blocks, full_gate, full_up):
     size = len(blocks)
     steps = step_order(size)[run]
     used = {2 * pair + parity for pair, _ in steps for parity in (0, 1)}
     places, arrays = flat_pieces([part if s in used else [] for s, part in enumerate(blocks)])
     rows = max(first + count for _, first, count in places)
     depth = arrays[0].shape[1]
-    units = gate_up.shape[2]
+    units = full_gate.shape[1]
     turn = rows % 128 == 0
 
     def block(width):
@@ -605,8 +669,7 @@
     return pl.pallas_call(
         functools.partial(hidden_kernel, places, steps, turn),
         grid=(len(steps),),
-        in_specs=[pl.BlockSpec(memory_space=pl.ANY)] * len(arrays)
-        + [pl.BlockSpec(gate_up.shape, lambda s: (0, 0, 0, 0), pipeline_mode=pl.Buffered(1))],
+        in_specs=[pl.BlockSpec(memory_space=pltpu.HBM)] * (len(arrays) + 2),
         out_specs=[block(depth), block(units), block(units), block(units), turned],
         out_shape=[
             jax.ShapeDtypeStruct((len(steps) * rows, depth), LOW),
@@ -615,7 +678,12 @@
             jax.ShapeDtypeStruct((len(steps) * rows, units), LOW),
             jax.ShapeDtypeStruct(turned_shape, LOW),
         ],
-        scratch_shapes=[pltpu.VMEM((2, rows, depth), LOW), pltpu.SemaphoreType.DMA((2, 2))],
+        scratch_shapes=[
+            pltpu.VMEM((2, rows, depth), LOW),
+            pltpu.VMEM((2, units, depth), LOW),
+            pltpu.SemaphoreType.DMA((2, 2)),
+            pltpu.SemaphoreType.DMA((2, full_gate.shape[0])),
+        ],
         compiler_params=pltpu.CompilerParams(vmem_limit_bytes=VMEM_LIMIT),
         cost_estimate=pl.CostEstimate(
             flops=4 * len(steps) * rows * depth * units,
@@ -623,20 +691,31 @@
             transcendentals=len(steps) * rows * units,
         ),
         name="hidden_units",
-    )(*arrays, gate_up)
+    )(*arrays, full_gate, full_up)
 
 
 def hidden_back_kernel(
-    turn, cot_ref, gate_ref, up_ref, gate_up_ref, down_ref, dg_ref, du_ref, even_ref, odd_ref
+    turn,
+    cot_ref,
+    gate_ref,
+    up_ref,
+    full_gate_ref,
+    full_up_ref,
+    source_ref,
+    dg_ref,
+    du_ref,
+    even_ref,
+    odd_ref,
+    down_ref,
+    both_ref,
+    sem_ref,
 ):
-    groups, _, chunk = down_ref.shape
+    groups, _, chunk = full_gate_ref.shape
+    beside([source_ref], down_ref, sem_ref, [(full_gate_ref, 0), (full_up_ref, 1)], both_ref)
     gate = gate_ref[...]
     upward = up_ref[...]
     sigma = jax.nn.sigmoid(gate)
-    d_hidden = 0.0
-    for group in range(groups):
-        cols = slice(group * chunk, (group + 1) * chunk)
-        d_hidden = d_hidden + contract(cot_ref[:, cols], down_ref[group], 1, 1)
+    d_hidden = contract(cot_ref[...], down_ref[0], 1, 1)
     d_gate = d_hidden * upward * sigma * (1.0 + gate * (1.0 - sigma))
     d_up = d_hidden * gate * sigma
     dg_ref[...] = (d_gate.T if turn else d_gate).astype(LOW)
@@ -644,14 +723,14 @@
     d_gate = d_gate.astype(LOW)
     d_up = d_up.astype(LOW)
     for group in range(groups):
-        part = contract(d_gate, gate_up_ref[group, 0], 1, 0)
-        part = (part + contract(d_up, gate_up_ref[group, 1], 1, 0)).astype(LOW)
+        part = contract(d_gate, both_ref[0, group], 1, 0)
+        part = (part + contract(d_up, both_ref[1, group], 1, 0)).astype(LOW)
         cols = slice(group * chunk, (group + 1) * chunk)
         even_ref[0, :, cols] = part[: part.shape[0] // 2]
         odd_ref[0, :, cols] = part[part.shape[0] // 2 :]
 
 
-def hidden_back(cotangent, gate, upward, gate_up, down, steps):
+def hidden_back(cotangent, gate, upward, full_gate, full_up, down, steps):
     tokens, depth = cotangent.shape
     rows = tokens // steps
     units = gate.shape[1]
@@ -674,8 +753,9 @@
             block(depth),
             block(units),
             block(units),
-            pl.BlockSpec(gate_up.shape, lambda s: (0, 0, 0, 0), pipeline_mode=pl.Buffered(1)),
-            pl.BlockSpec(down.shape, lambda s: (0, 0, 0), pipeline_mode=pl.Buffered(1)),
+            pl.BlockSpec(memory_space=pltpu.HBM),
+            pl.BlockSpec(memory_space=pltpu.HBM),
+            pl.BlockSpec(memory_space=pltpu.HBM),
         ],
         out_specs=[turned, turned, half, half],
         out_shape=[
@@ -684,14 +764,19 @@
             jax.ShapeDtypeStruct((steps, rows // 2, depth), LOW),
             jax.ShapeDtypeStruct((steps, rows // 2, depth), LOW),
         ],
-        compiler_params=pltpu.CompilerParams(vmem_limit_bytes=VMEM_LIMIT),
+        scratch_shapes=[
+            pltpu.VMEM((1, units, depth), LOW),
+            pltpu.VMEM((2,) + full_gate.shape, LOW),
+            pltpu.SemaphoreType.DMA((3, down.shape[0])),
+        ],
+        compiler_params=pltpu.CompilerParams(vmem_limit_bytes=VMEM_MOST),
         cost_estimate=pl.CostEstimate(
             flops=6 * steps * rows * depth * units,
             bytes_accessed=4 * steps * rows * depth,
             transcendentals=steps * rows * units,
         ),
         name="hidden_back",
-    )(cotangent, gate, upward, gate_up, down)
+    )(cotangent, gate, upward, full_gate, full_up, down)
 
 
 def hidden_out_kernel(hidden_ref, down_ref, even_ref, odd_ref):
@@ -823,31 +908,37 @@
     return row, col, jnp.where(row == col, 1.0, 0.0)
 
 
-def packed_kernel(width, matrix_ref, *gram_refs):
+def packed_kernel(width, slots, *refs):
+    matrix_refs, out_ref = refs[:-1], refs[-1]
     row, col, eye = eye_of(width)
-    for block, gram_ref in enumerate(gram_refs):
-        part = matrix_ref[block * width : (block + 1) * width, :]
+    for slot in range(out_ref.shape[0]):
+        if slot not in [used for _, _, used in slots]:
+            out_ref[slot] = jnp.zeros_like(out_ref[slot])
+    for number, block, slot in slots:
+        part = matrix_refs[number][block * width : (block + 1) * width, :]
         gram = fine_dot(part, part, 1, 1)
         high = wide(gram.astype(LOW))
         low = gram - high
-        gram_ref[:width, :] = jnp.where(col >= row, high, low).astype(LOW)
+        out_ref[slot, :width, :] = jnp.where(col >= row, high, low).astype(LOW)
         last = jnp.sum(low * eye, axis=0, keepdims=True)
-        gram_ref[width:, :] = jnp.broadcast_to(
-            last, (gram_ref.shape[0] - width, width)
+        out_ref[slot, width:, :] = jnp.broadcast_to(
+            last, (out_ref.shape[1] - width, width)
         ).astype(LOW)
 
 
-def packed_grams(matrix, width):
-    count = matrix.shape[0] // width
-    return pl.pallas_call(
-        functools.partial(packed_kernel, width),
-        out_shape=[jax.ShapeDtypeStruct((width + 16, width), LOW)] * count,
+def owners_parts(matrices, width, slots, size):
+    packed = pl.pallas_call(
+        functools.partial(packed_kernel, width, slots),
+        out_shape=jax.ShapeDtypeStruct((size, width + 16, width), LOW),
         compiler_params=pltpu.CompilerParams(vmem_limit_bytes=VMEM_LIMIT),
         cost_estimate=pl.CostEstimate(
-            flops=6 * matrix.size * width, bytes_accessed=4 * matrix.size, transcendentals=0
+            flops=6 * len(matrices) * matrices[0].size * width,
+            bytes_accessed=4 * len(matrices) * matrices[0].size,
+            transcendentals=0,
         ),
         name="packed_grams",
-    )(matrix)
+    )(*matrices)
+    return packed
 
 
 def gram_kernel(width, by_rows, matrix_ref, *gram_refs):
@@ -892,9 +983,10 @@
 
     @pl.when(own_ref[0] != 0)
     def _():
-        total = wide(part_refs[0][...])
-        for part_ref in part_refs[1:]:
-            total = total + wide(part_ref[...])
+        total = 0.0
+        for part_ref in part_refs:
+            part = wide(part_ref[...])
+            total = total + (part if part.ndim == 2 else jnp.sum(part, axis=0))
         _, _, eye = eye_of(width)
         packed = total[:width]
         gram = packed + packed.T + eye * (total[width : width + 1] - packed)
@@ -906,7 +998,7 @@
 
 
 def block_factor(own, parts):
-    width = parts[0].shape[1]
+    width = parts[0].shape[-1]
     vmem = pl.BlockSpec(memory_space=pltpu.VMEM)
     return pl.pallas_call(
         factor_kernel,
@@ -954,22 +1046,26 @@
     )(places, matrix, weight, *choices)
 
 
-def update_kernel(width, count, by_rows, matrix_ref, weight_ref, *refs):
-    part_refs, new_ref = refs[:-1], refs[-1]
-    for block in range(count):
-        gram = part_refs[0][block]
-        for part_ref in part_refs[1:]:
-            gram = gram + part_ref[block]
-        factor = newton_factor(gram)
-        place = slice(block * width, (block + 1) * width)
-        if by_rows:
-            new_ref[place, :] = weight_ref[place, :] - MUON_RATE * fine_dot(
-                factor, matrix_ref[place, :]
-            )
-        else:
-            new_ref[:, place] = weight_ref[:, place] - MUON_RATE * fine_dot(
-                matrix_ref[:, place], factor
-            )
+def update_kernel(sizes, counts, *refs):
+    firsts = [2 * len(sizes) + sum(counts[:n]) for n in range(len(sizes))]
+    for number, (width, by_rows) in enumerate(sizes):
+        matrix_ref, weight_ref = refs[2 * number], refs[2 * number + 1]
+        part_refs = refs[firsts[number] : firsts[number] + counts[number]]
+        new_ref = refs[2 * len(sizes) + sum(counts) + number]
+        for block in range(part_refs[0].shape[0]):
+            gram = part_refs[0][block]
+            for part_ref in part_refs[1:]:
+                gram = gram + part_ref[block]
+            factor = newton_factor(gram)
+            place = slice(block * width, (block + 1) * width)
+            if by_rows:
+                new_ref[place, :] = weight_ref[place, :] - MUON_RATE * fine_dot(
+                    factor, matrix_ref[place, :]
+                )
+            else:
+                new_ref[:, place] = weight_ref[:, place] - MUON_RATE * fine_dot(
+                    matrix_ref[:, place], factor
+                )
 
 
 def gather_grams(moment, width, by_rows):
@@ -981,32 +1077,35 @@
     ]
 
 
+def small_updates(items):
+    vmem = pl.BlockSpec(memory_space=pltpu.VMEM)
+    flat = [array for moment, weight, _, _, _ in items for array in (moment, weight)]
+    flat = flat + [part for item in items for part in item[4]]
+    counts = [len(item[4]) for item in items]
+    return pl.pallas_call(
+        functools.partial(update_kernel, [(item[2], item[3]) for item in items], counts),
+        in_specs=[vmem] * len(flat),
+        out_specs=[vmem] * len(items),
+        out_shape=[jax.ShapeDtypeStruct(item[0].shape, jnp.float32) for item in items],
+        compiler_params=pltpu.CompilerParams(vmem_limit_bytes=VMEM_LIMIT),
+        cost_estimate=pl.CostEstimate(
+            flops=sum(100 * item[4][0].size * item[2] for item in items),
+            bytes_accessed=sum(12 * item[0].size for item in items),
+            transcendentals=0,
+        ),
+        name="small_update",
+    )(*flat)
+
+
 def small_update(moment, weight, width, by_rows, parts=None):
     if parts is None:
         parts = gather_grams(moment, width, by_rows)
-    size = len(parts)
-    grams = parts[0]
-    vmem = pl.BlockSpec(memory_space=pltpu.VMEM)
-    count = grams.shape[0]
-    return pl.pallas_call(
-        functools.partial(update_kernel, width, count, by_rows),
-        in_specs=[vmem] * (2 + size),
-        out_specs=vmem,
-        out_shape=jax.ShapeDtypeStruct(moment.shape, jnp.float32),
-        compiler_params=pltpu.CompilerParams(vmem_limit_bytes=VMEM_LIMIT),
-        cost_estimate=pl.CostEstimate(
-            flops=200 * count * width**3, bytes_accessed=12 * moment.size, transcendentals=0
-        ),
-        name="small_update",
-    )(moment, weight, *parts)
+    return small_updates([(moment, weight, width, by_rows, parts)])[0]
 
 
 def exchange(values, owners):
     size = lax.axis_size("dp")
     me = lax.axis_index("dp")
-    if owners == tuple(range(size)):
-        parts = lax.all_to_all(jnp.stack(values), "dp", 0, 0, tiled=True)
-        return [parts[number] for number in range(size)]
     parts = []
     for shift in range(size):
         target = (me + shift) % size
@@ -1044,12 +1143,12 @@
     size = len(blocks)
     height = max(first + count for _, first, count in places)
     width = arrays[0].shape[1]
-    gram_width = parts[0].shape[1]
+    gram_width = parts[0].shape[-1]
     vmem = pl.BlockSpec(memory_space=pltpu.VMEM)
     return pl.pallas_call(
         functools.partial(back_factor_kernel, places, len(parts)),
         in_specs=[pl.BlockSpec(memory_space=pltpu.SMEM)]
-        + [pl.BlockSpec(memory_space=pl.ANY)] * len(arrays)
+        + [pl.BlockSpec(memory_space=pltpu.HBM)] * len(arrays)
         + [vmem] * (1 + len(parts)),
         out_specs=[vmem, vmem],
         out_shape=[
@@ -1060,7 +1159,7 @@
             pltpu.VMEM((size, height, width), LOW),
             pltpu.SemaphoreType.DMA((len(arrays),)),
         ],
-        compiler_params=pltpu.CompilerParams(vmem_limit_bytes=VMEM_LIMIT),
+        compiler_params=pltpu.CompilerParams(vmem_limit_bytes=VMEM_MOST),
         cost_estimate=pl.CostEstimate(
             flops=2 * rows.size * depth + 100 * gram_width**3,
             bytes_accessed=2 * (size * height * width + 3 * rows.size),
@@ -1127,9 +1226,9 @@
     low_keyval = w_keyval.astype(LOW).reshape(-1, query_cols)
     query_block = rows_of(jnp.concatenate([w_query.astype(LOW), low_keyval], axis=0))
     out_block = rows_of(w_out.astype(LOW))
-    full_gate_up = rows_of(gate_up_t.astype(LOW))
-    out_block, low_down = tie(out_block, down_t.astype(LOW))
-    full_down = rows_of(low_down)
+    full_gate = rows_of(gate_up_t[0].astype(LOW))
+    full_up = rows_of(gate_up_t[1].astype(LOW))
+    full_down = rows_of(down_t.astype(LOW))
     order = jnp.array(gather_order(size), jnp.int32)
     place = jnp.zeros((size,), jnp.int32).at[order].set(jnp.arange(size, dtype=jnp.int32))
     place = place[me ^ jnp.arange(size)]
@@ -1139,11 +1238,6 @@
     cot.first()
     full_keyval = query_block[:, w_query.shape[0] :].reshape(model_width, 2 * head_dim)
     query_block = query_block[:, : w_query.shape[0]].reshape(model_width, query_cols)
-    cot.parts, query_block = tie(cot.parts, query_block)
-    query_gather = Gather(query_block, size)
-    query_gather.first()
-    cot.relay()
-
     own_positions = me * own_rows + jnp.arange(own_rows, dtype=jnp.int32)
     key_positions = jnp.concatenate(
         [(me ^ s) * own_rows + jnp.arange(own_rows, dtype=jnp.int32) for s in gather_order(size)]
@@ -1170,9 +1264,18 @@
     own_keyval = jnp.concatenate(
         [rotate(own_keyval[:, :head_dim], flat_cos, flat_sin), own_keyval[:, head_dim:]], axis=1
     ).astype(LOW)
-    keyval = gather_small(own_keyval.reshape(batches, own_rows, 2 * head_dim), size)
+    cot.parts, query_block = tie(cot.parts, query_block)
+    query_gather = Gather(query_block, size)
+    query_gather.first()
+    own_keyval = query_gather.cut(own_keyval)
+    flips = flips_of(size)
+    keyval = own_keyval.reshape(1, batches, own_rows, 2 * head_dim)
+    for flip in flips:
+        keyval = jnp.concatenate([keyval, swap(keyval, flip, size)], axis=0)
+        if flip == flips[-2]:
+            keyval, cot.parts = tie(keyval, cot.parts)
+            cot.relay()
     keyval = jnp.swapaxes(keyval, 0, 1).reshape(batches, seq_len, 2 * head_dim)
-    query_gather.parts, cot.parts, keyval = tie(query_gather.parts, cot.parts, keyval)
     query_gather.second()
     query_gather.relay()
     query_gather.parts, out_block = tie(query_gather.parts, out_block)
@@ -1182,20 +1285,20 @@
     query_pieces = query_gather.pieces()
     queries = project(normed, query_pieces, head_dim, (flat_cos, flat_sin))
     queries = queries.reshape(batches, own_rows, -1)
-    contexts = []
-    logs = []
+    done = ()
     for batch in range(batches):
-        context, log_sums = attention_forward(batch, queries, keyval, qid, kid, head_dim)
-        contexts.append(context)
-        logs.append(log_sums)
+        done = attention_forward(batch, queries, keyval, qid, kid, head_dim, done)
         if batch == 0:
-            out_gather.parts, queries, contexts = tie(out_gather.parts, queries, contexts)
+            out_gather.parts, queries, done = tie(out_gather.parts, queries, done)
             out_gather.second()
             out_gather.relay()
-    out_gather.parts, contexts, cot.parts = tie(out_gather.parts, contexts, cot.parts)
+    out_gather.parts, done, full_gate, cot.parts = tie(
+        out_gather.parts, done, full_gate, cot.parts
+    )
     out_gather.third()
     cot.second()
-    context = jnp.concatenate(contexts, axis=0).reshape(tokens, -1)
+    context, logs = done
+    context = context.reshape(tokens, -1)
     out_pieces = out_gather.pieces()
     mid = x_rows + project_back(context, out_pieces, model_width)
     mid_scale = inverse_scale(mid)
@@ -1204,14 +1307,14 @@
     mid_gather.first()
     cot.third()
     full_cot = [in_steps(run, cot.pieces()) for run in range(2)]
-    mid_gather.parts, full_cot = tie(mid_gather.parts, full_cot)
+    mid_gather.parts, full_cot[1], full_up = tie(mid_gather.parts, full_cot[1], full_up)
     mid_gather.second()
     mid_gather.relay()
     units = [None, None]
-    units[1] = hidden_units(1, mid_gather.pieces(), full_gate_up)
+    units[1] = hidden_units(1, mid_gather.pieces(), full_gate, full_up)
     mid_gather.parts, units[1] = tie(mid_gather.parts, units[1])
     mid_gather.third()
-    units[0] = hidden_units(0, mid_gather.pieces(), full_gate_up)
+    units[0] = hidden_units(0, mid_gather.pieces(), full_gate, full_up)
     normed_mid = [unit[0] for unit in units]
     (sum_down,) = units_sum([[unit[4] for unit in units]], full_cot, groups)
     sum_down, units = tie(sum_down, units)
@@ -1221,7 +1324,7 @@
     for run in range(2):
         _, gate, upward, _, _ = units[run]
         *grads, evens, odds = hidden_back(
-            full_cot[run], gate, upward, full_gate_up, full_down, steps
+            full_cot[run], gate, upward, full_gate, full_up, full_down, steps
         )
         turned.append(grads)
         if run == 0:
@@ -1273,18 +1376,13 @@
     last_owners = (1, 2)
     if fast:
         moment_down, moment_gate, d_context = tie(moment_down, moment_gate, d_context)
-        down_grams = packed_grams(moment_down, FF_BLOCK)
-        gate_grams = packed_grams(moment_gate, FF_BLOCK)
-        down_grams, gate_grams, d_context = tie(down_grams, gate_grams, d_context)
-        first_parts = exchange(
-            (gate_grams[0], down_grams[0], down_grams[1], gate_grams[1]), first_owners
-        )
-    backs = []
+        slots = ((0, 0, 1), (0, 1, 2), (1, 0, 0), (1, 1, 3))
+        first_parts = owners_parts((moment_down, moment_gate), FF_BLOCK, slots, groups)
+        first_parts = lax.all_to_all(first_parts, "dp", 0, 0, tiled=True)
+    backs = ()
     for batch in range(batches):
-        backs.append(
-            attention_backward(
-                batch, queries, d_context, logs[batch], keyval, qid, kid, cosine, sine, head_dim
-            )
+        backs = attention_backward(
+            batch, queries, d_context, logs, keyval, qid, kid, cosine, sine, head_dim, backs
         )
         if batch == 0:
             backs, mlp_sum.parts, d_context = tie(backs, mlp_sum.parts, d_context)
@@ -1292,9 +1390,8 @@
     if fast:
         backs, first_parts = tie(backs, first_parts)
     backs, out_sum.parts, grad_up = tie(backs, out_sum.parts, grad_up)
-    backs = out_sum.third(backs)
-    d_queries = jnp.concatenate([back[0] for back in backs], axis=0).reshape(tokens, -1)
-    d_keyval = jnp.concatenate([back[1] for back in backs], axis=0).astype(LOW)
+    d_queries, d_keyval = out_sum.third(backs)
+    d_queries = d_queries.reshape(tokens, -1)
 
     def own_rows_of(total, width):
         return scatter_rows(total.astype(LOW).reshape(groups, -1, width))
@@ -1308,19 +1405,21 @@
     d_keyval = lax.all_to_all(d_keyval, "mp", 0, 0, tiled=True)
     output = (mid + mlp_sum.total()).astype(LOW).reshape(inputs.shape)
     moment_up = DECAY * old_gate_up[1] + wide(grad_up)
-    query_parts, d_queries, moment_up = tie(query_parts, d_queries, moment_up)
+    own = is_owner(first_owners)
+    query_parts, own, moment_up = tie(query_parts, own, moment_up)
     if fast:
-        up_grams = packed_grams(moment_up, FF_BLOCK)
-        query_sum.parts, up_grams, d_queries = tie(query_sum.parts, up_grams, d_queries)
-        last_parts = exchange(up_grams, last_owners)
-    out_sum.parts, d_queries = tie(out_sum.parts, d_queries)
+        up_grams = owners_parts((moment_up,), FF_BLOCK, ((0, 0, 0), (0, 1, 1)), 2)
+        query_sum.parts, up_grams, own = tie(query_sum.parts, up_grams, own)
+        last_parts = exchange((up_grams[0], up_grams[1]), last_owners)
+    out_sum.parts, own = tie(out_sum.parts, own)
     grad_out = own_rows_of(out_sum.total(), query_cols)
-    d_queries = query_sum.second(d_queries)
     if fast:
+        own = query_sum.second(own)
         d_normed, first_factor = back_and_factor(
-            d_queries, query_pieces, model_width, is_owner(first_owners), first_parts
+            d_queries, query_pieces, model_width, own, [first_parts]
         )
     else:
+        d_queries = query_sum.second(d_queries)
         d_normed = project_back(d_queries, query_pieces, model_width)
     d_keyval, d_normed, query_sum.parts = tie(d_keyval, d_normed, query_sum.parts)
     d_normed = query_sum.third(d_normed)
@@ -1354,7 +1453,7 @@
     else:
         new_down = small_update(moment_down, down_t, FF_BLOCK, True)
         new_gate = small_update(moment_gate, gate_up_t[0], FF_BLOCK, True)
-    share_parts, new_gate = tie(share_parts, new_gate)
+    share_parts, new_down = tie(share_parts, new_down)
     grad_keyval = jnp.sum(wide(share_parts), axis=0)
     grad_keyval = gather_small(grad_keyval.astype(LOW), size)
     if fast:
@@ -1369,8 +1468,12 @@
     grad_query = wide(grad_query)
     moment_query = DECAY * m_query + grad_query
     query_grams = gather_grams(moment_query, head_dim, False)
-    new_keyval = small_update(moment_keyval, w_keyval, 2 * head_dim, False, keyval_grams)
-    new_query = small_update(moment_query, w_query, head_dim, False, query_grams)
+    new_keyval, new_query = small_updates(
+        [
+            (moment_keyval, w_keyval, 2 * head_dim, False, keyval_grams),
+            (moment_query, w_query, head_dim, False, query_grams),
+        ]
+    )
     grad_gains = add_all(add_all(jnp.stack([gain_input, gain_mid], axis=0), "mp"), "dp")
     grad_gate_up = wide(jnp.stack([grad_gate, grad_up]))
     moment_gate_up = DECAY * old_gate_up + grad_gate_up

time: 810 us -> 770 us (0.951)
  local copies, waits for them, and re-layouts: 118 us -> 101 us
  Pallas kernels: 293 us -> 277 us
  waiting for transfers between devices: 154 us -> 143 us
    ppermute x66, waiting for transfers between devices: 95.9 us -> 64.8 us  [swap(): return lax.ppermute(value, 'mp', [(i, i ^ flip) for i in range(size)])]
    unnamed x363 -> x299, local copies, waits for them, and re-layouts: 82.7 us -> 54 us
    pallas_call x2, Pallas kernels: 42.8 us -> 28.5 us  [attention_backward(): pl.pallas_call(functools.partial(backward_kernel, heads, head_dim), grid=...]
    all_gather x4 -> x5, waiting for transfers between devices: 41.6 us -> 50.7 us  [rows_of(): return lax.all_gather(value, 'dp', axis=0, tiled=False)]
    pallas_call x6 -> x4, Pallas kernels: 22 us -> 20.3 us  [the longest x2 16.5 us: small_updates(): pl.pallas_call(functools.partial(update_kernel, [(item[2], item[3]) for i...]
  transfers between devices with their start and end apart: 102 -> 103, of which waited for: 24 -> 31; matrix products, arithmetic and copies ran while one was open for 20% -> 23% of each run, Pallas kernels for 33% -> 32%
where the time goes in v3:
time: 770 us; the launch traced here: 762 us
  Pallas kernels  277 us (36%)
  waiting for transfers between devices  143 us (19%)
  starting transfers between devices  109 us (14%)
  other arithmetic  109 us (14%)
  local copies, waits for them, and re-layouts  101 us (13%)
  between operations  16.3 us (2%)
    ppermute x66, waiting for transfers between devices, swap(): return lax.ppermute(value, 'mp', [(i, i ^ flip) for i in range(size)])  64.8 us
    unnamed x299, local copies, waits for them, and re-layouts  54 us
    all_gather x5, waiting for transfers between devices, rows_of(): return lax.all_gather(value, 'dp', axis=0, tiled=False)  50.7 us
    pallas_call x2, Pallas kernels, hidden_back(): pl.pallas_call(functools.partial(hidden_back_kernel, turn), grid=(steps,)...  49.1 us
    ppermute x66, starting transfers between devices, swap(): return lax.ppermute(value, 'mp', [(i, i ^ flip) for i in range(size)])  47.7 us
    pallas_call x2, Pallas kernels, units_sum(): pl.pallas_call(functools.partial(units_sum_kernel, len(rows), turn), grid...  34.8 us
    pallas_call x2, Pallas kernels, hidden_units(): pl.pallas_call(functools.partial(hidden_kernel, places, steps, turn), gri...  34.1 us
    pallas_call x2, Pallas kernels, attention_backward(): pl.pallas_call(functools.partial(backward_kernel, heads, head_dim), grid=...  28.5 us
  transfers between devices with their start and end apart: 103, of which 31 were waited for; matrix products, arithmetic and copies ran while one was open for 23% of the time, Pallas kernels for 32%

profile of v3, /device:TPU:0, one launch (start us, length us, event | category | flops | bytes accessed | tf_op | source)
XLA Modules:
  0.0 762.2 jit_solution(14029916739045583963)
XLA Ops:
  22.7 36.5 %all-gather.13.cloned.1.call-done = bf16[4096,256]{1,0:T(8,128)(2,1)} async-done(((bf16[1024,256]{1,0:T(8,128)(2,1)}), bf16[4096,256]{1,0:T(8,128)(2,1)}) %all-gather.13.cloned.1.call-update) | async-done | bytes 2097168 | tf_op jit(solution)/shard_map/all_gather | solution.py:1222
  78.3 8.5 %collective-permute-done.6.refs_2_.refs_3_ = bf16[2048,256]{1,0:T(8,128)(2,1)S(1)} collective-permute-done((bf16[2048,256]{1,0:T(8,128)(2,1)S(1)}, bf16[2048,256]{1,0:T(8,128)(2,1)S(1)}, u32[]{:S(2)}, u32[]{:S(2)}) %collective-permute-start.6) | collective-permute-done | bytes 1048608 | tf_op jit(solution)/shard_map/ppermute | solution.py:90
  92.3 4.3 collective-permute-done.15
  129.9 10.0 %project.2 = bf16[384,2048]{1,0:T(8,128)(2,1)S(1)} custom-call(bf16[2048,256]{1,0:T(8,128)(2,1)S(1)} %bitcast.220, bf16[2048,256]{1,0:T(8,128)(2,1)} %collective-permute-done.5.refs_1_.refs_2_, bf16[2048,256]{1,0:T(8,128)(2,1)S(1)} %collective-permute-done.6.refs_2_.refs_3_, bf16[2048,256]{1,0:T(8,128)(2,1)} %collective-permute-done.9.refs_3_.refs_4_, ...), custom_call_target="tpu_custom_call" | custom-call | flops 3221225472 | bytes 11534336 | tf_op jit(solution)/shard_map/project/pallas_call | solution.py:499
  139.9 8.9 %attention_forward.2 = (bf16[2,192,2048]{2,1,0:T(8,128)(2,1)S(1)}, f32[2,192,2048]{2,1,0:T(8,128)S(1)}) custom-call(bf16[2,192,2048]{2,1,0:T(8,128)(2,1)S(1)} %bitcast.230, bf16[2,1536,256]{2,1,0:T(8,128)(2,1)S(1)} %bitcast.225, s32[2,192,2]{2,1,0:T(8,128)S(1)} %copy-done.60, s32[2,2,1536]{2,1,0:T(2,128)S(1)} %pad_add_fusion.kid_ref), custom_call_target="tpu_custom_call" | custom-call | flops 4831838208 | bytes 3145728 | tf_op jit(solution)/shard_map/attention_forward/pallas_call | solution.py:303
  159.3 9.0 %attention_forward.3 = (bf16[2,192,2048]{2,1,0:T(8,128)(2,1)S(1)}, f32[2,192,2048]{2,1,0:T(8,128)S(1)}) custom-call(bf16[2,192,2048]{2,1,0:T(8,128)(2,1)S(1)} %bitcast.231, bf16[2,1536,256]{2,1,0:T(8,128)(2,1)S(1)} %bitcast.226, s32[2,192,2]{2,1,0:T(8,128)S(1)} %copy-done.60, ...), custom_call_target="tpu_custom_call", output_to_operand_aliasing={{0}: (4, {}), {1}: (5, {})} | custom-call | flops 4831838208 | bytes 3145728 | tf_op jit(solution)/shard_map/attention_forward/pallas_call | solution.py:303
  176.7 5.2 project_back.1
  182.4 12.0 %collective-permute-done.26 = bf16[192,2048]{1,0:T(8,128)(2,1)S(1)} collective-permute-done((bf16[192,2048]{1,0:T(8,128)(2,1)S(1)}, bf16[192,2048]{1,0:T(8,128)(2,1)S(1)}, u32[]{:S(2)}, u32[]{:S(2)}) %collective-permute-start.26) | collective-permute-done | bytes 786464 | tf_op jit(solution)/shard_map/ppermute | solution.py:90
  215.9 14.2 %all-gather.11.cloned.1.call-done.refs_7_.refs_9_.full_up_ref = bf16[4,704,512]{2,1,0:T(8,128)(2,1)} async-done(((bf16[1,704,512]{2,1,0:T(8,128)(2,1)}), bf16[4,704,512]{2,1,0:T(8,128)(2,1)}) %all-gather.11.cloned.1.call-update) | async-done | bytes 2883600 | tf_op jit(solution)/shard_map/all_gather | solution.py:1222
  240.4 17.3 %hidden_units.2 = (bf16[1536,2048]{1,0:T(8,128)(2,1)}, f32[1536,704]{1,0:T(8,128)}, f32[1536,704]{1,0:T(8,128)}, bf16[1536,704]{1,0:T(8,128)(2,1)S(1)}, bf16[704,1536]{1,0:T(8,128)(2,1)S(1)}) custom-call(bf16[384,2048]{1,0:T(8,128)(2,1)} %multiply_convert_fusion.refs_0_, bf16[384,2048]{1,0:T(8,128)(2,1)} %collective-permute-done.31.refs_1_, ...), custom_call_target="tpu_custom_call" | custom-call | flops 8858370048 | bytes 12582912 | tf_op jit(solution)/shard_map/hidden_units/pallas_call | solution.py:669
  263.9 16.9 %hidden_units.3 = (bf16[1536,2048]{1,0:T(8,128)(2,1)}, f32[1536,704]{1,0:T(8,128)}, f32[1536,704]{1,0:T(8,128)}, bf16[1536,704]{1,0:T(8,128)(2,1)S(1)}, bf16[704,1536]{1,0:T(8,128)(2,1)S(1)}) custom-call(bf16[384,2048]{1,0:T(8,128)(2,1)} %collective-permute-done.32.refs_2_.refs_0_, bf16[384,2048]{1,0:T(8,128)(2,1)} %collective-permute-done.36.refs_3_.refs_1_, ...), custom_call_target="tpu_custom_call" | custom-call | flops 8858370048 | bytes 12582912 | tf_op jit(solution)/shard_map/hidden_units/pallas_call | solution.py:669
  283.8 13.1 %units_sum.2 = bf16[4,704,512]{2,1,0:T(8,128)(2,1)} custom-call(bf16[1536,2048]{1,0:T(8,128)(2,1)S(1)} %bitcast.235, bf16[1536,2048]{1,0:T(8,128)(2,1)} %slice_dynamic-update-slice_fusion.refs_1_.cot_ref, bf16[704,1536]{1,0:T(8,128)(2,1)S(1)} %get-tuple-element.332.refs_2_, bf16[704,1536]{1,0:T(8,128)(2,1)S(1)} %copy-done.84), custom_call_target="tpu_custom_call" | custom-call | flops 8858370048 | bytes 16908288 | tf_op jit(solution)/shard_map/units_sum/pallas_call | solution.py:834
  297.0 24.1 %hidden_back.2 = (bf16[704,1536]{1,0:T(8,128)(2,1)}, bf16[704,1536]{1,0:T(8,128)(2,1)}, bf16[4,192,2048]{2,1,0:T(8,128)(2,1)}, bf16[4,192,2048]{2,1,0:T(8,128)(2,1)}) custom-call(bf16[1536,2048]{1,0:T(8,128)(2,1)} %copy-done.64, f32[1536,704]{1,0:T(8,128)} %get-tuple-element.342.gate_ref, f32[1536,704]{1,0:T(8,128)} %get-tuple-element.343.up_ref, ...), custom_call_target="tpu_custom_call" | custom-call | flops 13287555072 | bytes 12582912 | tf_op jit(solution)/shard_map/hidden_back/pallas_call | solution.py:749
  321.4 25.0 %hidden_back.3 = (bf16[704,1536]{1,0:T(8,128)(2,1)}, bf16[704,1536]{1,0:T(8,128)(2,1)}, bf16[4,192,2048]{2,1,0:T(8,128)(2,1)}, bf16[4,192,2048]{2,1,0:T(8,128)(2,1)}) custom-call(bf16[1536,2048]{1,0:T(8,128)(2,1)} %slice_dynamic-update-slice_fusion.refs_1_.cot_ref, f32[1536,704]{1,0:T(8,128)} %get-tuple-element.350.gate_ref, ...), custom_call_target="tpu_custom_call" | custom-call | flops 13287555072 | bytes 12582912 | tf_op jit(solution)/shard_map/hidden_back/pallas_call | solution.py:749
  346.8 4.6 add_convert_fusion.2
  353.8 21.7 %units_sum.3 = (bf16[4,704,512]{2,1,0:T(8,128)(2,1)}, bf16[4,704,512]{2,1,0:T(8,128)(2,1)}) custom-call(bf16[1536,2048]{1,0:T(8,128)(2,1)} %get-tuple-element.334.refs_0_, bf16[1536,2048]{1,0:T(8,128)(2,1)} %get-tuple-element.338.refs_1_, bf16[704,1536]{1,0:T(8,128)(2,1)S(1)} %copy-done.85, bf16[704,1536]{1,0:T(8,128)(2,1)S(1)} %copy-done.87, ...), custom_call_target="tpu_custom_call" | custom-call | flops 17716740096 | bytes 33816576 | tf_op jit(solution)/shard_map/units_sum/pallas_call | solution.py:834
  375.4 12.6 %collective-permute-done.41 = bf16[2,192,2048]{2,1,0:T(8,128)(2,1)S(1)} collective-permute-done((bf16[2,192,2048]{2,1,0:T(8,128)(2,1)S(1)}, bf16[2,192,2048]{2,1,0:T(8,128)(2,1)S(1)}, u32[]{:S(2)}, u32[]{:S(2)}) %collective-permute-start.41) | collective-permute-done | bytes 1572896 | tf_op jit(solution)/shard_map/ppermute | solution.py:90
  393.8 6.6 hidden_out.2
  402.1 6.5 hidden_out.3
  414.5 3.9 bitcast_add_fusion.4
  422.4 4.1 blocks_sum.5
  429.3 4.1 blocks_sum.4
  436.0 3.7 slice_bitcast_fusion.1
  443.6 5.5 add_convert_fusion
  451.1 8.2 %project.3 = bf16[384,2048]{1,0:T(8,128)(2,1)S(1)} custom-call(bf16[2048,256]{1,0:T(8,128)(2,1)S(1)} %copy-done.47, bf16[2048,256]{1,0:T(8,128)(2,1)S(1)} %copy-done.50, bf16[2048,256]{1,0:T(8,128)(2,1)} %collective-permute-done.12.refs_2_, bf16[2048,256]{1,0:T(8,128)(2,1)} %collective-permute-done.21.refs_3_, ...), custom_call_target="tpu_custom_call" | custom-call | flops 3221225472 | bytes 11534336 | tf_op jit(solution)/shard_map/project/pallas_call | solution.py:499
  460.5 3.5 add_convert_fusion.6
  471.3 4.7 all-to-all-start
  481.7 14.2 %attention_backward.2 = (bf16[2,192,2048]{2,1,0:T(8,128)(2,1)S(1)}, bf16[2,1536,256]{2,1,0:T(8,128)(2,1)S(1)}) custom-call(bf16[2,192,2048]{2,1,0:T(8,128)(2,1)S(1)} %bitcast.232, bf16[2,192,2048]{2,1,0:T(8,128)(2,1)S(1)} %bitcast.244, f32[2,192,2048]{2,1,0:T(8,128)S(1)} %copy-done.77, bf16[2,1536,256]{2,1,0:T(8,128)(2,1)S(1)} %bitcast.227, ...), custom_call_target="tpu_custom_call" | custom-call | flops 12079595520 | bytes 4718592 | tf_op jit(solution)/shard_map/attention_backward/pallas_call | solution.py:401
  496.0 4.1 fusion.25
  504.1 14.2 %attention_backward.3 = (bf16[2,192,2048]{2,1,0:T(8,128)(2,1)S(1)}, bf16[2,1536,256]{2,1,0:T(8,128)(2,1)S(1)}) custom-call(bf16[2,192,2048]{2,1,0:T(8,128)(2,1)S(1)} %bitcast.233, bf16[2,192,2048]{2,1,0:T(8,128)(2,1)S(1)} %bitcast.245, f32[2,192,2048]{2,1,0:T(8,128)S(1)} %copy-done.78, ...), custom_call_target="tpu_custom_call", output_to_operand_aliasing={{0}: (8, {}), {1}: (9, {})} | custom-call | flops 12079595520 | bytes 4718592 | tf_op jit(solution)/shard_map/attention_backward/pallas_call | solution.py:401
  530.5 4.2 blocks_sum.7
  536.0 4.2 blocks_sum.6
  542.2 3.6 bitcast_add_fusion.2
  557.5 4.3 all-to-all-start.1
  569.6 3.6 add_convert_fusion.4
  577.7 4.4 collective-permute-start.63
  588.9 19.4 %back_and_factor.1 = (f32[384,2048]{1,0:T(8,128)}, bf16[352,352]{1,0:T(8,128)(2,1)}) custom-call(s32[1]{0:T(128)S(6)} %add.552.refs_0_, bf16[2048,256]{1,0:T(8,128)(2,1)} %bitcast.221, bf16[2048,256]{1,0:T(8,128)(2,1)} %collective-permute-done.5.refs_1_.refs_2_, bf16[2048,256]{1,0:T(8,128)(2,1)} %copy-done.21, ...), custom_call_target="tpu_custom_call" | custom-call | flops 7582646272 | bytes 13107200 | tf_op jit(solution)/shard_map/back_and_factor/pallas_call | solution.py:1148
  615.7 4.7 collective-permute-start.67
  621.5 4.3 all-to-all-start.2
  625.8 10.4 %block_factor.1.refs_0_ = bf16[352,352]{1,0:T(8,128)(2,1)} custom-call(s32[1]{0:T(128)S(6)} %add.561.own_ref, bf16[368,352]{1,0:T(8,128)(2,1)S(1)} %copy-done.59, bf16[368,352]{1,0:T(8,128)(2,1)} %collective-permute-done.63.refs_1_, bf16[368,352]{1,0:T(8,128)(2,1)} %collective-permute-done.64.refs_2_, bf16[368,352]{1,0:T(8,128)(2,1)} %collective-permute-done.65.refs_3_), custom_call_target="tpu_custom_call" | custom-call | flops 4361420800 | bytes 2478080 | tf_op jit(solution)/shard_map/block_factor/pallas_call | solution.py:1003
  644.9 6.4 fusion.9
  653.6 6.4 all-to-all-start.3
  675.2 6.4 collective-permute-start.82
  687.1 3.7 collective-permute-done.70
  701.1 5.7 small_update.2
  723.1 9.2 %collective-permute-done.84.refs_6_ = f32[1,256,256]{2,1,0:T(8,128)} collective-permute-done((f32[1,256,256]{2,1,0:T(8,128)}, f32[1,256,256]{2,1,0:T(8,128)}, u32[]{:S(2)}, u32[]{:S(2)}) %collective-permute-start.84) | collective-permute-done | bytes 262176 | tf_op jit(solution)/shard_map/ppermute | solution.py:1075
  734.9 9.4 %collective-permute-done.87.refs_10_ = f32[2,128,128]{2,1,0:T(8,128)S(1)} collective-permute-done((f32[2,128,128]{2,1,0:T(8,128)S(1)}, f32[2,128,128]{2,1,0:T(8,128)S(1)}, u32[]{:S(2)}, u32[]{:S(2)}) %collective-permute-start.87) | collective-permute-done | bytes 131104 | tf_op jit(solution)/shard_map/ppermute | solution.py:1075
  744.3 10.8 %small_update.3 = (f32[512,256]{1,0:T(8,128)}, f32[512,256]{1,0:T(8,128)}) custom-call(f32[512,256]{1,0:T(8,128)S(1)} %get-tuple-element.511.matrix_ref.refs_0_, f32[512,256]{1,0:T(8,128)S(1)} %copy-done.57, f32[512,256]{1,0:T(8,128)S(1)} %get-tuple-element.513.matrix_ref.refs_2_, f32[512,256]{1,0:T(8,128)S(1)} %copy-done.58, ...), custom_call_target="tpu_custom_call" | custom-call | flops 2097152000 | bytes 3145728 | tf_op jit(solution)/shard_map/small_update/pallas_call | solution.py:1085
  (631 shorter events, 298.0 us)
Async XLA Ops:
  7.2 52.0 %all-gather.13.cloned.1.call-start = ((), (), s32[]{:S(2)}) async-start(), calls=%async_computation.16 | async-start | bytes 2621440 | tf_op jit(solution)/shard_map/all_gather | solution.py:1222
  10.4 111.8 %all-gather.15.cloned.1.call-start = ((), (), s32[]{:S(2)}) async-start(), calls=%async_computation.17 | async-start | bytes 1310720 | tf_op jit(solution)/shard_map/all_gather | solution.py:1222
  11.2 158.9 %all-gather.9.cloned.1.call-start = ((), (), s32[]{:S(2)}) async-start(), calls=%async_computation.9 | async-start | bytes 3604480 | tf_op jit(solution)/shard_map/all_gather | solution.py:1222
  11.3 50.6 %collective-permute-start = (bf16[384,2048]{1,0:T(8,128)(2,1)S(1)}, bf16[384,2048]{1,0:T(8,128)(2,1)}, u32[]{:S(2)}, u32[]{:S(2)}) collective-permute-start(bf16[384,2048]{1,0:T(8,128)(2,1)S(1)} %bitcast.258), channel_id=1, source_target_pairs={{0,4},{1,5},{2,6},{3,7},{4,0},{5,1},{6,2},{7,3},{8,12},{9,13},{10,... | collective-permute-start | bytes 4718600 | tf_op jit(solution)/shard_map/ppermute | solution.py:90
  14.3 47.5 %collective-permute-start.1 = (bf16[384,2048]{1,0:T(8,128)(2,1)S(1)}, bf16[384,2048]{1,0:T(8,128)(2,1)}, u32[]{:S(2)}, u32[]{:S(2)}) collective-permute-start(bf16[384,2048]{1,0:T(8,128)(2,1)S(1)} %bitcast.259), channel_id=1, source_target_pairs={{0,1},{1,0},{2,3},{3,2},{4,5},{5,4},{6,7},{7,6},{8,9},{9,8},{10,11... | collective-permute-start | bytes 4718600 | tf_op jit(solution)/shard_map/ppermute | solution.py:90
  14.3 47.6 %collective-permute-start.2 = (bf16[384,2048]{1,0:T(8,128)(2,1)S(1)}, bf16[384,2048]{1,0:T(8,128)(2,1)}, u32[]{:S(2)}, u32[]{:S(2)}) collective-permute-start(bf16[384,2048]{1,0:T(8,128)(2,1)S(1)} %bitcast.260), channel_id=1, source_target_pairs={{0,2},{1,3},{2,0},{3,1},{4,6},{5,7},{6,4},{7,5},{8,10},{9,11},{10,... | collective-permute-start | bytes 4718600 | tf_op jit(solution)/shard_map/ppermute | solution.py:90
  18.9 211.1 %all-gather.11.cloned.1.call-start = ((), (), s32[]{:S(2)}) async-start(), calls=%async_computation.10 | async-start | bytes 3604480 | tf_op jit(solution)/shard_map/all_gather | solution.py:1222
  91.8 30.4 %collective-permute-start.4 = (bf16[2048,256]{1,0:T(8,128)(2,1)S(1)}, bf16[2048,256]{1,0:T(8,128)(2,1)}, u32[]{:S(2)}, u32[]{:S(2)}) collective-permute-start(bf16[2048,256]{1,0:T(8,128)(2,1)S(1)} %collective-permute-done.3.refs_4_.refs_5_), channel_id=1, source_target_pairs={{0,1},{1,0},{2,3},{3,2},{4,5},{5,4},{6,7},{7,6},{8,9},{9,8},{10,11... | collective-permute-start | bytes 3145736 | tf_op jit(solution)/shard_map/ppermute | solution.py:90
  92.3 29.9 %collective-permute-start.9 = (bf16[2048,256]{1,0:T(8,128)(2,1)S(1)}, bf16[2048,256]{1,0:T(8,128)(2,1)}, u32[]{:S(2)}, u32[]{:S(2)}) collective-permute-start(bf16[2048,256]{1,0:T(8,128)(2,1)S(1)} %collective-permute-done.6.refs_2_.refs_3_), channel_id=1, source_target_pairs={{0,1},{1,0},{2,3},{3,2},{4,5},{5,4},{6,7},{7,6},{8,9},{9,8},{10,11... | collective-permute-start | bytes 3145736 | tf_op jit(solution)/shard_map/ppermute | solution.py:90
  124.9 32.9 %collective-permute-start.22 = (bf16[384,2048]{1,0:T(8,128)(2,1)}, bf16[384,2048]{1,0:T(8,128)(2,1)S(1)}, u32[]{:S(2)}, u32[]{:S(2)}) collective-permute-start(bf16[384,2048]{1,0:T(8,128)(2,1)} %collective-permute-done), channel_id=1, source_target_pairs={{0,1},{1,0},{2,3},{3,2},{4,5},{5,4},{6,7},{7,6},{8,9},{9,8},{10,11... | collective-permute-start | bytes 4718600 | tf_op jit(solution)/shard_map/ppermute | solution.py:90
  126.0 25.8 %collective-permute-start.12 = (bf16[2048,256]{1,0:T(8,128)(2,1)S(1)}, bf16[2048,256]{1,0:T(8,128)(2,1)}, u32[]{:S(2)}, u32[]{:S(2)}) collective-permute-start(bf16[2048,256]{1,0:T(8,128)(2,1)S(1)} %copy-done.45), channel_id=1, source_target_pairs={{0,2},{1,3},{2,0},{3,1},{4,6},{5,7},{6,4},{7,5},{8,10},{9,11},{10,... | collective-permute-start | bytes 3145736 | tf_op jit(solution)/shard_map/ppermute | solution.py:90
  129.6 40.5 %collective-permute-start.23 = (bf16[384,2048]{1,0:T(8,128)(2,1)}, bf16[384,2048]{1,0:T(8,128)(2,1)}, u32[]{:S(2)}, u32[]{:S(2)}) collective-permute-start(bf16[384,2048]{1,0:T(8,128)(2,1)} %collective-permute-done.2), channel_id=1, source_target_pairs={{0,1},{1,0},{2,3},{3,2},{4,5},{5,4},{6,7},{7,6},{8,9},{9,8},{10,11... | collective-permute-start | bytes 4718600 | tf_op jit(solution)/shard_map/ppermute | solution.py:90
  172.2 124.8 %all-gather.17.cloned.1.call-start = ((), (), s32[]{:S(2)}) async-start(), calls=%async_computation.18 | async-start | bytes 3604480 | tf_op jit(solution)/shard_map/all_gather | solution.py:1222
  195.8 37.1 %collective-permute-start.30 = (bf16[384,2048]{1,0:T(8,128)(2,1)}, bf16[384,2048]{1,0:T(8,128)(2,1)}, u32[]{:S(2)}, u32[]{:S(2)}) collective-permute-start(bf16[384,2048]{1,0:T(8,128)(2,1)} %multiply_convert_fusion.refs_0_), channel_id=1, source_target_pairs={{0,4},{1,5},{2,6},{3,7},{4,0},{5,1},{6,2},{7,3},{8,12},{9,13},{10,... | collective-permute-start | bytes 4718600 | tf_op jit(solution)/shard_map/ppermute | solution.py:90
  197.3 35.7 %collective-permute-start.31 = (bf16[384,2048]{1,0:T(8,128)(2,1)}, bf16[384,2048]{1,0:T(8,128)(2,1)}, u32[]{:S(2)}, u32[]{:S(2)}) collective-permute-start(bf16[384,2048]{1,0:T(8,128)(2,1)} %multiply_convert_fusion.refs_0_), channel_id=1, source_target_pairs={{0,1},{1,0},{2,3},{3,2},{4,5},{5,4},{6,7},{7,6},{8,9},{9,8},{10,11... | collective-permute-start | bytes 4718600 | tf_op jit(solution)/shard_map/ppermute | solution.py:90
  197.5 36.9 %collective-permute-start.32 = (bf16[384,2048]{1,0:T(8,128)(2,1)}, bf16[384,2048]{1,0:T(8,128)(2,1)}, u32[]{:S(2)}, u32[]{:S(2)}) collective-permute-start(bf16[384,2048]{1,0:T(8,128)(2,1)} %multiply_convert_fusion.refs_0_), channel_id=1, source_target_pairs={{0,2},{1,3},{2,0},{3,1},{4,6},{5,7},{6,4},{7,5},{8,10},{9,11},{10,... | collective-permute-start | bytes 4718600 | tf_op jit(solution)/shard_map/ppermute | solution.py:90
  235.9 152.5 %reduce-scatter.6.cloned.1.call-start = ((), (), s32[]{:S(2)}) async-start(), calls=%async_computation.11 | async-start | bytes 3604480 | tf_op jit(solution)/shard_map/reduce_scatter | solution.py:1338
  321.0 25.4 %collective-permute-start.39 = (bf16[4,192,2048]{2,1,0:T(8,128)(2,1)}, bf16[4,192,2048]{2,1,0:T(8,128)(2,1)}, u32[]{:S(2)}, u32[]{:S(2)}) collective-permute-start(bf16[4,192,2048]{2,1,0:T(8,128)(2,1)} %get-tuple-element.349), channel_id=1, source_target_pairs={{0,1},{1,0},{2,3},{3,2},{4,5},{5,4},{6,7},{7,6},{8,9},{9,8},{10,11... | collective-permute-start | bytes 9437192 | tf_op jit(solution)/shard_map/ppermute | solution.py:90
  321.3 139.1 %reduce-scatter.8.cloned.1.call-start = ((), (), s32[]{:S(2)}) async-start(), calls=%async_computation.12 | async-start | bytes 3604480 | tf_op jit(solution)/shard_map/reduce_scatter | solution.py:1338
  346.4 41.9 %collective-permute-start.40 = (bf16[4,192,2048]{2,1,0:T(8,128)(2,1)}, bf16[4,192,2048]{2,1,0:T(8,128)(2,1)}, u32[]{:S(2)}, u32[]{:S(2)}) collective-permute-start(bf16[4,192,2048]{2,1,0:T(8,128)(2,1)} %get-tuple-element.353), channel_id=1, source_target_pairs={{0,1},{1,0},{2,3},{3,2},{4,5},{5,4},{6,7},{7,6},{8,9},{9,8},{10,11... | collective-permute-start | bytes 9437192 | tf_op jit(solution)/shard_map/ppermute | solution.py:90
  351.4 36.6 %collective-permute-start.41 = (bf16[2,192,2048]{2,1,0:T(8,128)(2,1)S(1)}, bf16[2,192,2048]{2,1,0:T(8,128)(2,1)S(1)}, u32[]{:S(2)}, u32[]{:S(2)}) collective-permute-start(bf16[2,192,2048]{2,1,0:T(8,128)(2,1)S(1)} %get-tuple-element.360), channel_id=1, source_target_pairs={{0,4},{1,5},{2,6},{3,7},{4,0},{5,1},{6,2},{7,3},{8,12},{9,13},{10,... | collective-permute-start | bytes 4718600 | tf_op jit(solution)/shard_map/ppermute | solution.py:90
  352.2 36.1 %collective-permute-start.42 = (bf16[2,192,2048]{2,1,0:T(8,128)(2,1)S(1)}, bf16[2,192,2048]{2,1,0:T(8,128)(2,1)}, u32[]{:S(2)}, u32[]{:S(2)}) collective-permute-start(bf16[2,192,2048]{2,1,0:T(8,128)(2,1)S(1)} %get-tuple-element.361), channel_id=1, source_target_pairs={{0,2},{1,3},{2,0},{3,1},{4,6},{5,7},{6,4},{7,5},{8,10},{9,11},{10,... | collective-permute-start | bytes 4718600 | tf_op jit(solution)/shard_map/ppermute | solution.py:90
  388.4 135.7 %reduce-scatter.10.cloned.1.call-start = ((), (), s32[]{:S(2)}) async-start(), calls=%async_computation.13 | async-start | bytes 3604480 | tf_op jit(solution)/shard_map/reduce_scatter | solution.py:1338
  433.4 27.0 %collective-permute-start.47 = (bf16[4,1024,256]{2,1,0:T(8,128)(2,1)}, bf16[4,1024,256]{2,1,0:T(8,128)(2,1)}, u32[]{:S(2)}, u32[]{:S(2)}) collective-permute-start(bf16[4,1024,256]{2,1,0:T(8,128)(2,1)} %get-tuple-element.396), channel_id=1, source_target_pairs={{0,1},{1,0},{2,3},{3,2},{4,5},{5,4},{6,7},{7,6},{8,9},{9,8},{10,11... | collective-permute-start | bytes 6291464 | tf_op jit(solution)/shard_map/ppermute | solution.py:90
  433.4 27.0 %collective-permute-start.48 = (bf16[4,1024,256]{2,1,0:T(8,128)(2,1)}, bf16[4,1024,256]{2,1,0:T(8,128)(2,1)}, u32[]{:S(2)}, u32[]{:S(2)}) collective-permute-start(bf16[4,1024,256]{2,1,0:T(8,128)(2,1)} %get-tuple-element.397), channel_id=1, source_target_pairs={{0,1},{1,0},{2,3},{3,2},{4,5},{5,4},{6,7},{7,6},{8,9},{9,8},{10,11... | collective-permute-start | bytes 6291464 | tf_op jit(solution)/shard_map/ppermute | solution.py:90
  449.1 46.8 %collective-permute-start.49 = (bf16[2,192,2048]{2,1,0:T(8,128)(2,1)}, bf16[2,192,2048]{2,1,0:T(8,128)(2,1)}, u32[]{:S(2)}, u32[]{:S(2)}) collective-permute-start(bf16[2,192,2048]{2,1,0:T(8,128)(2,1)} %get-tuple-element.413), channel_id=1, source_target_pairs={{0,4},{1,5},{2,6},{3,7},{4,0},{5,1},{6,2},{7,3},{8,12},{9,13},{10,... | collective-permute-start | bytes 4718600 | tf_op jit(solution)/shard_map/ppermute | solution.py:90
  449.6 46.3 %collective-permute-start.50 = (bf16[2,192,2048]{2,1,0:T(8,128)(2,1)}, bf16[2,192,2048]{2,1,0:T(8,128)(2,1)}, u32[]{:S(2)}, u32[]{:S(2)}) collective-permute-start(bf16[2,192,2048]{2,1,0:T(8,128)(2,1)} %get-tuple-element.414), channel_id=1, source_target_pairs={{0,2},{1,3},{2,0},{3,1},{4,6},{5,7},{6,4},{7,5},{8,10},{9,11},{10,... | collective-permute-start | bytes 4718600 | tf_op jit(solution)/shard_map/ppermute | solution.py:90
  471.3 52.8 %all-to-all-start = ((bf16[4,368,352]{1,2,0:T(8,128)(2,1)}), bf16[4,368,352]{1,2,0:T(8,128)(2,1)}, u32[]{:S(2)}, u32[]{:S(2)}) async-start(bf16[4,368,352]{1,2,0:T(8,128)(2,1)} %copy.92), calls=%async_computation.2 | async-start | bytes 2162688 | tf_op jit(solution)/shard_map/all_to_all | solution.py:1381
  500.1 26.4 %collective-permute-start.53 = (bf16[2,1024,256]{2,1,0:T(8,128)(2,1)}, bf16[2,1024,256]{2,1,0:T(8,128)(2,1)}, u32[]{:S(2)}, u32[]{:S(2)}) collective-permute-start(bf16[2,1024,256]{2,1,0:T(8,128)(2,1)} %get-tuple-element.432), channel_id=1, source_target_pairs={{0,4},{1,5},{2,6},{3,7},{4,0},{5,1},{6,2},{7,3},{8,12},{9,13},{10,... | collective-permute-start | bytes 3145736 | tf_op jit(solution)/shard_map/ppermute | solution.py:90
  500.7 26.4 %collective-permute-start.54 = (bf16[2,1024,256]{2,1,0:T(8,128)(2,1)}, bf16[2,1024,256]{2,1,0:T(8,128)(2,1)}, u32[]{:S(2)}, u32[]{:S(2)}) collective-permute-start(bf16[2,1024,256]{2,1,0:T(8,128)(2,1)} %get-tuple-element.433), channel_id=1, source_target_pairs={{0,2},{1,3},{2,0},{3,1},{4,6},{5,7},{6,4},{7,5},{8,10},{9,11},{10,... | collective-permute-start | bytes 3145736 | tf_op jit(solution)/shard_map/ppermute | solution.py:90
  502.1 39.7 %collective-permute-start.51 = (bf16[192,2048]{1,0:T(8,128)(2,1)}, bf16[192,2048]{1,0:T(8,128)(2,1)}, u32[]{:S(2)}, u32[]{:S(2)}) collective-permute-start(bf16[192,2048]{1,0:T(8,128)(2,1)} %get-tuple-element.419), channel_id=1, source_target_pairs={{0,4},{1,5},{2,6},{3,7},{4,0},{5,1},{6,2},{7,3},{8,12},{9,13},{10,... | collective-permute-start | bytes 2359304 | tf_op jit(solution)/shard_map/ppermute | solution.py:90
  502.7 39.5 %collective-permute-start.52 = (bf16[192,2048]{1,0:T(8,128)(2,1)}, bf16[192,2048]{1,0:T(8,128)(2,1)}, u32[]{:S(2)}, u32[]{:S(2)}) collective-permute-start(bf16[192,2048]{1,0:T(8,128)(2,1)} %get-tuple-element.420), channel_id=1, source_target_pairs={{0,2},{1,3},{2,0},{3,1},{4,6},{5,7},{6,4},{7,5},{8,10},{9,11},{10,... | collective-permute-start | bytes 2359304 | tf_op jit(solution)/shard_map/ppermute | solution.py:90
  536.0 33.6 %collective-permute-start.56 = (bf16[4,1024,256]{2,1,0:T(8,128)(2,1)}, bf16[4,1024,256]{2,1,0:T(8,128)(2,1)}, u32[]{:S(2)}, u32[]{:S(2)}) collective-permute-start(bf16[4,1024,256]{2,1,0:T(8,128)(2,1)} %get-tuple-element.444), channel_id=1, source_target_pairs={{0,1},{1,0},{2,3},{3,2},{4,5},{5,4},{6,7},{7,6},{8,9},{9,8},{10,11... | collective-permute-start | bytes 6291464 | tf_op jit(solution)/shard_map/ppermute | solution.py:90
  540.3 29.3 %collective-permute-start.55 = (bf16[4,1024,256]{2,1,0:T(8,128)(2,1)}, bf16[4,1024,256]{2,1,0:T(8,128)(2,1)}, u32[]{:S(2)}, u32[]{:S(2)}) collective-permute-start(bf16[4,1024,256]{2,1,0:T(8,128)(2,1)} %get-tuple-element.443), channel_id=1, source_target_pairs={{0,1},{1,0},{2,3},{3,2},{4,5},{5,4},{6,7},{7,6},{8,9},{9,8},{10,11... | collective-permute-start | bytes 6291464 | tf_op jit(solution)/shard_map/ppermute | solution.py:90
  557.5 50.8 %all-to-all-start.1 = ((bf16[8,2,192,256]{3,2,1,0:T(8,128)(2,1)}), bf16[8,2,192,256]{3,2,1,0:T(8,128)(2,1)}, u32[]{:S(2)}, u32[]{:S(2)}) async-start(bf16[8,2,192,256]{3,2,1,0:T(8,128)(2,1)} %gather_fusion.1), calls=%async_computation.4 | async-start | bytes 3145728 | tf_op jit(solution)/shard_map/all_to_all | solution.py:1405
  561.8 121.2 %reduce-scatter.14.cloned.1.call-start = ((), (), s32[]{:S(2)}) async-start(), calls=%async_computation.15 | async-start | bytes 1310720 | tf_op jit(solution)/shard_map/reduce_scatter | solution.py:1338
  573.2 35.1 %collective-permute-start.59 = (bf16[2,1024,256]{2,1,0:T(8,128)(2,1)}, bf16[2,1024,256]{2,1,0:T(8,128)(2,1)}, u32[]{:S(2)}, u32[]{:S(2)}) collective-permute-start(bf16[2,1024,256]{2,1,0:T(8,128)(2,1)} %get-tuple-element.458), channel_id=1, source_target_pairs={{0,4},{1,5},{2,6},{3,7},{4,0},{5,1},{6,2},{7,3},{8,12},{9,13},{10,... | collective-permute-start | bytes 3145736 | tf_op jit(solution)/shard_map/ppermute | solution.py:90
  575.1 33.2 %collective-permute-start.60 = (bf16[2,1024,256]{2,1,0:T(8,128)(2,1)}, bf16[2,1024,256]{2,1,0:T(8,128)(2,1)}, u32[]{:S(2)}, u32[]{:S(2)}) collective-permute-start(bf16[2,1024,256]{2,1,0:T(8,128)(2,1)} %get-tuple-element.459), channel_id=1, source_target_pairs={{0,2},{1,3},{2,0},{3,1},{4,6},{5,7},{6,4},{7,5},{8,10},{9,11},{10,... | collective-permute-start | bytes 3145736 | tf_op jit(solution)/shard_map/ppermute | solution.py:90
  577.7 37.9 %collective-permute-start.63 = (bf16[368,352]{1,0:T(8,128)(2,1)}, bf16[368,352]{1,0:T(8,128)(2,1)}, u32[]{:S(2)}, u32[]{:S(2)}) collective-permute-start(bf16[368,352]{1,0:T(8,128)(2,1)} %get-tuple-element.562), channel_id=1, source_target_pairs={{0,8},{8,16},{1,9},{9,17},{2,10},{10,18},{3,11},{11,19},{4,12},{12... | collective-permute-start | bytes 777224 | tf_op jit(solution)/shard_map/ppermute | solution.py:1117
  582.0 33.6 %collective-permute-start.64 = (bf16[368,352]{1,0:T(8,128)(2,1)}, bf16[368,352]{1,0:T(8,128)(2,1)}, u32[]{:S(2)}, u32[]{:S(2)}) collective-permute-start(bf16[368,352]{1,0:T(8,128)(2,1)} %get-tuple-element.560), channel_id=1, source_target_pairs={{24,8},{0,16},{25,9},{1,17},{26,10},{2,18},{27,11},{3,19},{28,12},... | collective-permute-start | bytes 777224 | tf_op jit(solution)/shard_map/ppermute | solution.py:1117
  584.2 36.2 %collective-permute-start.65 = (bf16[368,352]{1,0:T(8,128)(2,1)}, bf16[368,352]{1,0:T(8,128)(2,1)}, u32[]{:S(2)}, u32[]{:S(2)}) collective-permute-start(bf16[368,352]{1,0:T(8,128)(2,1)} %get-tuple-element.559), channel_id=1, source_target_pairs={{16,8},{24,16},{17,9},{25,17},{18,10},{26,18},{19,11},{27,19},{20,... | collective-permute-start | bytes 777224 | tf_op jit(solution)/shard_map/ppermute | solution.py:1117
  615.6 46.1 %collective-permute-start.66 = (bf16[352,352]{1,0:T(8,128)(2,1)S(1)}, bf16[352,352]{1,0:T(8,128)(2,1)S(1)}, u32[]{:S(2)}, u32[]{:S(2)}) collective-permute-start(bf16[352,352]{1,0:T(8,128)(2,1)S(1)} %copy-done.44), channel_id=1, source_target_pairs={{0,8},{8,16},{16,24},{24,0},{1,9},{9,17},{17,25},{25,1},{2,10},{10... | collective-permute-start | bytes 743432 | tf_op jit(solution)/shard_map/ppermute | solution.py:1125
  615.7 46.0 %collective-permute-start.67 = (bf16[352,352]{1,0:T(8,128)(2,1)S(1)}, bf16[352,352]{1,0:T(8,128)(2,1)}, u32[]{:S(2)}, u32[]{:S(2)}) collective-permute-start(bf16[352,352]{1,0:T(8,128)(2,1)S(1)} %copy-done.44), channel_id=1, source_target_pairs={{0,16},{8,24},{16,0},{24,8},{1,17},{9,25},{17,1},{25,9},{2,18},{10... | collective-permute-start | bytes 743432 | tf_op jit(solution)/shard_map/ppermute | solution.py:1125
  620.4 41.3 %collective-permute-start.68 = (bf16[352,352]{1,0:T(8,128)(2,1)S(1)}, bf16[352,352]{1,0:T(8,128)(2,1)}, u32[]{:S(2)}, u32[]{:S(2)}) collective-permute-start(bf16[352,352]{1,0:T(8,128)(2,1)S(1)} %copy-done.44), channel_id=1, source_target_pairs={{0,24},{8,0},{16,8},{24,16},{1,25},{9,1},{17,9},{25,17},{2,26},{10... | collective-permute-start | bytes 743432 | tf_op jit(solution)/shard_map/ppermute | solution.py:1125
  621.5 29.9 %all-to-all-start.2 = ((bf16[8,4,64,256]{3,2,1,0:T(8,128)(2,1)}), bf16[8,4,64,256]{3,2,1,0:T(8,128)(2,1)}, u32[]{:S(2)}, u32[]{:S(2)}) async-start(bf16[8,4,64,256]{3,2,1,0:T(8,128)(2,1)} %bitcast.212), calls=%async_computation.5 | async-start | bytes 2097152 | tf_op jit(solution)/shard_map/all_to_all | solution.py:1432
  625.8 88.7 %reduce-scatter.12.cloned.1.call-start = ((), (), s32[]{:S(2)}) async-start(), calls=%async_computation.14 | async-start | bytes 1310720 | tf_op jit(solution)/shard_map/reduce_scatter | solution.py:1338
  653.6 28.0 %all-to-all-start.3 = ((bf16[4,64,256]{2,1,0:T(8,128)(2,1)}), bf16[4,64,256]{2,1,0:T(8,128)(2,1)}, u32[]{:S(2)}, u32[]{:S(2)}) async-start(bf16[4,64,256]{2,1,0:T(8,128)(2,1)} %reduce_sum.163), calls=%async_computation.7 | async-start | bytes 262144 | tf_op jit(solution)/shard_map/all_to_all | solution.py:1446
  716.9 27.4 %collective-permute-start.87 = (f32[2,128,128]{2,1,0:T(8,128)S(1)}, f32[2,128,128]{2,1,0:T(8,128)S(1)}, u32[]{:S(2)}, u32[]{:S(2)}) collective-permute-start(f32[2,128,128]{2,1,0:T(8,128)S(1)} %pad_maximum_fusion.12.refs_8_), channel_id=1, source_target_pairs={{0,16},{8,24},{16,0},{24,8},{1,17},{9,25},{17,1},{25,9},{2,18},{10... | collective-permute-start | bytes 393224 | tf_op jit(solution)/shard_map/ppermute | solution.py:1075
  (198 other events, 2646.3 us)
Sparse Core Ops, SparseCore 0:
  10.5 48.6 all-gather.12
  61.3 26.6 all-gather.14
  90.1 58.6 all-gather.8
  172.3 57.6 all-gather.10
  236.0 56.7 all-gather.16
  321.5 54.7 reduce-scatter.5
  388.5 54.2 reduce-scatter.7
  445.7 73.1 reduce-scatter.9
  589.0 27.4 reduce-scatter.13
  643.3 32.6 reduce-scatter.11

commit v4 on v3

--- a/solution.py
+++ b/solution.py
@@ -251,15 +251,15 @@
         return jnp.concatenate([top, low], axis=0)
 
 
-def add_all(value, axis):
-    size = lax.axis_size(axis)
-    if size & (size - 1):
-        return lax.psum(value, axis)
-    flip = 1
-    while flip < size:
-        value = value + lax.ppermute(value, axis, [(i, i ^ flip) for i in range(size)])
-        flip = 2 * flip
-    return value
+def as_rows(value, width):
+    value = value.reshape(-1, width)
+    high = value.astype(LOW)
+    return jnp.concatenate([high, (value - wide(high)).astype(LOW)], axis=0)
+
+
+def from_rows(rows):
+    half = rows.shape[0] // 2
+    return wide(rows[:half]) + wide(rows[half:])
 
 
 def masked_bias(qid_ref, kid_ref):
@@ -459,7 +459,7 @@
     return copies
 
 
-def project_kernel(places, head_dim, turned, *refs):
+def project_kernel(places, head_dim, turned, turns, *refs):
     count = len(places)
     piece_refs, refs = refs[:count], refs[count:]
     if turned:
@@ -482,6 +482,11 @@
                 cosine = cos_ref[...]
                 sine = sin_ref[...]
                 place = block * width + head * head_dim
+                if turns is not None and place >= turns * head_dim:
+                    out_ref[:, place : place + head_dim] = product[
+                        :, head * head_dim : (head + 1) * head_dim
+                    ].astype(LOW)
+                    continue
                 out_ref[:, place : place + head_dim] = jnp.concatenate(
                     [first * cosine - second * sine, second * cosine + first * sine], axis=1
                 ).astype(LOW)
@@ -489,7 +494,7 @@
             out_ref[:, block * width : (block + 1) * width] = product.astype(LOW)
 
 
-def project(rows, blocks, head_dim, tables=None):
+def project(rows, blocks, head_dim, tables=None, turns=None):
     places, arrays = flat_pieces(blocks)
     size = len(blocks)
     depth = max(first + count for _, first, count in places)
@@ -497,7 +502,7 @@
     vmem = pl.BlockSpec(memory_space=pltpu.VMEM)
     turned = tables is not None
     return pl.pallas_call(
-        functools.partial(project_kernel, places, head_dim, turned),
+        functools.partial(project_kernel, places, head_dim, turned, turns),
         in_specs=[pl.BlockSpec(memory_space=pltpu.HBM)] * len(arrays) + [vmem] * (3 if turned else 1),
         out_specs=vmem,
         out_shape=jax.ShapeDtypeStruct((rows.shape[0], size * width), LOW),
@@ -908,27 +913,43 @@
     return row, col, jnp.where(row == col, 1.0, 0.0)
 
 
-def packed_kernel(width, slots, *refs):
+def pack(gram):
+    row, col, eye = eye_of(gram.shape[0])
+    high = wide(gram.astype(LOW))
+    low = gram - high
+    packed = jnp.where(col >= row, high, low).astype(LOW)
+    return packed, jnp.sum(low * eye, axis=0, keepdims=True)
+
+
+def unpack(total):
+    width = total.shape[1]
+    _, _, eye = eye_of(width)
+    packed = total[:width]
+    return packed + packed.T + eye * (total[width : width + 1] - packed)
+
+
+def packed_kernel(width, slots, by_rows, *refs):
     matrix_refs, out_ref = refs[:-1], refs[-1]
-    row, col, eye = eye_of(width)
     for slot in range(out_ref.shape[0]):
         if slot not in [used for _, _, used in slots]:
             out_ref[slot] = jnp.zeros_like(out_ref[slot])
     for number, block, slot in slots:
-        part = matrix_refs[number][block * width : (block + 1) * width, :]
-        gram = fine_dot(part, part, 1, 1)
-        high = wide(gram.astype(LOW))
-        low = gram - high
-        out_ref[slot, :width, :] = jnp.where(col >= row, high, low).astype(LOW)
-        last = jnp.sum(low * eye, axis=0, keepdims=True)
+        place = slice(block * width, (block + 1) * width)
+        if by_rows:
+            part = matrix_refs[number][place, :]
+            packed, last = pack(fine_dot(part, part, 1, 1))
+        else:
+            part = matrix_refs[number][:, place]
+            packed, last = pack(fine_dot(part, part, 0, 0))
+        out_ref[slot, :width, :] = packed
         out_ref[slot, width:, :] = jnp.broadcast_to(
             last, (out_ref.shape[1] - width, width)
         ).astype(LOW)
 
 
-def owners_parts(matrices, width, slots, size):
-    packed = pl.pallas_call(
-        functools.partial(packed_kernel, width, slots),
+def packed_grams(matrices, width, slots, size, by_rows=True):
+    return pl.pallas_call(
+        functools.partial(packed_kernel, width, slots, by_rows),
         out_shape=jax.ShapeDtypeStruct((size, width + 16, width), LOW),
         compiler_params=pltpu.CompilerParams(vmem_limit_bytes=VMEM_LIMIT),
         cost_estimate=pl.CostEstimate(
@@ -938,29 +959,6 @@
         ),
         name="packed_grams",
     )(*matrices)
-    return packed
-
-
-def gram_kernel(width, by_rows, matrix_ref, *gram_refs):
-    for block, gram_ref in enumerate(gram_refs):
-        place = slice(block * width, (block + 1) * width)
-        if by_rows:
-            gram_ref[...] = fine_dot(matrix_ref[place, :], matrix_ref[place, :], 1, 1)
-        else:
-            gram_ref[...] = fine_dot(matrix_ref[:, place], matrix_ref[:, place], 0, 0)
-
-
-def block_grams(matrix, width, by_rows):
-    count = matrix.shape[0 if by_rows else 1] // width
-    return pl.pallas_call(
-        functools.partial(gram_kernel, width, by_rows),
-        out_shape=[jax.ShapeDtypeStruct((width, width), jnp.float32)] * count,
-        compiler_params=pltpu.CompilerParams(vmem_limit_bytes=VMEM_LIMIT),
-        cost_estimate=pl.CostEstimate(
-            flops=12 * matrix.size * width, bytes_accessed=4 * matrix.size, transcendentals=0
-        ),
-        name="block_grams",
-    )(matrix)
 
 
 def newton_factor(gram):
@@ -987,10 +985,7 @@
         for part_ref in part_refs:
             part = wide(part_ref[...])
             total = total + (part if part.ndim == 2 else jnp.sum(part, axis=0))
-        _, _, eye = eye_of(width)
-        packed = total[:width]
-        gram = packed + packed.T + eye * (total[width : width + 1] - packed)
-        factor_ref[...] = newton_factor(gram).astype(LOW)
+        factor_ref[...] = newton_factor(unpack(total)).astype(LOW)
 
     @pl.when(own_ref[0] == 0)
     def _():
@@ -1053,10 +1048,10 @@
         part_refs = refs[firsts[number] : firsts[number] + counts[number]]
         new_ref = refs[2 * len(sizes) + sum(counts) + number]
         for block in range(part_refs[0].shape[0]):
-            gram = part_refs[0][block]
-            for part_ref in part_refs[1:]:
-                gram = gram + part_ref[block]
-            factor = newton_factor(gram)
+            total = 0.0
+            for part_ref in part_refs:
+                total = total + wide(part_ref[block])
+            factor = newton_factor(unpack(total))
             place = slice(block * width, (block + 1) * width)
             if by_rows:
                 new_ref[place, :] = weight_ref[place, :] - MUON_RATE * fine_dot(
@@ -1069,7 +1064,9 @@
 
 
 def gather_grams(moment, width, by_rows):
-    grams = jnp.stack(block_grams(moment, width, by_rows))
+    count = moment.shape[0 if by_rows else 1] // width
+    slots = tuple((0, block, block) for block in range(count))
+    grams = packed_grams((moment,), width, slots, count, by_rows)
     size = lax.axis_size("dp")
     return [grams] + [
         lax.ppermute(grams, "dp", [(i, (i + shift) % size) for i in range(size)])
@@ -1223,21 +1220,10 @@
 
     gate_up_t = jnp.transpose(w_gate_up, (1, 2, 0))
     down_t = jnp.transpose(w_down)
-    low_keyval = w_keyval.astype(LOW).reshape(-1, query_cols)
-    query_block = rows_of(jnp.concatenate([w_query.astype(LOW), low_keyval], axis=0))
-    out_block = rows_of(w_out.astype(LOW))
-    full_gate = rows_of(gate_up_t[0].astype(LOW))
-    full_up = rows_of(gate_up_t[1].astype(LOW))
-    full_down = rows_of(down_t.astype(LOW))
-    order = jnp.array(gather_order(size), jnp.int32)
-    place = jnp.zeros((size,), jnp.int32).at[order].set(jnp.arange(size, dtype=jnp.int32))
-    place = place[me ^ jnp.arange(size)]
-
     cot_rows = cotangent.reshape(tokens, model_width)
     cot = Gather(cot_rows, size)
     cot.first()
-    full_keyval = query_block[:, w_query.shape[0] :].reshape(model_width, 2 * head_dim)
-    query_block = query_block[:, : w_query.shape[0]].reshape(model_width, query_cols)
+    query_block = rows_of(w_query.astype(LOW))
     own_positions = me * own_rows + jnp.arange(own_rows, dtype=jnp.int32)
     key_positions = jnp.concatenate(
         [(me ^ s) * own_rows + jnp.arange(own_rows, dtype=jnp.int32) for s in gather_order(size)]
@@ -1260,14 +1246,27 @@
     x_rows = wide(inputs).reshape(tokens, model_width)
     x_scale = inverse_scale(x_rows)
     normed = (x_rows * x_scale * gains[0]).astype(LOW)
-    own_keyval = plain_dot(normed, full_keyval)
-    own_keyval = jnp.concatenate(
-        [rotate(own_keyval[:, :head_dim], flat_cos, flat_sin), own_keyval[:, head_dim:]], axis=1
-    ).astype(LOW)
-    cot.parts, query_block = tie(cot.parts, query_block)
-    query_gather = Gather(query_block, size)
+    cot.parts, query_block, low_keyval, normed, flat_cos, flat_sin, qid, kid = tie(
+        cot.parts, query_block, w_keyval.astype(LOW), normed, flat_cos, flat_sin, qid, kid
+    )
+    full_keyval = rows_of(low_keyval)
+    query_gather = Gather(query_block.reshape(model_width, query_cols), size)
     query_gather.first()
-    own_keyval = query_gather.cut(own_keyval)
+    full_keyval, query_gather.parts, low_out = tie(
+        full_keyval, query_gather.parts, w_out.astype(LOW)
+    )
+    query_gather.second()
+    out_block = rows_of(low_out)
+    full_gate = rows_of(gate_up_t[0].astype(LOW))
+    full_up = rows_of(gate_up_t[1].astype(LOW))
+    full_down = rows_of(down_t.astype(LOW))
+    order = jnp.array(gather_order(size), jnp.int32)
+    place = jnp.zeros((size,), jnp.int32).at[order].set(jnp.arange(size, dtype=jnp.int32))
+    place = place[me ^ jnp.arange(size)]
+
+    full_keyval = full_keyval.reshape(model_width, 2 * head_dim)
+    own_keyval = project(normed, [[(0, full_keyval)]], head_dim, (flat_cos, flat_sin), 1)
+    query_gather.parts, own_keyval = tie(query_gather.parts, own_keyval)
     flips = flips_of(size)
     keyval = own_keyval.reshape(1, batches, own_rows, 2 * head_dim)
     for flip in flips:
@@ -1276,7 +1275,6 @@
             keyval, cot.parts = tie(keyval, cot.parts)
             cot.relay()
     keyval = jnp.swapaxes(keyval, 0, 1).reshape(batches, seq_len, 2 * head_dim)
-    query_gather.second()
     query_gather.relay()
     query_gather.parts, out_block = tie(query_gather.parts, out_block)
     out_gather = Gather(out_block.reshape(model_width, query_cols), size)
@@ -1377,7 +1375,7 @@
     if fast:
         moment_down, moment_gate, d_context = tie(moment_down, moment_gate, d_context)
         slots = ((0, 0, 1), (0, 1, 2), (1, 0, 0), (1, 1, 3))
-        first_parts = owners_parts((moment_down, moment_gate), FF_BLOCK, slots, groups)
+        first_parts = packed_grams((moment_down, moment_gate), FF_BLOCK, slots, groups)
         first_parts = lax.all_to_all(first_parts, "dp", 0, 0, tiled=True)
     backs = ()
     for batch in range(batches):
@@ -1408,7 +1406,7 @@
     own = is_owner(first_owners)
     query_parts, own, moment_up = tie(query_parts, own, moment_up)
     if fast:
-        up_grams = owners_parts((moment_up,), FF_BLOCK, ((0, 0, 0), (0, 1, 1)), 2)
+        up_grams = packed_grams((moment_up,), FF_BLOCK, ((0, 0, 0), (0, 1, 1)), 2)
         query_sum.parts, up_grams, own = tie(query_sum.parts, up_grams, own)
         last_parts = exchange((up_grams[0], up_grams[1]), last_owners)
     out_sum.parts, own = tie(out_sum.parts, own)
@@ -1423,6 +1421,8 @@
         d_normed = project_back(d_queries, query_pieces, model_width)
     d_keyval, d_normed, query_sum.parts = tie(d_keyval, d_normed, query_sum.parts)
     d_normed = query_sum.third(d_normed)
+    if fast:
+        first_choices = share_out(first_factor, first_owners)
     d_keyval = jnp.sum(wide(d_keyval), axis=0).reshape(tokens, 2 * head_dim)
     d_keyval = jnp.concatenate(
         [rotate(d_keyval[:, :head_dim], flat_cos, -flat_sin), d_keyval[:, head_dim:]], axis=1
@@ -1433,8 +1433,9 @@
     if fast:
         last_parts, d_keyval = tie(last_parts, d_keyval)
         last_factor = owned_factor(last_parts, last_owners)
-        query_sum.parts, last_factor, d_normed = tie(query_sum.parts, last_factor, d_normed)
-        first_choices = share_out(first_factor, first_owners)
+        query_sum.parts, last_factor, d_normed, first_choices[1] = tie(
+            query_sum.parts, last_factor, d_normed, first_choices[1]
+        )
         last_choices = share_out(last_factor, last_owners)
     grad_query = own_rows_of(query_sum.total(), query_cols)
     d_normed = d_normed + rows_dot(d_keyval, full_keyval)
@@ -1443,7 +1444,10 @@
     gain_input = jnp.sum(d_normed * x_rows * x_scale, axis=0)
     share_sums = jnp.sum(wide(sum_keyval), axis=0).astype(LOW)
     share_sums, input_grad = tie(share_sums, input_grad)
-    share_parts = lax.all_to_all(share_sums, "dp", 0, 0, tiled=True)
+    gain_rows = as_rows(jnp.stack([gain_input, gain_mid], axis=0), 2 * head_dim)
+    gain_rows = jnp.broadcast_to(gain_rows[None], (groups,) + gain_rows.shape)
+    share_parts = jnp.concatenate([share_sums, gain_rows], axis=1)
+    share_parts = lax.all_to_all(share_parts, "dp", 0, 0, tiled=True)
     grad_out = wide(grad_out)
     moment_out = DECAY * m_out + grad_out
     out_grams = gather_grams(moment_out, head_dim, False)
@@ -1455,14 +1459,18 @@
         new_gate = small_update(moment_gate, gate_up_t[0], FF_BLOCK, True)
     share_parts, new_down = tie(share_parts, new_down)
     grad_keyval = jnp.sum(wide(share_parts), axis=0)
-    grad_keyval = gather_small(grad_keyval.astype(LOW), size)
+    gain_rows = as_rows(from_rows(grad_keyval[share:]), 2 * head_dim)
+    grad_keyval = jnp.concatenate([grad_keyval[:share].astype(LOW), gain_rows], axis=0)
+    grad_keyval = lax.all_gather(grad_keyval, "mp", axis=0, tiled=False)
     if fast:
         new_up = owned_update(moment_up, gate_up_t[1], last_choices, last_owners)
     else:
         new_up = small_update(moment_up, gate_up_t[1], FF_BLOCK, True)
     new_out = small_update(moment_out, w_out, head_dim, False, out_grams)
     grad_keyval, new_out, new_up = tie(grad_keyval, new_out, new_up)
-    grad_keyval = wide(grad_keyval[place]).reshape(w_keyval.shape)
+    grad_keyval = wide(grad_keyval)
+    grad_gains = from_rows(jnp.sum(grad_keyval[:, share:], axis=0)).reshape(gains.shape)
+    grad_keyval = grad_keyval[:, :share].reshape(w_keyval.shape)
     moment_keyval = DECAY * m_keyval + grad_keyval
     keyval_grams = gather_grams(moment_keyval, 2 * head_dim, False)
     grad_query = wide(grad_query)
@@ -1474,7 +1482,6 @@
             (moment_query, w_query, head_dim, False, query_grams),
         ]
     )
-    grad_gains = add_all(add_all(jnp.stack([gain_input, gain_mid], axis=0), "mp"), "dp")
     grad_gate_up = wide(jnp.stack([grad_gate, grad_up]))
     moment_gate_up = DECAY * old_gate_up + grad_gate_up
     new_gate_up = jnp.stack([new_gate, new_up])

time: 770 us -> 749 us (0.973)
  other arithmetic: 109 us -> 95.3 us
  blocking collectives: 0 us -> 9.58 us
    ppermute x66 -> x63, waiting for transfers between devices: 64.8 us -> 105 us  [swap(): return lax.ppermute(value, 'mp', [(i, i ^ flip) for i in range(size)])]
    all_gather x5 -> x6, waiting for transfers between devices: 50.7 us -> 21.2 us  [rows_of(): return lax.all_gather(value, 'dp', axis=0, tiled=False)]
    ppermute x9, waiting for transfers between devices: 24.1 us -> 10.1 us  [gather_grams(): lax.ppermute(grams, 'dp', [(i, (i + shift) % size) for i in range(size)])]
    all_to_all x1, starting transfers between devices: 6.44 us -> 19.3 us  [shards(): share_parts = lax.all_to_all(share_parts, 'dp', 0, 0, tiled=True)]
    ppermute x5 -> x0, starting transfers between devices: 12.8 us -> none  [add_all(): lax.ppermute(value, axis, [(i, i ^ flip) for i in range(size)])]
    unnamed x299 -> x291, local copies, waits for them, and re-layouts: 54 us -> 65.5 us
    all_gather x0 -> x1, blocking collectives: none -> 9.58 us  [shards(): grad_keyval = lax.all_gather(grad_keyval, 'mp', axis=0, tiled=False)]
    pallas_call x1, Pallas kernels: 10.4 us -> 2.21 us  [block_factor(): pl.pallas_call(factor_kernel, in_specs=[pl.BlockSpec(memory_space=pltpu.S...]
  transfers between devices with their start and end apart: 103 -> 96, of which waited for: 31 -> 28; matrix products, arithmetic and copies ran while one was open for 23% -> 19% of each run, Pallas kernels for 32% -> 32%
where the time goes in v4:
time: 749 us; the launch traced here: 744 us
  Pallas kernels  272 us (36%)
  waiting for transfers between devices  139 us (19%)
  starting transfers between devices  112 us (15%)
  local copies, waits for them, and re-layouts  97 us (13%)
  other arithmetic  95.3 us (13%)
  between operations  16.1 us (2%)
  blocking collectives  9.58 us (1%)
    ppermute x63, waiting for transfers between devices, swap(): return lax.ppermute(value, 'mp', [(i, i ^ flip) for i in range(size)])  105 us
    unnamed x291, local copies, waits for them, and re-layouts  65.5 us
    pallas_call x2, Pallas kernels, hidden_back(): pl.pallas_call(functools.partial(hidden_back_kernel, turn), grid=(steps,)...  49.2 us
    ppermute x63, starting transfers between devices, swap(): return lax.ppermute(value, 'mp', [(i, i ^ flip) for i in range(size)])  47.1 us
    pallas_call x2, Pallas kernels, hidden_units(): pl.pallas_call(functools.partial(hidden_kernel, places, steps, turn), gri...  34.3 us
    pallas_call x2, Pallas kernels, units_sum(): pl.pallas_call(functools.partial(units_sum_kernel, len(rows), turn), grid...  33.9 us
    pallas_call x2, Pallas kernels, attention_backward(): pl.pallas_call(functools.partial(backward_kernel, heads, head_dim), grid=...  28.5 us
    all_gather x6, waiting for transfers between devices, rows_of(): return lax.all_gather(value, 'dp', axis=0, tiled=False)  21.2 us
  transfers between devices with their start and end apart: 96, of which 28 were waited for; matrix products, arithmetic and copies ran while one was open for 19% of the time, Pallas kernels for 32%

profile of v4, /device:TPU:0, one launch (start us, length us, event | category | flops | bytes accessed | tf_op | source)
XLA Modules:
  0.0 743.8 jit_solution(5389798128026324331)
XLA Ops:
  22.3 22.7 %collective-permute-done = bf16[384,2048]{1,0:T(8,128)(2,1)} collective-permute-done((bf16[384,2048]{1,0:T(8,128)(2,1)}, bf16[384,2048]{1,0:T(8,128)(2,1)}, u32[]{:S(2)}, u32[]{:S(2)}) %collective-permute-start) | collective-permute-done | bytes 1572896 | tf_op jit(solution)/shard_map/ppermute | solution.py:90
  50.3 22.3 %collective-permute-done.3.refs_4_.refs_5_ = bf16[2048,256]{1,0:T(8,128)(2,1)S(1)} collective-permute-done((bf16[2048,256]{1,0:T(8,128)(2,1)}, bf16[2048,256]{1,0:T(8,128)(2,1)S(1)}, u32[]{:S(2)}, u32[]{:S(2)}) %collective-permute-start.3) | collective-permute-done | bytes 1048608 | tf_op jit(solution)/shard_map/ppermute | solution.py:90
  85.4 9.8 %collective-permute-done.6.refs_7_.refs_8_ = bf16[1024,256]{1,0:T(8,128)(2,1)S(1)} collective-permute-done((bf16[1024,256]{1,0:T(8,128)(2,1)S(1)}, bf16[1024,256]{1,0:T(8,128)(2,1)S(1)}, u32[]{:S(2)}, u32[]{:S(2)}) %collective-permute-start.6) | collective-permute-done | bytes 524320 | tf_op jit(solution)/shard_map/ppermute | solution.py:90
  98.3 4.6 collective-permute-done.15
  104.5 7.4 collective-permute-done.16
  124.2 9.5 %project.4 = bf16[384,2048]{1,0:T(8,128)(2,1)S(1)} custom-call(bf16[2048,256]{1,0:T(8,128)(2,1)S(1)} %copy-done.53, bf16[2048,256]{1,0:T(8,128)(2,1)} %collective-permute-done.4.refs_1_.refs_2_, bf16[2048,256]{1,0:T(8,128)(2,1)} %collective-permute-done.5.refs_2_.refs_3_, bf16[2048,256]{1,0:T(8,128)(2,1)S(1)} %copy-done.57, ...), custom_call_target="tpu_custom_call" | custom-call | flops 3221225472 | bytes 11534336 | tf_op jit(solution)/shard_map/project/pallas_call | solution.py:504
  133.8 9.5 %attention_forward.2 = (bf16[2,192,2048]{2,1,0:T(8,128)(2,1)S(1)}, f32[2,192,2048]{2,1,0:T(8,128)S(1)}) custom-call(bf16[2,192,2048]{2,1,0:T(8,128)(2,1)S(1)} %bitcast.223, bf16[2,1536,256]{2,1,0:T(8,128)(2,1)S(1)} %bitcast.218, s32[2,192,2]{2,1,0:T(8,128)S(1)} %copy-done.70, s32[2,2,1536]{2,1,0:T(2,128)S(1)} %copy-done.74), custom_call_target="tpu_custom_call" | custom-call | flops 4831838208 | bytes 3145728 | tf_op jit(solution)/shard_map/attention_forward/pallas_call | solution.py:303
  149.7 8.9 %attention_forward.3 = (bf16[2,192,2048]{2,1,0:T(8,128)(2,1)S(1)}, f32[2,192,2048]{2,1,0:T(8,128)S(1)}) custom-call(bf16[2,192,2048]{2,1,0:T(8,128)(2,1)S(1)} %bitcast.224, bf16[2,1536,256]{2,1,0:T(8,128)(2,1)S(1)} %bitcast.219, s32[2,192,2]{2,1,0:T(8,128)S(1)} %copy-done.70, ...), custom_call_target="tpu_custom_call", output_to_operand_aliasing={{0}: (4, {}), {1}: (5, {})} | custom-call | flops 4831838208 | bytes 3145728 | tf_op jit(solution)/shard_map/attention_forward/pallas_call | solution.py:303
  160.3 5.9 all-gather.12.cloned.1.call-done.refs_6_.refs_8_.full_gate_ref
  172.4 5.9 project_back.1
  178.8 10.1 %collective-permute-done.26 = bf16[192,2048]{1,0:T(8,128)(2,1)S(1)} collective-permute-done((bf16[192,2048]{1,0:T(8,128)(2,1)S(1)}, bf16[192,2048]{1,0:T(8,128)(2,1)S(1)}, u32[]{:S(2)}, u32[]{:S(2)}) %collective-permute-start.26) | collective-permute-done | bytes 786464 | tf_op jit(solution)/shard_map/ppermute | solution.py:90
  212.8 13.3 %all-gather.14.cloned.1.call-done.refs_7_.refs_9_.full_up_ref = bf16[4,704,512]{2,1,0:T(8,128)(2,1)} async-done(((bf16[1,704,512]{2,1,0:T(8,128)(2,1)}), bf16[4,704,512]{2,1,0:T(8,128)(2,1)}) %all-gather.14.cloned.1.call-update) | async-done | bytes 2883600 | tf_op jit(solution)/shard_map/all_gather | solution.py:1219
  235.0 17.4 %hidden_units.2 = (bf16[1536,2048]{1,0:T(8,128)(2,1)}, f32[1536,704]{1,0:T(8,128)}, f32[1536,704]{1,0:T(8,128)}, bf16[1536,704]{1,0:T(8,128)(2,1)S(1)}, bf16[704,1536]{1,0:T(8,128)(2,1)S(1)}) custom-call(bf16[384,2048]{1,0:T(8,128)(2,1)} %multiply_convert_fusion.refs_0_, bf16[384,2048]{1,0:T(8,128)(2,1)} %collective-permute-done.31.refs_1_, ...), custom_call_target="tpu_custom_call" | custom-call | flops 8858370048 | bytes 12582912 | tf_op jit(solution)/shard_map/hidden_units/pallas_call | solution.py:674
  258.7 16.9 %hidden_units.3 = (bf16[1536,2048]{1,0:T(8,128)(2,1)}, f32[1536,704]{1,0:T(8,128)}, f32[1536,704]{1,0:T(8,128)}, bf16[1536,704]{1,0:T(8,128)(2,1)S(1)}, bf16[704,1536]{1,0:T(8,128)(2,1)S(1)}) custom-call(bf16[384,2048]{1,0:T(8,128)(2,1)} %collective-permute-done.32.refs_2_.refs_0_, bf16[384,2048]{1,0:T(8,128)(2,1)} %collective-permute-done.36.refs_3_.refs_1_, ...), custom_call_target="tpu_custom_call" | custom-call | flops 8858370048 | bytes 12582912 | tf_op jit(solution)/shard_map/hidden_units/pallas_call | solution.py:674
  278.6 12.6 %units_sum.2 = bf16[4,704,512]{2,1,0:T(8,128)(2,1)S(1)} custom-call(bf16[1536,2048]{1,0:T(8,128)(2,1)S(1)} %bitcast.228, bf16[1536,2048]{1,0:T(8,128)(2,1)} %slice_dynamic-update-slice_fusion.refs_1_.cot_ref, bf16[704,1536]{1,0:T(8,128)(2,1)S(1)} %get-tuple-element.365.refs_2_, bf16[704,1536]{1,0:T(8,128)(2,1)S(1)} %copy-done.91), custom_call_target="tpu_custom_call" | custom-call | flops 8858370048 | bytes 16908288 | tf_op jit(solution)/shard_map/units_sum/pallas_call | solution.py:839
  292.8 24.1 %hidden_back.2 = (bf16[704,1536]{1,0:T(8,128)(2,1)}, bf16[704,1536]{1,0:T(8,128)(2,1)}, bf16[4,192,2048]{2,1,0:T(8,128)(2,1)}, bf16[4,192,2048]{2,1,0:T(8,128)(2,1)}) custom-call(bf16[1536,2048]{1,0:T(8,128)(2,1)} %copy-done.73, f32[1536,704]{1,0:T(8,128)} %get-tuple-element.375.gate_ref, f32[1536,704]{1,0:T(8,128)} %get-tuple-element.376.up_ref, ...), custom_call_target="tpu_custom_call" | custom-call | flops 13287555072 | bytes 12582912 | tf_op jit(solution)/shard_map/hidden_back/pallas_call | solution.py:754
  317.2 25.1 %hidden_back.3 = (bf16[704,1536]{1,0:T(8,128)(2,1)}, bf16[704,1536]{1,0:T(8,128)(2,1)}, bf16[4,192,2048]{2,1,0:T(8,128)(2,1)}, bf16[4,192,2048]{2,1,0:T(8,128)(2,1)}) custom-call(bf16[1536,2048]{1,0:T(8,128)(2,1)} %slice_dynamic-update-slice_fusion.refs_1_.cot_ref, f32[1536,704]{1,0:T(8,128)} %get-tuple-element.383.gate_ref, ...), custom_call_target="tpu_custom_call" | custom-call | flops 13287555072 | bytes 12582912 | tf_op jit(solution)/shard_map/hidden_back/pallas_call | solution.py:754
  342.7 3.6 add_convert_fusion.2
  348.7 21.3 %units_sum.3 = (bf16[4,704,512]{2,1,0:T(8,128)(2,1)S(1)}, bf16[4,704,512]{2,1,0:T(8,128)(2,1)S(1)}) custom-call(bf16[1536,2048]{1,0:T(8,128)(2,1)} %get-tuple-element.367.refs_0_, bf16[1536,2048]{1,0:T(8,128)(2,1)} %get-tuple-element.371.refs_1_, bf16[704,1536]{1,0:T(8,128)(2,1)S(1)} %copy-done.92, bf16[704,1536]{1,0:T(8,128)(2,1)S(1)} %copy-done.94, ...), custom_call_target="tpu_custom_call" | custom-call | flops 17716740096 | bytes 33816576 | tf_op jit(solution)/shard_map/units_sum/pallas_call | solution.py:839
  373.2 9.7 %collective-permute-done.41 = bf16[2,192,2048]{2,1,0:T(8,128)(2,1)S(1)} collective-permute-done((bf16[2,192,2048]{2,1,0:T(8,128)(2,1)S(1)}, bf16[2,192,2048]{2,1,0:T(8,128)(2,1)S(1)}, u32[]{:S(2)}, u32[]{:S(2)}) %collective-permute-start.41) | collective-permute-done | bytes 1572896 | tf_op jit(solution)/shard_map/ppermute | solution.py:90
  389.6 6.9 hidden_out.2
  398.2 6.5 hidden_out.3
  409.0 3.8 bitcast_add_fusion.4
  416.9 4.1 blocks_sum.5
  422.4 4.1 blocks_sum.4
  430.4 3.7 slice_bitcast_fusion.1
  437.9 5.5 add_convert_fusion
  445.6 8.4 %project.5 = bf16[384,2048]{1,0:T(8,128)(2,1)S(1)} custom-call(bf16[2048,256]{1,0:T(8,128)(2,1)S(1)} %copy-done.59, bf16[2048,256]{1,0:T(8,128)(2,1)} %collective-permute-done.11.refs_1_, bf16[2048,256]{1,0:T(8,128)(2,1)} %collective-permute-done.12.refs_2_, bf16[2048,256]{1,0:T(8,128)(2,1)} %collective-permute-done.21.refs_3_, ...), custom_call_target="tpu_custom_call" | custom-call | flops 3221225472 | bytes 11534336 | tf_op jit(solution)/shard_map/project/pallas_call | solution.py:504
  455.2 4.2 add_convert_fusion.6
  466.6 4.5 all-to-all-start
  478.2 14.2 %attention_backward.2 = (bf16[2,192,2048]{2,1,0:T(8,128)(2,1)S(1)}, bf16[2,1536,256]{2,1,0:T(8,128)(2,1)S(1)}) custom-call(bf16[2,192,2048]{2,1,0:T(8,128)(2,1)S(1)} %bitcast.225, bf16[2,192,2048]{2,1,0:T(8,128)(2,1)S(1)} %bitcast.233, f32[2,192,2048]{2,1,0:T(8,128)S(1)} %copy-done.84, bf16[2,1536,256]{2,1,0:T(8,128)(2,1)S(1)} %bitcast.220, ...), custom_call_target="tpu_custom_call" | custom-call | flops 12079595520 | bytes 4718592 | tf_op jit(solution)/shard_map/attention_backward/pallas_call | solution.py:401
  492.5 4.1 fusion.23
  500.7 14.2 %attention_backward.3 = (bf16[2,192,2048]{2,1,0:T(8,128)(2,1)S(1)}, bf16[2,1536,256]{2,1,0:T(8,128)(2,1)S(1)}) custom-call(bf16[2,192,2048]{2,1,0:T(8,128)(2,1)S(1)} %bitcast.226, bf16[2,192,2048]{2,1,0:T(8,128)(2,1)S(1)} %bitcast.234, f32[2,192,2048]{2,1,0:T(8,128)S(1)} %copy-done.85, ...), custom_call_target="tpu_custom_call", output_to_operand_aliasing={{0}: (8, {}), {1}: (9, {})} | custom-call | flops 12079595520 | bytes 4718592 | tf_op jit(solution)/shard_map/attention_backward/pallas_call | solution.py:401
  527.4 4.1 blocks_sum.7
  532.9 4.5 blocks_sum.6
  539.2 3.6 bitcast_add_fusion.2
  554.4 4.3 all-to-all-start.1
  566.5 3.6 add_convert_fusion.4
  574.5 4.3 collective-permute-start.63
  585.8 19.4 %back_and_factor.1 = (f32[384,2048]{1,0:T(8,128)}, bf16[352,352]{1,0:T(8,128)(2,1)}) custom-call(s32[1]{0:T(128)S(6)} %add.537.refs_0_, bf16[2048,256]{1,0:T(8,128)(2,1)} %all-gather.16.cloned.1.call-done, bf16[2048,256]{1,0:T(8,128)(2,1)} %collective-permute-done.4.refs_1_.refs_2_, bf16[2048,256]{1,0:T(8,128)(2,1)} %collective-permute-done.5.refs_2_.refs_3_, ...), custom_call_target="tpu_custom_call" | custom-call | flops 7582646272 | bytes 13107200 | tf_op jit(solution)/shard_map/back_and_factor/pallas_call | solution.py:1145
  612.1 4.7 collective-permute-start.67
  617.9 4.2 all-to-all-start.2
  640.9 5.0 fusion.7
  649.7 19.3 %all-to-all-start.3 = ((bf16[4,96,256]{2,1,0:T(8,128)(2,1)}), bf16[4,96,256]{2,1,0:T(8,128)(2,1)}, u32[]{:S(2)}, u32[]{:S(2)}) async-start(bf16[4,96,256]{2,1,0:T(8,128)(2,1)} %pad_maximum_fusion.8), calls=%async_computation.7 | async-start | bytes 393216 | tf_op jit(solution)/shard_map/all_to_all | solution.py:1450
  686.0 5.8 small_update.2
  692.7 9.6 %all-gather.4 = bf16[768,256]{1,0:T(8,128)(2,1)S(1)} all-gather(bf16[96,256]{1,0:T(8,128)(2,1)S(1)} %pad_maximum_fusion.9), channel_id=6, replica_groups=mesh['dp'=4,'mp'=8] {'mp'}, dimensions={0}, use_global_device_ids=true | all-gather | bytes 442368 | tf_op jit(solution)/shard_map/all_gather | solution.py:1464
  721.2 4.9 collective-permute-done.79.refs_10_
  726.1 10.9 %small_update.3 = (f32[512,256]{1,0:T(8,128)}, f32[512,256]{1,0:T(8,128)}) custom-call(f32[512,256]{1,0:T(8,128)S(1)} %multiply_add_fusion.refs_0_, f32[512,256]{1,0:T(8,128)S(1)} %copy-done.68, f32[512,256]{1,0:T(8,128)S(1)} %get-tuple-element.540.refs_0_.refs_2_, f32[512,256]{1,0:T(8,128)S(1)} %copy-done.66, bf16[1,272,256]{2,1,0:T(8,128)(2,1)} %packed_grams.8.refs_4_, ...), custom_call_target="tpu_custom_call" | custom-call | flops 2254438400 | bytes 3145728 | tf_op jit(solution)/shard_map/small_update/pallas_call | solution.py:1082
  (604 shorter events, 274.8 us)
Async XLA Ops:
  7.2 40.2 %all-gather.16.cloned.1.call-start = ((), (), s32[]{:S(2)}) async-start(), calls=%async_computation.16 | async-start | bytes 1310720 | tf_op jit(solution)/shard_map/all_gather | solution.py:1219
  7.3 37.7 %collective-permute-start = (bf16[384,2048]{1,0:T(8,128)(2,1)}, bf16[384,2048]{1,0:T(8,128)(2,1)}, u32[]{:S(2)}, u32[]{:S(2)}) collective-permute-start(bf16[384,2048]{1,0:T(8,128)(2,1)} %bitcast.244), channel_id=1, source_target_pairs={{0,4},{1,5},{2,6},{3,7},{4,0},{5,1},{6,2},{7,3},{8,12},{9,13},{10,... | collective-permute-start | bytes 4718600 | tf_op jit(solution)/shard_map/ppermute | solution.py:90
  10.3 34.7 %collective-permute-start.1 = (bf16[384,2048]{1,0:T(8,128)(2,1)}, bf16[384,2048]{1,0:T(8,128)(2,1)}, u32[]{:S(2)}, u32[]{:S(2)}) collective-permute-start(bf16[384,2048]{1,0:T(8,128)(2,1)} %bitcast.245), channel_id=1, source_target_pairs={{0,1},{1,0},{2,3},{3,2},{4,5},{5,4},{6,7},{7,6},{8,9},{9,8},{10,11... | collective-permute-start | bytes 4718600 | tf_op jit(solution)/shard_map/ppermute | solution.py:90
  10.3 37.1 %collective-permute-start.2 = (bf16[384,2048]{1,0:T(8,128)(2,1)}, bf16[384,2048]{1,0:T(8,128)(2,1)}, u32[]{:S(2)}, u32[]{:S(2)}) collective-permute-start(bf16[384,2048]{1,0:T(8,128)(2,1)} %bitcast.246), channel_id=1, source_target_pairs={{0,2},{1,3},{2,0},{3,1},{4,6},{5,7},{6,4},{7,5},{8,10},{9,11},{10,... | collective-permute-start | bytes 4718600 | tf_op jit(solution)/shard_map/ppermute | solution.py:90
  13.6 62.2 %all-gather.18.cloned.1.call-start = ((), (), s32[]{:S(2)}) async-start(), calls=%async_computation.17 | async-start | bytes 1310720 | tf_op jit(solution)/shard_map/all_gather | solution.py:1219
  47.4 67.4 %all-gather.20.cloned.1.call-start = ((), (), s32[]{:S(2)}) async-start(), calls=%async_computation.18 | async-start | bytes 1310720 | tf_op jit(solution)/shard_map/all_gather | solution.py:1219
  47.8 25.9 %collective-permute-start.5 = (bf16[2048,256]{1,0:T(8,128)(2,1)}, bf16[2048,256]{1,0:T(8,128)(2,1)}, u32[]{:S(2)}, u32[]{:S(2)}) collective-permute-start(bf16[2048,256]{1,0:T(8,128)(2,1)} %all-gather.16.cloned.1.call-done), channel_id=1, source_target_pairs={{0,2},{1,3},{2,0},{3,1},{4,6},{5,7},{6,4},{7,5},{8,10},{9,11},{10,... | collective-permute-start | bytes 3145736 | tf_op jit(solution)/shard_map/ppermute | solution.py:90
  75.9 90.3 %all-gather.12.cloned.1.call-start = ((), (), s32[]{:S(2)}) async-start(), calls=%async_computation.9 | async-start | bytes 3604480 | tf_op jit(solution)/shard_map/all_gather | solution.py:1219
  79.0 147.0 %all-gather.14.cloned.1.call-start = ((), (), s32[]{:S(2)}) async-start(), calls=%async_computation.10 | async-start | bytes 3604480 | tf_op jit(solution)/shard_map/all_gather | solution.py:1219
  115.3 27.9 %collective-permute-start.10 = (bf16[2048,256]{1,0:T(8,128)(2,1)}, bf16[2048,256]{1,0:T(8,128)(2,1)}, u32[]{:S(2)}, u32[]{:S(2)}) collective-permute-start(bf16[2048,256]{1,0:T(8,128)(2,1)} %all-gather.20.cloned.1.call-done), channel_id=1, source_target_pairs={{0,4},{1,5},{2,6},{3,7},{4,0},{5,1},{6,2},{7,3},{8,12},{9,13},{10,... | collective-permute-start | bytes 3145736 | tf_op jit(solution)/shard_map/ppermute | solution.py:90
  116.8 26.5 %collective-permute-start.11 = (bf16[2048,256]{1,0:T(8,128)(2,1)}, bf16[2048,256]{1,0:T(8,128)(2,1)}, u32[]{:S(2)}, u32[]{:S(2)}) collective-permute-start(bf16[2048,256]{1,0:T(8,128)(2,1)} %all-gather.20.cloned.1.call-done), channel_id=1, source_target_pairs={{0,1},{1,0},{2,3},{3,2},{4,5},{5,4},{6,7},{7,6},{8,9},{9,8},{10,11... | collective-permute-start | bytes 3145736 | tf_op jit(solution)/shard_map/ppermute | solution.py:90
  117.0 26.2 %collective-permute-start.12 = (bf16[2048,256]{1,0:T(8,128)(2,1)}, bf16[2048,256]{1,0:T(8,128)(2,1)}, u32[]{:S(2)}, u32[]{:S(2)}) collective-permute-start(bf16[2048,256]{1,0:T(8,128)(2,1)} %all-gather.20.cloned.1.call-done), channel_id=1, source_target_pairs={{0,2},{1,3},{2,0},{3,1},{4,6},{5,7},{6,4},{7,5},{8,10},{9,11},{10,... | collective-permute-start | bytes 3145736 | tf_op jit(solution)/shard_map/ppermute | solution.py:90
  118.6 30.0 %collective-permute-start.22 = (bf16[384,2048]{1,0:T(8,128)(2,1)}, bf16[384,2048]{1,0:T(8,128)(2,1)}, u32[]{:S(2)}, u32[]{:S(2)}) collective-permute-start(bf16[384,2048]{1,0:T(8,128)(2,1)} %collective-permute-done), channel_id=1, source_target_pairs={{0,1},{1,0},{2,3},{3,2},{4,5},{5,4},{6,7},{7,6},{8,9},{9,8},{10,11... | collective-permute-start | bytes 4718600 | tf_op jit(solution)/shard_map/ppermute | solution.py:90
  121.5 44.7 %collective-permute-start.23 = (bf16[384,2048]{1,0:T(8,128)(2,1)}, bf16[384,2048]{1,0:T(8,128)(2,1)}, u32[]{:S(2)}, u32[]{:S(2)}) collective-permute-start(bf16[384,2048]{1,0:T(8,128)(2,1)} %collective-permute-done.2), channel_id=1, source_target_pairs={{0,1},{1,0},{2,3},{3,2},{4,5},{5,4},{6,7},{7,6},{8,9},{9,8},{10,11... | collective-permute-start | bytes 4718600 | tf_op jit(solution)/shard_map/ppermute | solution.py:90
  166.8 126.0 %all-gather.22.cloned.1.call-start = ((), (), s32[]{:S(2)}) async-start(), calls=%async_computation.19 | async-start | bytes 3604480 | tf_op jit(solution)/shard_map/all_gather | solution.py:1219
  190.4 37.1 %collective-permute-start.30 = (bf16[384,2048]{1,0:T(8,128)(2,1)}, bf16[384,2048]{1,0:T(8,128)(2,1)}, u32[]{:S(2)}, u32[]{:S(2)}) collective-permute-start(bf16[384,2048]{1,0:T(8,128)(2,1)} %multiply_convert_fusion.refs_0_), channel_id=1, source_target_pairs={{0,4},{1,5},{2,6},{3,7},{4,0},{5,1},{6,2},{7,3},{8,12},{9,13},{10,... | collective-permute-start | bytes 4718600 | tf_op jit(solution)/shard_map/ppermute | solution.py:90
  191.9 35.7 %collective-permute-start.31 = (bf16[384,2048]{1,0:T(8,128)(2,1)}, bf16[384,2048]{1,0:T(8,128)(2,1)}, u32[]{:S(2)}, u32[]{:S(2)}) collective-permute-start(bf16[384,2048]{1,0:T(8,128)(2,1)} %multiply_convert_fusion.refs_0_), channel_id=1, source_target_pairs={{0,1},{1,0},{2,3},{3,2},{4,5},{5,4},{6,7},{7,6},{8,9},{9,8},{10,11... | collective-permute-start | bytes 4718600 | tf_op jit(solution)/shard_map/ppermute | solution.py:90
  192.1 36.9 %collective-permute-start.32 = (bf16[384,2048]{1,0:T(8,128)(2,1)}, bf16[384,2048]{1,0:T(8,128)(2,1)}, u32[]{:S(2)}, u32[]{:S(2)}) collective-permute-start(bf16[384,2048]{1,0:T(8,128)(2,1)} %multiply_convert_fusion.refs_0_), channel_id=1, source_target_pairs={{0,2},{1,3},{2,0},{3,1},{4,6},{5,7},{6,4},{7,5},{8,10},{9,11},{10,... | collective-permute-start | bytes 4718600 | tf_op jit(solution)/shard_map/ppermute | solution.py:90
  230.5 153.8 %reduce-scatter.6.cloned.1.call-start = ((), (), s32[]{:S(2)}) async-start(), calls=%async_computation.11 | async-start | bytes 3604480 | tf_op jit(solution)/shard_map/reduce_scatter | solution.py:1336
  317.1 138.1 %reduce-scatter.8.cloned.1.call-start = ((), (), s32[]{:S(2)}) async-start(), calls=%async_computation.12 | async-start | bytes 3604480 | tf_op jit(solution)/shard_map/reduce_scatter | solution.py:1336
  342.3 42.0 %collective-permute-start.40 = (bf16[4,192,2048]{2,1,0:T(8,128)(2,1)}, bf16[4,192,2048]{2,1,0:T(8,128)(2,1)}, u32[]{:S(2)}, u32[]{:S(2)}) collective-permute-start(bf16[4,192,2048]{2,1,0:T(8,128)(2,1)} %get-tuple-element.386), channel_id=1, source_target_pairs={{0,1},{1,0},{2,3},{3,2},{4,5},{5,4},{6,7},{7,6},{8,9},{9,8},{10,11... | collective-permute-start | bytes 9437192 | tf_op jit(solution)/shard_map/ppermute | solution.py:90
  346.4 36.5 %collective-permute-start.41 = (bf16[2,192,2048]{2,1,0:T(8,128)(2,1)S(1)}, bf16[2,192,2048]{2,1,0:T(8,128)(2,1)S(1)}, u32[]{:S(2)}, u32[]{:S(2)}) collective-permute-start(bf16[2,192,2048]{2,1,0:T(8,128)(2,1)S(1)} %get-tuple-element.393), channel_id=1, source_target_pairs={{0,4},{1,5},{2,6},{3,7},{4,0},{5,1},{6,2},{7,3},{8,12},{9,13},{10,... | collective-permute-start | bytes 4718600 | tf_op jit(solution)/shard_map/ppermute | solution.py:90
  348.0 36.3 %collective-permute-start.42 = (bf16[2,192,2048]{2,1,0:T(8,128)(2,1)S(1)}, bf16[2,192,2048]{2,1,0:T(8,128)(2,1)}, u32[]{:S(2)}, u32[]{:S(2)}) collective-permute-start(bf16[2,192,2048]{2,1,0:T(8,128)(2,1)S(1)} %get-tuple-element.394), channel_id=1, source_target_pairs={{0,2},{1,3},{2,0},{3,1},{4,6},{5,7},{6,4},{7,5},{8,10},{9,11},{10,... | collective-permute-start | bytes 4718600 | tf_op jit(solution)/shard_map/ppermute | solution.py:90
  384.3 135.2 %reduce-scatter.10.cloned.1.call-start = ((), (), s32[]{:S(2)}) async-start(), calls=%async_computation.13 | async-start | bytes 3604480 | tf_op jit(solution)/shard_map/reduce_scatter | solution.py:1336
  427.8 27.4 %collective-permute-start.47 = (bf16[4,1024,256]{2,1,0:T(8,128)(2,1)}, bf16[4,1024,256]{2,1,0:T(8,128)(2,1)}, u32[]{:S(2)}, u32[]{:S(2)}) collective-permute-start(bf16[4,1024,256]{2,1,0:T(8,128)(2,1)} %get-tuple-element.429), channel_id=1, source_target_pairs={{0,1},{1,0},{2,3},{3,2},{4,5},{5,4},{6,7},{7,6},{8,9},{9,8},{10,11... | collective-permute-start | bytes 6291464 | tf_op jit(solution)/shard_map/ppermute | solution.py:90
  427.8 27.4 %collective-permute-start.48 = (bf16[4,1024,256]{2,1,0:T(8,128)(2,1)}, bf16[4,1024,256]{2,1,0:T(8,128)(2,1)}, u32[]{:S(2)}, u32[]{:S(2)}) collective-permute-start(bf16[4,1024,256]{2,1,0:T(8,128)(2,1)} %get-tuple-element.430), channel_id=1, source_target_pairs={{0,1},{1,0},{2,3},{3,2},{4,5},{5,4},{6,7},{7,6},{8,9},{9,8},{10,11... | collective-permute-start | bytes 6291464 | tf_op jit(solution)/shard_map/ppermute | solution.py:90
  443.4 49.0 %collective-permute-start.49 = (bf16[2,192,2048]{2,1,0:T(8,128)(2,1)}, bf16[2,192,2048]{2,1,0:T(8,128)(2,1)}, u32[]{:S(2)}, u32[]{:S(2)}) collective-permute-start(bf16[2,192,2048]{2,1,0:T(8,128)(2,1)} %get-tuple-element.446), channel_id=1, source_target_pairs={{0,4},{1,5},{2,6},{3,7},{4,0},{5,1},{6,2},{7,3},{8,12},{9,13},{10,... | collective-permute-start | bytes 4718600 | tf_op jit(solution)/shard_map/ppermute | solution.py:90
  444.8 47.6 %collective-permute-start.50 = (bf16[2,192,2048]{2,1,0:T(8,128)(2,1)}, bf16[2,192,2048]{2,1,0:T(8,128)(2,1)}, u32[]{:S(2)}, u32[]{:S(2)}) collective-permute-start(bf16[2,192,2048]{2,1,0:T(8,128)(2,1)} %get-tuple-element.447), channel_id=1, source_target_pairs={{0,2},{1,3},{2,0},{3,1},{4,6},{5,7},{6,4},{7,5},{8,10},{9,11},{10,... | collective-permute-start | bytes 4718600 | tf_op jit(solution)/shard_map/ppermute | solution.py:90
  466.6 53.0 %all-to-all-start = ((bf16[4,368,352]{1,2,0:T(8,128)(2,1)}), bf16[4,368,352]{1,2,0:T(8,128)(2,1)}, u32[]{:S(2)}, u32[]{:S(2)}) async-start(bf16[4,368,352]{1,2,0:T(8,128)(2,1)} %copy.65), calls=%async_computation.2 | async-start | bytes 2162688 | tf_op jit(solution)/shard_map/all_to_all | solution.py:1379
  496.6 26.4 %collective-permute-start.53 = (bf16[2,1024,256]{2,1,0:T(8,128)(2,1)}, bf16[2,1024,256]{2,1,0:T(8,128)(2,1)}, u32[]{:S(2)}, u32[]{:S(2)}) collective-permute-start(bf16[2,1024,256]{2,1,0:T(8,128)(2,1)} %get-tuple-element.465), channel_id=1, source_target_pairs={{0,4},{1,5},{2,6},{3,7},{4,0},{5,1},{6,2},{7,3},{8,12},{9,13},{10,... | collective-permute-start | bytes 3145736 | tf_op jit(solution)/shard_map/ppermute | solution.py:90
  497.7 26.4 %collective-permute-start.54 = (bf16[2,1024,256]{2,1,0:T(8,128)(2,1)}, bf16[2,1024,256]{2,1,0:T(8,128)(2,1)}, u32[]{:S(2)}, u32[]{:S(2)}) collective-permute-start(bf16[2,1024,256]{2,1,0:T(8,128)(2,1)} %get-tuple-element.466), channel_id=1, source_target_pairs={{0,2},{1,3},{2,0},{3,1},{4,6},{5,7},{6,4},{7,5},{8,10},{9,11},{10,... | collective-permute-start | bytes 3145736 | tf_op jit(solution)/shard_map/ppermute | solution.py:90
  498.3 39.9 %collective-permute-start.51 = (bf16[192,2048]{1,0:T(8,128)(2,1)}, bf16[192,2048]{1,0:T(8,128)(2,1)}, u32[]{:S(2)}, u32[]{:S(2)}) collective-permute-start(bf16[192,2048]{1,0:T(8,128)(2,1)} %get-tuple-element.452), channel_id=1, source_target_pairs={{0,4},{1,5},{2,6},{3,7},{4,0},{5,1},{6,2},{7,3},{8,12},{9,13},{10,... | collective-permute-start | bytes 2359304 | tf_op jit(solution)/shard_map/ppermute | solution.py:90
  499.7 39.5 %collective-permute-start.52 = (bf16[192,2048]{1,0:T(8,128)(2,1)}, bf16[192,2048]{1,0:T(8,128)(2,1)}, u32[]{:S(2)}, u32[]{:S(2)}) collective-permute-start(bf16[192,2048]{1,0:T(8,128)(2,1)} %get-tuple-element.453), channel_id=1, source_target_pairs={{0,2},{1,3},{2,0},{3,1},{4,6},{5,7},{6,4},{7,5},{8,10},{9,11},{10,... | collective-permute-start | bytes 2359304 | tf_op jit(solution)/shard_map/ppermute | solution.py:90
  532.9 33.5 %collective-permute-start.56 = (bf16[4,1024,256]{2,1,0:T(8,128)(2,1)}, bf16[4,1024,256]{2,1,0:T(8,128)(2,1)}, u32[]{:S(2)}, u32[]{:S(2)}) collective-permute-start(bf16[4,1024,256]{2,1,0:T(8,128)(2,1)} %get-tuple-element.477), channel_id=1, source_target_pairs={{0,1},{1,0},{2,3},{3,2},{4,5},{5,4},{6,7},{7,6},{8,9},{9,8},{10,11... | collective-permute-start | bytes 6291464 | tf_op jit(solution)/shard_map/ppermute | solution.py:90
  537.4 29.0 %collective-permute-start.55 = (bf16[4,1024,256]{2,1,0:T(8,128)(2,1)}, bf16[4,1024,256]{2,1,0:T(8,128)(2,1)}, u32[]{:S(2)}, u32[]{:S(2)}) collective-permute-start(bf16[4,1024,256]{2,1,0:T(8,128)(2,1)} %get-tuple-element.476), channel_id=1, source_target_pairs={{0,1},{1,0},{2,3},{3,2},{4,5},{5,4},{6,7},{7,6},{8,9},{9,8},{10,11... | collective-permute-start | bytes 6291464 | tf_op jit(solution)/shard_map/ppermute | solution.py:90
  554.4 50.8 %all-to-all-start.1 = ((bf16[8,2,192,256]{3,2,1,0:T(8,128)(2,1)}), bf16[8,2,192,256]{3,2,1,0:T(8,128)(2,1)}, u32[]{:S(2)}, u32[]{:S(2)}) async-start(bf16[8,2,192,256]{3,2,1,0:T(8,128)(2,1)} %gather_fusion.1), calls=%async_computation.4 | async-start | bytes 3145728 | tf_op jit(solution)/shard_map/all_to_all | solution.py:1403
  558.7 110.3 %reduce-scatter.14.cloned.1.call-start = ((), (), s32[]{:S(2)}) async-start(), calls=%async_computation.15 | async-start | bytes 1310720 | tf_op jit(solution)/shard_map/reduce_scatter | solution.py:1336
  570.1 35.1 %collective-permute-start.59 = (bf16[2,1024,256]{2,1,0:T(8,128)(2,1)}, bf16[2,1024,256]{2,1,0:T(8,128)(2,1)}, u32[]{:S(2)}, u32[]{:S(2)}) collective-permute-start(bf16[2,1024,256]{2,1,0:T(8,128)(2,1)} %get-tuple-element.491), channel_id=1, source_target_pairs={{0,4},{1,5},{2,6},{3,7},{4,0},{5,1},{6,2},{7,3},{8,12},{9,13},{10,... | collective-permute-start | bytes 3145736 | tf_op jit(solution)/shard_map/ppermute | solution.py:90
  571.9 33.2 %collective-permute-start.60 = (bf16[2,1024,256]{2,1,0:T(8,128)(2,1)}, bf16[2,1024,256]{2,1,0:T(8,128)(2,1)}, u32[]{:S(2)}, u32[]{:S(2)}) collective-permute-start(bf16[2,1024,256]{2,1,0:T(8,128)(2,1)} %get-tuple-element.492), channel_id=1, source_target_pairs={{0,2},{1,3},{2,0},{3,1},{4,6},{5,7},{6,4},{7,5},{8,10},{9,11},{10,... | collective-permute-start | bytes 3145736 | tf_op jit(solution)/shard_map/ppermute | solution.py:90
  574.5 37.5 %collective-permute-start.63 = (bf16[368,352]{1,0:T(8,128)(2,1)}, bf16[368,352]{1,0:T(8,128)(2,1)}, u32[]{:S(2)}, u32[]{:S(2)}) collective-permute-start(bf16[368,352]{1,0:T(8,128)(2,1)} %get-tuple-element.593), channel_id=1, source_target_pairs={{0,8},{8,16},{1,9},{9,17},{2,10},{10,18},{3,11},{11,19},{4,12},{12... | collective-permute-start | bytes 777224 | tf_op jit(solution)/shard_map/ppermute | solution.py:1114
  578.8 33.3 %collective-permute-start.64 = (bf16[368,352]{1,0:T(8,128)(2,1)}, bf16[368,352]{1,0:T(8,128)(2,1)}, u32[]{:S(2)}, u32[]{:S(2)}) collective-permute-start(bf16[368,352]{1,0:T(8,128)(2,1)} %get-tuple-element.591), channel_id=1, source_target_pairs={{24,8},{0,16},{25,9},{1,17},{26,10},{2,18},{27,11},{3,19},{28,12},... | collective-permute-start | bytes 777224 | tf_op jit(solution)/shard_map/ppermute | solution.py:1114
  581.1 35.7 %collective-permute-start.65 = (bf16[368,352]{1,0:T(8,128)(2,1)}, bf16[368,352]{1,0:T(8,128)(2,1)}, u32[]{:S(2)}, u32[]{:S(2)}) collective-permute-start(bf16[368,352]{1,0:T(8,128)(2,1)} %get-tuple-element.590), channel_id=1, source_target_pairs={{16,8},{24,16},{17,9},{25,17},{18,10},{26,18},{19,11},{27,19},{20,... | collective-permute-start | bytes 777224 | tf_op jit(solution)/shard_map/ppermute | solution.py:1114
  617.9 28.0 %all-to-all-start.2 = ((bf16[8,4,64,256]{3,2,1,0:T(8,128)(2,1)}), bf16[8,4,64,256]{3,2,1,0:T(8,128)(2,1)}, u32[]{:S(2)}, u32[]{:S(2)}) async-start(bf16[8,4,64,256]{3,2,1,0:T(8,128)(2,1)} %bitcast.207), calls=%async_computation.5 | async-start | bytes 2097152 | tf_op jit(solution)/shard_map/all_to_all | solution.py:1432
  622.2 87.3 %reduce-scatter.12.cloned.1.call-start = ((), (), s32[]{:S(2)}) async-start(), calls=%async_computation.14 | async-start | bytes 1310720 | tf_op jit(solution)/shard_map/reduce_scatter | solution.py:1336
  624.5 51.3 %collective-permute-start.72 = (bf16[352,352]{1,0:T(8,128)(2,1)}, bf16[352,352]{1,0:T(8,128)(2,1)}, u32[]{:S(2)}, u32[]{:S(2)}) collective-permute-start(bf16[352,352]{1,0:T(8,128)(2,1)} %block_factor.1.refs_0_), channel_id=1, source_target_pairs={{8,16},{16,24},{9,17},{17,25},{10,18},{18,26},{11,19},{19,27},{12,... | collective-permute-start | bytes 743432 | tf_op jit(solution)/shard_map/ppermute | solution.py:1122
  626.1 54.8 %collective-permute-start.73 = (bf16[352,352]{1,0:T(8,128)(2,1)}, bf16[352,352]{1,0:T(8,128)(2,1)}, u32[]{:S(2)}, u32[]{:S(2)}) collective-permute-start(bf16[352,352]{1,0:T(8,128)(2,1)} %block_factor.1.refs_0_), channel_id=1, source_target_pairs={{8,24},{16,0},{9,25},{17,1},{10,26},{18,2},{11,27},{19,3},{12,28},... | collective-permute-start | bytes 743432 | tf_op jit(solution)/shard_map/ppermute | solution.py:1122
  627.3 53.5 %collective-permute-start.74 = (bf16[352,352]{1,0:T(8,128)(2,1)}, bf16[352,352]{1,0:T(8,128)(2,1)}, u32[]{:S(2)}, u32[]{:S(2)}) collective-permute-start(bf16[352,352]{1,0:T(8,128)(2,1)} %block_factor.1.refs_0_), channel_id=1, source_target_pairs={{8,0},{16,8},{9,1},{17,9},{10,2},{18,10},{11,3},{19,11},{12,4},{20... | collective-permute-start | bytes 743432 | tf_op jit(solution)/shard_map/ppermute | solution.py:1122
  649.7 42.0 %all-to-all-start.3 = ((bf16[4,96,256]{2,1,0:T(8,128)(2,1)}), bf16[4,96,256]{2,1,0:T(8,128)(2,1)}, u32[]{:S(2)}, u32[]{:S(2)}) async-start(bf16[4,96,256]{2,1,0:T(8,128)(2,1)} %pad_maximum_fusion.8), calls=%async_computation.7 | async-start | bytes 393216 | tf_op jit(solution)/shard_map/all_to_all | solution.py:1450
  (188 other events, 2434.7 us)
Sparse Core Ops, SparseCore 0:
  13.7 27.2 all-gather.15
  47.6 28.2 all-gather.17
  78.0 27.4 all-gather.19
  107.4 58.6 all-gather.11
  168.1 57.8 all-gather.13
  230.6 56.9 all-gather.21
  317.3 54.0 reduce-scatter.5
  384.4 53.7 reduce-scatter.7
  441.1 73.1 reduce-scatter.9
  585.9 27.4 reduce-scatter.13
  635.3 46.4 reduce-scatter.11

commit v5 on v4

--- a/solution.py
+++ b/solution.py
@@ -1246,9 +1246,18 @@
     x_rows = wide(inputs).reshape(tokens, model_width)
     x_scale = inverse_scale(x_rows)
     normed = (x_rows * x_scale * gains[0]).astype(LOW)
-    cot.parts, query_block, low_keyval, normed, flat_cos, flat_sin, qid, kid = tie(
-        cot.parts, query_block, w_keyval.astype(LOW), normed, flat_cos, flat_sin, qid, kid
+    first_one = "one" if size == 8 else "1"
+    cot.parts[first_one], query_block, low_keyval, normed, flat_cos, flat_sin, qid, kid = tie(
+        cot.parts[first_one],
+        query_block,
+        w_keyval.astype(LOW),
+        normed,
+        flat_cos,
+        flat_sin,
+        qid,
+        kid,
     )
+    cot.parts, query_block = tie(cot.parts, query_block)
     full_keyval = rows_of(low_keyval)
     query_gather = Gather(query_block.reshape(model_width, query_cols), size)
     query_gather.first()

time: 749 us -> 747 us (level)
    ppermute x63, waiting for transfers between devices: 105 us -> 85.6 us  [swap(): return lax.ppermute(value, 'mp', [(i, i ^ flip) for i in range(size)])]
    all_gather x6, waiting for transfers between devices: 21.2 us -> 37.5 us  [rows_of(): return lax.all_gather(value, 'dp', axis=0, tiled=False)]
  transfers between devices with their start and end apart: 96 -> 96, of which waited for: 28 -> 28; matrix products, arithmetic and copies ran while one was open for 19% -> 20% of each run, Pallas kernels for 32% -> 32%
where the time goes in v5:
time: 747 us; the launch traced here: 741 us
  Pallas kernels  271 us (36%)
  waiting for transfers between devices  136 us (18%)
  starting transfers between devices  112 us (15%)
  local copies, waits for them, and re-layouts  97 us (13%)
  other arithmetic  95.3 us (13%)
  between operations  16.1 us (2%)
  blocking collectives  9.58 us (1%)
    ppermute x63, waiting for transfers between devices, swap(): return lax.ppermute(value, 'mp', [(i, i ^ flip) for i in range(size)])  85.6 us
    unnamed x291, local copies, waits for them, and re-layouts  65.5 us
    pallas_call x2, Pallas kernels, hidden_back(): pl.pallas_call(functools.partial(hidden_back_kernel, turn), grid=(steps,)...  49.1 us
    ppermute x63, starting transfers between devices, swap(): return lax.ppermute(value, 'mp', [(i, i ^ flip) for i in range(size)])  47.4 us
    all_gather x6, waiting for transfers between devices, rows_of(): return lax.all_gather(value, 'dp', axis=0, tiled=False)  37.5 us
    pallas_call x2, Pallas kernels, hidden_units(): pl.pallas_call(functools.partial(hidden_kernel, places, steps, turn), gri...  34.3 us
    pallas_call x2, Pallas kernels, units_sum(): pl.pallas_call(functools.partial(units_sum_kernel, len(rows), turn), grid...  33.9 us
    pallas_call x2, Pallas kernels, attention_backward(): pl.pallas_call(functools.partial(backward_kernel, heads, head_dim), grid=...  28.5 us
  transfers between devices with their start and end apart: 96, of which 28 were waited for; matrix products, arithmetic and copies ran while one was open for 20% of the time, Pallas kernels for 32%

profile of v5, /device:TPU:0, one launch (start us, length us, event | category | flops | bytes accessed | tf_op | source)
XLA Modules:
  0.0 741.3 jit_solution(253501502971326848)
XLA Ops:
  22.4 18.7 %all-gather.16.cloned.1.call-done = bf16[2048,256]{1,0:T(8,128)(2,1)} async-done(((bf16[512,256]{1,0:T(8,128)(2,1)}), bf16[2048,256]{1,0:T(8,128)(2,1)}) %all-gather.16.cloned.1.call-update) | async-done | bytes 1048592 | tf_op jit(solution)/shard_map/all_gather | solution.py:1219
  41.2 4.5 collective-permute-done.1
  49.9 21.9 %collective-permute-done.3.refs_4_.refs_5_ = bf16[2048,256]{1,0:T(8,128)(2,1)S(1)} collective-permute-done((bf16[2048,256]{1,0:T(8,128)(2,1)}, bf16[2048,256]{1,0:T(8,128)(2,1)S(1)}, u32[]{:S(2)}, u32[]{:S(2)}) %collective-permute-start.3) | collective-permute-done | bytes 1048608 | tf_op jit(solution)/shard_map/ppermute | solution.py:90
  83.2 9.6 %collective-permute-done.6.refs_7_.refs_8_ = bf16[1024,256]{1,0:T(8,128)(2,1)S(1)} collective-permute-done((bf16[1024,256]{1,0:T(8,128)(2,1)S(1)}, bf16[1024,256]{1,0:T(8,128)(2,1)S(1)}, u32[]{:S(2)}, u32[]{:S(2)}) %collective-permute-start.6) | collective-permute-done | bytes 524320 | tf_op jit(solution)/shard_map/ppermute | solution.py:90
  96.0 4.7 collective-permute-done.15
  102.3 7.4 collective-permute-done.16
  122.0 9.5 %project.4 = bf16[384,2048]{1,0:T(8,128)(2,1)S(1)} custom-call(bf16[2048,256]{1,0:T(8,128)(2,1)S(1)} %copy-done.53, bf16[2048,256]{1,0:T(8,128)(2,1)} %collective-permute-done.4.refs_1_.refs_2_, bf16[2048,256]{1,0:T(8,128)(2,1)} %collective-permute-done.5.refs_2_.refs_3_, bf16[2048,256]{1,0:T(8,128)(2,1)S(1)} %copy-done.57, ...), custom_call_target="tpu_custom_call" | custom-call | flops 3221225472 | bytes 11534336 | tf_op jit(solution)/shard_map/project/pallas_call | solution.py:504
  131.6 9.5 %attention_forward.2 = (bf16[2,192,2048]{2,1,0:T(8,128)(2,1)S(1)}, f32[2,192,2048]{2,1,0:T(8,128)S(1)}) custom-call(bf16[2,192,2048]{2,1,0:T(8,128)(2,1)S(1)} %bitcast.223, bf16[2,1536,256]{2,1,0:T(8,128)(2,1)S(1)} %bitcast.218, s32[2,192,2]{2,1,0:T(8,128)S(1)} %copy-done.70, s32[2,2,1536]{2,1,0:T(2,128)S(1)} %copy-done.74), custom_call_target="tpu_custom_call" | custom-call | flops 4831838208 | bytes 3145728 | tf_op jit(solution)/shard_map/attention_forward/pallas_call | solution.py:303
  147.6 8.9 %attention_forward.3 = (bf16[2,192,2048]{2,1,0:T(8,128)(2,1)S(1)}, f32[2,192,2048]{2,1,0:T(8,128)S(1)}) custom-call(bf16[2,192,2048]{2,1,0:T(8,128)(2,1)S(1)} %bitcast.224, bf16[2,1536,256]{2,1,0:T(8,128)(2,1)S(1)} %bitcast.219, s32[2,192,2]{2,1,0:T(8,128)S(1)} %copy-done.70, ...), custom_call_target="tpu_custom_call", output_to_operand_aliasing={{0}: (4, {}), {1}: (5, {})} | custom-call | flops 4831838208 | bytes 3145728 | tf_op jit(solution)/shard_map/attention_forward/pallas_call | solution.py:303
  158.1 5.5 all-gather.12.cloned.1.call-done.refs_6_.refs_8_.full_gate_ref
  169.8 5.9 project_back.1
  176.3 10.1 %collective-permute-done.26 = bf16[192,2048]{1,0:T(8,128)(2,1)S(1)} collective-permute-done((bf16[192,2048]{1,0:T(8,128)(2,1)S(1)}, bf16[192,2048]{1,0:T(8,128)(2,1)S(1)}, u32[]{:S(2)}, u32[]{:S(2)}) %collective-permute-start.26) | collective-permute-done | bytes 786464 | tf_op jit(solution)/shard_map/ppermute | solution.py:90
  210.3 13.3 %all-gather.14.cloned.1.call-done.refs_7_.refs_9_.full_up_ref = bf16[4,704,512]{2,1,0:T(8,128)(2,1)} async-done(((bf16[1,704,512]{2,1,0:T(8,128)(2,1)}), bf16[4,704,512]{2,1,0:T(8,128)(2,1)}) %all-gather.14.cloned.1.call-update) | async-done | bytes 2883600 | tf_op jit(solution)/shard_map/all_gather | solution.py:1219
  232.5 17.4 %hidden_units.2 = (bf16[1536,2048]{1,0:T(8,128)(2,1)}, f32[1536,704]{1,0:T(8,128)}, f32[1536,704]{1,0:T(8,128)}, bf16[1536,704]{1,0:T(8,128)(2,1)S(1)}, bf16[704,1536]{1,0:T(8,128)(2,1)S(1)}) custom-call(bf16[384,2048]{1,0:T(8,128)(2,1)} %multiply_convert_fusion.refs_0_, bf16[384,2048]{1,0:T(8,128)(2,1)} %collective-permute-done.31.refs_1_, ...), custom_call_target="tpu_custom_call" | custom-call | flops 8858370048 | bytes 12582912 | tf_op jit(solution)/shard_map/hidden_units/pallas_call | solution.py:674
  256.2 16.9 %hidden_units.3 = (bf16[1536,2048]{1,0:T(8,128)(2,1)}, f32[1536,704]{1,0:T(8,128)}, f32[1536,704]{1,0:T(8,128)}, bf16[1536,704]{1,0:T(8,128)(2,1)S(1)}, bf16[704,1536]{1,0:T(8,128)(2,1)S(1)}) custom-call(bf16[384,2048]{1,0:T(8,128)(2,1)} %collective-permute-done.32.refs_2_.refs_0_, bf16[384,2048]{1,0:T(8,128)(2,1)} %collective-permute-done.36.refs_3_.refs_1_, ...), custom_call_target="tpu_custom_call" | custom-call | flops 8858370048 | bytes 12582912 | tf_op jit(solution)/shard_map/hidden_units/pallas_call | solution.py:674
  276.1 12.6 %units_sum.2 = bf16[4,704,512]{2,1,0:T(8,128)(2,1)S(1)} custom-call(bf16[1536,2048]{1,0:T(8,128)(2,1)S(1)} %bitcast.228, bf16[1536,2048]{1,0:T(8,128)(2,1)} %slice_dynamic-update-slice_fusion.refs_1_.cot_ref, bf16[704,1536]{1,0:T(8,128)(2,1)S(1)} %get-tuple-element.369.refs_2_, bf16[704,1536]{1,0:T(8,128)(2,1)S(1)} %copy-done.91), custom_call_target="tpu_custom_call" | custom-call | flops 8858370048 | bytes 16908288 | tf_op jit(solution)/shard_map/units_sum/pallas_call | solution.py:839
  290.3 24.1 %hidden_back.2 = (bf16[704,1536]{1,0:T(8,128)(2,1)}, bf16[704,1536]{1,0:T(8,128)(2,1)}, bf16[4,192,2048]{2,1,0:T(8,128)(2,1)}, bf16[4,192,2048]{2,1,0:T(8,128)(2,1)}) custom-call(bf16[1536,2048]{1,0:T(8,128)(2,1)} %copy-done.73, f32[1536,704]{1,0:T(8,128)} %get-tuple-element.379.gate_ref, f32[1536,704]{1,0:T(8,128)} %get-tuple-element.380.up_ref, ...), custom_call_target="tpu_custom_call" | custom-call | flops 13287555072 | bytes 12582912 | tf_op jit(solution)/shard_map/hidden_back/pallas_call | solution.py:754
  314.7 25.1 %hidden_back.3 = (bf16[704,1536]{1,0:T(8,128)(2,1)}, bf16[704,1536]{1,0:T(8,128)(2,1)}, bf16[4,192,2048]{2,1,0:T(8,128)(2,1)}, bf16[4,192,2048]{2,1,0:T(8,128)(2,1)}) custom-call(bf16[1536,2048]{1,0:T(8,128)(2,1)} %slice_dynamic-update-slice_fusion.refs_1_.cot_ref, f32[1536,704]{1,0:T(8,128)} %get-tuple-element.387.gate_ref, ...), custom_call_target="tpu_custom_call" | custom-call | flops 13287555072 | bytes 12582912 | tf_op jit(solution)/shard_map/hidden_back/pallas_call | solution.py:754
  340.2 3.6 add_convert_fusion.2
  346.1 21.3 %units_sum.3 = (bf16[4,704,512]{2,1,0:T(8,128)(2,1)S(1)}, bf16[4,704,512]{2,1,0:T(8,128)(2,1)S(1)}) custom-call(bf16[1536,2048]{1,0:T(8,128)(2,1)} %get-tuple-element.371.refs_0_, bf16[1536,2048]{1,0:T(8,128)(2,1)} %get-tuple-element.375.refs_1_, bf16[704,1536]{1,0:T(8,128)(2,1)S(1)} %copy-done.92, bf16[704,1536]{1,0:T(8,128)(2,1)S(1)} %copy-done.94, ...), custom_call_target="tpu_custom_call" | custom-call | flops 17716740096 | bytes 33816576 | tf_op jit(solution)/shard_map/units_sum/pallas_call | solution.py:839
  370.6 9.7 %collective-permute-done.41 = bf16[2,192,2048]{2,1,0:T(8,128)(2,1)S(1)} collective-permute-done((bf16[2,192,2048]{2,1,0:T(8,128)(2,1)S(1)}, bf16[2,192,2048]{2,1,0:T(8,128)(2,1)S(1)}, u32[]{:S(2)}, u32[]{:S(2)}) %collective-permute-start.41) | collective-permute-done | bytes 1572896 | tf_op jit(solution)/shard_map/ppermute | solution.py:90
  387.1 6.9 hidden_out.2
  395.7 6.5 hidden_out.3
  406.5 3.8 bitcast_add_fusion.4
  414.4 4.1 blocks_sum.5
  419.9 4.1 blocks_sum.4
  427.9 3.7 slice_bitcast_fusion.1
  435.4 5.5 add_convert_fusion
  443.1 8.4 %project.5 = bf16[384,2048]{1,0:T(8,128)(2,1)S(1)} custom-call(bf16[2048,256]{1,0:T(8,128)(2,1)S(1)} %copy-done.59, bf16[2048,256]{1,0:T(8,128)(2,1)} %collective-permute-done.11.refs_1_, bf16[2048,256]{1,0:T(8,128)(2,1)} %collective-permute-done.12.refs_2_, bf16[2048,256]{1,0:T(8,128)(2,1)} %collective-permute-done.21.refs_3_, ...), custom_call_target="tpu_custom_call" | custom-call | flops 3221225472 | bytes 11534336 | tf_op jit(solution)/shard_map/project/pallas_call | solution.py:504
  452.7 4.2 add_convert_fusion.6
  464.1 4.5 all-to-all-start
  475.7 14.2 %attention_backward.2 = (bf16[2,192,2048]{2,1,0:T(8,128)(2,1)S(1)}, bf16[2,1536,256]{2,1,0:T(8,128)(2,1)S(1)}) custom-call(bf16[2,192,2048]{2,1,0:T(8,128)(2,1)S(1)} %bitcast.225, bf16[2,192,2048]{2,1,0:T(8,128)(2,1)S(1)} %bitcast.233, f32[2,192,2048]{2,1,0:T(8,128)S(1)} %copy-done.84, bf16[2,1536,256]{2,1,0:T(8,128)(2,1)S(1)} %bitcast.220, ...), custom_call_target="tpu_custom_call" | custom-call | flops 12079595520 | bytes 4718592 | tf_op jit(solution)/shard_map/attention_backward/pallas_call | solution.py:401
  490.0 4.1 fusion.23
  498.2 14.2 %attention_backward.3 = (bf16[2,192,2048]{2,1,0:T(8,128)(2,1)S(1)}, bf16[2,1536,256]{2,1,0:T(8,128)(2,1)S(1)}) custom-call(bf16[2,192,2048]{2,1,0:T(8,128)(2,1)S(1)} %bitcast.226, bf16[2,192,2048]{2,1,0:T(8,128)(2,1)S(1)} %bitcast.234, f32[2,192,2048]{2,1,0:T(8,128)S(1)} %copy-done.85, ...), custom_call_target="tpu_custom_call", output_to_operand_aliasing={{0}: (8, {}), {1}: (9, {})} | custom-call | flops 12079595520 | bytes 4718592 | tf_op jit(solution)/shard_map/attention_backward/pallas_call | solution.py:401
  524.9 4.1 blocks_sum.7
  530.4 4.5 blocks_sum.6
  536.6 3.6 bitcast_add_fusion.2
  551.8 4.3 all-to-all-start.1
  572.0 4.3 collective-permute-start.63
  583.2 19.4 %back_and_factor.1 = (f32[384,2048]{1,0:T(8,128)}, bf16[352,352]{1,0:T(8,128)(2,1)}) custom-call(s32[1]{0:T(128)S(6)} %add.537.refs_0_, bf16[2048,256]{1,0:T(8,128)(2,1)} %all-gather.16.cloned.1.call-done, bf16[2048,256]{1,0:T(8,128)(2,1)} %collective-permute-done.4.refs_1_.refs_2_, bf16[2048,256]{1,0:T(8,128)(2,1)} %collective-permute-done.5.refs_2_.refs_3_, ...), custom_call_target="tpu_custom_call" | custom-call | flops 7582646272 | bytes 13107200 | tf_op jit(solution)/shard_map/back_and_factor/pallas_call | solution.py:1145
  609.5 4.7 collective-permute-start.67
  615.4 4.2 all-to-all-start.2
  638.4 5.0 fusion.7
  647.2 19.3 %all-to-all-start.3 = ((bf16[4,96,256]{2,1,0:T(8,128)(2,1)}), bf16[4,96,256]{2,1,0:T(8,128)(2,1)}, u32[]{:S(2)}, u32[]{:S(2)}) async-start(bf16[4,96,256]{2,1,0:T(8,128)(2,1)} %pad_maximum_fusion.8), calls=%async_computation.7 | async-start | bytes 393216 | tf_op jit(solution)/shard_map/all_to_all | solution.py:1459
  683.4 5.8 small_update.2
  690.2 9.6 %all-gather.4 = bf16[768,256]{1,0:T(8,128)(2,1)S(1)} all-gather(bf16[96,256]{1,0:T(8,128)(2,1)S(1)} %pad_maximum_fusion.9), channel_id=6, replica_groups=mesh['dp'=4,'mp'=8] {'mp'}, dimensions={0}, use_global_device_ids=true | all-gather | bytes 442368 | tf_op jit(solution)/shard_map/all_gather | solution.py:1473
  718.6 4.9 collective-permute-done.79.refs_10_
  723.6 10.9 %small_update.3 = (f32[512,256]{1,0:T(8,128)}, f32[512,256]{1,0:T(8,128)}) custom-call(f32[512,256]{1,0:T(8,128)S(1)} %multiply_add_fusion.refs_0_, f32[512,256]{1,0:T(8,128)S(1)} %copy-done.68, f32[512,256]{1,0:T(8,128)S(1)} %get-tuple-element.544.refs_0_.refs_2_, f32[512,256]{1,0:T(8,128)S(1)} %copy-done.66, bf16[1,272,256]{2,1,0:T(8,128)(2,1)} %packed_grams.8.refs_4_, ...), custom_call_target="tpu_custom_call" | custom-call | flops 2254438400 | bytes 3145728 | tf_op jit(solution)/shard_map/small_update/pallas_call | solution.py:1082
  (604 shorter events, 276.3 us)
Async XLA Ops:
  7.2 33.9 %all-gather.16.cloned.1.call-start = ((), (), s32[]{:S(2)}) async-start(), calls=%async_computation.16 | async-start | bytes 1310720 | tf_op jit(solution)/shard_map/all_gather | solution.py:1219
  7.8 37.9 %collective-permute-start.1 = (bf16[384,2048]{1,0:T(8,128)(2,1)}, bf16[384,2048]{1,0:T(8,128)(2,1)}, u32[]{:S(2)}, u32[]{:S(2)}) collective-permute-start(bf16[384,2048]{1,0:T(8,128)(2,1)} %bitcast.245), channel_id=1, source_target_pairs={{0,4},{1,5},{2,6},{3,7},{4,0},{5,1},{6,2},{7,3},{8,12},{9,13},{10,... | collective-permute-start | bytes 4718600 | tf_op jit(solution)/shard_map/ppermute | solution.py:90
  10.4 36.8 %collective-permute-start.2 = (bf16[384,2048]{1,0:T(8,128)(2,1)}, bf16[384,2048]{1,0:T(8,128)(2,1)}, u32[]{:S(2)}, u32[]{:S(2)}) collective-permute-start(bf16[384,2048]{1,0:T(8,128)(2,1)} %bitcast.246), channel_id=1, source_target_pairs={{0,2},{1,3},{2,0},{3,1},{4,6},{5,7},{6,4},{7,5},{8,10},{9,11},{10,... | collective-permute-start | bytes 4718600 | tf_op jit(solution)/shard_map/ppermute | solution.py:90
  13.7 59.7 %all-gather.18.cloned.1.call-start = ((), (), s32[]{:S(2)}) async-start(), calls=%async_computation.17 | async-start | bytes 1310720 | tf_op jit(solution)/shard_map/all_gather | solution.py:1219
  41.1 71.5 %all-gather.20.cloned.1.call-start = ((), (), s32[]{:S(2)}) async-start(), calls=%async_computation.18 | async-start | bytes 1310720 | tf_op jit(solution)/shard_map/all_gather | solution.py:1219
  47.4 25.9 %collective-permute-start.5 = (bf16[2048,256]{1,0:T(8,128)(2,1)}, bf16[2048,256]{1,0:T(8,128)(2,1)}, u32[]{:S(2)}, u32[]{:S(2)}) collective-permute-start(bf16[2048,256]{1,0:T(8,128)(2,1)} %all-gather.16.cloned.1.call-done), channel_id=1, source_target_pairs={{0,2},{1,3},{2,0},{3,1},{4,6},{5,7},{6,4},{7,5},{8,10},{9,11},{10,... | collective-permute-start | bytes 3145736 | tf_op jit(solution)/shard_map/ppermute | solution.py:90
  73.4 90.3 %all-gather.12.cloned.1.call-start = ((), (), s32[]{:S(2)}) async-start(), calls=%async_computation.9 | async-start | bytes 3604480 | tf_op jit(solution)/shard_map/all_gather | solution.py:1219
  76.5 147.0 %all-gather.14.cloned.1.call-start = ((), (), s32[]{:S(2)}) async-start(), calls=%async_computation.10 | async-start | bytes 3604480 | tf_op jit(solution)/shard_map/all_gather | solution.py:1219
  113.1 27.9 %collective-permute-start.10 = (bf16[2048,256]{1,0:T(8,128)(2,1)}, bf16[2048,256]{1,0:T(8,128)(2,1)}, u32[]{:S(2)}, u32[]{:S(2)}) collective-permute-start(bf16[2048,256]{1,0:T(8,128)(2,1)} %all-gather.20.cloned.1.call-done), channel_id=1, source_target_pairs={{0,4},{1,5},{2,6},{3,7},{4,0},{5,1},{6,2},{7,3},{8,12},{9,13},{10,... | collective-permute-start | bytes 3145736 | tf_op jit(solution)/shard_map/ppermute | solution.py:90
  114.7 26.4 %collective-permute-start.11 = (bf16[2048,256]{1,0:T(8,128)(2,1)}, bf16[2048,256]{1,0:T(8,128)(2,1)}, u32[]{:S(2)}, u32[]{:S(2)}) collective-permute-start(bf16[2048,256]{1,0:T(8,128)(2,1)} %all-gather.20.cloned.1.call-done), channel_id=1, source_target_pairs={{0,1},{1,0},{2,3},{3,2},{4,5},{5,4},{6,7},{7,6},{8,9},{9,8},{10,11... | collective-permute-start | bytes 3145736 | tf_op jit(solution)/shard_map/ppermute | solution.py:90
  114.9 26.2 %collective-permute-start.12 = (bf16[2048,256]{1,0:T(8,128)(2,1)}, bf16[2048,256]{1,0:T(8,128)(2,1)}, u32[]{:S(2)}, u32[]{:S(2)}) collective-permute-start(bf16[2048,256]{1,0:T(8,128)(2,1)} %all-gather.20.cloned.1.call-done), channel_id=1, source_target_pairs={{0,2},{1,3},{2,0},{3,1},{4,6},{5,7},{6,4},{7,5},{8,10},{9,11},{10,... | collective-permute-start | bytes 3145736 | tf_op jit(solution)/shard_map/ppermute | solution.py:90
  116.4 30.1 %collective-permute-start.22 = (bf16[384,2048]{1,0:T(8,128)(2,1)}, bf16[384,2048]{1,0:T(8,128)(2,1)}, u32[]{:S(2)}, u32[]{:S(2)}) collective-permute-start(bf16[384,2048]{1,0:T(8,128)(2,1)} %collective-permute-done.1), channel_id=1, source_target_pairs={{0,1},{1,0},{2,3},{3,2},{4,5},{5,4},{6,7},{7,6},{8,9},{9,8},{10,11... | collective-permute-start | bytes 4718600 | tf_op jit(solution)/shard_map/ppermute | solution.py:90
  119.3 44.3 %collective-permute-start.23 = (bf16[384,2048]{1,0:T(8,128)(2,1)}, bf16[384,2048]{1,0:T(8,128)(2,1)}, u32[]{:S(2)}, u32[]{:S(2)}) collective-permute-start(bf16[384,2048]{1,0:T(8,128)(2,1)} %collective-permute-done.2), channel_id=1, source_target_pairs={{0,1},{1,0},{2,3},{3,2},{4,5},{5,4},{6,7},{7,6},{8,9},{9,8},{10,11... | collective-permute-start | bytes 4718600 | tf_op jit(solution)/shard_map/ppermute | solution.py:90
  164.3 126.0 %all-gather.22.cloned.1.call-start = ((), (), s32[]{:S(2)}) async-start(), calls=%async_computation.19 | async-start | bytes 3604480 | tf_op jit(solution)/shard_map/all_gather | solution.py:1219
  187.9 37.1 %collective-permute-start.30 = (bf16[384,2048]{1,0:T(8,128)(2,1)}, bf16[384,2048]{1,0:T(8,128)(2,1)}, u32[]{:S(2)}, u32[]{:S(2)}) collective-permute-start(bf16[384,2048]{1,0:T(8,128)(2,1)} %multiply_convert_fusion.refs_0_), channel_id=1, source_target_pairs={{0,4},{1,5},{2,6},{3,7},{4,0},{5,1},{6,2},{7,3},{8,12},{9,13},{10,... | collective-permute-start | bytes 4718600 | tf_op jit(solution)/shard_map/ppermute | solution.py:90
  189.4 35.7 %collective-permute-start.31 = (bf16[384,2048]{1,0:T(8,128)(2,1)}, bf16[384,2048]{1,0:T(8,128)(2,1)}, u32[]{:S(2)}, u32[]{:S(2)}) collective-permute-start(bf16[384,2048]{1,0:T(8,128)(2,1)} %multiply_convert_fusion.refs_0_), channel_id=1, source_target_pairs={{0,1},{1,0},{2,3},{3,2},{4,5},{5,4},{6,7},{7,6},{8,9},{9,8},{10,11... | collective-permute-start | bytes 4718600 | tf_op jit(solution)/shard_map/ppermute | solution.py:90
  189.6 36.9 %collective-permute-start.32 = (bf16[384,2048]{1,0:T(8,128)(2,1)}, bf16[384,2048]{1,0:T(8,128)(2,1)}, u32[]{:S(2)}, u32[]{:S(2)}) collective-permute-start(bf16[384,2048]{1,0:T(8,128)(2,1)} %multiply_convert_fusion.refs_0_), channel_id=1, source_target_pairs={{0,2},{1,3},{2,0},{3,1},{4,6},{5,7},{6,4},{7,5},{8,10},{9,11},{10,... | collective-permute-start | bytes 4718600 | tf_op jit(solution)/shard_map/ppermute | solution.py:90
  228.0 153.8 %reduce-scatter.6.cloned.1.call-start = ((), (), s32[]{:S(2)}) async-start(), calls=%async_computation.11 | async-start | bytes 3604480 | tf_op jit(solution)/shard_map/reduce_scatter | solution.py:1345
  314.4 25.4 %collective-permute-start.39 = (bf16[4,192,2048]{2,1,0:T(8,128)(2,1)}, bf16[4,192,2048]{2,1,0:T(8,128)(2,1)}, u32[]{:S(2)}, u32[]{:S(2)}) collective-permute-start(bf16[4,192,2048]{2,1,0:T(8,128)(2,1)} %get-tuple-element.386), channel_id=1, source_target_pairs={{0,1},{1,0},{2,3},{3,2},{4,5},{5,4},{6,7},{7,6},{8,9},{9,8},{10,11... | collective-permute-start | bytes 9437192 | tf_op jit(solution)/shard_map/ppermute | solution.py:90
  314.6 138.1 %reduce-scatter.8.cloned.1.call-start = ((), (), s32[]{:S(2)}) async-start(), calls=%async_computation.12 | async-start | bytes 3604480 | tf_op jit(solution)/shard_map/reduce_scatter | solution.py:1345
  339.8 42.0 %collective-permute-start.40 = (bf16[4,192,2048]{2,1,0:T(8,128)(2,1)}, bf16[4,192,2048]{2,1,0:T(8,128)(2,1)}, u32[]{:S(2)}, u32[]{:S(2)}) collective-permute-start(bf16[4,192,2048]{2,1,0:T(8,128)(2,1)} %get-tuple-element.390), channel_id=1, source_target_pairs={{0,1},{1,0},{2,3},{3,2},{4,5},{5,4},{6,7},{7,6},{8,9},{9,8},{10,11... | collective-permute-start | bytes 9437192 | tf_op jit(solution)/shard_map/ppermute | solution.py:90
  343.9 36.5 %collective-permute-start.41 = (bf16[2,192,2048]{2,1,0:T(8,128)(2,1)S(1)}, bf16[2,192,2048]{2,1,0:T(8,128)(2,1)S(1)}, u32[]{:S(2)}, u32[]{:S(2)}) collective-permute-start(bf16[2,192,2048]{2,1,0:T(8,128)(2,1)S(1)} %get-tuple-element.397), channel_id=1, source_target_pairs={{0,4},{1,5},{2,6},{3,7},{4,0},{5,1},{6,2},{7,3},{8,12},{9,13},{10,... | collective-permute-start | bytes 4718600 | tf_op jit(solution)/shard_map/ppermute | solution.py:90
  345.5 36.3 %collective-permute-start.42 = (bf16[2,192,2048]{2,1,0:T(8,128)(2,1)S(1)}, bf16[2,192,2048]{2,1,0:T(8,128)(2,1)}, u32[]{:S(2)}, u32[]{:S(2)}) collective-permute-start(bf16[2,192,2048]{2,1,0:T(8,128)(2,1)S(1)} %get-tuple-element.398), channel_id=1, source_target_pairs={{0,2},{1,3},{2,0},{3,1},{4,6},{5,7},{6,4},{7,5},{8,10},{9,11},{10,... | collective-permute-start | bytes 4718600 | tf_op jit(solution)/shard_map/ppermute | solution.py:90
  381.8 135.3 %reduce-scatter.10.cloned.1.call-start = ((), (), s32[]{:S(2)}) async-start(), calls=%async_computation.13 | async-start | bytes 3604480 | tf_op jit(solution)/shard_map/reduce_scatter | solution.py:1345
  425.3 27.4 %collective-permute-start.47 = (bf16[4,1024,256]{2,1,0:T(8,128)(2,1)}, bf16[4,1024,256]{2,1,0:T(8,128)(2,1)}, u32[]{:S(2)}, u32[]{:S(2)}) collective-permute-start(bf16[4,1024,256]{2,1,0:T(8,128)(2,1)} %get-tuple-element.433), channel_id=1, source_target_pairs={{0,1},{1,0},{2,3},{3,2},{4,5},{5,4},{6,7},{7,6},{8,9},{9,8},{10,11... | collective-permute-start | bytes 6291464 | tf_op jit(solution)/shard_map/ppermute | solution.py:90
  425.3 27.3 %collective-permute-start.48 = (bf16[4,1024,256]{2,1,0:T(8,128)(2,1)}, bf16[4,1024,256]{2,1,0:T(8,128)(2,1)}, u32[]{:S(2)}, u32[]{:S(2)}) collective-permute-start(bf16[4,1024,256]{2,1,0:T(8,128)(2,1)} %get-tuple-element.434), channel_id=1, source_target_pairs={{0,1},{1,0},{2,3},{3,2},{4,5},{5,4},{6,7},{7,6},{8,9},{9,8},{10,11... | collective-permute-start | bytes 6291464 | tf_op jit(solution)/shard_map/ppermute | solution.py:90
  440.9 49.0 %collective-permute-start.49 = (bf16[2,192,2048]{2,1,0:T(8,128)(2,1)}, bf16[2,192,2048]{2,1,0:T(8,128)(2,1)}, u32[]{:S(2)}, u32[]{:S(2)}) collective-permute-start(bf16[2,192,2048]{2,1,0:T(8,128)(2,1)} %get-tuple-element.450), channel_id=1, source_target_pairs={{0,4},{1,5},{2,6},{3,7},{4,0},{5,1},{6,2},{7,3},{8,12},{9,13},{10,... | collective-permute-start | bytes 4718600 | tf_op jit(solution)/shard_map/ppermute | solution.py:90
  442.3 47.6 %collective-permute-start.50 = (bf16[2,192,2048]{2,1,0:T(8,128)(2,1)}, bf16[2,192,2048]{2,1,0:T(8,128)(2,1)}, u32[]{:S(2)}, u32[]{:S(2)}) collective-permute-start(bf16[2,192,2048]{2,1,0:T(8,128)(2,1)} %get-tuple-element.451), channel_id=1, source_target_pairs={{0,2},{1,3},{2,0},{3,1},{4,6},{5,7},{6,4},{7,5},{8,10},{9,11},{10,... | collective-permute-start | bytes 4718600 | tf_op jit(solution)/shard_map/ppermute | solution.py:90
  464.1 53.0 %all-to-all-start = ((bf16[4,368,352]{1,2,0:T(8,128)(2,1)}), bf16[4,368,352]{1,2,0:T(8,128)(2,1)}, u32[]{:S(2)}, u32[]{:S(2)}) async-start(bf16[4,368,352]{1,2,0:T(8,128)(2,1)} %copy.65), calls=%async_computation.2 | async-start | bytes 2162688 | tf_op jit(solution)/shard_map/all_to_all | solution.py:1388
  494.1 26.4 %collective-permute-start.53 = (bf16[2,1024,256]{2,1,0:T(8,128)(2,1)}, bf16[2,1024,256]{2,1,0:T(8,128)(2,1)}, u32[]{:S(2)}, u32[]{:S(2)}) collective-permute-start(bf16[2,1024,256]{2,1,0:T(8,128)(2,1)} %get-tuple-element.469), channel_id=1, source_target_pairs={{0,4},{1,5},{2,6},{3,7},{4,0},{5,1},{6,2},{7,3},{8,12},{9,13},{10,... | collective-permute-start | bytes 3145736 | tf_op jit(solution)/shard_map/ppermute | solution.py:90
  495.2 26.4 %collective-permute-start.54 = (bf16[2,1024,256]{2,1,0:T(8,128)(2,1)}, bf16[2,1024,256]{2,1,0:T(8,128)(2,1)}, u32[]{:S(2)}, u32[]{:S(2)}) collective-permute-start(bf16[2,1024,256]{2,1,0:T(8,128)(2,1)} %get-tuple-element.470), channel_id=1, source_target_pairs={{0,2},{1,3},{2,0},{3,1},{4,6},{5,7},{6,4},{7,5},{8,10},{9,11},{10,... | collective-permute-start | bytes 3145736 | tf_op jit(solution)/shard_map/ppermute | solution.py:90
  495.8 39.9 %collective-permute-start.51 = (bf16[192,2048]{1,0:T(8,128)(2,1)}, bf16[192,2048]{1,0:T(8,128)(2,1)}, u32[]{:S(2)}, u32[]{:S(2)}) collective-permute-start(bf16[192,2048]{1,0:T(8,128)(2,1)} %get-tuple-element.456), channel_id=1, source_target_pairs={{0,4},{1,5},{2,6},{3,7},{4,0},{5,1},{6,2},{7,3},{8,12},{9,13},{10,... | collective-permute-start | bytes 2359304 | tf_op jit(solution)/shard_map/ppermute | solution.py:90
  497.2 39.5 %collective-permute-start.52 = (bf16[192,2048]{1,0:T(8,128)(2,1)}, bf16[192,2048]{1,0:T(8,128)(2,1)}, u32[]{:S(2)}, u32[]{:S(2)}) collective-permute-start(bf16[192,2048]{1,0:T(8,128)(2,1)} %get-tuple-element.457), channel_id=1, source_target_pairs={{0,2},{1,3},{2,0},{3,1},{4,6},{5,7},{6,4},{7,5},{8,10},{9,11},{10,... | collective-permute-start | bytes 2359304 | tf_op jit(solution)/shard_map/ppermute | solution.py:90
  530.4 33.5 %collective-permute-start.56 = (bf16[4,1024,256]{2,1,0:T(8,128)(2,1)}, bf16[4,1024,256]{2,1,0:T(8,128)(2,1)}, u32[]{:S(2)}, u32[]{:S(2)}) collective-permute-start(bf16[4,1024,256]{2,1,0:T(8,128)(2,1)} %get-tuple-element.481), channel_id=1, source_target_pairs={{0,1},{1,0},{2,3},{3,2},{4,5},{5,4},{6,7},{7,6},{8,9},{9,8},{10,11... | collective-permute-start | bytes 6291464 | tf_op jit(solution)/shard_map/ppermute | solution.py:90
  534.9 29.0 %collective-permute-start.55 = (bf16[4,1024,256]{2,1,0:T(8,128)(2,1)}, bf16[4,1024,256]{2,1,0:T(8,128)(2,1)}, u32[]{:S(2)}, u32[]{:S(2)}) collective-permute-start(bf16[4,1024,256]{2,1,0:T(8,128)(2,1)} %get-tuple-element.480), channel_id=1, source_target_pairs={{0,1},{1,0},{2,3},{3,2},{4,5},{5,4},{6,7},{7,6},{8,9},{9,8},{10,11... | collective-permute-start | bytes 6291464 | tf_op jit(solution)/shard_map/ppermute | solution.py:90
  551.8 50.8 %all-to-all-start.1 = ((bf16[8,2,192,256]{3,2,1,0:T(8,128)(2,1)}), bf16[8,2,192,256]{3,2,1,0:T(8,128)(2,1)}, u32[]{:S(2)}, u32[]{:S(2)}) async-start(bf16[8,2,192,256]{3,2,1,0:T(8,128)(2,1)} %gather_fusion.1), calls=%async_computation.4 | async-start | bytes 3145728 | tf_op jit(solution)/shard_map/all_to_all | solution.py:1412
  556.1 110.3 %reduce-scatter.14.cloned.1.call-start = ((), (), s32[]{:S(2)}) async-start(), calls=%async_computation.15 | async-start | bytes 1310720 | tf_op jit(solution)/shard_map/reduce_scatter | solution.py:1345
  567.5 35.1 %collective-permute-start.59 = (bf16[2,1024,256]{2,1,0:T(8,128)(2,1)}, bf16[2,1024,256]{2,1,0:T(8,128)(2,1)}, u32[]{:S(2)}, u32[]{:S(2)}) collective-permute-start(bf16[2,1024,256]{2,1,0:T(8,128)(2,1)} %get-tuple-element.495), channel_id=1, source_target_pairs={{0,4},{1,5},{2,6},{3,7},{4,0},{5,1},{6,2},{7,3},{8,12},{9,13},{10,... | collective-permute-start | bytes 3145736 | tf_op jit(solution)/shard_map/ppermute | solution.py:90
  569.4 33.2 %collective-permute-start.60 = (bf16[2,1024,256]{2,1,0:T(8,128)(2,1)}, bf16[2,1024,256]{2,1,0:T(8,128)(2,1)}, u32[]{:S(2)}, u32[]{:S(2)}) collective-permute-start(bf16[2,1024,256]{2,1,0:T(8,128)(2,1)} %get-tuple-element.496), channel_id=1, source_target_pairs={{0,2},{1,3},{2,0},{3,1},{4,6},{5,7},{6,4},{7,5},{8,10},{9,11},{10,... | collective-permute-start | bytes 3145736 | tf_op jit(solution)/shard_map/ppermute | solution.py:90
  572.0 37.5 %collective-permute-start.63 = (bf16[368,352]{1,0:T(8,128)(2,1)}, bf16[368,352]{1,0:T(8,128)(2,1)}, u32[]{:S(2)}, u32[]{:S(2)}) collective-permute-start(bf16[368,352]{1,0:T(8,128)(2,1)} %get-tuple-element.597), channel_id=1, source_target_pairs={{0,8},{8,16},{1,9},{9,17},{2,10},{10,18},{3,11},{11,19},{4,12},{12... | collective-permute-start | bytes 777224 | tf_op jit(solution)/shard_map/ppermute | solution.py:1114
  576.3 33.3 %collective-permute-start.64 = (bf16[368,352]{1,0:T(8,128)(2,1)}, bf16[368,352]{1,0:T(8,128)(2,1)}, u32[]{:S(2)}, u32[]{:S(2)}) collective-permute-start(bf16[368,352]{1,0:T(8,128)(2,1)} %get-tuple-element.595), channel_id=1, source_target_pairs={{24,8},{0,16},{25,9},{1,17},{26,10},{2,18},{27,11},{3,19},{28,12},... | collective-permute-start | bytes 777224 | tf_op jit(solution)/shard_map/ppermute | solution.py:1114
  578.6 35.7 %collective-permute-start.65 = (bf16[368,352]{1,0:T(8,128)(2,1)}, bf16[368,352]{1,0:T(8,128)(2,1)}, u32[]{:S(2)}, u32[]{:S(2)}) collective-permute-start(bf16[368,352]{1,0:T(8,128)(2,1)} %get-tuple-element.594), channel_id=1, source_target_pairs={{16,8},{24,16},{17,9},{25,17},{18,10},{26,18},{19,11},{27,19},{20,... | collective-permute-start | bytes 777224 | tf_op jit(solution)/shard_map/ppermute | solution.py:1114
  615.4 28.0 %all-to-all-start.2 = ((bf16[8,4,64,256]{3,2,1,0:T(8,128)(2,1)}), bf16[8,4,64,256]{3,2,1,0:T(8,128)(2,1)}, u32[]{:S(2)}, u32[]{:S(2)}) async-start(bf16[8,4,64,256]{3,2,1,0:T(8,128)(2,1)} %bitcast.207), calls=%async_computation.5 | async-start | bytes 2097152 | tf_op jit(solution)/shard_map/all_to_all | solution.py:1441
  619.7 87.3 %reduce-scatter.12.cloned.1.call-start = ((), (), s32[]{:S(2)}) async-start(), calls=%async_computation.14 | async-start | bytes 1310720 | tf_op jit(solution)/shard_map/reduce_scatter | solution.py:1345
  622.0 51.3 %collective-permute-start.72 = (bf16[352,352]{1,0:T(8,128)(2,1)}, bf16[352,352]{1,0:T(8,128)(2,1)}, u32[]{:S(2)}, u32[]{:S(2)}) collective-permute-start(bf16[352,352]{1,0:T(8,128)(2,1)} %block_factor.1.refs_0_), channel_id=1, source_target_pairs={{8,16},{16,24},{9,17},{17,25},{10,18},{18,26},{11,19},{19,27},{12,... | collective-permute-start | bytes 743432 | tf_op jit(solution)/shard_map/ppermute | solution.py:1122
  623.5 54.8 %collective-permute-start.73 = (bf16[352,352]{1,0:T(8,128)(2,1)}, bf16[352,352]{1,0:T(8,128)(2,1)}, u32[]{:S(2)}, u32[]{:S(2)}) collective-permute-start(bf16[352,352]{1,0:T(8,128)(2,1)} %block_factor.1.refs_0_), channel_id=1, source_target_pairs={{8,24},{16,0},{9,25},{17,1},{10,26},{18,2},{11,27},{19,3},{12,28},... | collective-permute-start | bytes 743432 | tf_op jit(solution)/shard_map/ppermute | solution.py:1122
  624.8 53.5 %collective-permute-start.74 = (bf16[352,352]{1,0:T(8,128)(2,1)}, bf16[352,352]{1,0:T(8,128)(2,1)}, u32[]{:S(2)}, u32[]{:S(2)}) collective-permute-start(bf16[352,352]{1,0:T(8,128)(2,1)} %block_factor.1.refs_0_), channel_id=1, source_target_pairs={{8,0},{16,8},{9,1},{17,9},{10,2},{18,10},{11,3},{19,11},{12,4},{20... | collective-permute-start | bytes 743432 | tf_op jit(solution)/shard_map/ppermute | solution.py:1122
  647.2 42.0 %all-to-all-start.3 = ((bf16[4,96,256]{2,1,0:T(8,128)(2,1)}), bf16[4,96,256]{2,1,0:T(8,128)(2,1)}, u32[]{:S(2)}, u32[]{:S(2)}) async-start(bf16[4,96,256]{2,1,0:T(8,128)(2,1)} %pad_maximum_fusion.8), calls=%async_computation.7 | async-start | bytes 393216 | tf_op jit(solution)/shard_map/all_to_all | solution.py:1459
  (188 other events, 2414.4 us)
Sparse Core Ops, SparseCore 0:
  13.8 27.2 all-gather.15
  43.3 27.4 all-gather.17
  73.5 29.3 all-gather.19
  104.9 58.6 all-gather.11
  165.6 57.8 all-gather.13
  228.1 56.9 all-gather.21
  314.8 54.0 reduce-scatter.5
  381.9 53.7 reduce-scatter.7
  438.6 73.1 reduce-scatter.9
  583.3 27.4 reduce-scatter.13
  632.8 46.4 reduce-scatter.11
